TPU v7x, 32 devices: a whole 2x2x4 slice. The times are simulated.
32 devices in a mesh: dp: 16 (over z, y, x), mp: 2 (over core).
Axes of the slice: x: 2, y: 2, z: 4, core: 2. Of those that a mesh axis runs over, the one named last changes fastest.
Arguments:
- tokens: bfloat16 [8192, 2048], P('dp'), may hold values from -6 to 6
- q_weight: bfloat16 [2048, 256], P('dp', 'mp'), may hold values from -0.125 to 0.125
- k_weight: bfloat16 [2048, 256], P('dp', 'mp'), may hold values from -0.125 to 0.125
- v_weight: bfloat16 [2048, 2048], P('dp', 'mp'), may hold values from -0.125 to 0.125
- adapter_down: bfloat16 [2048, 256], P(None, 'mp'), may hold values from -0.125 to 0.125
- adapter_up: bfloat16 [256, 2048], P(None, 'mp'), may hold values from -1.5 to 1.5
- lengths: int32 [4], replicated, may hold values from 1 to 4096, 8192 in all
- adapter_ids: int32 [4], replicated, may hold values from 0 to 15
- head_gain: float32 [2048], P('mp'), may hold values from 0.1 to 1.9
- out_weight: bfloat16 [2048, 2048], P('mp', 'dp'), may hold values from -0.125 to 0.125
Outputs:
- layer_out: bfloat16 [8192, 2048], P('dp', 'mp')
Inputs may be any that keep to these rules, and one draw needn't show every extreme that they name: The lengths sum to 8192 and the longest request has exactly 8192 // 2 tokens.
All inputs are finite; a program needn't handle non-finite values.
Results may differ from a plain program's by a relative error of at most 0.022.
Values may be sent and summed in bfloat16 or wider, within the bound.
No kernel may reach another device: no remote copies, remote signals or barrier semaphores. Data moves between devices by JAX's collectives and lax.ppermute only.
A program may use at most 128 MiB of HBM per device.

v0:
```python
import math

import jax
import jax.numpy as jnp
from jax import lax
from jax.sharding import PartitionSpec as P

F = 16
R = 16


EPSILON = 1e-05


def carried_in(value, axis, combine, identity):
    length, place = (lax.axis_size(axis), lax.axis_index(axis))
    everything = jax.tree.map(
        lambda part, kind: lax.all_gather(part.astype(kind), axis),
        value,
        (jnp.bfloat16, jnp.bfloat16),
    )
    start = jax.tree.map(
        lambda part, zero: jnp.broadcast_to(jnp.asarray(zero, part.dtype), part.shape),
        value,
        identity,
    )

    def turn(k, before):
        reached = k < place
        new = combine(
            before, jax.tree.map(lambda part, own: part[k].astype(own.dtype), everything, value)
        )
        return jax.tree.map(lambda a, b: jnp.where(reached, a, b), new, before)

    return lax.fori_loop(0, length, turn, start)


def taylor(inputs):
    squares = (inputs[..., :, None] * inputs[..., None, :]).reshape(
        inputs.shape[:-1] + (inputs.shape[-1] * inputs.shape[-1],)
    )
    constant = jnp.ones(inputs.shape[:-1] + (1,), jnp.float32)
    return jnp.concatenate([constant, 0.5 * inputs, squares * (0.25 / math.sqrt(2.0))], axis=-1)


def token_tables(lengths, adapter_ids, positions):
    bounds = jnp.cumsum(lengths)
    request = jnp.sum((positions[:, None] >= bounds[None, :]).astype(jnp.int32), axis=1)
    openings = bounds - lengths
    starts = jnp.any(positions[:, None] == openings[None, :], axis=1)
    picked = request[:, None] == jnp.arange(lengths.shape[0], dtype=jnp.int32)[None, :]
    adapter = jnp.sum(jnp.where(picked, adapter_ids[None, :], 0), axis=1)
    return (request, starts, adapter)


def block_local(query, key_rows, values, request, starts):
    scores = jnp.einsum("ihd,jhd->hij", query, key_rows, preferred_element_type=jnp.float32) * 0.25
    weights = 1.0 + scores + 0.5 * scores * scores
    indexes = jnp.arange(request.shape[0], dtype=jnp.int32)
    allowed = (indexes[None, :] <= indexes[:, None]) & (request[None, :] == request[:, None])
    weights = jnp.where(allowed[None], weights, 0.0).astype(jnp.bfloat16)
    within = jnp.einsum("hij,jhe->ihe", weights, values, preferred_element_type=jnp.float32)
    query_map = taylor(query.astype(jnp.float32)).astype(jnp.bfloat16)
    key_map = taylor(key_rows.astype(jnp.float32)).astype(jnp.bfloat16)
    tail_mask = (request == request[-1]).astype(jnp.bfloat16)
    masked_keys = key_map * tail_mask[:, None, None]
    summary = jnp.einsum("ihf,ihe->hfe", masked_keys, values, preferred_element_type=jnp.float32)
    restart = jnp.max(starts.astype(jnp.float32))
    return (within, query_map, summary, restart)


def finish(within, query_map, carried, request, starts, gains):
    follows = ((request == request[0]) & jnp.logical_not(starts[0])).astype(jnp.float32)
    cross = jnp.einsum(
        "ihf,hfe->ihe", query_map, carried.astype(jnp.bfloat16), preferred_element_type=jnp.float32
    )
    combined = within + follows[:, None, None] * cross
    factor = lax.rsqrt(jnp.mean(combined * combined, axis=-1, keepdims=True) + EPSILON)
    return (combined * factor * gains[None]).astype(jnp.bfloat16)


def combine(earlier, later):
    return (
        jnp.maximum(earlier[0], later[0]),
        jnp.where(later[0] > 0, later[1], earlier[1] + later[1]),
    )


def per_device(
    tokens,
    q_weight,
    k_weight,
    v_weight,
    adapter_down,
    adapter_up,
    lengths,
    adapter_ids,
    head_gain,
    out_weight,
):
    row_count = tokens.shape[0]
    heads_here = q_weight.shape[1] // F
    value_width = v_weight.shape[1] // heads_here
    positions = lax.axis_index("dp") * row_count + jnp.arange(row_count, dtype=jnp.int32)
    request, starts, adapter = token_tables(lengths, adapter_ids, positions)
    query_sum = jnp.dot(
        tokens,
        lax.all_gather(q_weight, "dp", axis=0, tiled=True),
        preferred_element_type=jnp.float32,
    )
    key_sum = jnp.dot(
        tokens,
        lax.all_gather(k_weight, "dp", axis=0, tiled=True),
        preferred_element_type=jnp.float32,
    )
    value_sum = jnp.dot(
        tokens,
        lax.all_gather(v_weight, "dp", axis=0, tiled=True),
        preferred_element_type=jnp.float32,
    )
    query = query_sum.astype(jnp.bfloat16).reshape(row_count, heads_here, F)
    key_rows = key_sum.astype(jnp.bfloat16).reshape(row_count, heads_here, F)
    piece = lax.all_gather(adapter_down, "mp", axis=1, tiled=True)
    partial_low = jnp.dot(tokens, piece, preferred_element_type=jnp.float32)
    owners = jnp.arange(piece.shape[1], dtype=jnp.int32) // R
    low_rank = jnp.where(adapter[:, None] == owners[None, :], partial_low, 0.0).astype(jnp.bfloat16)
    values = value_sum + jnp.dot(low_rank, adapter_up, preferred_element_type=jnp.float32)
    values = values.astype(jnp.bfloat16).reshape(row_count, heads_here, value_width)
    within, query_map, summary, restart = block_local(query, key_rows, values, request, starts)
    identity = (jnp.zeros((), jnp.float32), jnp.zeros_like(summary))
    _, carried = carried_in((restart, summary), "dp", combine, identity)
    gains = head_gain.reshape(heads_here, value_width)
    normed = finish(within, query_map, carried, request, starts, gains).reshape(
        row_count, heads_here * value_width
    )
    partial_terms = jnp.dot(
        normed,
        lax.all_gather(out_weight, "dp", axis=1, tiled=True),
        preferred_element_type=jnp.float32,
    )
    return lax.psum_scatter(
        partial_terms.astype(jnp.bfloat16), "mp", scatter_dimension=1, tiled=True
    )


def solution(mesh):
    placed = (
        P("dp", None),
        P("dp", "mp"),
        P("dp", "mp"),
        P("dp", "mp"),
        P(None, "mp"),
        P(None, "mp"),
        P(),
        P(),
        P("mp"),
        P("mp", "dp"),
    )
    return jax.shard_map(
        per_device, mesh=mesh, in_specs=placed, out_specs=P("dp", "mp"), check_vma=False
    )
```

profile of v0, /device:TPU:0, one launch (start us, length us, event | category | flops | bytes accessed | tf_op | source)
XLA Modules:
  0.0 373.1 jit_solution(17115568398799284730)
XLA Ops:
  6.5 0.7 all-gather.6.cloned.1.call-update
  7.3 0.7 all-gather.8.cloned.1.call-update
  8.1 46.1 %all_gather.30 = bf16[2048,128]{1,0:T(8,128)(2,1)S(1)} all-gather(bf16[128,128]{1,0:T(8,128)(2,1)} %param.14), channel_id=1, replica_groups=mesh['dp'=16,'mp'=2] {'dp'}, dimensions={0}, use_global_device_ids=true | all-gather | bytes 557056 | tf_op jit(solution)/shard_map/all_gather | solution.py:113
  54.2 0.8 convolution_convert_fusion.1
  55.1 0.7 multiply_convert_fusion.3
  56.0 0.6 fusion.42
  56.8 1.9 compare_convert_fusion
  59.3 2.0 multiply_convert_fusion.1
  61.2 29.3 %all-gather.6.cloned.1.call-done = bf16[2048,1024]{1,0:T(8,128)(2,1)} async-done(((bf16[128,1024]{1,0:T(8,128)(2,1)}), bf16[2048,1024]{1,0:T(8,128)(2,1)}) %all-gather.6.cloned.1.call-update) | async-done | bytes 4194320 | tf_op jit(solution)/shard_map/all_gather | solution.py:118
  90.6 5.9 %fusion.43 = f32[512,1024]{1,0:T(8,128)} fusion(bf16[512,2048]{1,0:T(8,128)(2,1)S(1)} %copy-done, bf16[2048,1024]{1,0:T(8,128)(2,1)} %all-gather.6.cloned.1.call-done), kind=kOutput, calls=%fused_computation.72 | convolution fusion | flops 2147483648 | bytes 8388608 | tf_op jit(solution)/shard_map/dot_general | solution.py:116
  96.4 3.3 all-gather.8.cloned.1.call-done
  99.7 3.6 fusion.19
  103.4 3.0 fusion.20
  106.4 0.9 copy.19
  108.0 0.6 convert_reduce_fusion.1
  108.9 46.2 %all_gather.29 = bf16[2048,128]{1,0:T(8,128)(2,1)S(1)} all-gather(bf16[128,128]{1,0:T(8,128)(2,1)S(1)} %copy-done.3), channel_id=1, replica_groups=mesh['dp'=16,'mp'=2] {'dp'}, dimensions={0}, use_global_device_ids=true | all-gather | bytes 557056 | tf_op jit(solution)/shard_map/all_gather | solution.py:108
  155.1 0.8 convolution_convert_fusion.2
  156.0 0.6 dynamic-slice
  156.6 1.3 dynamic-update-slice
  157.9 37.5 %all-reduce = bf16[16]{0:T(256)(128)(2,1)S(1)} all-reduce(bf16[16]{0:T(256)(128)(2,1)S(1)} %dynamic-update-slice), channel_id=1, replica_groups=mesh['dp'=16,'mp'=2] {'dp'}, use_global_device_ids=true, to_apply=%add | all-reduce | flops 16 | bytes 64
  195.4 2.0 multiply_convert_fusion
  197.4 5.8 %fusion.1 = f32[8,128,512]{2,1,0:T(8,128)} fusion(pred[512,512]{1,0:T(8,128)(4,1)S(1)} %fusion.27, bf16[512,8,16]{0,2,1:T(8,128)(2,1)S(1)} %bitcast.63, bf16[512,8,16]{0,2,1:T(8,128)(2,1)S(1)} %bitcast.60, bf16[64,8,8,128]{3,2,1,0:T(8,128)(2,1)} %copy-done.1), kind=kOutput, calls=%fused_computation.7 | convolution fusion | flops 618659840 | bytes 3670016 | tf_op jit(solution)/shard_map/hij,jhe->ihe/dot_general | solution.py:62
  203.1 59.6 %all-gather.12.cloned.1.call-done = bf16[128,273,128]{2,0,1:T(8,128)(2,1)} async-done(((bf16[8,273,128]{2,0,1:T(8,128)(2,1)}), bf16[128,273,128]{2,0,1:T(8,128)(2,1)}) %all-gather.12.cloned.1.call-update) | async-done | bytes 8945680 | tf_op jit(solution)/shard_map/all_gather | solution.py:18
  262.7 76.4 %while.14 = (s32[]{:T(128)}, f32[8,273,128]{2,1,0:T(8,128)}, s32[]{:T(128)}, bf16[16]{0:T(256)(128)(2,1)S(1)}, bf16[16,8,273,128]{3,1,0,2:T(8,128)(2,1)}, /*index=5*/s32[]{:T(128)}, s32[]{:T(128)}, f32[1]{0:T(128)}) while((s32[]{:T(128)}, f32[8,273,128]{2,1,0:T(8,128)}, s32[]{:T(128)}, bf16[16]{0:T(256)(128)(2,1)S(1)}, ...), condition=%wide.region_6.7_spmd.clone, body=%wide.region_5.6_spmd.clone.sunk | while | flops 1397765 | bytes 3913853 | solution.py:35
  262.7 0.6 dynamic_slice.20
  263.9 1.1 constant_dynamic-slice_fusion.2
  265.0 1.2 fusion.58
  266.3 0.6 dynamic_slice.20
  267.5 1.1 constant_dynamic-slice_fusion.2
  268.6 2.5 fusion.58
  271.1 0.6 dynamic_slice.20
  272.4 1.1 constant_dynamic-slice_fusion.2
  273.5 2.5 fusion.58
  276.0 0.6 dynamic_slice.20
  277.2 1.1 constant_dynamic-slice_fusion.2
  278.3 2.5 fusion.58
  282.1 1.1 constant_dynamic-slice_fusion.2
  283.2 2.5 fusion.58
  286.9 1.1 constant_dynamic-slice_fusion.2
  288.0 2.5 fusion.58
  291.8 1.1 constant_dynamic-slice_fusion.2
  292.9 2.5 fusion.58
  296.6 1.1 constant_dynamic-slice_fusion.2
  297.7 2.5 fusion.58
  301.4 1.1 constant_dynamic-slice_fusion.2
  302.6 2.5 fusion.58
  306.3 1.1 constant_dynamic-slice_fusion.2
  307.4 2.5 fusion.58
  311.1 1.1 constant_dynamic-slice_fusion.2
  312.2 2.5 fusion.58
  316.0 1.1 constant_dynamic-slice_fusion.2
  317.1 2.5 fusion.58
  320.9 1.1 constant_dynamic-slice_fusion.2
  322.0 2.5 fusion.58
  325.8 1.1 constant_dynamic-slice_fusion.2
  326.9 2.5 fusion.58
  330.6 1.1 constant_dynamic-slice_fusion.2
  331.7 2.5 fusion.58
  335.4 1.1 constant_dynamic-slice_fusion.2
  336.6 2.5 fusion.58
  339.1 4.0 %fusion.14 = (f32[512,8]{0,1:T(8,128)S(1)}, f32[8,128,512]{2,1,0:T(8,128)S(1)}) fusion(f32[8,128,512]{2,1,0:T(8,128)} %fusion.1, bf16[512,8,256]{0,2,1:T(8,128)(2,1)} %bitcast.56, bf16[512,8,16]{0,2,1:T(8,128)(2,1)S(1)} %multiply_convert_fusion.2, bf16[273]{0:T(512)(128)(2,1)S(1)} %pad.3.clone, f32[8,273,128]{2,1,0:T(8,128)} %get-tuple-element.99, ...), kind=kOutput, calls=%fused_computation.23 | convolution fusion | flops 295343104 | bytes 7559714 | tf_op jit(solution)/shard_map/ihf,hfe->ihe/dot_general | solution.py:74
  343.4 9.3 %all-gather.10.cloned.1.call-done = bf16[1024,2048]{1,0:T(8,128)(2,1)} async-done(((bf16[1024,128]{1,0:T(8,128)(2,1)}), bf16[1024,2048]{1,0:T(8,128)(2,1)}) %all-gather.10.cloned.1.call-update) | async-done | bytes 4194320 | tf_op jit(solution)/shard_map/all_gather | solution.py:138
  352.7 5.9 %convolution_convert_fusion = bf16[512,2048]{1,0:T(8,128)(2,1)} fusion(bf16[512,1024]{0,1:T(8,128)(2,1)S(1)} %bitcast.64, bf16[1024,2048]{1,0:T(8,128)(2,1)} %all-gather.10.cloned.1.call-done), kind=kOutput, calls=%fused_computation.10 | convolution fusion | flops 2148532224 | bytes 7340032 | tf_op jit(solution)/shard_map/dot_general | solution.py:136
  358.6 8.0 %reduce-scatter.2.cloned.1.call-done = bf16[512,1024]{1,0:T(8,128)(2,1)} async-done(((bf16[512,2048]{1,0:T(8,128)(2,1)}), bf16[512,1024]{1,0:T(8,128)(2,1)}) %reduce-scatter.2.cloned.1.call-update) | async-done | bytes 1048592 | tf_op jit(solution)/shard_map/reduce_scatter | solution.py:141
  (60 shorter events, 9.4 us)
Async XLA Ops:
  6.5 47.7 %copy-start = (bf16[512,2048]{1,0:T(8,128)(2,1)S(1)}, bf16[512,2048]{1,0:T(8,128)(2,1)}, u32[]{:S(2)}) copy-start(bf16[512,2048]{1,0:T(8,128)(2,1)} %param.12) | copy-start | bytes 6291460
  6.5 84.0 %all-gather.6.cloned.1.call-start = ((), (), s32[]{:S(2)}) async-start(), calls=%async_computation.1 | async-start | bytes 4456448 | tf_op jit(solution)/shard_map/all_gather | solution.py:118
  7.3 92.5 %all-gather.8.cloned.1.call-start = ((), (), s32[]{:S(2)}) async-start(), calls=%async_computation.2 | async-start | bytes 1572864 | tf_op jit(solution)/shard_map/all_gather | solution.py:123
  8.0 47.7 %copy-start.10 = (s32[4]{0:T(128)S(1)}, s32[4]{0:T(128)}, u32[]{:S(2)}) copy-start(s32[4]{0:T(128)} %param.18) | copy-start | bytes 52
  8.0 48.7 %copy-start.7 = (s32[4]{0:T(128)S(1)}, s32[4]{0:T(128)}, u32[]{:S(2)}) copy-start(s32[4]{0:T(128)} %param.19) | copy-start | bytes 52
  8.0 254.7 %all-gather.12.cloned.1.call-start = ((), (), s32[]{:S(2)}) async-start(), calls=%async_computation.5 | async-start | bytes 9504768 | tf_op jit(solution)/shard_map/all_gather | solution.py:18
  56.7 39.7 %copy-start.8 = (pred[512]{0:T(512)(128)(4,1)}, pred[512]{0:T(512)(128)(4,1)S(1)}, u32[]{:S(2)}) copy-start(pred[512]{0:T(512)(128)(4,1)S(1)} %compare_reduce_fusion) | copy-start | bytes 1540
  61.2 38.5 %copy-start.6 = (s32[256]{0:T(256)S(1)}, s32[256]{0:T(256)}, u32[]{:S(2)}) copy-start(s32[256]{0:T(256)} %and_select_fusion) | copy-start | bytes 3076
  96.4 6.9 %copy-start.2 = (bf16[512,8,16]{0,2,1:T(8,128)(2,1)S(1)}, bf16[512,8,16]{0,2,1:T(8,128)(2,1)}, u32[]{:S(2)}) copy-start(bf16[512,8,16]{0,2,1:T(8,128)(2,1)} %multiply_convert_fusion.3) | copy-start | bytes 393220
  96.4 6.9 %copy-start.5 = (bf16[512]{0:T(512)(128)(2,1)S(1)}, bf16[512]{0:T(512)(128)(2,1)}, u32[]{:S(2)}) copy-start(bf16[512]{0:T(512)(128)(2,1)} %get-tuple-element.138) | copy-start | bytes 3076
  103.3 3.1 copy-start.1
  103.3 4.6 %copy-start.9 = (pred[512]{0:T(512)(128)(4,1)S(1)}, pred[512]{0:T(512)(128)(4,1)}, u32[]{:S(2)}) copy-start(pred[512]{0:T(512)(128)(4,1)} %copy-done.8) | copy-start | bytes 1540
  106.4 2.4 copy-start.3
  107.3 48.6 %copy-start.11 = (u32[32]{0:T(128)S(1)}, u32[32]{0:T(128)}, u32[]{:S(2)}) copy-start(u32[32]{0:T(128)} %constant.87) | copy-start | bytes 388
  107.4 245.3 %all-gather.10.cloned.1.call-start = ((), (), s32[]{:S(2)}) async-start(), calls=%async_computation.3 | async-start | bytes 4456448 | tf_op jit(solution)/shard_map/all_gather | solution.py:138
  107.9 258.6 %reduce-scatter.2.cloned.1.call-start = ((), (), s32[]{:S(2)}) async-start(), calls=%async_computation.4 | async-start | bytes 3145728 | tf_op jit(solution)/shard_map/reduce_scatter | solution.py:141
  339.0 4.0 %copy-start.4 = (f32[1024]{0:T(1024)S(1)}, f32[1024]{0:T(1024)}, u32[]{:S(2)}) copy-start(f32[1024]{0:T(1024)} %param.20) | copy-start | bytes 12292
Sparse Core Ops, SparseCore 0:
  10.1 80.3 all-gather.5
  92.1 7.5 all-gather.7
  107.5 155.1 all-gather.11
  265.2 87.3 all-gather.9
  358.7 7.7 reduce-scatter.1
where the time goes:
time: 375 us; the launch traced here: 373 us
  blocking collectives  130 us (35%)
  waiting for transfers between devices  111 us (30%)
  other arithmetic  47.4 us (13%)
  local copies, waits for them, and re-layouts  30.4 us (8%)
  matrix products  29.8 us (8%)
  between operations  13.4 us (4%)
  loops' own time  10.7 us (3%)
    all_gather x1, waiting for transfers between devices, carried_in(): lax.all_gather(part.astype(kind), axis)  59.6 us
    all_gather x1, blocking collectives, per_device(): lax.all_gather(q_weight, 'dp', axis=0, tiled=True)  46.2 us
    all_gather x1, blocking collectives, per_device(): lax.all_gather(k_weight, 'dp', axis=0, tiled=True)  46.1 us
    select_n x16, other arithmetic, turn(): return jax.tree.map(lambda a, b: jnp.where(reached, a, b), new, before)  38.7 us
    unnamed x1, blocking collectives  37.5 us
    all_gather x1, waiting for transfers between devices, per_device(): lax.all_gather(v_weight, 'dp', axis=0, tiled=True)  29.3 us
    dynamic_slice x32, local copies, waits for them, and re-layouts, turn(): part[k].astype(own.dtype)  26.9 us
    another operation x1, loops' own time, carried_in(): return lax.fori_loop(0, length, turn, start)  10.7 us
  transfers between devices with their start and end apart: 5, of which 5 were waited for; matrix products, arithmetic and copies ran while one was open for 25% of the time, Pallas kernels for 0%

commit v1 on v0

--- a/solution.py
+++ b/solution.py
@@ -1,15 +1,22 @@
+import functools
 import math
 
 import jax
 import jax.numpy as jnp
+import numpy as np
 from jax import lax
+from jax.experimental import pallas as pl
+from jax.experimental.pallas import tpu as pltpu
 from jax.sharding import PartitionSpec as P
 
 F = 16
 R = 16
-
-
 EPSILON = 1e-05
+SQUARES = [(a, b) for a in range(F) for b in range(a, F)]
+FEATS = 160
+VMEM_LIMIT = 56 * 1024 * 1024
+VMEM = pl.BlockSpec(memory_space=pltpu.VMEM)
+SMEM = pl.BlockSpec(memory_space=pltpu.SMEM)
 
 
 def carried_in(value, axis, combine, identity):
@@ -86,7 +93,7 @@
     )
 
 
-def per_device(
+def per_device_general(
     tokens,
     q_weight,
     k_weight,
@@ -103,23 +110,14 @@
     value_width = v_weight.shape[1] // heads_here
     positions = lax.axis_index("dp") * row_count + jnp.arange(row_count, dtype=jnp.int32)
     request, starts, adapter = token_tables(lengths, adapter_ids, positions)
-    query_sum = jnp.dot(
-        tokens,
-        lax.all_gather(q_weight, "dp", axis=0, tiled=True),
-        preferred_element_type=jnp.float32,
-    )
-    key_sum = jnp.dot(
-        tokens,
-        lax.all_gather(k_weight, "dp", axis=0, tiled=True),
-        preferred_element_type=jnp.float32,
-    )
-    value_sum = jnp.dot(
-        tokens,
-        lax.all_gather(v_weight, "dp", axis=0, tiled=True),
-        preferred_element_type=jnp.float32,
-    )
-    query = query_sum.astype(jnp.bfloat16).reshape(row_count, heads_here, F)
-    key_rows = key_sum.astype(jnp.bfloat16).reshape(row_count, heads_here, F)
+    together = lax.all_gather(
+        jnp.concatenate([q_weight, k_weight, v_weight], axis=1), "dp", axis=0, tiled=True
+    )
+    sums = jnp.dot(tokens, together, preferred_element_type=jnp.float32)
+    width = heads_here * F
+    query = sums[:, :width].astype(jnp.bfloat16).reshape(row_count, heads_here, F)
+    key_rows = sums[:, width : 2 * width].astype(jnp.bfloat16).reshape(row_count, heads_here, F)
+    value_sum = sums[:, 2 * width :]
     piece = lax.all_gather(adapter_down, "mp", axis=1, tiled=True)
     partial_low = jnp.dot(tokens, piece, preferred_element_type=jnp.float32)
     owners = jnp.arange(piece.shape[1], dtype=jnp.int32) // R
@@ -143,6 +141,305 @@
     )
 
 
+def feature_tables(heads):
+    first = np.zeros((heads, FEATS, heads * F), np.float32)
+    second = np.zeros((heads, FEATS, heads * F), np.float32)
+    scale = np.zeros((8, FEATS), np.float32)
+    scale[0, 0] = scale[1, 0] = scale[2, 0] = scale[3, 0] = 1.0
+    for a in range(F):
+        first[np.arange(heads), 1 + a, np.arange(heads) * F + a] = 1.0
+        scale[1, 1 + a] = 1.0
+        scale[2, 1 + a] = scale[3, 1 + a] = 0.5
+    for at, (a, b) in enumerate(SQUARES):
+        row = 1 + F + at
+        first[np.arange(heads), row, np.arange(heads) * F + a] = 1.0
+        second[np.arange(heads), row, np.arange(heads) * F + b] = 1.0
+        scale[2, row] = 0.25 / math.sqrt(2.0)
+        scale[3, row] = (0.25 if a == b else 0.5) / math.sqrt(2.0)
+    return first.astype(jnp.bfloat16), second.astype(jnp.bfloat16), scale
+
+
+def chip(place, x):
+    z, y = (place, 0) if place < 4 else (7 - place, 1)
+    return z * 4 + y * 2 + x
+
+
+def moves(step, flip):
+    return [
+        (chip(r, x), chip((r + step) % 8, x ^ flip)) for r in range(8) for x in range(2)
+    ]
+
+
+UP, DOWN, ACROSS = moves(1, 0), moves(-1, 0), moves(0, 1)
+
+
+def ring_places():
+    here = lax.axis_index("dp")
+    z, y, x = here // 4, (here // 2) % 2, here % 2
+    place = jnp.where(y == 0, z, 7 - z)
+    there = (place + jnp.arange(8, dtype=jnp.int32)) % 8
+    base = jnp.where(there < 4, there * 4, (7 - there) * 4 + 2)
+    return jnp.concatenate([base + x, base + 1 - x]).astype(jnp.int32)
+
+
+def send(value, pairs):
+    return lax.ppermute(value, "dp", pairs)
+
+
+def gather_rows(block):
+    rows = block.shape[0]
+    half, quarter = rows // 2, rows // 4
+    alone, pair = block[:half], block[half:]
+    pair = jnp.concatenate([pair, send(pair, ACROSS)], axis=0)
+
+    def ring(piece):
+        middle = piece.shape[0] // 2
+        up, down = [piece], [piece]
+        for _ in range(3):
+            up.append(send(up[-1], UP))
+            down.append(send(down[-1], DOWN))
+        up.append(send(up[-1][:middle], UP))
+        down.append(send(down[-1][middle:], DOWN))
+        return up, down
+
+    pieces = []
+    up, down = ring(alone)
+    for k in range(4):
+        for distance, piece in ((-k % 8, up[k]), (k, down[k]))[: 1 if k == 0 else 2]:
+            pieces.append((piece, [(distance, 0, half, 0)]))
+            pieces.append((send(piece, ACROSS), [(8 + distance, 0, half, 0)]))
+    for piece, row in ((up[4], 0), (down[4], quarter)):
+        pieces.append((piece, [(4, row, quarter, 0)]))
+        pieces.append((send(piece, ACROSS), [(12, row, quarter, 0)]))
+    up, down = ring(pair)
+    for k in range(4):
+        for distance, piece in ((-k % 8, up[k]), (k, down[k]))[: 1 if k == 0 else 2]:
+            pieces.append(
+                (piece, [(distance, half, half, 0), (8 + distance, half, half, half)])
+            )
+    pieces.append((up[4], [(4, half, half, 0)]))
+    pieces.append((down[4], [(12, half, half, 0)]))
+    return pieces
+
+
+NT = (((1,), (1,)), ((), ()))
+
+
+def project_kernel(layout, rows, heads, width, slots, tokens, low, up, tail, first, second, scale,
+                   *refs):
+    pieces, (query, keys, values, state, held) = refs[: len(layout)], refs[len(layout) :]
+    for piece, places in zip(pieces, layout):
+        for slot, row, count, source in places:
+            at = pl.multiple_of(slots[slot] * rows + row, rows // 4)
+            held[pl.ds(at, count), :] = piece[source : source + count, :]
+    wide = heads * width
+    small = heads * F
+    both = jnp.dot(tokens[...], held[:, wide:], preferred_element_type=jnp.float32)
+    query[...] = both[:, :small].astype(jnp.bfloat16)
+    key_rows = both[:, small:].astype(jnp.bfloat16)
+    keys[...] = key_rows
+    for h in range(0, heads, 2):
+        cols = slice(h * width, (h + 2) * width)
+        total = jnp.dot(tokens[...], held[:, cols], preferred_element_type=jnp.float32)
+        total += jnp.dot(low[...], up[:, cols], preferred_element_type=jnp.float32)
+        values[:, cols] = total.astype(jnp.bfloat16)
+        for g in (h, h + 1):
+            a = lax.dot_general(first[g], key_rows, NT, preferred_element_type=jnp.float32)
+            b = lax.dot_general(second[g], key_rows, NT, preferred_element_type=jnp.float32)
+            mapped = ((a + scale[:, 0:1]) * (b + scale[:, 1:2])) * scale[:, 2:3]
+            mapped = (mapped * tail[...]).astype(jnp.bfloat16)
+            state[g] = jnp.dot(
+                mapped, values[:, g * width : (g + 1) * width], preferred_element_type=jnp.float32
+            ).astype(jnp.bfloat16)
+
+
+def within_kernel(heads, width, query, keys, values, row, col, within):
+    count = query.shape[0]
+    cut = count // 2
+    lanes = lax.broadcasted_iota(jnp.int32, (1, heads * F), 1)
+    parts = ((0, cut), (cut, count))
+    for low, high in parts:
+        i = lax.broadcasted_iota(jnp.int32, (high - low, high), 0) + low
+        j = lax.broadcasted_iota(jnp.int32, (high - low, high), 1)
+        allowed = (j <= i) & (row[:, :high] == col[low:high, :])
+        for h in range(heads):
+            mine = jnp.where(lanes // F == h, 0.25, 0.0).astype(jnp.bfloat16)
+            s = lax.dot_general(
+                query[low:high, :] * mine, keys[:high, :], NT, preferred_element_type=jnp.float32
+            )
+            weights = 1.0 + s + 0.5 * s * s
+            weights = jnp.where(allowed, weights, 0.0).astype(jnp.bfloat16)
+            cols = slice(h * width, (h + 1) * width)
+            within[low:high, cols] = jnp.dot(
+                weights, values[:high, cols], preferred_element_type=jnp.float32
+            )
+
+
+def mix_kernel(blocks, marks, states, mixed):
+    for b in range(blocks):
+        total = jnp.zeros(states.shape[1:], jnp.float32)
+        for e in range(b):
+            total += marks[b * blocks + e] * states[e].astype(jnp.float32)
+        mixed[b] = total.astype(jnp.bfloat16)
+
+
+def finish_kernel(heads, width, within, query, carried, first, second, scale, follows, gains,
+                  normed):
+    rows = query[...]
+    for h in range(heads):
+        a = lax.dot_general(rows, first[h], NT, preferred_element_type=jnp.float32)
+        b = lax.dot_general(rows, second[h], NT, preferred_element_type=jnp.float32)
+        mapped = ((a + scale[0:1, :]) * (b + scale[1:2, :])) * scale[3:4, :]
+        cross = jnp.dot(mapped.astype(jnp.bfloat16), carried[h], preferred_element_type=jnp.float32)
+        cols = slice(h * width, (h + 1) * width)
+        combined = within[:, cols] + follows[...] * cross
+        factor = lax.rsqrt(jnp.mean(combined * combined, axis=-1, keepdims=True) + EPSILON)
+        normed[:, cols] = (combined * factor * gains[:, cols]).astype(jnp.bfloat16)
+
+
+def out_kernel(which, normed, weight, out):
+    out[...] = jnp.dot(normed[...], weight[...], preferred_element_type=jnp.float32).astype(
+        out.dtype
+    )
+
+
+def out_half(which, normed, weight, kind):
+    rows, depth = normed.shape
+    half = weight.shape[1] // 2
+    tile = 256
+    return pl.pallas_call(
+        out_kernel,
+        out_shape=jax.ShapeDtypeStruct((rows, half), kind),
+        grid_spec=pltpu.PrefetchScalarGridSpec(
+            num_scalar_prefetch=1,
+            grid=(half // tile,),
+            in_specs=[
+                pl.BlockSpec((rows, depth), lambda j, s: (0, 0)),
+                pl.BlockSpec((depth, tile), lambda j, s: (0, s[0] * (half // tile) + j)),
+            ],
+            out_specs=pl.BlockSpec((rows, tile), lambda j, s: (0, j)),
+        ),
+        compiler_params=pltpu.CompilerParams(vmem_limit_bytes=VMEM_LIMIT),
+        cost_estimate=pl.CostEstimate(
+            flops=2 * rows * depth * half, bytes_accessed=2 * depth * half, transcendentals=0
+        ),
+        name="out_half",
+    )(which, normed, weight)
+
+
+def per_device_fast(
+    tokens,
+    q_weight,
+    k_weight,
+    v_weight,
+    adapter_down,
+    adapter_up,
+    lengths,
+    adapter_ids,
+    head_gain,
+    out_weight,
+):
+    count, depth = tokens.shape
+    blocks = lax.axis_size("dp")
+    heads = q_weight.shape[1] // F
+    width = v_weight.shape[1] // heads
+    here, core = lax.axis_index("dp"), lax.axis_index("mp")
+    params = pltpu.CompilerParams(vmem_limit_bytes=VMEM_LIMIT)
+
+    out_all = lax.all_gather(out_weight, "dp", axis=1, tiled=True)
+
+    positions = here * count + jnp.arange(count, dtype=jnp.int32)
+    request, starts, adapter = token_tables(lengths, adapter_ids, positions)
+    bounds = jnp.cumsum(lengths)
+    opens = jnp.arange(blocks, dtype=jnp.int32) * count
+    ends = opens + (count - 1)
+    first_request = jnp.sum((opens[:, None] >= bounds[None, :]).astype(jnp.int32), axis=1)
+    last_request = jnp.sum((ends[:, None] >= bounds[None, :]).astype(jnp.int32), axis=1)
+    marks = (first_request[:, None] == last_request[None, :]).astype(jnp.float32).reshape(-1)
+    tail = (request == request[-1]).astype(jnp.float32).reshape(1, count)
+    follows = (request == request[0]).astype(jnp.float32).reshape(count, 1)
+
+    other = lax.ppermute(adapter_down, "mp", [(0, 1), (1, 0)])
+    wide = adapter_down.shape[1]
+    owners = jnp.arange(wide, dtype=jnp.int32) // R
+    lows = []
+    for piece, place in ((adapter_down, core), (other, 1 - core)):
+        partial = jnp.dot(tokens, piece, preferred_element_type=jnp.float32)
+        kept = adapter[:, None] == owners[None, :] + place * (wide // R)
+        lows.append(jnp.where(kept, partial, 0.0).astype(jnp.bfloat16))
+    low = jnp.where(core == 0, jnp.concatenate(lows, 1), jnp.concatenate(lows[::-1], 1))
+
+    first, second, scale = feature_tables(heads)
+    first, second, scale = jnp.asarray(first), jnp.asarray(second), jnp.asarray(scale)
+
+    rows = v_weight.shape[0]
+    gathered = gather_rows(jnp.concatenate([v_weight, q_weight, k_weight], axis=1))
+    layout = [places for _, places in gathered]
+    pieces = [piece for piece, _ in gathered]
+    total_width = heads * (width + 2 * F)
+    query, keys, values, state = pl.pallas_call(
+        functools.partial(project_kernel, layout, rows, heads, width),
+        out_shape=(
+            jax.ShapeDtypeStruct((count, heads * F), jnp.bfloat16),
+            jax.ShapeDtypeStruct((count, heads * F), jnp.bfloat16),
+            jax.ShapeDtypeStruct((count, heads * width), jnp.bfloat16),
+            jax.ShapeDtypeStruct((heads, FEATS, width), jnp.bfloat16),
+        ),
+        in_specs=[SMEM] + [VMEM] * (7 + len(pieces)),
+        out_specs=(VMEM,) * 4,
+        scratch_shapes=[pltpu.VMEM((depth, total_width), jnp.bfloat16)],
+        compiler_params=params,
+        cost_estimate=pl.CostEstimate(
+            flops=2 * count * depth * total_width, bytes_accessed=2 * depth * total_width * 2,
+            transcendentals=0,
+        ),
+        name="project",
+    )(ring_places(), tokens, low, adapter_up, tail, first, second, scale.T, *pieces)
+
+    parts = state.reshape(blocks, heads * FEATS // blocks, width)
+    parts = lax.all_to_all(parts, "dp", 0, 0, tiled=True)
+    mixed = pl.pallas_call(
+        functools.partial(mix_kernel, blocks),
+        out_shape=jax.ShapeDtypeStruct(parts.shape, jnp.bfloat16),
+        in_specs=[SMEM, VMEM],
+        out_specs=VMEM,
+        compiler_params=params,
+        name="mix",
+    )(marks, parts)
+    carried = lax.all_to_all(mixed, "dp", 0, 0, tiled=True).reshape(heads, FEATS, width)
+
+    within = pl.pallas_call(
+        functools.partial(within_kernel, heads, width),
+        out_shape=jax.ShapeDtypeStruct((count, heads * width), jnp.float32),
+        in_specs=[VMEM] * 5,
+        out_specs=VMEM,
+        compiler_params=params,
+        cost_estimate=pl.CostEstimate(
+            flops=4 * count * count * width * heads, bytes_accessed=4 * count * heads * width,
+            transcendentals=0,
+        ),
+        name="within",
+    )(query, keys, values, request.reshape(1, count), request.reshape(count, 1))
+
+    normed = pl.pallas_call(
+        functools.partial(finish_kernel, heads, width),
+        out_shape=jax.ShapeDtypeStruct((count, heads * width), jnp.bfloat16),
+        in_specs=[VMEM] * 8,
+        out_specs=VMEM,
+        compiler_params=params,
+        cost_estimate=pl.CostEstimate(
+            flops=4 * count * FEATS * width * heads, bytes_accessed=4 * count * heads * width,
+            transcendentals=0,
+        ),
+        name="finish",
+    )(within, query, carried, first, second, scale, follows, head_gain.reshape(1, -1))
+
+    theirs = out_half((1 - core).reshape(1).astype(jnp.int32), normed, out_all, jnp.bfloat16)
+    received = lax.ppermute(theirs, "mp", [(0, 1), (1, 0)])
+    mine = out_half(core.reshape(1).astype(jnp.int32), normed, out_all, jnp.float32)
+    return (mine + received.astype(jnp.float32)).astype(jnp.bfloat16)
+
+
 def solution(mesh):
     placed = (
         P("dp", None),
@@ -156,6 +453,11 @@
         P("mp"),
         P("mp", "dp"),
     )
+    fast = mesh.shape["dp"] == 16 and mesh.shape["mp"] == 2
     return jax.shard_map(
-        per_device, mesh=mesh, in_specs=placed, out_specs=P("dp", "mp"), check_vma=False
-    )
+        per_device_fast if fast else per_device_general,
+        mesh=mesh,
+        in_specs=placed,
+        out_specs=P("dp", "mp"),
+        check_vma=False,
+    )

time: 375 us -> 166 us (0.44)
  blocking collectives: 130 us -> 0 us
  waiting for transfers between devices: 111 us -> 42.7 us
  starting transfers between devices: 0.16 us -> 55.2 us
  other arithmetic: 47.4 us -> 8.1 us
  Pallas kernels: 0 us -> 34.7 us
  matrix products: 29.8 us -> 4.06 us
  local copies, waits for them, and re-layouts: 30.4 us -> 6.82 us
  loops' own time: 10.7 us -> 0 us
    all_gather x4 -> x1, waiting for transfers between devices: 101 us -> 0.01 us  [per_device_fast(): out_all = lax.all_gather(out_weight, 'dp', axis=1, tiled=True)]
    all_gather x2 -> x0, blocking collectives: 92.3 us -> none  [the longest x1 46.2 us: per_device(): lax.all_gather(q_weight, 'dp', axis=0, tiled=True)]
    select_n x17 -> x1, other arithmetic: 39.3 us -> 0.78 us  [per_device_fast(): jnp.where(core == 0, jnp.concatenate(lows, 1), jnp.concatenate(lows[::-1]...]
    unnamed x1 -> x0, blocking collectives: 37.5 us -> none
    pallas_call x0 -> x6, Pallas kernels: none -> 34.7 us  [the longest x1 11.8 us: per_device_fast(): pl.pallas_call(functools.partial(project_kernel, layout, rows, heads, wid...]
    ppermute x0 -> x28, starting transfers between devices: none -> 33.4 us  [the longest x26 33.4 us: send(): return lax.ppermute(value, 'dp', pairs)]
    ppermute x0 -> x28, waiting for transfers between devices: none -> 28.4 us  [the longest x26 28.4 us: send(): return lax.ppermute(value, 'dp', pairs)]
    dynamic_slice x32 -> x0, local copies, waits for them, and re-layouts: 26.9 us -> none  [turn(): part[k].astype(own.dtype)]
  transfers between devices with their start and end apart: 5 -> 31, of which waited for: 5 -> 12; matrix products, arithmetic and copies ran while one was open for 25% -> 8% of each run, Pallas kernels for 0% -> 18%
where the time goes in v1:
time: 166 us; the launch traced here: 165 us
  starting transfers between devices  55.2 us (33%)
  waiting for transfers between devices  42.7 us (26%)
  Pallas kernels  34.7 us (21%)
  between operations  13.7 us (8%)
  other arithmetic  8.1 us (5%)
  local copies, waits for them, and re-layouts  6.82 us (4%)
  matrix products  4.06 us (2%)
    ppermute x26, starting transfers between devices, send(): return lax.ppermute(value, 'dp', pairs)  33.4 us
    ppermute x26, waiting for transfers between devices, send(): return lax.ppermute(value, 'dp', pairs)  28.4 us
    all_to_all x1, starting transfers between devices, per_device_fast(): parts = lax.all_to_all(parts, 'dp', 0, 0, tiled=True)  17.4 us
    pallas_call x1, Pallas kernels, per_device_fast(): pl.pallas_call(functools.partial(project_kernel, layout, rows, heads, wid...  11.8 us
    all_to_all x1, waiting for transfers between devices, per_device_fast(): parts = lax.all_to_all(parts, 'dp', 0, 0, tiled=True)  11.3 us
    pallas_call x2, Pallas kernels, out_half(): pl.pallas_call(out_kernel, out_shape=jax.ShapeDtypeStruct((rows, half), k...  9.87 us
    pallas_call x1, Pallas kernels, per_device_fast(): pl.pallas_call(functools.partial(finish_kernel, heads, width), out_shape=...  5.63 us
    pallas_call x1, Pallas kernels, per_device_fast(): pl.pallas_call(functools.partial(within_kernel, heads, width), out_shape=...  5.26 us
  transfers between devices with their start and end apart: 31, of which 12 were waited for; matrix products, arithmetic and copies ran while one was open for 8% of the time, Pallas kernels for 18%

profile of v1, /device:TPU:0, one launch (start us, length us, event | category | flops | bytes accessed | tf_op | source)
XLA Modules:
  0.0 165.3 jit_solution(862279058336087780)
XLA Ops:
  6.5 0.7 all-gather.2.cloned.1.call-update
  7.3 1.0 constant_dynamic-update-slice_fusion.2
  8.2 0.8 constant_dynamic-update-slice_fusion.1
  9.0 0.8 constant_dynamic-update-slice_fusion
  9.8 3.0 %collective-permute-start.18 = (bf16[64,1280]{1,0:T(8,128)(2,1)S(1)}, bf16[64,1280]{1,0:T(8,128)(2,1)S(1)}, u32[]{:S(2)}, u32[]{:S(2)}) collective-permute-start(bf16[64,1280]{1,0:T(8,128)(2,1)S(1)} %get-tuple-element.15), channel_id=1, source_target_pairs={{0,2},{2,0},{8,10},{10,8},{16,18},{18,16},{24,26},{26,24},{28,30},... | collective-permute-start | bytes 491528 | tf_op jit(solution)/shard_map/ppermute | solution.py:186
  12.8 1.6 collective-permute-start.2
  14.4 0.5 collective-permute-start.4
  14.9 0.8 reduce-window.8
  15.8 1.8 %collective-permute-done.18 = bf16[64,1280]{1,0:T(8,128)(2,1)S(1)} collective-permute-done((bf16[64,1280]{1,0:T(8,128)(2,1)S(1)}, bf16[64,1280]{1,0:T(8,128)(2,1)S(1)}, u32[]{:S(2)}, u32[]{:S(2)}) %collective-permute-start.18) | collective-permute-done | bytes 163872 | tf_op jit(solution)/shard_map/ppermute | solution.py:186
  17.6 2.1 %collective-permute-start.19 = (bf16[128,1280]{1,0:T(8,128)(2,1)S(1)}, bf16[128,1280]{1,0:T(8,128)(2,1)S(1)}, u32[]{:S(2)}, u32[]{:S(2)}) collective-permute-start(bf16[128,1280]{1,0:T(8,128)(2,1)S(1)} %pad_maximum_fusion.refs_18_), channel_id=1, source_target_pairs={{0,8},{2,10},{8,16},{10,18},{16,24},{18,26},{24,28},{26,30},{28,20... | collective-permute-start | bytes 983048 | tf_op jit(solution)/shard_map/ppermute | solution.py:186
  19.7 0.1 convert_reduce_fusion
  19.8 2.1 %collective-permute-start.6 = (bf16[64,1280]{1,0:T(8,128)(2,1)}, bf16[64,1280]{1,0:T(8,128)(2,1)}, u32[]{:S(2)}, u32[]{:S(2)}) collective-permute-start(bf16[64,1280]{1,0:T(8,128)(2,1)} %collective-permute-done.2.refs_2_), channel_id=1, source_target_pairs={{0,8},{2,10},{8,16},{10,18},{16,24},{18,26},{24,28},{26,30},{28,20... | collective-permute-start | bytes 491528 | tf_op jit(solution)/shard_map/ppermute | solution.py:186
  21.9 0.1 select_reduce_fusion
  22.0 1.9 %collective-permute-start.3 = (bf16[64,1280]{1,0:T(8,128)(2,1)}, bf16[64,1280]{1,0:T(8,128)(2,1)S(1)}, u32[]{:S(2)}, u32[]{:S(2)}) collective-permute-start(bf16[64,1280]{1,0:T(8,128)(2,1)} %collective-permute-done.2.refs_2_), channel_id=1, source_target_pairs={{0,2},{2,0},{8,10},{10,8},{16,18},{18,16},{24,26},{26,24},{28,30},... | collective-permute-start | bytes 491528 | tf_op jit(solution)/shard_map/ppermute | solution.py:186
  23.9 0.4 collective-permute-start.8
  24.4 8.1 %collective-permute-done.6.refs_6_ = bf16[64,1280]{1,0:T(8,128)(2,1)} collective-permute-done((bf16[64,1280]{1,0:T(8,128)(2,1)}, bf16[64,1280]{1,0:T(8,128)(2,1)}, u32[]{:S(2)}, u32[]{:S(2)}) %collective-permute-start.6) | collective-permute-done | bytes 163872 | tf_op jit(solution)/shard_map/ppermute | solution.py:186
  32.4 1.5 collective-permute-start.5
  34.0 2.0 %collective-permute-start.22 = (bf16[128,1280]{1,0:T(8,128)(2,1)S(1)}, bf16[128,1280]{1,0:T(8,128)(2,1)}, u32[]{:S(2)}, u32[]{:S(2)}) collective-permute-start(bf16[128,1280]{1,0:T(8,128)(2,1)S(1)} %collective-permute-done.20.refs_20_), channel_id=1, source_target_pairs={{0,4},{2,6},{8,0},{10,2},{16,8},{18,10},{24,16},{26,18},{28,24},{3... | collective-permute-start | bytes 983048 | tf_op jit(solution)/shard_map/ppermute | solution.py:186
  36.0 1.8 %fusion = bf16[512,128]{1,0:T(8,128)(2,1)S(1)} fusion(bf16[512,2048]{1,0:T(8,128)(2,1)S(1)} %copy-done.11, bf16[2048,128]{1,0:T(8,128)(2,1)} %param.17, s32[128]{0:T(128)S(1)} %broadcast_add_fusion.2, s32[512]{0:T(512)S(1)} %select_reduce_fusion), kind=kOutput, calls=%fused_computation.3 | convolution fusion | flops 268632064 | bytes 2755072 | tf_op jit(solution)/shard_map/dot_general | solution.py:367
  37.8 0.6 fusion.4
  38.4 0.1 collective-permute-start.10
  38.5 2.0 %collective-permute-start.12 = (bf16[64,1280]{1,0:T(8,128)(2,1)}, bf16[64,1280]{1,0:T(8,128)(2,1)S(1)}, u32[]{:S(2)}, u32[]{:S(2)}) collective-permute-start(bf16[64,1280]{1,0:T(8,128)(2,1)} %collective-permute-done.8.refs_8_), channel_id=1, source_target_pairs={{0,4},{2,6},{8,0},{10,2},{16,8},{18,10},{24,16},{26,18},{28,24},{3... | collective-permute-start | bytes 491528 | tf_op jit(solution)/shard_map/ppermute | solution.py:186
  40.5 2.3 %collective-permute-done.21.refs_21_ = bf16[128,1280]{1,0:T(8,128)(2,1)} collective-permute-done((bf16[128,1280]{1,0:T(8,128)(2,1)S(1)}, bf16[128,1280]{1,0:T(8,128)(2,1)}, u32[]{:S(2)}, u32[]{:S(2)}) %collective-permute-start.21) | collective-permute-done | bytes 327712 | tf_op jit(solution)/shard_map/ppermute | solution.py:186
  42.7 4.2 %collective-permute-done.22.refs_22_ = bf16[128,1280]{1,0:T(8,128)(2,1)} collective-permute-done((bf16[128,1280]{1,0:T(8,128)(2,1)S(1)}, bf16[128,1280]{1,0:T(8,128)(2,1)}, u32[]{:S(2)}, u32[]{:S(2)}) %collective-permute-start.22) | collective-permute-done | bytes 327712 | tf_op jit(solution)/shard_map/ppermute | solution.py:186
  46.9 2.6 %collective-permute-start.24 = (bf16[128,1280]{1,0:T(8,128)(2,1)}, bf16[128,1280]{1,0:T(8,128)(2,1)S(1)}, u32[]{:S(2)}, u32[]{:S(2)}) collective-permute-start(bf16[128,1280]{1,0:T(8,128)(2,1)} %collective-permute-done.22.refs_22_), channel_id=1, source_target_pairs={{0,4},{2,6},{8,0},{10,2},{16,8},{18,10},{24,16},{26,18},{28,24},{3... | collective-permute-start | bytes 983048 | tf_op jit(solution)/shard_map/ppermute | solution.py:186
  49.5 1.2 compare_convert_fusion.2.tail
  50.8 1.2 collective-permute-done.12.refs_12_
  52.0 0.8 collective-permute-start.9
  52.8 4.5 %collective-permute-done.23.refs_23_ = bf16[128,1280]{1,0:T(8,128)(2,1)S(1)} collective-permute-done((bf16[128,1280]{1,0:T(8,128)(2,1)}, bf16[128,1280]{1,0:T(8,128)(2,1)S(1)}, u32[]{:S(2)}, u32[]{:S(2)}) %collective-permute-start.23) | collective-permute-done | bytes 327712 | tf_op jit(solution)/shard_map/ppermute | solution.py:186
  57.3 4.3 %collective-permute-start.14 = (bf16[32,1280]{1,0:T(8,128)(2,1)S(1)}, bf16[32,1280]{1,0:T(8,128)(2,1)S(1)}, u32[]{:S(2)}, u32[]{:S(2)}) collective-permute-start(bf16[32,1280]{1,0:T(8,128)(2,1)S(1)} %slice.33), channel_id=1, source_target_pairs={{0,8},{2,10},{8,16},{10,18},{16,24},{18,26},{24,28},{26,30},{28,20... | collective-permute-start | bytes 245768 | tf_op jit(solution)/shard_map/ppermute | solution.py:186
  61.7 0.9 collective-permute-done.24.refs_24_
  62.6 0.2 collective-permute-start.16
  62.8 0.6 pad_add_fusion.slots
  63.6 0.5 collective-permute-start.11
  64.0 1.6 collective-permute-start.13
  65.7 0.2 collective-permute-done.14.refs_14_
  65.8 1.5 collective-permute-start.15
  67.3 2.7 %collective-permute-start.25 = (bf16[64,1280]{1,0:T(8,128)(2,1)S(1)}, bf16[64,1280]{1,0:T(8,128)(2,1)S(1)}, u32[]{:S(2)}, u32[]{:S(2)}) collective-permute-start(bf16[64,1280]{1,0:T(8,128)(2,1)S(1)} %slice.36), channel_id=1, source_target_pairs={{0,8},{2,10},{8,16},{10,18},{16,24},{18,26},{24,28},{26,30},{28,20... | collective-permute-start | bytes 491528 | tf_op jit(solution)/shard_map/ppermute | solution.py:186
  70.0 1.0 collective-permute-start.26
  71.0 2.3 %fusion.1 = bf16[512,128]{1,0:T(8,128)(2,1)S(1)} fusion(bf16[512,2048]{1,0:T(8,128)(2,1)} %tokens.1, bf16[2048,128]{1,0:T(8,128)(2,1)S(1)} %collective-permute-done, s32[128]{0:T(128)S(1)} %broadcast_add_fusion.1, s32[512]{0:T(512)S(1)} %select_reduce_fusion), kind=kOutput, calls=%fused_computation.4 | convolution fusion | flops 268632064 | bytes 2755072 | tf_op jit(solution)/shard_map/dot_general | solution.py:367
  73.3 1.1 collective-permute-done.15.refs_15_
  74.4 0.8 collective-permute-start.17
  75.3 0.8 maximum_select_fusion.low
  76.0 4.2 %collective-permute-done.17.refs_17_ = bf16[32,1280]{1,0:T(8,128)(2,1)S(1)} collective-permute-done((bf16[32,1280]{1,0:T(8,128)(2,1)S(1)}, bf16[32,1280]{1,0:T(8,128)(2,1)S(1)}, u32[]{:S(2)}, u32[]{:S(2)}) %collective-permute-start.17) | collective-permute-done | bytes 81952 | tf_op jit(solution)/shard_map/ppermute | solution.py:186
  80.3 0.5 copy-done.26
  81.0 0.7 copy-done.22
  81.7 11.8 %project.1 = (bf16[512,128]{1,0:T(8,128)(2,1)}, bf16[512,128]{1,0:T(8,128)(2,1)}, bf16[512,1024]{1,0:T(8,128)(2,1)}, bf16[8,160,128]{2,1,0:T(8,128)(2,1)}) custom-call(s32[16]{0:T(128)} %pad_add_fusion.slots, bf16[512,2048]{1,0:T(8,128)(2,1)} %tokens.1, bf16[512,256]{1,0:T(8,128)(2,1)} %maximum_select_fusion.low, bf16[256,1024]{1,0:T(8,128)(2,1)} %up.1, ...), custom_call_target="tpu_custom_call" | custom-call | flops 2684354560 | bytes 10485760 | tf_op jit(solution)/shard_map/project/pallas_call | solution.py:380
  93.4 17.4 %all-to-all-start = ((bf16[16,80,128]{2,1,0:T(8,128)(2,1)}), bf16[16,80,128]{2,1,0:T(8,128)(2,1)S(1)}, u32[]{:S(2)}, u32[]{:S(2)}) async-start(bf16[16,80,128]{2,1,0:T(8,128)(2,1)} %bitcast.16), calls=%async_computation | async-start | bytes 655360 | tf_op jit(solution)/shard_map/all_to_all | solution.py:400
  110.8 0.1 convert_reduce_fusion.2
  110.9 0.1 compare_convert_fusion.1
  111.0 0.7 reshape.111.marks
  111.7 11.3 %all-to-all-done.states = bf16[16,80,128]{2,1,0:T(8,128)(2,1)S(1)} async-done(((bf16[16,80,128]{2,1,0:T(8,128)(2,1)}), bf16[16,80,128]{2,1,0:T(8,128)(2,1)S(1)}, u32[]{:S(2)}, u32[]{:S(2)}) %all-to-all-start) | async-done | bytes 327712 | tf_op jit(solution)/shard_map/all_to_all | solution.py:400
  123.0 0.7 copy-done.1
  123.7 2.2 %mix.1 = bf16[16,80,128]{2,1,0:T(8,128)(2,1)} custom-call(f32[256]{0:T(256)} %reshape.111.marks, bf16[16,80,128]{2,1,0:T(8,128)(2,1)} %copy-done.1), custom_call_target="tpu_custom_call" | custom-call | tf_op jit(solution)/shard_map/mix/pallas_call | solution.py:401
  125.9 4.4 %all-to-all-start.1 = ((bf16[16,80,128]{2,1,0:T(8,128)(2,1)}), bf16[16,80,128]{2,1,0:T(8,128)(2,1)S(1)}, u32[]{:S(2)}, u32[]{:S(2)}) async-start(bf16[16,80,128]{2,1,0:T(8,128)(2,1)} %mix.1), calls=%async_computation.1 | async-start | bytes 655360 | tf_op jit(solution)/shard_map/all_to_all | solution.py:409
  130.3 0.1 copy.26.col
  130.4 1.3 compare_convert_fusion.follows
  131.8 5.3 %within.1 = f32[512,1024]{1,0:T(8,128)} custom-call(bf16[512,128]{1,0:T(8,128)(2,1)} %get-tuple-element.9.query, bf16[512,128]{1,0:T(8,128)(2,1)} %get-tuple-element.10.keys, bf16[512,1024]{1,0:T(8,128)(2,1)} %get-tuple-element.11.values, s32[1,512]{1,0:T(1,128)} %bitcast.19, s32[512,1]{1,0:T(8,128)} %copy-done.2), custom_call_target="tpu_custom_call" | custom-call | flops 1073741824 | bytes 2097152 | tf_op jit(solution)/shard_map/within/pallas_call | solution.py:411
  137.0 2.2 %all-to-all-done.1 = bf16[16,80,128]{2,1,0:T(8,128)(2,1)S(1)} async-done(((bf16[16,80,128]{2,1,0:T(8,128)(2,1)}), bf16[16,80,128]{2,1,0:T(8,128)(2,1)S(1)}, u32[]{:S(2)}, u32[]{:S(2)}) %all-to-all-start.1) | async-done | bytes 327712 | tf_op jit(solution)/shard_map/all_to_all | solution.py:409
  139.3 0.7 copy-done
  140.0 5.6 %finish.1.normed = bf16[512,1024]{1,0:T(8,128)(2,1)} custom-call(f32[512,1024]{1,0:T(8,128)} %within.1, bf16[512,128]{1,0:T(8,128)(2,1)} %get-tuple-element.9.query, bf16[8,160,128]{2,1,0:T(8,128)(2,1)} %bitcast.15, bf16[8,160,128]{2,1,0:T(8,128)(2,1)} %constant.101.clone.first, bf16[8,160,128]{2,1,0:T(8,128)(2,1)} %constant.102.clone.second, ...), custom_call_target="tpu_custom_call" | custom-call | flops 335544320 | bytes 2097152 | tf_op jit(solution)/shard_map/finish/pallas_call | solution.py:424
  145.6 4.8 %out_half.3 = bf16[512,1024]{1,0:T(8,128)(2,1)} custom-call(s32[1]{0:T(128)} %bitcast.10.which, bf16[512,1024]{1,0:T(8,128)(2,1)} %finish.1.normed, bf16[1024,2048]{1,0:T(8,128)(2,1)} %all-gather.2.cloned.1.call-done.weight), custom_call_target="tpu_custom_call" | custom-call | flops 1073741824 | bytes 2097152 | tf_op jit(solution)/shard_map/out_half/pallas_call | solution.py:310
  150.4 5.1 %out_half.2 = f32[512,1024]{1,0:T(8,128)} custom-call(s32[1]{0:T(128)} %bitcast.which, bf16[512,1024]{1,0:T(8,128)(2,1)} %finish.1.normed, bf16[1024,2048]{1,0:T(8,128)(2,1)} %all-gather.2.cloned.1.call-done.weight), custom_call_target="tpu_custom_call" | custom-call | flops 1073741824 | bytes 2097152 | tf_op jit(solution)/shard_map/out_half/pallas_call | solution.py:310
  155.5 3.0 %add_convert_fusion = bf16[512,1024]{1,0:T(8,128)(2,1)} fusion(f32[512,1024]{1,0:T(8,128)} %out_half.2, bf16[512,1024]{1,0:T(8,128)(2,1)S(1)} %collective-permute-done.27), kind=kLoop, calls=%fused_computation | loop fusion | flops 1572864 | bytes 4194304 | tf_op jit(solution)/shard_map/convert_element_type | solution.py:440
  (88 shorter events, 0.6 us)
Async XLA Ops:
  6.5 15.3 %copy-start.10 = (s32[4]{0:T(128)S(1)}, s32[4]{0:T(128)}, u32[]{:S(2)}) copy-start(s32[4]{0:T(128)} %param.20) | copy-start | bytes 52
  6.5 29.5 %copy-start.11 = (bf16[512,2048]{1,0:T(8,128)(2,1)S(1)}, bf16[512,2048]{1,0:T(8,128)(2,1)}, u32[]{:S(2)}) copy-start(bf16[512,2048]{1,0:T(8,128)(2,1)} %tokens.1) | copy-start | bytes 6291460
  6.5 139.1 %all-gather.2.cloned.1.call-start = ((), (), s32[]{:S(2)}) async-start(), calls=%async_computation.2 | async-start | bytes 4456448 | tf_op jit(solution)/shard_map/all_gather | solution.py:349
  9.8 28.6 %copy-start.12 = (bf16[2048,128]{1,0:T(8,128)(2,1)S(1)}, bf16[2048,128]{1,0:T(8,128)(2,1)}, u32[]{:S(2)}) copy-start(bf16[2048,128]{1,0:T(8,128)(2,1)} %param.17) | copy-start | bytes 1572868
  9.8 53.7 %copy-start.4 = (bf16[64,1280]{1,0:T(8,128)(2,1)}, bf16[64,1280]{1,0:T(8,128)(2,1)S(1)}, u32[]{:S(2)}) copy-start(bf16[64,1280]{1,0:T(8,128)(2,1)S(1)} %get-tuple-element.16.refs_0_) | copy-start | bytes 491524
  9.8 7.7 %collective-permute-start.18 = (bf16[64,1280]{1,0:T(8,128)(2,1)S(1)}, bf16[64,1280]{1,0:T(8,128)(2,1)S(1)}, u32[]{:S(2)}, u32[]{:S(2)}) collective-permute-start(bf16[64,1280]{1,0:T(8,128)(2,1)S(1)} %get-tuple-element.15), channel_id=1, source_target_pairs={{0,2},{2,0},{8,10},{10,8},{16,18},{18,16},{24,26},{26,24},{28,30},... | collective-permute-start | bytes 491528 | tf_op jit(solution)/shard_map/ppermute | solution.py:186
  12.8 7.0 %collective-permute-start.2 = (bf16[64,1280]{1,0:T(8,128)(2,1)S(1)}, bf16[64,1280]{1,0:T(8,128)(2,1)}, u32[]{:S(2)}, u32[]{:S(2)}) collective-permute-start(bf16[64,1280]{1,0:T(8,128)(2,1)S(1)} %get-tuple-element.16.refs_0_), channel_id=1, source_target_pairs={{0,8},{2,10},{8,16},{10,18},{16,24},{18,26},{24,28},{26,30},{28,20... | collective-permute-start | bytes 491528 | tf_op jit(solution)/shard_map/ppermute | solution.py:186
  14.4 7.6 %collective-permute-start.4 = (bf16[64,1280]{1,0:T(8,128)(2,1)S(1)}, bf16[64,1280]{1,0:T(8,128)(2,1)}, u32[]{:S(2)}, u32[]{:S(2)}) collective-permute-start(bf16[64,1280]{1,0:T(8,128)(2,1)S(1)} %get-tuple-element.16.refs_0_), channel_id=1, source_target_pairs={{0,4},{2,6},{8,0},{10,2},{16,8},{18,10},{24,16},{26,18},{28,24},{3... | collective-permute-start | bytes 491528 | tf_op jit(solution)/shard_map/ppermute | solution.py:186
  14.9 9.0 %collective-permute-start.1 = (bf16[64,1280]{1,0:T(8,128)(2,1)S(1)}, bf16[64,1280]{1,0:T(8,128)(2,1)}, u32[]{:S(2)}, u32[]{:S(2)}) collective-permute-start(bf16[64,1280]{1,0:T(8,128)(2,1)S(1)} %get-tuple-element.16.refs_0_), channel_id=1, source_target_pairs={{0,2},{2,0},{8,10},{10,8},{16,18},{18,16},{24,26},{26,24},{28,30},... | collective-permute-start | bytes 491528 | tf_op jit(solution)/shard_map/ppermute | solution.py:186
  17.6 55.7 %copy-start.3 = (bf16[128,1280]{1,0:T(8,128)(2,1)}, bf16[128,1280]{1,0:T(8,128)(2,1)S(1)}, u32[]{:S(2)}) copy-start(bf16[128,1280]{1,0:T(8,128)(2,1)S(1)} %pad_maximum_fusion.refs_18_) | copy-start | bytes 983044
  17.6 16.4 %collective-permute-start.19 = (bf16[128,1280]{1,0:T(8,128)(2,1)S(1)}, bf16[128,1280]{1,0:T(8,128)(2,1)S(1)}, u32[]{:S(2)}, u32[]{:S(2)}) collective-permute-start(bf16[128,1280]{1,0:T(8,128)(2,1)S(1)} %pad_maximum_fusion.refs_18_), channel_id=1, source_target_pairs={{0,8},{2,10},{8,16},{10,18},{16,24},{18,26},{24,28},{26,30},{28,20... | collective-permute-start | bytes 983048 | tf_op jit(solution)/shard_map/ppermute | solution.py:186
  19.7 14.3 %collective-permute-start.20 = (bf16[128,1280]{1,0:T(8,128)(2,1)S(1)}, bf16[128,1280]{1,0:T(8,128)(2,1)S(1)}, u32[]{:S(2)}, u32[]{:S(2)}) collective-permute-start(bf16[128,1280]{1,0:T(8,128)(2,1)S(1)} %pad_maximum_fusion.refs_18_), channel_id=1, source_target_pairs={{0,4},{2,6},{8,0},{10,2},{16,8},{18,10},{24,16},{26,18},{28,24},{3... | collective-permute-start | bytes 983048 | tf_op jit(solution)/shard_map/ppermute | solution.py:186
  19.8 110.5 %copy-start.7 = (s32[512]{0:T(512)}, s32[512]{0:T(512)S(1)}, u32[]{:S(2)}) copy-start(s32[512]{0:T(512)S(1)} %convert_reduce_fusion) | copy-start | bytes 6148
  19.8 12.6 %collective-permute-start.6 = (bf16[64,1280]{1,0:T(8,128)(2,1)}, bf16[64,1280]{1,0:T(8,128)(2,1)}, u32[]{:S(2)}, u32[]{:S(2)}) collective-permute-start(bf16[64,1280]{1,0:T(8,128)(2,1)} %collective-permute-done.2.refs_2_), channel_id=1, source_target_pairs={{0,8},{2,10},{8,16},{10,18},{16,24},{18,26},{24,28},{26,30},{28,20... | collective-permute-start | bytes 491528 | tf_op jit(solution)/shard_map/ppermute | solution.py:186
  22.0 16.4 %collective-permute-start.3 = (bf16[64,1280]{1,0:T(8,128)(2,1)}, bf16[64,1280]{1,0:T(8,128)(2,1)S(1)}, u32[]{:S(2)}, u32[]{:S(2)}) collective-permute-start(bf16[64,1280]{1,0:T(8,128)(2,1)} %collective-permute-done.2.refs_2_), channel_id=1, source_target_pairs={{0,2},{2,0},{8,10},{10,8},{16,18},{18,16},{24,26},{26,24},{28,30},... | collective-permute-start | bytes 491528 | tf_op jit(solution)/shard_map/ppermute | solution.py:186
  23.9 14.4 %collective-permute-start.8 = (bf16[64,1280]{1,0:T(8,128)(2,1)}, bf16[64,1280]{1,0:T(8,128)(2,1)}, u32[]{:S(2)}, u32[]{:S(2)}) collective-permute-start(bf16[64,1280]{1,0:T(8,128)(2,1)} %collective-permute-done.4.refs_4_), channel_id=1, source_target_pairs={{0,4},{2,6},{8,0},{10,2},{16,8},{18,10},{24,16},{26,18},{28,24},{3... | collective-permute-start | bytes 491528 | tf_op jit(solution)/shard_map/ppermute | solution.py:186
  32.4 6.1 %collective-permute-start.5 = (bf16[64,1280]{1,0:T(8,128)(2,1)}, bf16[64,1280]{1,0:T(8,128)(2,1)S(1)}, u32[]{:S(2)}, u32[]{:S(2)}) collective-permute-start(bf16[64,1280]{1,0:T(8,128)(2,1)} %collective-permute-done.4.refs_4_), channel_id=1, source_target_pairs={{0,2},{2,0},{8,10},{10,8},{16,18},{18,16},{24,26},{26,24},{28,30},... | collective-permute-start | bytes 491528 | tf_op jit(solution)/shard_map/ppermute | solution.py:186
  34.0 8.8 %copy-start.13 = (bf16[128,1280]{1,0:T(8,128)(2,1)}, bf16[128,1280]{1,0:T(8,128)(2,1)S(1)}, u32[]{:S(2)}) copy-start(bf16[128,1280]{1,0:T(8,128)(2,1)S(1)} %collective-permute-done.19.refs_19_) | copy-start | bytes 983044
  34.0 8.8 %collective-permute-start.21 = (bf16[128,1280]{1,0:T(8,128)(2,1)S(1)}, bf16[128,1280]{1,0:T(8,128)(2,1)}, u32[]{:S(2)}, u32[]{:S(2)}) collective-permute-start(bf16[128,1280]{1,0:T(8,128)(2,1)S(1)} %collective-permute-done.19.refs_19_), channel_id=1, source_target_pairs={{0,8},{2,10},{8,16},{10,18},{16,24},{18,26},{24,28},{26,30},{28,20... | collective-permute-start | bytes 983048 | tf_op jit(solution)/shard_map/ppermute | solution.py:186
  34.0 12.9 %copy-start.14 = (bf16[128,1280]{1,0:T(8,128)(2,1)}, bf16[128,1280]{1,0:T(8,128)(2,1)S(1)}, u32[]{:S(2)}) copy-start(bf16[128,1280]{1,0:T(8,128)(2,1)S(1)} %collective-permute-done.20.refs_20_) | copy-start | bytes 983044
  34.0 12.9 %collective-permute-start.22 = (bf16[128,1280]{1,0:T(8,128)(2,1)S(1)}, bf16[128,1280]{1,0:T(8,128)(2,1)}, u32[]{:S(2)}, u32[]{:S(2)}) collective-permute-start(bf16[128,1280]{1,0:T(8,128)(2,1)S(1)} %collective-permute-done.20.refs_20_), channel_id=1, source_target_pairs={{0,4},{2,6},{8,0},{10,2},{16,8},{18,10},{24,16},{26,18},{28,24},{3... | collective-permute-start | bytes 983048 | tf_op jit(solution)/shard_map/ppermute | solution.py:186
  38.3 29.0 %collective-permute-start = (bf16[2048,128]{1,0:T(8,128)(2,1)S(1)}, bf16[2048,128]{1,0:T(8,128)(2,1)S(1)}, u32[]{:S(2)}, u32[]{:S(2)}) collective-permute-start(bf16[2048,128]{1,0:T(8,128)(2,1)S(1)} %copy-done.12), channel_id=1, source_target_pairs={{0,1},{1,0},{2,3},{3,2},{4,5},{5,4},{6,7},{7,6},{8,9},{9,8},{10,11... | collective-permute-start | bytes 1572872 | tf_op jit(solution)/shard_map/ppermute | solution.py:362
  38.4 2.1 %copy-start.15 = (bf16[64,1280]{1,0:T(8,128)(2,1)}, bf16[64,1280]{1,0:T(8,128)(2,1)S(1)}, u32[]{:S(2)}) copy-start(bf16[64,1280]{1,0:T(8,128)(2,1)S(1)} %collective-permute-done.3.refs_3_) | copy-start | bytes 491524
  38.4 12.3 %collective-permute-start.10 = (bf16[64,1280]{1,0:T(8,128)(2,1)}, bf16[64,1280]{1,0:T(8,128)(2,1)S(1)}, u32[]{:S(2)}, u32[]{:S(2)}) collective-permute-start(bf16[64,1280]{1,0:T(8,128)(2,1)} %collective-permute-done.6.refs_6_), channel_id=1, source_target_pairs={{0,8},{2,10},{8,16},{10,18},{16,24},{18,26},{24,28},{26,30},{28,20... | collective-permute-start | bytes 491528 | tf_op jit(solution)/shard_map/ppermute | solution.py:186
  38.5 11.0 %copy-start.16 = (bf16[64,1280]{1,0:T(8,128)(2,1)}, bf16[64,1280]{1,0:T(8,128)(2,1)S(1)}, u32[]{:S(2)}) copy-start(bf16[64,1280]{1,0:T(8,128)(2,1)S(1)} %collective-permute-done.5.refs_5_) | copy-start | bytes 491524
  38.5 13.5 %collective-permute-start.12 = (bf16[64,1280]{1,0:T(8,128)(2,1)}, bf16[64,1280]{1,0:T(8,128)(2,1)S(1)}, u32[]{:S(2)}, u32[]{:S(2)}) collective-permute-start(bf16[64,1280]{1,0:T(8,128)(2,1)} %collective-permute-done.8.refs_8_), channel_id=1, source_target_pairs={{0,4},{2,6},{8,0},{10,2},{16,8},{18,10},{24,16},{26,18},{28,24},{3... | collective-permute-start | bytes 491528 | tf_op jit(solution)/shard_map/ppermute | solution.py:186
  42.7 14.6 %collective-permute-start.23 = (bf16[128,1280]{1,0:T(8,128)(2,1)}, bf16[128,1280]{1,0:T(8,128)(2,1)S(1)}, u32[]{:S(2)}, u32[]{:S(2)}) collective-permute-start(bf16[128,1280]{1,0:T(8,128)(2,1)} %collective-permute-done.21.refs_21_), channel_id=1, source_target_pairs={{0,8},{2,10},{8,16},{10,18},{16,24},{18,26},{24,28},{26,30},{28,20... | collective-permute-start | bytes 983048 | tf_op jit(solution)/shard_map/ppermute | solution.py:186
  46.9 15.7 %collective-permute-start.24 = (bf16[128,1280]{1,0:T(8,128)(2,1)}, bf16[128,1280]{1,0:T(8,128)(2,1)S(1)}, u32[]{:S(2)}, u32[]{:S(2)}) collective-permute-start(bf16[128,1280]{1,0:T(8,128)(2,1)} %collective-permute-done.22.refs_22_), channel_id=1, source_target_pairs={{0,4},{2,6},{8,0},{10,2},{16,8},{18,10},{24,16},{26,18},{28,24},{3... | collective-permute-start | bytes 983048 | tf_op jit(solution)/shard_map/ppermute | solution.py:186
  50.7 25.3 %copy-start.8 = (bf16[64,1280]{1,0:T(8,128)(2,1)}, bf16[64,1280]{1,0:T(8,128)(2,1)S(1)}, u32[]{:S(2)}) copy-start(bf16[64,1280]{1,0:T(8,128)(2,1)S(1)} %collective-permute-done.10.refs_10_) | copy-start | bytes 491524
  50.7 12.8 %collective-permute-start.7 = (bf16[64,1280]{1,0:T(8,128)(2,1)}, bf16[64,1280]{1,0:T(8,128)(2,1)S(1)}, u32[]{:S(2)}, u32[]{:S(2)}) collective-permute-start(bf16[64,1280]{1,0:T(8,128)(2,1)} %collective-permute-done.6.refs_6_), channel_id=1, source_target_pairs={{0,2},{2,0},{8,10},{10,8},{16,18},{18,16},{24,26},{26,24},{28,30},... | collective-permute-start | bytes 491528 | tf_op jit(solution)/shard_map/ppermute | solution.py:186
  52.0 24.0 %copy-start.9 = (bf16[64,1280]{1,0:T(8,128)(2,1)}, bf16[64,1280]{1,0:T(8,128)(2,1)S(1)}, u32[]{:S(2)}) copy-start(bf16[64,1280]{1,0:T(8,128)(2,1)S(1)} %collective-permute-done.12.refs_12_) | copy-start | bytes 491524
  52.0 12.0 %collective-permute-start.9 = (bf16[64,1280]{1,0:T(8,128)(2,1)}, bf16[64,1280]{1,0:T(8,128)(2,1)S(1)}, u32[]{:S(2)}, u32[]{:S(2)}) collective-permute-start(bf16[64,1280]{1,0:T(8,128)(2,1)} %collective-permute-done.8.refs_8_), channel_id=1, source_target_pairs={{0,2},{2,0},{8,10},{10,8},{16,18},{18,16},{24,26},{26,24},{28,30},... | collective-permute-start | bytes 491528 | tf_op jit(solution)/shard_map/ppermute | solution.py:186
  57.3 22.9 %copy-start.5 = (bf16[128,1280]{1,0:T(8,128)(2,1)}, bf16[128,1280]{1,0:T(8,128)(2,1)S(1)}, u32[]{:S(2)}) copy-start(bf16[128,1280]{1,0:T(8,128)(2,1)S(1)} %collective-permute-done.23.refs_23_) | copy-start | bytes 983044
  57.3 8.5 %collective-permute-start.14 = (bf16[32,1280]{1,0:T(8,128)(2,1)S(1)}, bf16[32,1280]{1,0:T(8,128)(2,1)S(1)}, u32[]{:S(2)}, u32[]{:S(2)}) collective-permute-start(bf16[32,1280]{1,0:T(8,128)(2,1)S(1)} %slice.33), channel_id=1, source_target_pairs={{0,8},{2,10},{8,16},{10,18},{16,24},{18,26},{24,28},{26,30},{28,20... | collective-permute-start | bytes 245768 | tf_op jit(solution)/shard_map/ppermute | solution.py:186
  62.6 17.6 %copy-start.6 = (bf16[128,1280]{1,0:T(8,128)(2,1)}, bf16[128,1280]{1,0:T(8,128)(2,1)S(1)}, u32[]{:S(2)}) copy-start(bf16[128,1280]{1,0:T(8,128)(2,1)S(1)} %collective-permute-done.24.refs_24_) | copy-start | bytes 983044
  62.6 7.4 %collective-permute-start.16 = (bf16[32,1280]{1,0:T(8,128)(2,1)S(1)}, bf16[32,1280]{1,0:T(8,128)(2,1)S(1)}, u32[]{:S(2)}, u32[]{:S(2)}) collective-permute-start(bf16[32,1280]{1,0:T(8,128)(2,1)S(1)} %slice.34), channel_id=1, source_target_pairs={{0,4},{2,6},{8,0},{10,2},{16,8},{18,10},{24,16},{26,18},{28,24},{3... | collective-permute-start | bytes 245768 | tf_op jit(solution)/shard_map/ppermute | solution.py:186
  63.6 16.7 %copy-start.17 = (bf16[64,1280]{1,0:T(8,128)(2,1)}, bf16[64,1280]{1,0:T(8,128)(2,1)S(1)}, u32[]{:S(2)}) copy-start(bf16[64,1280]{1,0:T(8,128)(2,1)S(1)} %collective-permute-done.7.refs_7_) | copy-start | bytes 491524
  63.6 16.6 %collective-permute-start.11 = (bf16[64,1280]{1,0:T(8,128)(2,1)S(1)}, bf16[64,1280]{1,0:T(8,128)(2,1)S(1)}, u32[]{:S(2)}, u32[]{:S(2)}) collective-permute-start(bf16[64,1280]{1,0:T(8,128)(2,1)S(1)} %collective-permute-done.10.refs_10_), channel_id=1, source_target_pairs={{0,2},{2,0},{8,10},{10,8},{16,18},{18,16},{24,26},{26,24},{28,30},... | collective-permute-start | bytes 491528 | tf_op jit(solution)/shard_map/ppermute | solution.py:186
  64.0 16.2 %copy-start.18 = (bf16[64,1280]{1,0:T(8,128)(2,1)}, bf16[64,1280]{1,0:T(8,128)(2,1)S(1)}, u32[]{:S(2)}) copy-start(bf16[64,1280]{1,0:T(8,128)(2,1)S(1)} %collective-permute-done.9.refs_9_) | copy-start | bytes 491524
  64.0 16.2 %collective-permute-start.13 = (bf16[64,1280]{1,0:T(8,128)(2,1)S(1)}, bf16[64,1280]{1,0:T(8,128)(2,1)S(1)}, u32[]{:S(2)}, u32[]{:S(2)}) collective-permute-start(bf16[64,1280]{1,0:T(8,128)(2,1)S(1)} %collective-permute-done.12.refs_12_), channel_id=1, source_target_pairs={{0,2},{2,0},{8,10},{10,8},{16,18},{18,16},{24,26},{26,24},{28,30},... | collective-permute-start | bytes 491528 | tf_op jit(solution)/shard_map/ppermute | solution.py:186
  65.8 14.5 %copy-start.23 = (bf16[32,1280]{1,0:T(8,128)(2,1)}, bf16[32,1280]{1,0:T(8,128)(2,1)S(1)}, u32[]{:S(2)}) copy-start(bf16[32,1280]{1,0:T(8,128)(2,1)S(1)} %collective-permute-done.14.refs_14_) | copy-start | bytes 245764
  65.8 8.6 %collective-permute-start.15 = (bf16[32,1280]{1,0:T(8,128)(2,1)S(1)}, bf16[32,1280]{1,0:T(8,128)(2,1)S(1)}, u32[]{:S(2)}, u32[]{:S(2)}) collective-permute-start(bf16[32,1280]{1,0:T(8,128)(2,1)S(1)} %collective-permute-done.14.refs_14_), channel_id=1, source_target_pairs={{0,2},{2,0},{8,10},{10,8},{16,18},{18,16},{24,26},{26,24},{28,30},... | collective-permute-start | bytes 245768 | tf_op jit(solution)/shard_map/ppermute | solution.py:186
  67.3 12.9 %collective-permute-start.25 = (bf16[64,1280]{1,0:T(8,128)(2,1)S(1)}, bf16[64,1280]{1,0:T(8,128)(2,1)S(1)}, u32[]{:S(2)}, u32[]{:S(2)}) collective-permute-start(bf16[64,1280]{1,0:T(8,128)(2,1)S(1)} %slice.36), channel_id=1, source_target_pairs={{0,8},{2,10},{8,16},{10,18},{16,24},{18,26},{24,28},{26,30},{28,20... | collective-permute-start | bytes 491528 | tf_op jit(solution)/shard_map/ppermute | solution.py:186
  70.0 10.3 %copy-start.24 = (bf16[32,1280]{1,0:T(8,128)(2,1)}, bf16[32,1280]{1,0:T(8,128)(2,1)S(1)}, u32[]{:S(2)}) copy-start(bf16[32,1280]{1,0:T(8,128)(2,1)S(1)} %collective-permute-done.16.refs_16_) | copy-start | bytes 245764
  70.0 10.2 %collective-permute-start.26 = (bf16[64,1280]{1,0:T(8,128)(2,1)S(1)}, bf16[64,1280]{1,0:T(8,128)(2,1)S(1)}, u32[]{:S(2)}, u32[]{:S(2)}) collective-permute-start(bf16[64,1280]{1,0:T(8,128)(2,1)S(1)} %slice.37), channel_id=1, source_target_pairs={{0,4},{2,6},{8,0},{10,2},{16,8},{18,10},{24,16},{26,18},{28,24},{3... | collective-permute-start | bytes 491528 | tf_op jit(solution)/shard_map/ppermute | solution.py:186
  74.4 5.9 %copy-start.25 = (bf16[32,1280]{1,0:T(8,128)(2,1)}, bf16[32,1280]{1,0:T(8,128)(2,1)S(1)}, u32[]{:S(2)}) copy-start(bf16[32,1280]{1,0:T(8,128)(2,1)S(1)} %collective-permute-done.15.refs_15_) | copy-start | bytes 245764
  74.4 5.8 %collective-permute-start.17 = (bf16[32,1280]{1,0:T(8,128)(2,1)S(1)}, bf16[32,1280]{1,0:T(8,128)(2,1)S(1)}, u32[]{:S(2)}, u32[]{:S(2)}) collective-permute-start(bf16[32,1280]{1,0:T(8,128)(2,1)S(1)} %collective-permute-done.16.refs_16_), channel_id=1, source_target_pairs={{0,2},{2,0},{8,10},{10,8},{16,18},{18,16},{24,26},{26,24},{28,30},... | collective-permute-start | bytes 245768 | tf_op jit(solution)/shard_map/ppermute | solution.py:186
  80.2 0.6 copy-start.26
  80.2 0.7 copy-start.19
  80.2 0.7 copy-start.20
  80.2 0.8 copy-start.21
  81.0 0.7 copy-start.22
  93.4 29.6 %all-to-all-start = ((bf16[16,80,128]{2,1,0:T(8,128)(2,1)}), bf16[16,80,128]{2,1,0:T(8,128)(2,1)S(1)}, u32[]{:S(2)}, u32[]{:S(2)}) async-start(bf16[16,80,128]{2,1,0:T(8,128)(2,1)} %bitcast.16), calls=%async_computation | async-start | bytes 655360 | tf_op jit(solution)/shard_map/all_to_all | solution.py:400
  123.0 0.7 copy-start.1
  125.9 13.4 %all-to-all-start.1 = ((bf16[16,80,128]{2,1,0:T(8,128)(2,1)}), bf16[16,80,128]{2,1,0:T(8,128)(2,1)S(1)}, u32[]{:S(2)}, u32[]{:S(2)}) async-start(bf16[16,80,128]{2,1,0:T(8,128)(2,1)} %mix.1), calls=%async_computation.1 | async-start | bytes 655360 | tf_op jit(solution)/shard_map/all_to_all | solution.py:409
  130.4 1.3 copy-start.2
  139.3 0.7 copy-start
  150.4 5.1 %collective-permute-start.27 = (bf16[512,1024]{1,0:T(8,128)(2,1)}, bf16[512,1024]{1,0:T(8,128)(2,1)S(1)}, u32[]{:S(2)}, u32[]{:S(2)}) collective-permute-start(bf16[512,1024]{1,0:T(8,128)(2,1)} %out_half.3), channel_id=1, source_target_pairs={{0,1},{1,0},{2,3},{3,2},{4,5},{5,4},{6,7},{7,6},{8,9},{9,8},{10,11... | collective-permute-start | bytes 3145736 | tf_op jit(solution)/shard_map/ppermute | solution.py:438
Sparse Core Ops, SparseCore 0:
  10.1 111.7 all-gather.1

commit v2 on v1

--- a/solution.py
+++ b/solution.py
@@ -17,6 +17,7 @@
 VMEM_LIMIT = 56 * 1024 * 1024
 VMEM = pl.BlockSpec(memory_space=pltpu.VMEM)
 SMEM = pl.BlockSpec(memory_space=pltpu.SMEM)
+ANY = pl.BlockSpec(memory_space=pl.ANY)
 
 
 def carried_in(value, axis, combine, identity):
@@ -187,39 +188,40 @@
 
 
 def gather_rows(block):
-    rows = block.shape[0]
-    half, quarter = rows // 2, rows // 4
-    alone, pair = block[:half], block[half:]
-    pair = jnp.concatenate([pair, send(pair, ACROSS)], axis=0)
-
-    def ring(piece):
-        middle = piece.shape[0] // 2
-        up, down = [piece], [piece]
-        for _ in range(3):
-            up.append(send(up[-1], UP))
-            down.append(send(down[-1], DOWN))
-        up.append(send(up[-1][:middle], UP))
-        down.append(send(down[-1][middle:], DOWN))
-        return up, down
-
-    pieces = []
-    up, down = ring(alone)
-    for k in range(4):
-        for distance, piece in ((-k % 8, up[k]), (k, down[k]))[: 1 if k == 0 else 2]:
-            pieces.append((piece, [(distance, 0, half, 0)]))
-            pieces.append((send(piece, ACROSS), [(8 + distance, 0, half, 0)]))
-    for piece, row in ((up[4], 0), (down[4], quarter)):
-        pieces.append((piece, [(4, row, quarter, 0)]))
-        pieces.append((send(piece, ACROSS), [(12, row, quarter, 0)]))
-    up, down = ring(pair)
-    for k in range(4):
-        for distance, piece in ((-k % 8, up[k]), (k, down[k]))[: 1 if k == 0 else 2]:
-            pieces.append(
-                (piece, [(distance, half, half, 0), (8 + distance, half, half, half)])
-            )
-    pieces.append((up[4], [(4, half, half, 0)]))
-    pieces.append((down[4], [(12, half, half, 0)]))
-    return pieces
+    n = block.shape[0]
+    h, q = n // 2, n // 4
+    alone, pair = block[:h], block[h:]
+    up1, down1, across = send(alone, UP), send(alone, DOWN), send(pair, ACROSS)
+    both = jnp.concatenate([pair, across], axis=0)
+    up2 = send(jnp.concatenate([both, up1], axis=0), UP)
+    down2 = send(jnp.concatenate([both, down1], axis=0), DOWN)
+    x1 = send(jnp.concatenate([alone, up1, down1], axis=0), ACROSS)
+    up3, down3 = send(up2, UP), send(down2, DOWN)
+    x2 = send(jnp.concatenate([up2[n:], down2[n:]], axis=0), ACROSS)
+    up4 = send(up3[: n + q], UP)
+    down4 = send(jnp.concatenate([down3[:n], down3[n + q :]], axis=0), DOWN)
+    x3 = send(jnp.concatenate([up3[n:], down3[n:]], axis=0), ACROSS)
+    up5, down5 = send(up4[:h], UP), send(down4[h:n], DOWN)
+    x4 = send(jnp.concatenate([up4[n:], down4[n:]], axis=0), ACROSS)
+    pieces = [
+        (block, [(0, 0, n, 0)]),
+        (across, [(8, h, h, 0)]),
+        (up1, [(7, 0, h, 0)]),
+        (down1, [(1, 0, h, 0)]),
+        (x1, [(8, 0, h, 0), (15, 0, h, h), (9, 0, h, n)]),
+        (up2, [(7, h, h, 0), (15, h, h, h), (6, 0, h, n)]),
+        (down2, [(1, h, h, 0), (9, h, h, h), (2, 0, h, n)]),
+        (x2, [(14, 0, h, 0), (10, 0, h, h)]),
+        (up3, [(6, h, h, 0), (14, h, h, h), (5, 0, h, n)]),
+        (down3, [(2, h, h, 0), (10, h, h, h), (3, 0, h, n)]),
+        (x3, [(13, 0, h, 0), (11, 0, h, h)]),
+        (up4, [(5, h, h, 0), (13, h, h, h), (4, 0, q, n)]),
+        (down4, [(3, h, h, 0), (11, h, h, h), (4, q, q, n)]),
+        (x4, [(12, 0, h, 0)]),
+        (up5, [(4, h, h, 0)]),
+        (down5, [(12, h, h, 0)]),
+    ]
+    return [piece for piece, _ in pieces], [places for _, places in pieces], up4
 
 
 NT = (((1,), (1,)), ((), ()))
@@ -297,34 +299,29 @@
         normed[:, cols] = (combined * factor * gains[:, cols]).astype(jnp.bfloat16)
 
 
-def out_kernel(which, normed, weight, out):
-    out[...] = jnp.dot(normed[...], weight[...], preferred_element_type=jnp.float32).astype(
-        out.dtype
-    )
-
-
-def out_half(which, normed, weight, kind):
-    rows, depth = normed.shape
-    half = weight.shape[1] // 2
-    tile = 256
-    return pl.pallas_call(
-        out_kernel,
-        out_shape=jax.ShapeDtypeStruct((rows, half), kind),
-        grid_spec=pltpu.PrefetchScalarGridSpec(
-            num_scalar_prefetch=1,
-            grid=(half // tile,),
-            in_specs=[
-                pl.BlockSpec((rows, depth), lambda j, s: (0, 0)),
-                pl.BlockSpec((depth, tile), lambda j, s: (0, s[0] * (half // tile) + j)),
-            ],
-            out_specs=pl.BlockSpec((rows, tile), lambda j, s: (0, j)),
-        ),
-        compiler_params=pltpu.CompilerParams(vmem_limit_bytes=VMEM_LIMIT),
-        cost_estimate=pl.CostEstimate(
-            flops=2 * rows * depth * half, bytes_accessed=2 * depth * half, transcendentals=0
-        ),
-        name="out_half",
-    )(which, normed, weight)
+def out_kernel(layout, tile, count, slots, which, normed, *refs):
+    pieces, (theirs, mine, held, done) = refs[: len(layout)], refs[len(layout) :]
+    copies = []
+    for piece, places in zip(pieces, layout):
+        for slot, row, rows, source in places:
+            copies.append(
+                pltpu.make_async_copy(
+                    piece.at[pl.ds(source, rows)],
+                    held.at[slots[slot], pl.ds(row, rows)],
+                    done.at[len(copies)],
+                )
+            )
+    for copy in copies:
+        copy.start()
+    for copy in copies:
+        copy.wait()
+    for out, half in ((theirs, 1 - which[0]), (mine, which[0])):
+        for j in range(0, count // 2, 2):
+            first = half * (count // 2) + j
+            pair = jnp.concatenate([held[first], held[first + 1]], axis=1)
+            out[:, j * tile : (j + 2) * tile] = jnp.dot(
+                normed[...], pair, preferred_element_type=jnp.float32
+            ).astype(out.dtype)
 
 
 def per_device_fast(
@@ -346,8 +343,6 @@
     here, core = lax.axis_index("dp"), lax.axis_index("mp")
     params = pltpu.CompilerParams(vmem_limit_bytes=VMEM_LIMIT)
 
-    out_all = lax.all_gather(out_weight, "dp", axis=1, tiled=True)
-
     positions = here * count + jnp.arange(count, dtype=jnp.int32)
     request, starts, adapter = token_tables(lengths, adapter_ids, positions)
     bounds = jnp.cumsum(lengths)
@@ -373,9 +368,10 @@
     first, second, scale = jnp.asarray(first), jnp.asarray(second), jnp.asarray(scale)
 
     rows = v_weight.shape[0]
-    gathered = gather_rows(jnp.concatenate([v_weight, q_weight, k_weight], axis=1))
-    layout = [places for _, places in gathered]
-    pieces = [piece for piece, _ in gathered]
+    slots = ring_places()
+    pieces, layout, late = gather_rows(jnp.concatenate([v_weight, q_weight, k_weight], axis=1))
+    out_block, _ = lax.optimization_barrier((out_weight, late))
+    out_pieces, out_layout, _ = gather_rows(out_block)
     total_width = heads * (width + 2 * F)
     query, keys, values, state = pl.pallas_call(
         functools.partial(project_kernel, layout, rows, heads, width),
@@ -394,7 +390,7 @@
             transcendentals=0,
         ),
         name="project",
-    )(ring_places(), tokens, low, adapter_up, tail, first, second, scale.T, *pieces)
+    )(slots, tokens, low, adapter_up, tail, first, second, scale.T, *pieces)
 
     parts = state.reshape(blocks, heads * FEATS // blocks, width)
     parts = lax.all_to_all(parts, "dp", 0, 0, tiled=True)
@@ -434,9 +430,29 @@
         name="finish",
     )(within, query, carried, first, second, scale, follows, head_gain.reshape(1, -1))
 
-    theirs = out_half((1 - core).reshape(1).astype(jnp.int32), normed, out_all, jnp.bfloat16)
+    tile = out_weight.shape[1]
+    held_shape = (blocks, heads * width, tile)
+    theirs, mine = pl.pallas_call(
+        functools.partial(out_kernel, out_layout, tile, blocks),
+        out_shape=(
+            jax.ShapeDtypeStruct((count, blocks * tile // 2), jnp.bfloat16),
+            jax.ShapeDtypeStruct((count, blocks * tile // 2), jnp.float32),
+        ),
+        in_specs=[SMEM, SMEM, VMEM] + [ANY] * len(out_pieces),
+        out_specs=(VMEM, VMEM),
+        scratch_shapes=[
+            pltpu.VMEM(held_shape, jnp.bfloat16),
+            pltpu.SemaphoreType.DMA((sum(len(places) for places in out_layout),)),
+        ],
+        compiler_params=params,
+        cost_estimate=pl.CostEstimate(
+            flops=2 * count * heads * width * blocks * tile,
+            bytes_accessed=4 * count * blocks * tile,
+            transcendentals=0,
+        ),
+        name="out",
+    )(slots, core.reshape(1).astype(jnp.int32), normed, *out_pieces)
     received = lax.ppermute(theirs, "mp", [(0, 1), (1, 0)])
-    mine = out_half(core.reshape(1).astype(jnp.int32), normed, out_all, jnp.float32)
     return (mine + received.astype(jnp.float32)).astype(jnp.bfloat16)
 
 

time: 166 us -> 139 us (0.84)
  between operations: 13.7 us -> 0.66 us
  starting transfers between devices: 55.2 us -> 46.6 us
  matrix products: 4.06 us -> 1.43 us
  Pallas kernels: 34.7 us -> 32.2 us
  waiting for transfers between devices: 42.7 us -> 40.3 us
    all_to_all x1, starting transfers between devices: 17.4 us -> 5 us  [per_device_fast(): parts = lax.all_to_all(parts, 'dp', 0, 0, tiled=True)]
    all_to_all x1, waiting for transfers between devices: 11.3 us -> 2.87 us  [per_device_fast(): parts = lax.all_to_all(parts, 'dp', 0, 0, tiled=True)]
    ppermute x26 -> x30, waiting for transfers between devices: 28.4 us -> 34.5 us  [send(): return lax.ppermute(value, 'dp', pairs)]
    ppermute x26 -> x30, starting transfers between devices: 33.4 us -> 37.5 us  [send(): return lax.ppermute(value, 'dp', pairs)]
    ppermute x1, waiting for transfers between devices: 0.01 us -> 2.86 us  [per_device_fast(): received = lax.ppermute(theirs, 'mp', [(0, 1), (1, 0)])]
    dot_general x2, matrix products: 4.06 us -> 1.43 us  [per_device_fast(): partial = jnp.dot(tokens, piece, preferred_element_type=jnp.float32)]
    pallas_call x2 -> x1, Pallas kernels: 9.87 us -> 7.37 us  [per_device_fast(): pl.pallas_call(functools.partial(out_kernel, out_layout, tile, blocks), o...]
    all_to_all x1, waiting for transfers between devices: 2.24 us -> 0.01 us  [per_device_fast(): lax.all_to_all(mixed, 'dp', 0, 0, tiled=True).reshape(heads, FEATS, width)]
  transfers between devices with their start and end apart: 31 -> 34, of which waited for: 12 -> 10; matrix products, arithmetic and copies ran while one was open for 8% -> 7% of each run, Pallas kernels for 18% -> 18%
where the time goes in v2:
time: 139 us
  starting transfers between devices  46.6 us (34%)
  waiting for transfers between devices  40.3 us (29%)
  Pallas kernels  32.2 us (23%)
  other arithmetic  9.23 us (7%)
  local copies, waits for them, and re-layouts  8.2 us (6%)
  matrix products  1.43 us (1%)
    ppermute x30, starting transfers between devices, send(): return lax.ppermute(value, 'dp', pairs)  37.5 us
    ppermute x30, waiting for transfers between devices, send(): return lax.ppermute(value, 'dp', pairs)  34.5 us
    pallas_call x1, Pallas kernels, per_device_fast(): pl.pallas_call(functools.partial(project_kernel, layout, rows, heads, wid...  11.8 us
    pallas_call x1, Pallas kernels, per_device_fast(): pl.pallas_call(functools.partial(out_kernel, out_layout, tile, blocks), o...  7.37 us
    pallas_call x1, Pallas kernels, per_device_fast(): pl.pallas_call(functools.partial(finish_kernel, heads, width), out_shape=...  5.63 us
    pallas_call x1, Pallas kernels, per_device_fast(): pl.pallas_call(functools.partial(within_kernel, heads, width), out_shape=...  5.24 us
    all_to_all x1, starting transfers between devices, per_device_fast(): parts = lax.all_to_all(parts, 'dp', 0, 0, tiled=True)  5 us
    unnamed x72, local copies, waits for them, and re-layouts  4.82 us
  transfers between devices with their start and end apart: 34, of which 10 were waited for; matrix products, arithmetic and copies ran while one was open for 7% of the time, Pallas kernels for 18%

profile of v2, /device:TPU:0, one launch (start us, length us, event | category | flops | bytes accessed | tf_op | source)
XLA Modules:
  0.0 138.5 jit_solution(9382300631904268158)
XLA Ops:
  0.0 1.0 constant_dynamic-update-slice_fusion.2
  1.0 0.8 constant_dynamic-update-slice_fusion.1
  1.8 0.8 constant_dynamic-update-slice_fusion.refs_0_
  2.6 3.1 %collective-permute-start.2 = (bf16[64,1280]{1,0:T(8,128)(2,1)S(1)}, bf16[64,1280]{1,0:T(8,128)(2,1)S(1)}, u32[]{:S(2)}, u32[]{:S(2)}) collective-permute-start(bf16[64,1280]{1,0:T(8,128)(2,1)S(1)} %get-tuple-element.24), channel_id=1, source_target_pairs={{0,8},{2,10},{8,16},{10,18},{16,24},{18,26},{24,28},{26,30},{28,20... | collective-permute-start | bytes 491528 | tf_op jit(solution)/shard_map/ppermute | solution.py:187
  5.7 1.9 %collective-permute-start.1 = (bf16[64,1280]{1,0:T(8,128)(2,1)S(1)}, bf16[64,1280]{1,0:T(8,128)(2,1)S(1)}, u32[]{:S(2)}, u32[]{:S(2)}) collective-permute-start(bf16[64,1280]{1,0:T(8,128)(2,1)S(1)} %get-tuple-element.25), channel_id=1, source_target_pairs={{0,2},{2,0},{8,10},{10,8},{16,18},{18,16},{24,26},{26,24},{28,30},... | collective-permute-start | bytes 491528 | tf_op jit(solution)/shard_map/ppermute | solution.py:187
  7.6 0.8 reduce-window.8
  8.6 0.6 fusion.5
  9.2 0.6 pad_add_fusion.slots
  9.8 0.9 select_reduce_fusion
  10.6 1.9 %collective-permute-done.1.refs_1_ = bf16[64,1280]{1,0:T(8,128)(2,1)S(1)} collective-permute-done((bf16[64,1280]{1,0:T(8,128)(2,1)S(1)}, bf16[64,1280]{1,0:T(8,128)(2,1)S(1)}, u32[]{:S(2)}, u32[]{:S(2)}) %collective-permute-start.1) | collective-permute-done | bytes 163872 | tf_op jit(solution)/shard_map/ppermute | solution.py:187
  12.6 1.9 %collective-permute-start.5 = (bf16[192,1280]{1,0:T(8,128)(2,1)S(1)}, bf16[192,1280]{1,0:T(8,128)(2,1)S(1)}, u32[]{:S(2)}, u32[]{:S(2)}) collective-permute-start(bf16[192,1280]{1,0:T(8,128)(2,1)S(1)} %get-tuple-element.22), channel_id=1, source_target_pairs={{0,8},{2,10},{8,16},{10,18},{16,24},{18,26},{24,28},{26,30},{28,20... | collective-permute-start | bytes 1474568 | tf_op jit(solution)/shard_map/ppermute | solution.py:187
  14.5 0.2 collective-permute-start.6
  14.7 1.2 compare_convert_fusion.2.tail
  16.0 0.7 fusion
  16.7 1.8 %collective-permute-start.4 = (bf16[192,1280]{1,0:T(8,128)(2,1)S(1)}, bf16[192,1280]{1,0:T(8,128)(2,1)S(1)}, u32[]{:S(2)}, u32[]{:S(2)}) collective-permute-start(bf16[192,1280]{1,0:T(8,128)(2,1)S(1)} %get-tuple-element.23), channel_id=1, source_target_pairs={{0,2},{2,0},{8,10},{10,8},{16,18},{18,16},{24,26},{26,24},{28,30},... | collective-permute-start | bytes 1474568 | tf_op jit(solution)/shard_map/ppermute | solution.py:187
  18.5 7.1 %collective-permute-done.5.refs_5_ = bf16[192,1280]{1,0:T(8,128)(2,1)S(1)} collective-permute-done((bf16[192,1280]{1,0:T(8,128)(2,1)S(1)}, bf16[192,1280]{1,0:T(8,128)(2,1)S(1)}, u32[]{:S(2)}, u32[]{:S(2)}) %collective-permute-start.5) | collective-permute-done | bytes 491552 | tf_op jit(solution)/shard_map/ppermute | solution.py:187
  25.6 1.7 %collective-permute-start.8 = (bf16[192,1280]{1,0:T(8,128)(2,1)S(1)}, bf16[192,1280]{1,0:T(8,128)(2,1)S(1)}, u32[]{:S(2)}, u32[]{:S(2)}) collective-permute-start(bf16[192,1280]{1,0:T(8,128)(2,1)S(1)} %collective-permute-done.5.refs_5_), channel_id=1, source_target_pairs={{0,8},{2,10},{8,16},{10,18},{16,24},{18,26},{24,28},{26,30},{28,20... | collective-permute-start | bytes 1474568 | tf_op jit(solution)/shard_map/ppermute | solution.py:187
  27.4 0.3 collective-permute-start.9
  27.7 0.7 fusion.1
  28.4 0.8 maximum_select_fusion.low
  29.3 1.7 %collective-permute-start.7 = (bf16[128,1280]{1,0:T(8,128)(2,1)S(1)}, bf16[128,1280]{1,0:T(8,128)(2,1)S(1)}, u32[]{:S(2)}, u32[]{:S(2)}) collective-permute-start(bf16[128,1280]{1,0:T(8,128)(2,1)S(1)} %pad_maximum_fusion.9), channel_id=1, source_target_pairs={{0,2},{2,0},{8,10},{10,8},{16,18},{18,16},{24,26},{26,24},{28,30},... | collective-permute-start | bytes 983048 | tf_op jit(solution)/shard_map/ppermute | solution.py:187
  31.0 6.8 %collective-permute-done.8.refs_8_ = bf16[192,1280]{1,0:T(8,128)(2,1)S(1)} collective-permute-done((bf16[192,1280]{1,0:T(8,128)(2,1)S(1)}, bf16[192,1280]{1,0:T(8,128)(2,1)S(1)}, u32[]{:S(2)}, u32[]{:S(2)}) %collective-permute-start.8) | collective-permute-done | bytes 491552 | tf_op jit(solution)/shard_map/ppermute | solution.py:187
  37.8 1.6 %collective-permute-start.11 = (bf16[160,1280]{1,0:T(8,128)(2,1)S(1)}, bf16[160,1280]{1,0:T(8,128)(2,1)S(1)}, u32[]{:S(2)}, u32[]{:S(2)}) collective-permute-start(bf16[160,1280]{1,0:T(8,128)(2,1)S(1)} %slice.118), channel_id=1, source_target_pairs={{0,8},{2,10},{8,16},{10,18},{16,24},{18,26},{24,28},{26,30},{28,20... | collective-permute-start | bytes 1228808 | tf_op jit(solution)/shard_map/ppermute | solution.py:187
  39.5 0.5 collective-permute-start.12
  40.1 1.6 %collective-permute-start.10 = (bf16[128,1280]{1,0:T(8,128)(2,1)S(1)}, bf16[128,1280]{1,0:T(8,128)(2,1)S(1)}, u32[]{:S(2)}, u32[]{:S(2)}) collective-permute-start(bf16[128,1280]{1,0:T(8,128)(2,1)S(1)} %pad_maximum_fusion.10), channel_id=1, source_target_pairs={{0,2},{2,0},{8,10},{10,8},{16,18},{18,16},{24,26},{26,24},{28,30},... | collective-permute-start | bytes 983048 | tf_op jit(solution)/shard_map/ppermute | solution.py:187
  41.6 5.7 %collective-permute-done.11.refs_11_ = bf16[160,1280]{1,0:T(8,128)(2,1)S(1)} collective-permute-done((bf16[160,1280]{1,0:T(8,128)(2,1)S(1)}, bf16[160,1280]{1,0:T(8,128)(2,1)S(1)}, u32[]{:S(2)}, u32[]{:S(2)}) %collective-permute-start.11) | collective-permute-done | bytes 409632 | tf_op jit(solution)/shard_map/ppermute | solution.py:187
  47.4 1.6 %collective-permute-start.17 = (bf16[512,128]{1,0:T(8,128)(2,1)S(1)}, bf16[512,128]{1,0:T(8,128)(2,1)S(1)}, u32[]{:S(2)}, u32[]{:S(2)}) collective-permute-start(bf16[512,128]{1,0:T(8,128)(2,1)S(1)} %get-tuple-element.29), channel_id=1, source_target_pairs={{0,8},{2,10},{8,16},{10,18},{16,24},{18,26},{24,28},{26,30},{28,20... | collective-permute-start | bytes 393224 | tf_op jit(solution)/shard_map/ppermute | solution.py:187
  49.1 0.5 collective-permute-start.18
  49.6 1.6 %collective-permute-start.16 = (bf16[512,128]{1,0:T(8,128)(2,1)S(1)}, bf16[512,128]{1,0:T(8,128)(2,1)S(1)}, u32[]{:S(2)}, u32[]{:S(2)}) collective-permute-start(bf16[512,128]{1,0:T(8,128)(2,1)S(1)} %get-tuple-element.30), channel_id=1, source_target_pairs={{0,2},{2,0},{8,10},{10,8},{16,18},{18,16},{24,26},{26,24},{28,30},... | collective-permute-start | bytes 393224 | tf_op jit(solution)/shard_map/ppermute | solution.py:187
  51.2 4.5 %collective-permute-done.16.refs_1_ = bf16[512,128]{1,0:T(8,128)(2,1)S(1)} collective-permute-done((bf16[512,128]{1,0:T(8,128)(2,1)S(1)}, bf16[512,128]{1,0:T(8,128)(2,1)S(1)}, u32[]{:S(2)}, u32[]{:S(2)}) %collective-permute-start.16) | collective-permute-done | bytes 131104 | tf_op jit(solution)/shard_map/ppermute | solution.py:187
  55.7 1.2 collective-permute-start.13
  56.9 1.6 %collective-permute-start.14 = (bf16[64,1280]{1,0:T(8,128)(2,1)S(1)}, bf16[64,1280]{1,0:T(8,128)(2,1)S(1)}, u32[]{:S(2)}, u32[]{:S(2)}) collective-permute-start(bf16[64,1280]{1,0:T(8,128)(2,1)S(1)} %slice.123), channel_id=1, source_target_pairs={{0,8},{2,10},{8,16},{10,18},{16,24},{18,26},{24,28},{26,30},{28,20... | collective-permute-start | bytes 491528 | tf_op jit(solution)/shard_map/ppermute | solution.py:187
  58.5 0.5 collective-permute-start.15
  59.1 1.6 %collective-permute-start.20 = (bf16[1536,128]{1,0:T(8,128)(2,1)S(1)}, bf16[1536,128]{1,0:T(8,128)(2,1)S(1)}, u32[]{:S(2)}, u32[]{:S(2)}) collective-permute-start(bf16[1536,128]{1,0:T(8,128)(2,1)S(1)} %get-tuple-element.27), channel_id=1, source_target_pairs={{0,8},{2,10},{8,16},{10,18},{16,24},{18,26},{24,28},{26,30},{28,20... | collective-permute-start | bytes 1179656 | tf_op jit(solution)/shard_map/ppermute | solution.py:187
  60.7 0.5 collective-permute-start.21
  61.2 1.0 collective-permute-done.14.refs_14_
  62.2 1.6 %collective-permute-done.15.refs_15_ = bf16[64,1280]{1,0:T(8,128)(2,1)S(1)} collective-permute-done((bf16[64,1280]{1,0:T(8,128)(2,1)S(1)}, bf16[64,1280]{1,0:T(8,128)(2,1)S(1)}, u32[]{:S(2)}, u32[]{:S(2)}) %collective-permute-start.15) | collective-permute-done | bytes 163872 | tf_op jit(solution)/shard_map/ppermute | solution.py:187
  63.9 0.7 copy-done.31
  64.5 11.8 %project.1 = (bf16[512,128]{1,0:T(8,128)(2,1)}, bf16[512,128]{1,0:T(8,128)(2,1)}, bf16[512,1024]{1,0:T(8,128)(2,1)}, bf16[8,160,128]{2,1,0:T(8,128)(2,1)}) custom-call(s32[16]{0:T(128)} %pad_add_fusion.slots, bf16[512,2048]{1,0:T(8,128)(2,1)} %tokens.1, bf16[512,256]{1,0:T(8,128)(2,1)} %maximum_select_fusion.low, bf16[256,1024]{1,0:T(8,128)(2,1)} %up.1, ...), custom_call_target="tpu_custom_call" | custom-call | flops 2684354560 | bytes 10485760 | tf_op jit(solution)/shard_map/project/pallas_call | solution.py:376
  76.3 5.0 %all-to-all-start = ((bf16[16,80,128]{2,1,0:T(8,128)(2,1)}), bf16[16,80,128]{2,1,0:T(8,128)(2,1)S(1)}, u32[]{:S(2)}, u32[]{:S(2)}) async-start(bf16[16,80,128]{2,1,0:T(8,128)(2,1)} %bitcast.15), calls=%async_computation | async-start | bytes 655360 | tf_op jit(solution)/shard_map/all_to_all | solution.py:396
  81.4 2.0 %collective-permute-start.23 = (bf16[1536,128]{1,0:T(8,128)(2,1)S(1)}, bf16[1536,128]{1,0:T(8,128)(2,1)S(1)}, u32[]{:S(2)}, u32[]{:S(2)}) collective-permute-start(bf16[1536,128]{1,0:T(8,128)(2,1)S(1)} %collective-permute-done.20.refs_5_), channel_id=1, source_target_pairs={{0,8},{2,10},{8,16},{10,18},{16,24},{18,26},{24,28},{26,30},{28,20... | collective-permute-start | bytes 1179656 | tf_op jit(solution)/shard_map/ppermute | solution.py:187
  83.8 0.7 reshape.107.marks
  84.5 1.9 %collective-permute-start.19 = (bf16[1536,128]{1,0:T(8,128)(2,1)S(1)}, bf16[1536,128]{1,0:T(8,128)(2,1)}, u32[]{:S(2)}, u32[]{:S(2)}) collective-permute-start(bf16[1536,128]{1,0:T(8,128)(2,1)S(1)} %get-tuple-element.28), channel_id=1, source_target_pairs={{0,2},{2,0},{8,10},{10,8},{16,18},{18,16},{24,26},{26,24},{28,30},... | collective-permute-start | bytes 1179656 | tf_op jit(solution)/shard_map/ppermute | solution.py:187
  86.4 0.9 slice.126
  87.3 0.2 collective-permute-start.22
  87.5 2.9 %all-to-all-done.states = bf16[16,80,128]{2,1,0:T(8,128)(2,1)S(1)} async-done(((bf16[16,80,128]{2,1,0:T(8,128)(2,1)}), bf16[16,80,128]{2,1,0:T(8,128)(2,1)S(1)}, u32[]{:S(2)}, u32[]{:S(2)}) %all-to-all-start) | async-done | bytes 327712 | tf_op jit(solution)/shard_map/all_to_all | solution.py:396
  90.4 0.7 copy-done.1
  91.1 2.2 %mix.1 = bf16[16,80,128]{2,1,0:T(8,128)(2,1)} custom-call(f32[256]{0:T(256)} %reshape.107.marks, bf16[16,80,128]{2,1,0:T(8,128)(2,1)} %copy-done.1), custom_call_target="tpu_custom_call" | custom-call | tf_op jit(solution)/shard_map/mix/pallas_call | solution.py:397
  93.3 4.0 %all-to-all-start.1 = ((bf16[16,80,128]{2,1,0:T(8,128)(2,1)}), bf16[16,80,128]{2,1,0:T(8,128)(2,1)S(1)}, u32[]{:S(2)}, u32[]{:S(2)}) async-start(bf16[16,80,128]{2,1,0:T(8,128)(2,1)} %mix.1), calls=%async_computation.1 | async-start | bytes 655360 | tf_op jit(solution)/shard_map/all_to_all | solution.py:405
  97.4 2.0 %collective-permute-start.26 = (bf16[1280,128]{1,0:T(8,128)(2,1)S(1)}, bf16[1280,128]{1,0:T(8,128)(2,1)S(1)}, u32[]{:S(2)}, u32[]{:S(2)}) collective-permute-start(bf16[1280,128]{1,0:T(8,128)(2,1)S(1)} %slice.129), channel_id=1, source_target_pairs={{0,8},{2,10},{8,16},{10,18},{16,24},{18,26},{24,28},{26,30},{28,20... | collective-permute-start | bytes 983048 | tf_op jit(solution)/shard_map/ppermute | solution.py:187
  99.4 0.3 collective-permute-start.27
  99.8 2.0 %collective-permute-start.25 = (bf16[1024,128]{1,0:T(8,128)(2,1)S(1)}, bf16[1024,128]{1,0:T(8,128)(2,1)S(1)}, u32[]{:S(2)}, u32[]{:S(2)}) collective-permute-start(bf16[1024,128]{1,0:T(8,128)(2,1)S(1)} %pad_maximum_fusion.13), channel_id=1, source_target_pairs={{0,2},{2,0},{8,10},{10,8},{16,18},{18,16},{24,26},{26,24},{28,30},... | collective-permute-start | bytes 786440 | tf_op jit(solution)/shard_map/ppermute | solution.py:187
  101.8 1.3 compare_convert_fusion.follows
  103.1 5.9 %collective-permute-done.27.refs_12_ = bf16[1280,128]{1,0:T(8,128)(2,1)S(1)} collective-permute-done((bf16[1280,128]{1,0:T(8,128)(2,1)S(1)}, bf16[1280,128]{1,0:T(8,128)(2,1)S(1)}, u32[]{:S(2)}, u32[]{:S(2)}) %collective-permute-start.27) | collective-permute-done | bytes 327712 | tf_op jit(solution)/shard_map/ppermute | solution.py:187
  109.1 1.5 %collective-permute-start.28 = (bf16[512,128]{1,0:T(8,128)(2,1)S(1)}, bf16[512,128]{1,0:T(8,128)(2,1)S(1)}, u32[]{:S(2)}, u32[]{:S(2)}) collective-permute-start(bf16[512,128]{1,0:T(8,128)(2,1)S(1)} %pad_maximum_fusion.15), channel_id=1, source_target_pairs={{0,2},{2,0},{8,10},{10,8},{16,18},{18,16},{24,26},{26,24},{28,30},... | collective-permute-start | bytes 393224 | tf_op jit(solution)/shard_map/ppermute | solution.py:187
  110.6 1.9 %collective-permute-start.29 = (bf16[512,128]{1,0:T(8,128)(2,1)S(1)}, bf16[512,128]{1,0:T(8,128)(2,1)S(1)}, u32[]{:S(2)}, u32[]{:S(2)}) collective-permute-start(bf16[512,128]{1,0:T(8,128)(2,1)S(1)} %slice.134), channel_id=1, source_target_pairs={{0,8},{2,10},{8,16},{10,18},{16,24},{18,26},{24,28},{26,30},{28,20... | collective-permute-start | bytes 393224 | tf_op jit(solution)/shard_map/ppermute | solution.py:187
  112.6 0.2 collective-permute-start.30
  112.8 5.2 %within.1 = f32[512,1024]{1,0:T(8,128)} custom-call(bf16[512,128]{1,0:T(8,128)(2,1)} %get-tuple-element.12.query, bf16[512,128]{1,0:T(8,128)(2,1)} %get-tuple-element.13.keys, bf16[512,1024]{1,0:T(8,128)(2,1)} %get-tuple-element.14.values, s32[1,512]{1,0:T(1,128)} %bitcast.18, s32[512,1]{1,0:T(8,128)} %copy-done.3), custom_call_target="tpu_custom_call" | custom-call | flops 1073741824 | bytes 2097152 | tf_op jit(solution)/shard_map/within/pallas_call | solution.py:407
  118.0 0.7 copy-done
  118.8 5.6 %finish.1.normed = bf16[512,1024]{1,0:T(8,128)(2,1)} custom-call(f32[512,1024]{1,0:T(8,128)} %within.1, bf16[512,128]{1,0:T(8,128)(2,1)} %get-tuple-element.12.query, bf16[8,160,128]{2,1,0:T(8,128)(2,1)} %bitcast.14, bf16[8,160,128]{2,1,0:T(8,128)(2,1)} %constant.101.clone.first, bf16[8,160,128]{2,1,0:T(8,128)(2,1)} %constant.102.clone.second, ...), custom_call_target="tpu_custom_call" | custom-call | flops 335544320 | bytes 2097152 | tf_op jit(solution)/shard_map/finish/pallas_call | solution.py:420
  124.5 0.6 copy-done.28
  125.3 7.4 %out.1 = (bf16[512,1024]{1,0:T(8,128)(2,1)}, f32[512,1024]{1,0:T(8,128)}) custom-call(s32[16]{0:T(128)} %pad_add_fusion.slots, s32[1]{0:T(128)} %bitcast.which, bf16[512,1024]{1,0:T(8,128)(2,1)} %finish.1.normed, bf16[1024,128]{1,0:T(8,128)(2,1)} %refs_0_, bf16[512,128]{1,0:T(8,128)(2,1)} %copy-done.16, bf16[512,128]{1,0:T(8,128)(2,1)} %copy-done.14, ...), custom_call_target="tpu_custom_call" | custom-call | flops 2147483648 | bytes 4194304 | tf_op jit(solution)/shard_map/out/pallas_call | solution.py:435
  132.7 2.9 %collective-permute-done.31 = bf16[512,1024]{1,0:T(8,128)(2,1)S(1)} collective-permute-done((bf16[512,1024]{1,0:T(8,128)(2,1)}, bf16[512,1024]{1,0:T(8,128)(2,1)S(1)}, u32[]{:S(2)}, u32[]{:S(2)}) %collective-permute-start.31) | collective-permute-done | bytes 1048608 | tf_op jit(solution)/shard_map/ppermute | solution.py:455
  135.6 3.0 %add_convert_fusion = bf16[512,1024]{1,0:T(8,128)(2,1)} fusion(f32[512,1024]{1,0:T(8,128)} %get-tuple-element.17, bf16[512,1024]{1,0:T(8,128)(2,1)S(1)} %collective-permute-done.31), kind=kLoop, calls=%fused_computation | loop fusion | flops 1572864 | bytes 4194304 | tf_op jit(solution)/shard_map/convert_element_type | solution.py:456
  (136 shorter events, 1.7 us)
Async XLA Ops:
  0.0 15.9 %copy-start.24 = (bf16[2048,128]{1,0:T(8,128)(2,1)S(1)}, bf16[2048,128]{1,0:T(8,128)(2,1)}, u32[]{:S(2)}) copy-start(bf16[2048,128]{1,0:T(8,128)(2,1)} %param.17) | copy-start | bytes 1572868
  2.6 14.1 %copy-start.2 = (bf16[128,1280]{1,0:T(8,128)(2,1)}, bf16[128,1280]{1,0:T(8,128)(2,1)S(1)}, u32[]{:S(2)}) copy-start(bf16[128,1280]{1,0:T(8,128)(2,1)S(1)} %constant_dynamic-update-slice_fusion.refs_0_) | copy-start | bytes 983044
  2.6 9.9 %collective-permute-start.2 = (bf16[64,1280]{1,0:T(8,128)(2,1)S(1)}, bf16[64,1280]{1,0:T(8,128)(2,1)S(1)}, u32[]{:S(2)}, u32[]{:S(2)}) collective-permute-start(bf16[64,1280]{1,0:T(8,128)(2,1)S(1)} %get-tuple-element.24), channel_id=1, source_target_pairs={{0,8},{2,10},{8,16},{10,18},{16,24},{18,26},{24,28},{26,30},{28,20... | collective-permute-start | bytes 491528 | tf_op jit(solution)/shard_map/ppermute | solution.py:187
  5.7 6.8 %collective-permute-start.3 = (bf16[64,1280]{1,0:T(8,128)(2,1)S(1)}, bf16[64,1280]{1,0:T(8,128)(2,1)S(1)}, u32[]{:S(2)}, u32[]{:S(2)}) collective-permute-start(bf16[64,1280]{1,0:T(8,128)(2,1)S(1)} %get-tuple-element.24), channel_id=1, source_target_pairs={{0,4},{2,6},{8,0},{10,2},{16,8},{18,10},{24,16},{26,18},{28,24},{3... | collective-permute-start | bytes 491528 | tf_op jit(solution)/shard_map/ppermute | solution.py:187
  5.7 22.0 %collective-permute-start = (bf16[2048,128]{1,0:T(8,128)(2,1)}, bf16[2048,128]{1,0:T(8,128)(2,1)S(1)}, u32[]{:S(2)}, u32[]{:S(2)}) collective-permute-start(bf16[2048,128]{1,0:T(8,128)(2,1)} %param.17), channel_id=1, source_target_pairs={{0,1},{1,0},{2,3},{3,2},{4,5},{5,4},{6,7},{7,6},{8,9},{9,8},{10,11... | collective-permute-start | bytes 1572872 | tf_op jit(solution)/shard_map/ppermute | solution.py:357
  5.7 6.8 %collective-permute-start.1 = (bf16[64,1280]{1,0:T(8,128)(2,1)S(1)}, bf16[64,1280]{1,0:T(8,128)(2,1)S(1)}, u32[]{:S(2)}, u32[]{:S(2)}) collective-permute-start(bf16[64,1280]{1,0:T(8,128)(2,1)S(1)} %get-tuple-element.25), channel_id=1, source_target_pairs={{0,2},{2,0},{8,10},{10,8},{16,18},{18,16},{24,26},{26,24},{28,30},... | collective-permute-start | bytes 491528 | tf_op jit(solution)/shard_map/ppermute | solution.py:187
  8.6 75.0 %copy-start.22 = (s32[512]{0:T(512)}, s32[512]{0:T(512)S(1)}, u32[]{:S(2)}) copy-start(s32[512]{0:T(512)S(1)} %convert_reduce_fusion) | copy-start | bytes 6148
  9.8 6.2 %copy-start.23 = (bf16[512,2048]{1,0:T(8,128)(2,1)S(1)}, bf16[512,2048]{1,0:T(8,128)(2,1)}, u32[]{:S(2)}) copy-start(bf16[512,2048]{1,0:T(8,128)(2,1)} %tokens.1) | copy-start | bytes 6291460
  12.5 4.2 %copy-start.11 = (bf16[64,1280]{1,0:T(8,128)(2,1)}, bf16[64,1280]{1,0:T(8,128)(2,1)S(1)}, u32[]{:S(2)}) copy-start(bf16[64,1280]{1,0:T(8,128)(2,1)S(1)} %collective-permute-done.1.refs_1_) | copy-start | bytes 491524
  12.5 4.2 %copy-start.9 = (bf16[64,1280]{1,0:T(8,128)(2,1)}, bf16[64,1280]{1,0:T(8,128)(2,1)S(1)}, u32[]{:S(2)}) copy-start(bf16[64,1280]{1,0:T(8,128)(2,1)S(1)} %collective-permute-done.2.refs_2_) | copy-start | bytes 491524
  12.5 4.2 %copy-start.10 = (bf16[64,1280]{1,0:T(8,128)(2,1)}, bf16[64,1280]{1,0:T(8,128)(2,1)S(1)}, u32[]{:S(2)}) copy-start(bf16[64,1280]{1,0:T(8,128)(2,1)S(1)} %collective-permute-done.3.refs_3_) | copy-start | bytes 491524
  12.6 13.0 %collective-permute-start.5 = (bf16[192,1280]{1,0:T(8,128)(2,1)S(1)}, bf16[192,1280]{1,0:T(8,128)(2,1)S(1)}, u32[]{:S(2)}, u32[]{:S(2)}) collective-permute-start(bf16[192,1280]{1,0:T(8,128)(2,1)S(1)} %get-tuple-element.22), channel_id=1, source_target_pairs={{0,8},{2,10},{8,16},{10,18},{16,24},{18,26},{24,28},{26,30},{28,20... | collective-permute-start | bytes 1474568 | tf_op jit(solution)/shard_map/ppermute | solution.py:187
  14.5 12.9 %collective-permute-start.6 = (bf16[192,1280]{1,0:T(8,128)(2,1)S(1)}, bf16[192,1280]{1,0:T(8,128)(2,1)S(1)}, u32[]{:S(2)}, u32[]{:S(2)}) collective-permute-start(bf16[192,1280]{1,0:T(8,128)(2,1)S(1)} %get-tuple-element.21), channel_id=1, source_target_pairs={{0,4},{2,6},{8,0},{10,2},{16,8},{18,10},{24,16},{26,18},{28,24},{3... | collective-permute-start | bytes 1474568 | tf_op jit(solution)/shard_map/ppermute | solution.py:187
  16.7 32.9 %collective-permute-start.4 = (bf16[192,1280]{1,0:T(8,128)(2,1)S(1)}, bf16[192,1280]{1,0:T(8,128)(2,1)S(1)}, u32[]{:S(2)}, u32[]{:S(2)}) collective-permute-start(bf16[192,1280]{1,0:T(8,128)(2,1)S(1)} %get-tuple-element.23), channel_id=1, source_target_pairs={{0,2},{2,0},{8,10},{10,8},{16,18},{18,16},{24,26},{26,24},{28,30},... | collective-permute-start | bytes 1474568 | tf_op jit(solution)/shard_map/ppermute | solution.py:187
  25.6 3.6 %copy-start.19 = (bf16[192,1280]{1,0:T(8,128)(2,1)}, bf16[192,1280]{1,0:T(8,128)(2,1)S(1)}, u32[]{:S(2)}) copy-start(bf16[192,1280]{1,0:T(8,128)(2,1)S(1)} %collective-permute-done.5.refs_5_) | copy-start | bytes 1474564
  25.6 12.1 %collective-permute-start.8 = (bf16[192,1280]{1,0:T(8,128)(2,1)S(1)}, bf16[192,1280]{1,0:T(8,128)(2,1)S(1)}, u32[]{:S(2)}, u32[]{:S(2)}) collective-permute-start(bf16[192,1280]{1,0:T(8,128)(2,1)S(1)} %collective-permute-done.5.refs_5_), channel_id=1, source_target_pairs={{0,8},{2,10},{8,16},{10,18},{16,24},{18,26},{24,28},{26,30},{28,20... | collective-permute-start | bytes 1474568 | tf_op jit(solution)/shard_map/ppermute | solution.py:187
  27.4 1.9 %copy-start.20 = (bf16[192,1280]{1,0:T(8,128)(2,1)}, bf16[192,1280]{1,0:T(8,128)(2,1)S(1)}, u32[]{:S(2)}) copy-start(bf16[192,1280]{1,0:T(8,128)(2,1)S(1)} %collective-permute-done.6.refs_6_) | copy-start | bytes 1474564
  27.4 12.0 %collective-permute-start.9 = (bf16[192,1280]{1,0:T(8,128)(2,1)S(1)}, bf16[192,1280]{1,0:T(8,128)(2,1)S(1)}, u32[]{:S(2)}, u32[]{:S(2)}) collective-permute-start(bf16[192,1280]{1,0:T(8,128)(2,1)S(1)} %collective-permute-done.6.refs_6_), channel_id=1, source_target_pairs={{0,4},{2,6},{8,0},{10,2},{16,8},{18,10},{24,16},{26,18},{28,24},{3... | collective-permute-start | bytes 1474568 | tf_op jit(solution)/shard_map/ppermute | solution.py:187
  29.2 18.1 %copy-start.8 = (bf16[1024,128]{1,0:T(8,128)(2,1)S(1)}, bf16[1024,128]{1,0:T(8,128)(2,1)}, u32[]{:S(2)}) copy-start(bf16[1024,128]{1,0:T(8,128)(2,1)} %refs_0_) | copy-start | bytes 786436
  29.3 29.8 %collective-permute-start.7 = (bf16[128,1280]{1,0:T(8,128)(2,1)S(1)}, bf16[128,1280]{1,0:T(8,128)(2,1)S(1)}, u32[]{:S(2)}, u32[]{:S(2)}) collective-permute-start(bf16[128,1280]{1,0:T(8,128)(2,1)S(1)} %pad_maximum_fusion.9), channel_id=1, source_target_pairs={{0,2},{2,0},{8,10},{10,8},{16,18},{18,16},{24,26},{26,24},{28,30},... | collective-permute-start | bytes 983048 | tf_op jit(solution)/shard_map/ppermute | solution.py:187
  37.7 9.7 %copy-start.4 = (bf16[192,1280]{1,0:T(8,128)(2,1)}, bf16[192,1280]{1,0:T(8,128)(2,1)S(1)}, u32[]{:S(2)}) copy-start(bf16[192,1280]{1,0:T(8,128)(2,1)S(1)} %collective-permute-done.8.refs_8_) | copy-start | bytes 1474564
  37.8 9.6 %collective-permute-start.11 = (bf16[160,1280]{1,0:T(8,128)(2,1)S(1)}, bf16[160,1280]{1,0:T(8,128)(2,1)S(1)}, u32[]{:S(2)}, u32[]{:S(2)}) collective-permute-start(bf16[160,1280]{1,0:T(8,128)(2,1)S(1)} %slice.118), channel_id=1, source_target_pairs={{0,8},{2,10},{8,16},{10,18},{16,24},{18,26},{24,28},{26,30},{28,20... | collective-permute-start | bytes 1228808 | tf_op jit(solution)/shard_map/ppermute | solution.py:187
  39.4 11.8 %copy-start.5 = (bf16[192,1280]{1,0:T(8,128)(2,1)}, bf16[192,1280]{1,0:T(8,128)(2,1)S(1)}, u32[]{:S(2)}) copy-start(bf16[192,1280]{1,0:T(8,128)(2,1)S(1)} %collective-permute-done.9.refs_9_) | copy-start | bytes 1474564
  39.5 9.6 %collective-permute-start.12 = (bf16[160,1280]{1,0:T(8,128)(2,1)S(1)}, bf16[160,1280]{1,0:T(8,128)(2,1)S(1)}, u32[]{:S(2)}, u32[]{:S(2)}) collective-permute-start(bf16[160,1280]{1,0:T(8,128)(2,1)S(1)} %pad_maximum_fusion.6), channel_id=1, source_target_pairs={{0,4},{2,6},{8,0},{10,2},{16,8},{18,10},{24,16},{26,18},{28,24},{3... | collective-permute-start | bytes 1228808 | tf_op jit(solution)/shard_map/ppermute | solution.py:187
  40.1 20.7 %collective-permute-start.10 = (bf16[128,1280]{1,0:T(8,128)(2,1)S(1)}, bf16[128,1280]{1,0:T(8,128)(2,1)S(1)}, u32[]{:S(2)}, u32[]{:S(2)}) collective-permute-start(bf16[128,1280]{1,0:T(8,128)(2,1)S(1)} %pad_maximum_fusion.10), channel_id=1, source_target_pairs={{0,2},{2,0},{8,10},{10,8},{16,18},{18,16},{24,26},{26,24},{28,30},... | collective-permute-start | bytes 983048 | tf_op jit(solution)/shard_map/ppermute | solution.py:187
  47.4 16.4 %copy-start.12 = (bf16[160,1280]{1,0:T(8,128)(2,1)}, bf16[160,1280]{1,0:T(8,128)(2,1)S(1)}, u32[]{:S(2)}) copy-start(bf16[160,1280]{1,0:T(8,128)(2,1)S(1)} %collective-permute-done.11.refs_11_) | copy-start | bytes 1228804
  47.4 9.5 %collective-permute-start.17 = (bf16[512,128]{1,0:T(8,128)(2,1)S(1)}, bf16[512,128]{1,0:T(8,128)(2,1)S(1)}, u32[]{:S(2)}, u32[]{:S(2)}) collective-permute-start(bf16[512,128]{1,0:T(8,128)(2,1)S(1)} %get-tuple-element.29), channel_id=1, source_target_pairs={{0,8},{2,10},{8,16},{10,18},{16,24},{18,26},{24,28},{26,30},{28,20... | collective-permute-start | bytes 393224 | tf_op jit(solution)/shard_map/ppermute | solution.py:187
  49.1 14.8 %copy-start.13 = (bf16[160,1280]{1,0:T(8,128)(2,1)}, bf16[160,1280]{1,0:T(8,128)(2,1)S(1)}, u32[]{:S(2)}) copy-start(bf16[160,1280]{1,0:T(8,128)(2,1)S(1)} %collective-permute-done.12.refs_12_) | copy-start | bytes 1228804
  49.1 9.4 %collective-permute-start.18 = (bf16[512,128]{1,0:T(8,128)(2,1)S(1)}, bf16[512,128]{1,0:T(8,128)(2,1)S(1)}, u32[]{:S(2)}, u32[]{:S(2)}) collective-permute-start(bf16[512,128]{1,0:T(8,128)(2,1)S(1)} %get-tuple-element.29), channel_id=1, source_target_pairs={{0,4},{2,6},{8,0},{10,2},{16,8},{18,10},{24,16},{26,18},{28,24},{3... | collective-permute-start | bytes 393224 | tf_op jit(solution)/shard_map/ppermute | solution.py:187
  49.6 14.2 %copy-start.25 = (bf16[192,1280]{1,0:T(8,128)(2,1)}, bf16[192,1280]{1,0:T(8,128)(2,1)S(1)}, u32[]{:S(2)}) copy-start(bf16[192,1280]{1,0:T(8,128)(2,1)S(1)} %collective-permute-done.4.refs_4_) | copy-start | bytes 1474564
  49.6 6.1 %collective-permute-start.16 = (bf16[512,128]{1,0:T(8,128)(2,1)S(1)}, bf16[512,128]{1,0:T(8,128)(2,1)S(1)}, u32[]{:S(2)}, u32[]{:S(2)}) collective-permute-start(bf16[512,128]{1,0:T(8,128)(2,1)S(1)} %get-tuple-element.30), channel_id=1, source_target_pairs={{0,2},{2,0},{8,10},{10,8},{16,18},{18,16},{24,26},{26,24},{28,30},... | collective-permute-start | bytes 393224 | tf_op jit(solution)/shard_map/ppermute | solution.py:187
  55.7 20.6 %copy-start.16 = (bf16[512,128]{1,0:T(8,128)(2,1)}, bf16[512,128]{1,0:T(8,128)(2,1)S(1)}, u32[]{:S(2)}) copy-start(bf16[512,128]{1,0:T(8,128)(2,1)S(1)} %collective-permute-done.16.refs_1_) | copy-start | bytes 393220
  55.7 5.5 %collective-permute-start.13 = (bf16[64,1280]{1,0:T(8,128)(2,1)S(1)}, bf16[64,1280]{1,0:T(8,128)(2,1)S(1)}, u32[]{:S(2)}, u32[]{:S(2)}) collective-permute-start(bf16[64,1280]{1,0:T(8,128)(2,1)S(1)} %pad_maximum_fusion.14), channel_id=1, source_target_pairs={{0,2},{2,0},{8,10},{10,8},{16,18},{18,16},{24,26},{26,24},{28,30},... | collective-permute-start | bytes 491528 | tf_op jit(solution)/shard_map/ppermute | solution.py:187
  56.9 19.4 %copy-start.14 = (bf16[512,128]{1,0:T(8,128)(2,1)}, bf16[512,128]{1,0:T(8,128)(2,1)S(1)}, u32[]{:S(2)}) copy-start(bf16[512,128]{1,0:T(8,128)(2,1)S(1)} %collective-permute-done.17.refs_2_) | copy-start | bytes 393220
  56.9 5.3 %collective-permute-start.14 = (bf16[64,1280]{1,0:T(8,128)(2,1)S(1)}, bf16[64,1280]{1,0:T(8,128)(2,1)S(1)}, u32[]{:S(2)}, u32[]{:S(2)}) collective-permute-start(bf16[64,1280]{1,0:T(8,128)(2,1)S(1)} %slice.123), channel_id=1, source_target_pairs={{0,8},{2,10},{8,16},{10,18},{16,24},{18,26},{24,28},{26,30},{28,20... | collective-permute-start | bytes 491528 | tf_op jit(solution)/shard_map/ppermute | solution.py:187
  58.5 17.8 %copy-start.15 = (bf16[512,128]{1,0:T(8,128)(2,1)}, bf16[512,128]{1,0:T(8,128)(2,1)S(1)}, u32[]{:S(2)}) copy-start(bf16[512,128]{1,0:T(8,128)(2,1)S(1)} %collective-permute-done.18.refs_3_) | copy-start | bytes 393220
  58.5 5.3 %collective-permute-start.15 = (bf16[64,1280]{1,0:T(8,128)(2,1)S(1)}, bf16[64,1280]{1,0:T(8,128)(2,1)S(1)}, u32[]{:S(2)}, u32[]{:S(2)}) collective-permute-start(bf16[64,1280]{1,0:T(8,128)(2,1)S(1)} %slice.124), channel_id=1, source_target_pairs={{0,4},{2,6},{8,0},{10,2},{16,8},{18,10},{24,16},{26,18},{28,24},{3... | collective-permute-start | bytes 491528 | tf_op jit(solution)/shard_map/ppermute | solution.py:187
  59.1 4.7 %copy-start.26 = (bf16[128,1280]{1,0:T(8,128)(2,1)}, bf16[128,1280]{1,0:T(8,128)(2,1)S(1)}, u32[]{:S(2)}) copy-start(bf16[128,1280]{1,0:T(8,128)(2,1)S(1)} %collective-permute-done.7.refs_7_) | copy-start | bytes 983044
  59.1 22.2 %collective-permute-start.20 = (bf16[1536,128]{1,0:T(8,128)(2,1)S(1)}, bf16[1536,128]{1,0:T(8,128)(2,1)S(1)}, u32[]{:S(2)}, u32[]{:S(2)}) collective-permute-start(bf16[1536,128]{1,0:T(8,128)(2,1)S(1)} %get-tuple-element.27), channel_id=1, source_target_pairs={{0,8},{2,10},{8,16},{10,18},{16,24},{18,26},{24,28},{26,30},{28,20... | collective-permute-start | bytes 1179656 | tf_op jit(solution)/shard_map/ppermute | solution.py:187
  60.7 3.1 %copy-start.27 = (bf16[128,1280]{1,0:T(8,128)(2,1)}, bf16[128,1280]{1,0:T(8,128)(2,1)S(1)}, u32[]{:S(2)}) copy-start(bf16[128,1280]{1,0:T(8,128)(2,1)S(1)} %collective-permute-done.10.refs_10_) | copy-start | bytes 983044
  60.7 22.6 %collective-permute-start.21 = (bf16[1536,128]{1,0:T(8,128)(2,1)S(1)}, bf16[1536,128]{1,0:T(8,128)(2,1)}, u32[]{:S(2)}, u32[]{:S(2)}) collective-permute-start(bf16[1536,128]{1,0:T(8,128)(2,1)S(1)} %get-tuple-element.26), channel_id=1, source_target_pairs={{0,4},{2,6},{8,0},{10,2},{16,8},{18,10},{24,16},{26,18},{28,24},{3... | collective-permute-start | bytes 1179656 | tf_op jit(solution)/shard_map/ppermute | solution.py:187
  61.2 2.6 %copy-start.29 = (bf16[64,1280]{1,0:T(8,128)(2,1)}, bf16[64,1280]{1,0:T(8,128)(2,1)S(1)}, u32[]{:S(2)}) copy-start(bf16[64,1280]{1,0:T(8,128)(2,1)S(1)} %collective-permute-done.13.refs_13_) | copy-start | bytes 491524
  62.2 1.6 %copy-start.30 = (bf16[64,1280]{1,0:T(8,128)(2,1)}, bf16[64,1280]{1,0:T(8,128)(2,1)S(1)}, u32[]{:S(2)}) copy-start(bf16[64,1280]{1,0:T(8,128)(2,1)S(1)} %collective-permute-done.14.refs_14_) | copy-start | bytes 491524
  76.3 14.0 %all-to-all-start = ((bf16[16,80,128]{2,1,0:T(8,128)(2,1)}), bf16[16,80,128]{2,1,0:T(8,128)(2,1)S(1)}, u32[]{:S(2)}, u32[]{:S(2)}) async-start(bf16[16,80,128]{2,1,0:T(8,128)(2,1)} %bitcast.15), calls=%async_computation | async-start | bytes 655360 | tf_op jit(solution)/shard_map/all_to_all | solution.py:396
  81.4 18.1 %copy-start.21 = (bf16[1536,128]{1,0:T(8,128)(2,1)}, bf16[1536,128]{1,0:T(8,128)(2,1)S(1)}, u32[]{:S(2)}) copy-start(bf16[1536,128]{1,0:T(8,128)(2,1)S(1)} %collective-permute-done.20.refs_5_) | copy-start | bytes 1179652
  81.4 16.0 %collective-permute-start.23 = (bf16[1536,128]{1,0:T(8,128)(2,1)S(1)}, bf16[1536,128]{1,0:T(8,128)(2,1)S(1)}, u32[]{:S(2)}, u32[]{:S(2)}) collective-permute-start(bf16[1536,128]{1,0:T(8,128)(2,1)S(1)} %collective-permute-done.20.refs_5_), channel_id=1, source_target_pairs={{0,8},{2,10},{8,16},{10,18},{16,24},{18,26},{24,28},{26,30},{28,20... | collective-permute-start | bytes 1179656 | tf_op jit(solution)/shard_map/ppermute | solution.py:187
  83.4 16.0 %collective-permute-start.24 = (bf16[1536,128]{1,0:T(8,128)(2,1)}, bf16[1536,128]{1,0:T(8,128)(2,1)S(1)}, u32[]{:S(2)}, u32[]{:S(2)}) collective-permute-start(bf16[1536,128]{1,0:T(8,128)(2,1)} %collective-permute-done.21.refs_6_), channel_id=1, source_target_pairs={{0,4},{2,6},{8,0},{10,2},{16,8},{18,10},{24,16},{26,18},{28,24},{3... | collective-permute-start | bytes 1179656 | tf_op jit(solution)/shard_map/ppermute | solution.py:187
  83.7 18.1 %copy-start.3 = (s32[512,1]{1,0:T(8,128)}, s32[512,1]{1,0:T(8,128)S(1)}, u32[]{:S(2)}) copy-start(s32[512,1]{1,0:T(8,128)S(1)} %copy.26.col) | copy-start | bytes 6148
  84.5 28.1 %collective-permute-start.19 = (bf16[1536,128]{1,0:T(8,128)(2,1)S(1)}, bf16[1536,128]{1,0:T(8,128)(2,1)}, u32[]{:S(2)}, u32[]{:S(2)}) collective-permute-start(bf16[1536,128]{1,0:T(8,128)(2,1)S(1)} %get-tuple-element.28), channel_id=1, source_target_pairs={{0,2},{2,0},{8,10},{10,8},{16,18},{18,16},{24,26},{26,24},{28,30},... | collective-permute-start | bytes 1179656 | tf_op jit(solution)/shard_map/ppermute | solution.py:187
  87.3 37.1 %collective-permute-start.22 = (bf16[1024,128]{1,0:T(8,128)(2,1)S(1)}, bf16[1024,128]{1,0:T(8,128)(2,1)}, u32[]{:S(2)}, u32[]{:S(2)}) collective-permute-start(bf16[1024,128]{1,0:T(8,128)(2,1)S(1)} %pad_maximum_fusion.12), channel_id=1, source_target_pairs={{0,2},{2,0},{8,10},{10,8},{16,18},{18,16},{24,26},{26,24},{28,30},... | collective-permute-start | bytes 786440 | tf_op jit(solution)/shard_map/ppermute | solution.py:187
  93.3 24.8 %all-to-all-start.1 = ((bf16[16,80,128]{2,1,0:T(8,128)(2,1)}), bf16[16,80,128]{2,1,0:T(8,128)(2,1)S(1)}, u32[]{:S(2)}, u32[]{:S(2)}) async-start(bf16[16,80,128]{2,1,0:T(8,128)(2,1)} %mix.1), calls=%async_computation.1 | async-start | bytes 655360 | tf_op jit(solution)/shard_map/all_to_all | solution.py:405
  97.3 13.3 %copy-start.6 = (bf16[1536,128]{1,0:T(8,128)(2,1)}, bf16[1536,128]{1,0:T(8,128)(2,1)S(1)}, u32[]{:S(2)}) copy-start(bf16[1536,128]{1,0:T(8,128)(2,1)S(1)} %collective-permute-done.23.refs_8_) | copy-start | bytes 1179652
  97.4 11.6 %collective-permute-start.26 = (bf16[1280,128]{1,0:T(8,128)(2,1)S(1)}, bf16[1280,128]{1,0:T(8,128)(2,1)S(1)}, u32[]{:S(2)}, u32[]{:S(2)}) collective-permute-start(bf16[1280,128]{1,0:T(8,128)(2,1)S(1)} %slice.129), channel_id=1, source_target_pairs={{0,8},{2,10},{8,16},{10,18},{16,24},{18,26},{24,28},{26,30},{28,20... | collective-permute-start | bytes 983048 | tf_op jit(solution)/shard_map/ppermute | solution.py:187
  99.4 18.7 %copy-start.7 = (bf16[1536,128]{1,0:T(8,128)(2,1)}, bf16[1536,128]{1,0:T(8,128)(2,1)S(1)}, u32[]{:S(2)}) copy-start(bf16[1536,128]{1,0:T(8,128)(2,1)S(1)} %collective-permute-done.24.refs_9_) | copy-start | bytes 1179652
  99.4 9.6 %collective-permute-start.27 = (bf16[1280,128]{1,0:T(8,128)(2,1)S(1)}, bf16[1280,128]{1,0:T(8,128)(2,1)S(1)}, u32[]{:S(2)}, u32[]{:S(2)}) collective-permute-start(bf16[1280,128]{1,0:T(8,128)(2,1)S(1)} %pad_maximum_fusion.11), channel_id=1, source_target_pairs={{0,4},{2,6},{8,0},{10,2},{16,8},{18,10},{24,16},{26,18},{28,24},{3... | collective-permute-start | bytes 983048 | tf_op jit(solution)/shard_map/ppermute | solution.py:187
  99.8 24.6 %collective-permute-start.25 = (bf16[1024,128]{1,0:T(8,128)(2,1)S(1)}, bf16[1024,128]{1,0:T(8,128)(2,1)S(1)}, u32[]{:S(2)}, u32[]{:S(2)}) collective-permute-start(bf16[1024,128]{1,0:T(8,128)(2,1)S(1)} %pad_maximum_fusion.13), channel_id=1, source_target_pairs={{0,2},{2,0},{8,10},{10,8},{16,18},{18,16},{24,26},{26,24},{28,30},... | collective-permute-start | bytes 786440 | tf_op jit(solution)/shard_map/ppermute | solution.py:187
  109.0 9.0 %copy-start.18 = (bf16[1280,128]{1,0:T(8,128)(2,1)}, bf16[1280,128]{1,0:T(8,128)(2,1)S(1)}, u32[]{:S(2)}) copy-start(bf16[1280,128]{1,0:T(8,128)(2,1)S(1)} %collective-permute-done.27.refs_12_) | copy-start | bytes 983044
  109.0 9.0 %copy-start.17 = (bf16[1280,128]{1,0:T(8,128)(2,1)}, bf16[1280,128]{1,0:T(8,128)(2,1)S(1)}, u32[]{:S(2)}) copy-start(bf16[1280,128]{1,0:T(8,128)(2,1)S(1)} %collective-permute-done.26.refs_11_) | copy-start | bytes 983044
  109.1 15.3 %collective-permute-start.28 = (bf16[512,128]{1,0:T(8,128)(2,1)S(1)}, bf16[512,128]{1,0:T(8,128)(2,1)S(1)}, u32[]{:S(2)}, u32[]{:S(2)}) collective-permute-start(bf16[512,128]{1,0:T(8,128)(2,1)S(1)} %pad_maximum_fusion.15), channel_id=1, source_target_pairs={{0,2},{2,0},{8,10},{10,8},{16,18},{18,16},{24,26},{26,24},{28,30},... | collective-permute-start | bytes 393224 | tf_op jit(solution)/shard_map/ppermute | solution.py:187
  110.6 13.8 %collective-permute-start.29 = (bf16[512,128]{1,0:T(8,128)(2,1)S(1)}, bf16[512,128]{1,0:T(8,128)(2,1)S(1)}, u32[]{:S(2)}, u32[]{:S(2)}) collective-permute-start(bf16[512,128]{1,0:T(8,128)(2,1)S(1)} %slice.134), channel_id=1, source_target_pairs={{0,8},{2,10},{8,16},{10,18},{16,24},{18,26},{24,28},{26,30},{28,20... | collective-permute-start | bytes 393224 | tf_op jit(solution)/shard_map/ppermute | solution.py:187
  112.6 11.9 %collective-permute-start.30 = (bf16[512,128]{1,0:T(8,128)(2,1)S(1)}, bf16[512,128]{1,0:T(8,128)(2,1)S(1)}, u32[]{:S(2)}, u32[]{:S(2)}) collective-permute-start(bf16[512,128]{1,0:T(8,128)(2,1)S(1)} %slice.135), channel_id=1, source_target_pairs={{0,4},{2,6},{8,0},{10,2},{16,8},{18,10},{24,16},{26,18},{28,24},{3... | collective-permute-start | bytes 393224 | tf_op jit(solution)/shard_map/ppermute | solution.py:187
  124.4 0.8 copy-start.33
  124.5 0.8 copy-start.34
  132.6 2.9 %collective-permute-start.31 = (bf16[512,1024]{1,0:T(8,128)(2,1)}, bf16[512,1024]{1,0:T(8,128)(2,1)S(1)}, u32[]{:S(2)}, u32[]{:S(2)}) collective-permute-start(bf16[512,1024]{1,0:T(8,128)(2,1)} %get-tuple-element.18), channel_id=1, source_target_pairs={{0,1},{1,0},{2,3},{3,2},{4,5},{5,4},{6,7},{7,6},{8,9},{9,8},{10,11... | collective-permute-start | bytes 3145736 | tf_op jit(solution)/shard_map/ppermute | solution.py:455
  (5 other events, 3.6 us)

commit v3 on v0

--- a/solution.py
+++ b/solution.py
@@ -1,15 +1,22 @@
+import functools
 import math
 
 import jax
 import jax.numpy as jnp
+import numpy as np
 from jax import lax
+from jax.experimental import pallas as pl
+from jax.experimental.pallas import tpu as pltpu
 from jax.sharding import PartitionSpec as P
 
 F = 16
 R = 16
-
-
 EPSILON = 1e-05
+SQUARES = [(a, b) for a in range(F) for b in range(a, F)]
+FEATS = 160
+VMEM = pl.BlockSpec(memory_space=pltpu.VMEM)
+SMEM = pl.BlockSpec(memory_space=pltpu.SMEM)
+ANY = pl.BlockSpec(memory_space=pl.ANY)
 
 
 def carried_in(value, axis, combine, identity):
@@ -86,7 +93,7 @@
     )
 
 
-def per_device(
+def per_device_general(
     tokens,
     q_weight,
     k_weight,
@@ -103,23 +110,14 @@
     value_width = v_weight.shape[1] // heads_here
     positions = lax.axis_index("dp") * row_count + jnp.arange(row_count, dtype=jnp.int32)
     request, starts, adapter = token_tables(lengths, adapter_ids, positions)
-    query_sum = jnp.dot(
-        tokens,
-        lax.all_gather(q_weight, "dp", axis=0, tiled=True),
-        preferred_element_type=jnp.float32,
-    )
-    key_sum = jnp.dot(
-        tokens,
-        lax.all_gather(k_weight, "dp", axis=0, tiled=True),
-        preferred_element_type=jnp.float32,
-    )
-    value_sum = jnp.dot(
-        tokens,
-        lax.all_gather(v_weight, "dp", axis=0, tiled=True),
-        preferred_element_type=jnp.float32,
-    )
-    query = query_sum.astype(jnp.bfloat16).reshape(row_count, heads_here, F)
-    key_rows = key_sum.astype(jnp.bfloat16).reshape(row_count, heads_here, F)
+    together = lax.all_gather(
+        jnp.concatenate([q_weight, k_weight, v_weight], axis=1), "dp", axis=0, tiled=True
+    )
+    sums = jnp.dot(tokens, together, preferred_element_type=jnp.float32)
+    width = heads_here * F
+    query = sums[:, :width].astype(jnp.bfloat16).reshape(row_count, heads_here, F)
+    key_rows = sums[:, width : 2 * width].astype(jnp.bfloat16).reshape(row_count, heads_here, F)
+    value_sum = sums[:, 2 * width :]
     piece = lax.all_gather(adapter_down, "mp", axis=1, tiled=True)
     partial_low = jnp.dot(tokens, piece, preferred_element_type=jnp.float32)
     owners = jnp.arange(piece.shape[1], dtype=jnp.int32) // R
@@ -143,6 +141,458 @@
     )
 
 
+def feature_tables():
+    first = np.zeros((FEATS, 128), np.float32)
+    second = np.zeros((FEATS, 128), np.float32)
+    scale = np.zeros((8, FEATS), np.float32)
+    scale[:, 0] = 1.0
+    for a in range(F):
+        first[1 + a, a] = 1.0
+        scale[1, 1 + a] = 1.0
+        scale[2, 1 + a] = scale[3, 1 + a] = 0.5
+    for at, (a, b) in enumerate(SQUARES):
+        row = 1 + F + at
+        first[row, a] = second[row, b] = 1.0
+        scale[2, row] = 0.25 / math.sqrt(2.0)
+        scale[3, row] = (0.25 if a == b else 0.5) / math.sqrt(2.0)
+    return jnp.asarray(first), jnp.asarray(second), jnp.asarray(scale)
+
+
+def table_of(table, head):
+    turned = pltpu.roll(table[...], head * F, 1) if head else table[...]
+    return turned.astype(jnp.bfloat16)
+
+
+def chip(place, x):
+    z, y = (place, 0) if place < 4 else (7 - place, 1)
+    return z * 4 + y * 2 + x
+
+
+def moves(step, flip):
+    return [
+        (chip(r, x), chip((r + step) % 8, x ^ flip)) for r in range(8) for x in range(2)
+    ]
+
+
+UP, DOWN, ACROSS = moves(1, 0), moves(-1, 0), moves(0, 1)
+
+
+def place_of(here, slot):
+    z, y, x = here // 4, (here // 2) % 2, here % 2
+    there = (jnp.where(y == 0, z, 7 - z) + slot % 8) % 8
+    base = jnp.where(there < 4, there * 4, (7 - there) * 4 + 2)
+    return base + (x if slot < 8 else 1 - x)
+
+
+def request_of(positions, lengths):
+    bound, request = 0, jnp.zeros_like(positions)
+    for k in range(lengths.shape[0]):
+        bound = bound + lengths[k]
+        request = request + jnp.where(positions >= bound, 1, 0)
+    return request
+
+
+def params(mebibytes):
+    return pltpu.CompilerParams(vmem_limit_bytes=mebibytes * 1024 * 1024)
+
+
+def send(value, pairs):
+    return lax.ppermute(value, "dp", pairs)
+
+
+def pack_kernel(recipes, sources, *refs):
+    for recipe, out in zip(recipes, refs[len(refs) - len(recipes) :]):
+        row = 0
+        for source, start, rows in recipe:
+            out[row : row + rows, :] = refs[source][start : start + rows, :]
+            row += rows
+
+
+def pack(recipes, sources, late=()):
+    wide = sources[0].shape[1]
+    return pl.pallas_call(
+        functools.partial(pack_kernel, recipes, len(sources)),
+        out_shape=[
+            jax.ShapeDtypeStruct((sum(part[2] for part in recipe), wide), jnp.bfloat16)
+            for recipe in recipes
+        ],
+        in_specs=[VMEM] * len(sources) + [ANY] * len(late),
+        out_specs=[VMEM] * len(recipes),
+        compiler_params=params(6),
+        name="pack",
+    )(*sources, *late)
+
+
+def gather_rows(alone, pair):
+    h = alone.shape[0]
+    n, q = 2 * h, h // 2
+    up1, down1, across = send(alone, UP), send(alone, DOWN), send(pair, ACROSS)
+    late = yield up1, down1, across
+    to_up, to_down, to_x = pack(
+        [
+            [(1, 0, h), (2, 0, h), (3, 0, h)],
+            [(1, 0, h), (2, 0, h), (4, 0, h)],
+            [(0, 0, h), (3, 0, h), (4, 0, h)],
+        ],
+        [alone, pair, across, up1, down1],
+        late,
+    )
+    up2, down2, x1 = send(to_up, UP), send(to_down, DOWN), send(to_x, ACROSS)
+    yield up2, down2, x1
+    up3, down3 = send(up2, UP), send(down2, DOWN)
+    (to_x,) = pack([[(0, n, h), (1, n, h)]], [up2, down2])
+    x2 = send(to_x, ACROSS)
+    late = yield up3, down3, x2
+    to_up, to_down, to_x = pack(
+        [[(0, 0, n + q)], [(1, 0, n), (1, n + q, q)], [(0, n, h), (1, n, h)]],
+        [up3, down3],
+        (x1,) + tuple(late),
+    )
+    up4, down4, x3 = send(to_up, UP), send(to_down, DOWN), send(to_x, ACROSS)
+    late = yield up4, down4, x3
+    to_up, to_down, to_x = pack(
+        [[(0, 0, h)], [(1, h, h)], [(0, n, q), (1, n, q)]], [up4, down4], (x2,) + tuple(late)
+    )
+    up5, down5, x4 = send(to_up, UP), send(to_down, DOWN), send(to_x, ACROSS)
+    yield up5, down5, x4
+    yield [
+        (alone, [(0, 0, h, 0)]),
+        (pair, [(0, h, h, 0)]),
+        (across, [(8, h, h, 0)]),
+        (up1, [(7, 0, h, 0)]),
+        (down1, [(1, 0, h, 0)]),
+        (x1, [(8, 0, h, 0), (15, 0, h, h), (9, 0, h, n)]),
+        (up2, [(7, h, h, 0), (15, h, h, h), (6, 0, h, n)]),
+        (down2, [(1, h, h, 0), (9, h, h, h), (2, 0, h, n)]),
+        (x2, [(14, 0, h, 0), (10, 0, h, h)]),
+        (up3, [(6, h, h, 0), (14, h, h, h), (5, 0, h, n)]),
+        (down3, [(2, h, h, 0), (10, h, h, h), (3, 0, h, n)]),
+        (x3, [(13, 0, h, 0), (11, 0, h, h)]),
+        (up4, [(5, h, h, 0), (13, h, h, h), (4, 0, q, n)]),
+        (down4, [(3, h, h, 0), (11, h, h, h), (4, q, q, n)]),
+        (x4, [(12, 0, h, 0)]),
+        (up5, [(4, h, h, 0)]),
+        (down5, [(12, h, h, 0)]),
+    ]
+
+
+def piece_rows(pieces, layout, slot, row, rows, cols=slice(None)):
+    found = []
+    while rows:
+        for piece, places in zip(pieces, layout):
+            for at, first, count, source in places:
+                if at == slot and first <= row < first + count and rows:
+                    take = min(rows, first + count - row)
+                    start = source + row - first
+                    found.append(piece[start : start + take, cols])
+                    row, rows = row + take, rows - take
+    return found[0] if len(found) == 1 else jnp.concatenate(found, axis=0)
+
+
+NT = (((1,), (1,)), ((), ()))
+
+
+def join_kernel(values, query, keys, alone, pair, done):
+    half, wide = alone.shape[0], values.shape[1]
+    small = query.shape[1]
+    copies = []
+    for out, row in ((alone, 0), (pair, half)):
+        for source, at in ((values, 0), (query, wide), (keys, wide + small)):
+            copies.append(
+                pltpu.make_async_copy(
+                    source.at[pl.ds(row, half)],
+                    out.at[:, pl.ds(at, source.shape[1])],
+                    done.at[len(copies)],
+                )
+            )
+    for copy in copies:
+        copy.start()
+    for copy in copies:
+        copy.wait()
+
+
+def join(values, query, keys):
+    rows, wide = values.shape[0], values.shape[1] + query.shape[1] + keys.shape[1]
+    return pl.pallas_call(
+        join_kernel,
+        out_shape=[jax.ShapeDtypeStruct((rows // 2, wide), values.dtype)] * 2,
+        in_specs=[ANY] * 3,
+        out_specs=[VMEM] * 2,
+        scratch_shapes=[pltpu.SemaphoreType.DMA((6,))],
+        compiler_params=params(4),
+        name="join",
+    )(values, query, keys)
+
+
+def turn_kernel(rows, info, tokens, turned):
+    for slot in range(tokens.shape[1] // rows):
+        source = pl.ds(pl.multiple_of(place_of(info[0], slot) * rows, rows), rows)
+        turned[:, slot * rows : (slot + 1) * rows] = tokens[:, source]
+
+
+def low_kernel(info, lengths, adapter_ids, tokens, own, other, low):
+    count, wide = tokens.shape[0], own.shape[1]
+    positions = lax.broadcasted_iota(jnp.int32, (count, 1), 0) + info[0] * count
+    request = request_of(positions, lengths)
+    adapter = jnp.zeros_like(request)
+    for k in range(lengths.shape[0]):
+        adapter = jnp.where(request == k, adapter_ids[k], adapter)
+    owners = lax.broadcasted_iota(jnp.int32, (1, wide), 1) // R
+    for piece, place in ((own, info[1]), (other, 1 - info[1])):
+        partial = jnp.dot(tokens[...], piece[...], preferred_element_type=jnp.float32)
+        kept = adapter == owners + place * (wide // R)
+        cols = pl.ds(pl.multiple_of(place * wide, wide), wide)
+        low[:, cols] = jnp.where(kept, partial, 0.0).astype(jnp.bfloat16)
+
+
+def project_kernel(layout, rows, heads, width, info, lengths, tokens, low, up, first, second,
+                   scale, *refs):
+    pieces, (query, keys, values, state) = refs[: len(layout)], refs[len(layout) :]
+    count, depth = tokens.shape
+    wide = heads * width
+    small = heads * F
+
+    def product(cols):
+        total = None
+        for slot in range(0, depth // rows, 2):
+            weight = jnp.concatenate(
+                [piece_rows(pieces, layout, at, 0, rows, cols) for at in (slot, slot + 1)], axis=0
+            )
+            term = jnp.dot(
+                tokens[:, slot * rows : (slot + 2) * rows], weight,
+                preferred_element_type=jnp.float32,
+            )
+            total = term if total is None else total + term
+        return total
+
+    both = product(slice(wide, wide + 2 * small))
+    query[...] = both[:, :small].astype(jnp.bfloat16)
+    key_rows = both[:, small:].astype(jnp.bfloat16)
+    keys[...] = key_rows
+    positions = lax.broadcasted_iota(jnp.int32, (1, count), 1) + info[0] * count
+    end = request_of(jnp.full((1, 1), count - 1, jnp.int32) + info[0] * count, lengths)
+    tail = jnp.where(request_of(positions, lengths) == end, 1.0, 0.0)
+    maps = []
+    for h in range(heads):
+        a = lax.dot_general(table_of(first, h), key_rows, NT, preferred_element_type=jnp.float32)
+        b = lax.dot_general(table_of(second, h), key_rows, NT, preferred_element_type=jnp.float32)
+        mapped = ((a + scale[:, 0:1]) * (b + scale[:, 1:2])) * scale[:, 2:3]
+        maps.append((mapped * tail).astype(jnp.bfloat16))
+    for h in range(0, heads, 2):
+        cols = slice(h * width, (h + 2) * width)
+        total = product(cols)
+        total += jnp.dot(low[...], up[:, cols], preferred_element_type=jnp.float32)
+        values[:, cols] = total.astype(jnp.bfloat16)
+    for h in range(heads):
+        state[h] = jnp.dot(
+            maps[h], values[:, h * width : (h + 1) * width], preferred_element_type=jnp.float32
+        ).astype(jnp.bfloat16)
+
+
+def within_kernel(heads, width, info, lengths, query, keys, values, first, second, scale, within,
+                  maps):
+    count = query.shape[0]
+    cut = count // 2
+    lanes = lax.broadcasted_iota(jnp.int32, (1, heads * F), 1)
+    start = info[0] * count
+    row = request_of(lax.broadcasted_iota(jnp.int32, (1, count), 1) + start, lengths)
+    col = request_of(lax.broadcasted_iota(jnp.int32, (count, 1), 0) + start, lengths)
+    for low, high in ((0, cut), (cut, count)):
+        i = lax.broadcasted_iota(jnp.int32, (high - low, high), 0) + low
+        j = lax.broadcasted_iota(jnp.int32, (high - low, high), 1)
+        allowed = (j <= i) & (row[:, :high] == col[low:high, :])
+        for h in range(heads):
+            mine = jnp.where(lanes // F == h, 0.25, 0.0).astype(jnp.bfloat16)
+            s = lax.dot_general(
+                query[low:high, :] * mine, keys[:high, :], NT, preferred_element_type=jnp.float32
+            )
+            weights = 1.0 + s + 0.5 * s * s
+            weights = jnp.where(allowed, weights, 0.0).astype(jnp.bfloat16)
+            cols = slice(h * width, (h + 1) * width)
+            within[low:high, cols] = jnp.dot(
+                weights, values[:high, cols], preferred_element_type=jnp.float32
+            )
+    for h in range(heads):
+        a = lax.dot_general(query[...], table_of(first, h), NT, preferred_element_type=jnp.float32)
+        b = lax.dot_general(query[...], table_of(second, h), NT, preferred_element_type=jnp.float32)
+        mapped = ((a + scale[0:1, :]) * (b + scale[1:2, :])) * scale[3:4, :]
+        maps[h] = mapped.astype(jnp.bfloat16)
+
+
+def mix_kernel(blocks, count, lengths, states, mixed):
+    def request(position):
+        bound, found = 0, 0
+        for k in range(lengths.shape[0]):
+            bound = bound + lengths[k]
+            found = found + jnp.where(position >= bound, 1, 0)
+        return found
+
+    begin = [request(b * count) for b in range(blocks)]
+    end = [request((b + 1) * count - 1) for b in range(blocks)]
+    total = jnp.zeros(states.shape[1:], jnp.float32)
+    mixed[0] = total.astype(jnp.bfloat16)
+    for b in range(1, blocks):
+        whole = jnp.where(begin[b - 1] == end[b - 1], 1.0, 0.0)
+        goes_on = jnp.where(end[b - 1] == begin[b], 1.0, 0.0)
+        total = (states[b - 1].astype(jnp.float32) + whole * total) * goes_on
+        mixed[b] = total.astype(jnp.bfloat16)
+
+
+def finish_kernel(heads, width, info, lengths, within, maps, carried, gains, normed):
+    count = within.shape[0]
+    positions = lax.broadcasted_iota(jnp.int32, (count, 1), 0) + info[0] * count
+    begin = request_of(jnp.zeros((1, 1), jnp.int32) + info[0] * count, lengths)
+    follows = jnp.where(request_of(positions, lengths) == begin, 1.0, 0.0)
+    for h in range(heads):
+        cross = jnp.dot(maps[h], carried[h], preferred_element_type=jnp.float32)
+        cols = slice(h * width, (h + 1) * width)
+        combined = within[:, cols] + follows * cross
+        factor = lax.rsqrt(jnp.mean(combined * combined, axis=-1, keepdims=True) + EPSILON)
+        normed[:, cols] = (combined * factor * gains[:, cols]).astype(jnp.bfloat16)
+
+
+def out_kernel(layout, tile, blocks, info, normed, *refs):
+    pieces, (out,) = refs[: len(layout)], refs[len(layout) :]
+    depth = normed.shape[1]
+    step = depth // 4
+    for near in range(blocks // 2):
+        pair = (near, near + blocks // 2)
+        total = None
+        for row in range(0, depth, step):
+            both = jnp.concatenate(
+                [piece_rows(pieces, layout, slot, row, step) for slot in pair], axis=1
+            )
+            term = jnp.dot(normed[:, row : row + step], both, preferred_element_type=jnp.float32)
+            total = term if total is None else total + term
+        for k, slot in enumerate(pair):
+            place = place_of(info[0], slot)
+            at = jnp.where(place // (blocks // 2) == info[1], 0, blocks // 2) + place % (blocks // 2)
+            out[at] = total[:, k * tile : (k + 1) * tile].astype(jnp.bfloat16)
+
+
+def add_kernel(partial, received, out):
+    tile = partial.shape[2]
+    for k in range(received.shape[0]):
+        total = partial[k].astype(jnp.float32) + received[k].astype(jnp.float32)
+        out[:, k * tile : (k + 1) * tile] = total.astype(jnp.bfloat16)
+
+
+def call(kernel, name, mebibytes, cost, shapes, scalars, arrays, late=()):
+    shapes = [jax.ShapeDtypeStruct(shape, kind) for shape, kind in shapes]
+    given = len(scalars) + len(arrays)
+
+    def body(*refs):
+        kernel(*refs[:given], *refs[given + len(late) :])
+
+    return pl.pallas_call(
+        body,
+        out_shape=shapes,
+        in_specs=[SMEM] * len(scalars) + [VMEM] * len(arrays) + [ANY] * len(late),
+        out_specs=[VMEM] * len(shapes),
+        compiler_params=params(mebibytes),
+        cost_estimate=pl.CostEstimate(flops=cost[0], bytes_accessed=cost[1], transcendentals=0),
+        name=name,
+    )(*scalars, *arrays, *late)
+
+
+def per_device_fast(
+    tokens,
+    q_weight,
+    k_weight,
+    v_weight,
+    adapter_down,
+    adapter_up,
+    lengths,
+    adapter_ids,
+    head_gain,
+    out_weight,
+):
+    count, depth = tokens.shape
+    blocks = lax.axis_size("dp")
+    heads = q_weight.shape[1] // F
+    width = v_weight.shape[1] // heads
+    rows = v_weight.shape[0]
+    wide, small, total = heads * width, heads * F, heads * (width + 2 * F)
+    tile = out_weight.shape[1]
+    half = jnp.bfloat16
+    info = jnp.stack([lax.axis_index("dp"), lax.axis_index("mp")]).astype(jnp.int32)
+    first, second, scale = feature_tables()
+
+    alone, pair = join(v_weight, q_weight, k_weight)
+    other = lax.ppermute(adapter_down, "mp", [(0, 1), (1, 0)])
+    (turned,) = call(
+        functools.partial(turn_kernel, rows), "turn", 8, (0, 4 * count * depth),
+        [((count, depth), half)], [info], [tokens],
+    )
+    (low,) = call(
+        low_kernel, "low", 8, (4 * count * depth * adapter_down.shape[1], 2 * count * depth),
+        [((count, 2 * adapter_down.shape[1]), half)], [info, lengths, adapter_ids],
+        [tokens, adapter_down, other],
+    )
+
+    chain = gather_rows(alone, pair)
+    next(chain)
+    second_round = chain.send(())
+    third = next(chain)
+    out_alone, out_pair = pack(
+        [[(0, 0, wide // 2)], [(0, wide // 2, wide // 2)]], [out_weight], second_round[:2]
+    )
+    out_chain = gather_rows(out_alone, out_pair)
+    out_first = next(out_chain)
+    chain.send((turned, low) + out_first)
+    out_second = out_chain.send(third[:2])
+    fifth = chain.send(())
+    gathered = next(chain)
+    out_third = next(out_chain)
+
+    pieces, layout = [piece for piece, _ in gathered], [places for _, places in gathered]
+    query, keys, values, state = call(
+        functools.partial(project_kernel, layout, rows, heads, width), "project", 14,
+        (2 * count * depth * total, 2 * depth * total),
+        [
+            ((count, small), half),
+            ((count, small), half),
+            ((count, wide), half),
+            ((heads, FEATS, width), half),
+        ],
+        [info, lengths], [turned, low, adapter_up, first, second, scale.T, *pieces],
+    )
+    parts = state.reshape(blocks, heads * FEATS // blocks, width)
+    parts = lax.all_to_all(parts, "dp", 0, 0, tiled=True)
+    out_fourth = out_chain.send(())
+    out_chain.send(())
+    out_gathered = next(out_chain)
+    (mixed,) = call(
+        functools.partial(mix_kernel, blocks, count), "mix", 4, (0, 4 * parts.size),
+        [(parts.shape, half)], [lengths], [parts], out_third[:2],
+    )
+    carried = lax.all_to_all(mixed, "dp", 0, 0, tiled=True).reshape(heads, FEATS, width)
+    within, maps = call(
+        functools.partial(within_kernel, heads, width), "within", 12,
+        (4 * count * count * wide, 8 * count * wide),
+        [((count, wide), jnp.float32), ((heads, count, FEATS), half)],
+        [info, lengths], [query, keys, values, first, second, scale],
+    )
+    (normed,) = call(
+        functools.partial(finish_kernel, heads, width), "finish", 10,
+        (2 * count * FEATS * wide, 8 * count * wide), [((count, wide), half)],
+        [info, lengths],
+        [within, maps, carried, head_gain.reshape(1, -1)], out_fourth[:2],
+    )
+    pieces, layout = [piece for piece, _ in out_gathered], [places for _, places in out_gathered]
+    (partial,) = call(
+        functools.partial(out_kernel, layout, tile, blocks), "out", 12,
+        (2 * count * wide * blocks * tile, 4 * count * blocks * tile),
+        [((blocks, count, tile), half)], [info], [normed, *pieces],
+    )
+    received = lax.ppermute(partial[blocks // 2 :], "mp", [(0, 1), (1, 0)])
+    (result,) = call(
+        add_kernel, "add", 8, (0, 8 * count * wide), [((count, blocks // 2 * tile), half)], [],
+        [partial, received],
+    )
+    return result
+
+
 def solution(mesh):
     placed = (
         P("dp", None),
@@ -156,6 +606,11 @@
         P("mp"),
         P("mp", "dp"),
     )
+    fast = mesh.shape["dp"] == 16 and mesh.shape["mp"] == 2
     return jax.shard_map(
-        per_device, mesh=mesh, in_specs=placed, out_specs=P("dp", "mp"), check_vma=False
-    )
+        per_device_fast if fast else per_device_general,
+        mesh=mesh,
+        in_specs=placed,
+        out_specs=P("dp", "mp"),
+        check_vma=False,
+    )

time: 375 us -> 128 us (0.34)
  blocking collectives: 130 us -> 0 us
  waiting for transfers between devices: 111 us -> 46.5 us
  other arithmetic: 47.4 us -> 0.07 us
  starting transfers between devices: 0.16 us -> 42.1 us
  matrix products: 29.8 us -> 0 us
  Pallas kernels: 0 us -> 28.8 us
  local copies, waits for them, and re-layouts: 30.4 us -> 8.96 us
  between operations: 13.4 us -> 0.59 us
  loops' own time: 10.7 us -> 0 us
    all_gather x4 -> x0, waiting for transfers between devices: 101 us -> none  [the longest x1 59.6 us: carried_in(): lax.all_gather(part.astype(kind), axis)]
    all_gather x2 -> x0, blocking collectives: 92.3 us -> none  [the longest x1 46.2 us: per_device(): lax.all_gather(q_weight, 'dp', axis=0, tiled=True)]
    ppermute x0 -> x32, waiting for transfers between devices: none -> 46.4 us  [the longest x30 43.8 us: send(): return lax.ppermute(value, 'dp', pairs)]
    select_n x17 -> x0, other arithmetic: 39.3 us -> none  [the longest x16 38.7 us: turn(): return jax.tree.map(lambda a, b: jnp.where(reached, a, b), new, before)]
    unnamed x1 -> x0, blocking collectives: 37.5 us -> none
    ppermute x0 -> x32, starting transfers between devices: none -> 32.7 us  [the longest x30 32.7 us: send(): return lax.ppermute(value, 'dp', pairs)]
    dot_general x8 -> x0, matrix products: 29.8 us -> none  [the longest x1 5.91 us: per_device(): jnp.dot(normed, lax.all_gather(out_weight, 'dp', axis=1, tiled=True), pre...]
    pallas_call x0 -> x18, Pallas kernels: none -> 28.8 us  [the longest x8 23.8 us: call(): pl.pallas_call(body, out_shape=shapes, in_specs=[SMEM] * len(scalars) + [...]
  transfers between devices with their start and end apart: 5 -> 34, of which waited for: 5 -> 15; matrix products, arithmetic and copies ran while one was open for 25% -> 0% of each run, Pallas kernels for 0% -> 17%
where the time goes in v3:
time: 128 us; the launch traced here: 127 us
  waiting for transfers between devices  46.5 us (36%)
  starting transfers between devices  42.1 us (33%)
  Pallas kernels  28.8 us (22%)
  local copies, waits for them, and re-layouts  8.96 us (7%)
    ppermute x30, waiting for transfers between devices, send(): return lax.ppermute(value, 'dp', pairs)  43.8 us
    ppermute x30, starting transfers between devices, send(): return lax.ppermute(value, 'dp', pairs)  32.7 us
    pallas_call x8, Pallas kernels, call(): pl.pallas_call(body, out_shape=shapes, in_specs=[SMEM] * len(scalars) + [...  23.8 us
    unnamed x96, local copies, waits for them, and re-layouts  8.89 us
    all_to_all x1, starting transfers between devices, per_device_fast(): lax.all_to_all(mixed, 'dp', 0, 0, tiled=True).reshape(heads, FEATS, width)  5.43 us
    pallas_call x9, Pallas kernels, pack(): pl.pallas_call(functools.partial(pack_kernel, recipes, len(sources)), out...  4.89 us
    all_to_all x1, starting transfers between devices, per_device_fast(): parts = lax.all_to_all(parts, 'dp', 0, 0, tiled=True)  3.96 us
    ppermute x1, waiting for transfers between devices, per_device_fast(): received = lax.ppermute(partial[blocks // 2:], 'mp', [(0, 1), (1, 0)])  2.65 us
  transfers between devices with their start and end apart: 34, of which 15 were waited for; matrix products, arithmetic and copies ran while one was open for 0% of the time, Pallas kernels for 17%

profile of v3, /device:TPU:0, one launch (start us, length us, event | category | flops | bytes accessed | tf_op | source)
XLA Modules:
  0.0 127.0 jit_solution(2611096869957004473)
XLA Ops:
  0.0 1.1 copy-done.19
  1.1 0.8 copy-done.30
  1.9 0.8 copy-done.31
  2.7 3.0 %collective-permute-start.1 = (bf16[64,1280]{1,0:T(8,128)(2,1)S(1)}, bf16[64,1280]{1,0:T(8,128)(2,1)S(1)}, u32[]{:S(2)}, u32[]{:S(2)}) collective-permute-start(bf16[64,1280]{1,0:T(8,128)(2,1)S(1)} %get-tuple-element.34.refs_1_.refs_9_), channel_id=1, source_target_pairs={{0,2},{2,0},{8,10},{10,8},{16,18},{18,16},{24,26},{26,24},{28,30},... | collective-permute-start | bytes 491528 | tf_op jit(solution)/shard_map/ppermute | solution.py:200
  5.7 1.6 %collective-permute-start.2 = (bf16[64,1280]{1,0:T(8,128)(2,1)S(1)}, bf16[64,1280]{1,0:T(8,128)(2,1)S(1)}, u32[]{:S(2)}, u32[]{:S(2)}) collective-permute-start(bf16[64,1280]{1,0:T(8,128)(2,1)S(1)} %get-tuple-element.33.refs_0_.refs_8_), channel_id=1, source_target_pairs={{0,8},{2,10},{8,16},{10,18},{16,24},{18,26},{24,28},{26,30},{28,20... | collective-permute-start | bytes 491528 | tf_op jit(solution)/shard_map/ppermute | solution.py:200
  7.3 0.4 collective-permute-start.3
  7.8 2.2 %collective-permute-done.1.refs_2_.refs_10_ = bf16[64,1280]{1,0:T(8,128)(2,1)S(1)} collective-permute-done((bf16[64,1280]{1,0:T(8,128)(2,1)S(1)}, bf16[64,1280]{1,0:T(8,128)(2,1)S(1)}, u32[]{:S(2)}, u32[]{:S(2)}) %collective-permute-start.1) | collective-permute-done | bytes 163872 | tf_op jit(solution)/shard_map/ppermute | solution.py:200
  9.9 1.5 %collective-permute-done.2.refs_3_.refs_11_ = bf16[64,1280]{1,0:T(8,128)(2,1)S(1)} collective-permute-done((bf16[64,1280]{1,0:T(8,128)(2,1)S(1)}, bf16[64,1280]{1,0:T(8,128)(2,1)S(1)}, u32[]{:S(2)}, u32[]{:S(2)}) %collective-permute-start.2) | collective-permute-done | bytes 163872 | tf_op jit(solution)/shard_map/ppermute | solution.py:200
  11.4 1.3 %collective-permute-done.3.refs_4_.refs_12_ = bf16[64,1280]{1,0:T(8,128)(2,1)S(1)} collective-permute-done((bf16[64,1280]{1,0:T(8,128)(2,1)S(1)}, bf16[64,1280]{1,0:T(8,128)(2,1)S(1)}, u32[]{:S(2)}, u32[]{:S(2)}) %collective-permute-start.3) | collective-permute-done | bytes 163872 | tf_op jit(solution)/shard_map/ppermute | solution.py:200
  12.7 0.9 pack.9
  13.6 1.6 %collective-permute-start.5 = (bf16[192,1280]{1,0:T(8,128)(2,1)S(1)}, bf16[192,1280]{1,0:T(8,128)(2,1)S(1)}, u32[]{:S(2)}, u32[]{:S(2)}) collective-permute-start(bf16[192,1280]{1,0:T(8,128)(2,1)S(1)} %get-tuple-element.36), channel_id=1, source_target_pairs={{0,8},{2,10},{8,16},{10,18},{16,24},{18,26},{24,28},{26,30},{28,20... | collective-permute-start | bytes 1474568 | tf_op jit(solution)/shard_map/ppermute | solution.py:200
  15.2 0.4 collective-permute-start.6
  15.6 0.5 collective-permute-start.4
  16.1 8.9 %collective-permute-done.5.refs_0_.refs_1_.refs_14_ = bf16[192,1280]{1,0:T(8,128)(2,1)S(1)} collective-permute-done((bf16[192,1280]{1,0:T(8,128)(2,1)S(1)}, bf16[192,1280]{1,0:T(8,128)(2,1)S(1)}, u32[]{:S(2)}, u32[]{:S(2)}) %collective-permute-start.5) | collective-permute-done | bytes 491552 | tf_op jit(solution)/shard_map/ppermute | solution.py:200
  25.1 1.6 %collective-permute-start.8 = (bf16[192,1280]{1,0:T(8,128)(2,1)S(1)}, bf16[192,1280]{1,0:T(8,128)(2,1)}, u32[]{:S(2)}, u32[]{:S(2)}) collective-permute-start(bf16[192,1280]{1,0:T(8,128)(2,1)S(1)} %collective-permute-done.5.refs_0_.refs_1_.refs_14_), channel_id=1, source_target_pairs={{0,8},{2,10},{8,16},{10,18},{16,24},{18,26},{24,28},{26,30},{28,20... | collective-permute-start | bytes 1474568 | tf_op jit(solution)/shard_map/ppermute | solution.py:200
  26.6 0.5 collective-permute-start.9
  27.1 0.9 copy-done.16
  28.1 1.6 %collective-permute-start.10 = (bf16[512,128]{1,0:T(8,128)(2,1)S(1)}, bf16[512,128]{1,0:T(8,128)(2,1)S(1)}, u32[]{:S(2)}, u32[]{:S(2)}) collective-permute-start(bf16[512,128]{1,0:T(8,128)(2,1)S(1)} %get-tuple-element.38.refs_0_.refs_2_), channel_id=1, source_target_pairs={{0,8},{2,10},{8,16},{10,18},{16,24},{18,26},{24,28},{26,30},{28,20... | collective-permute-start | bytes 393224 | tf_op jit(solution)/shard_map/ppermute | solution.py:200
  29.7 0.5 collective-permute-start.11
  30.2 0.5 collective-permute-start.12
  30.8 1.2 turn.1.refs_3_.refs_2_
  32.0 2.3 %low.1.refs_4_.refs_3_ = bf16[512,256]{1,0:T(8,128)(2,1)S(1)} custom-call(s32[2]{0:T(128)S(1)} %pad_add_fusion.refs_0_, s32[4]{0:T(128)S(1)} %copy-done.32, s32[4]{0:T(128)S(1)} %copy-done.34, bf16[512,2048]{1,0:T(8,128)(2,1)S(1)} %copy-done, bf16[2048,128]{1,0:T(8,128)(2,1)S(1)} %copy-done.9, bf16[2048,128]{1,0:T(8,128)(2,1)} %collective-permute-done.refs_5_), custom_call_target="tpu_custom_call" | custom-call | flops 536870912 | bytes 2097152 | tf_op jit(solution)/shard_map/low/pallas_call | solution.py:487
  34.4 4.2 %collective-permute-done.10.refs_5_.refs_3_ = bf16[512,128]{1,0:T(8,128)(2,1)S(1)} collective-permute-done((bf16[512,128]{1,0:T(8,128)(2,1)S(1)}, bf16[512,128]{1,0:T(8,128)(2,1)S(1)}, u32[]{:S(2)}, u32[]{:S(2)}) %collective-permute-start.10) | collective-permute-done | bytes 131104 | tf_op jit(solution)/shard_map/ppermute | solution.py:200
  38.5 1.3 %collective-permute-done.11.refs_6_.refs_4_ = bf16[512,128]{1,0:T(8,128)(2,1)S(1)} collective-permute-done((bf16[512,128]{1,0:T(8,128)(2,1)S(1)}, bf16[512,128]{1,0:T(8,128)(2,1)S(1)}, u32[]{:S(2)}, u32[]{:S(2)}) %collective-permute-start.11) | collective-permute-done | bytes 131104 | tf_op jit(solution)/shard_map/ppermute | solution.py:200
  39.9 1.3 %pack.12 = (bf16[160,1280]{1,0:T(8,128)(2,1)S(1)}, bf16[160,1280]{1,0:T(8,128)(2,1)S(1)}, bf16[128,1280]{1,0:T(8,128)(2,1)S(1)}) custom-call(bf16[192,1280]{1,0:T(8,128)(2,1)} %collective-permute-done.8.refs_0_.refs_17_.refs_5_, bf16[192,1280]{1,0:T(8,128)(2,1)} %collective-permute-done.9.refs_1_.refs_18_.refs_6_, ...), custom_call_target="tpu_custom_call" | custom-call | tf_op jit(solution)/shard_map/pack/pallas_call | solution.py:213
  41.3 1.6 %collective-permute-start.14 = (bf16[160,1280]{1,0:T(8,128)(2,1)S(1)}, bf16[160,1280]{1,0:T(8,128)(2,1)S(1)}, u32[]{:S(2)}, u32[]{:S(2)}) collective-permute-start(bf16[160,1280]{1,0:T(8,128)(2,1)S(1)} %get-tuple-element.41), channel_id=1, source_target_pairs={{0,8},{2,10},{8,16},{10,18},{16,24},{18,26},{24,28},{26,30},{28,20... | collective-permute-start | bytes 1228808 | tf_op jit(solution)/shard_map/ppermute | solution.py:200
  42.9 0.4 collective-permute-start.15
  43.4 0.6 collective-permute-start.7
  44.0 1.5 %collective-permute-start.13 = (bf16[128,1280]{1,0:T(8,128)(2,1)S(1)}, bf16[128,1280]{1,0:T(8,128)(2,1)S(1)}, u32[]{:S(2)}, u32[]{:S(2)}) collective-permute-start(bf16[128,1280]{1,0:T(8,128)(2,1)S(1)} %get-tuple-element.40), channel_id=1, source_target_pairs={{0,2},{2,0},{8,10},{10,8},{16,18},{18,16},{24,26},{26,24},{28,30},... | collective-permute-start | bytes 983048 | tf_op jit(solution)/shard_map/ppermute | solution.py:200
  45.5 8.6 %collective-permute-done.7.refs_2_.refs_16_ = bf16[128,1280]{1,0:T(8,128)(2,1)S(1)} collective-permute-done((bf16[128,1280]{1,0:T(8,128)(2,1)S(1)}, bf16[128,1280]{1,0:T(8,128)(2,1)S(1)}, u32[]{:S(2)}, u32[]{:S(2)}) %collective-permute-start.7) | collective-permute-done | bytes 327712 | tf_op jit(solution)/shard_map/ppermute | solution.py:200
  54.2 0.6 collective-permute-start.16
  54.8 1.6 %collective-permute-start.17 = (bf16[64,1280]{1,0:T(8,128)(2,1)S(1)}, bf16[64,1280]{1,0:T(8,128)(2,1)S(1)}, u32[]{:S(2)}, u32[]{:S(2)}) collective-permute-start(bf16[64,1280]{1,0:T(8,128)(2,1)S(1)} %get-tuple-element.44), channel_id=1, source_target_pairs={{0,8},{2,10},{8,16},{10,18},{16,24},{18,26},{24,28},{26,30},{28,20... | collective-permute-start | bytes 491528 | tf_op jit(solution)/shard_map/ppermute | solution.py:200
  56.3 0.4 collective-permute-start.18
  56.8 1.0 pack.14
  57.8 1.6 %collective-permute-start.19 = (bf16[1536,128]{1,0:T(8,128)(2,1)}, bf16[1536,128]{1,0:T(8,128)(2,1)S(1)}, u32[]{:S(2)}, u32[]{:S(2)}) collective-permute-start(bf16[1536,128]{1,0:T(8,128)(2,1)} %get-tuple-element.52), channel_id=1, source_target_pairs={{0,8},{2,10},{8,16},{10,18},{16,24},{18,26},{24,28},{26,30},{28,20... | collective-permute-start | bytes 1179656 | tf_op jit(solution)/shard_map/ppermute | solution.py:200
  59.4 0.5 collective-permute-start.21
  60.1 1.6 %collective-permute-done.18.refs_24_ = bf16[64,1280]{1,0:T(8,128)(2,1)S(1)} collective-permute-done((bf16[64,1280]{1,0:T(8,128)(2,1)S(1)}, bf16[64,1280]{1,0:T(8,128)(2,1)S(1)}, u32[]{:S(2)}, u32[]{:S(2)}) %collective-permute-start.18) | collective-permute-done | bytes 163872 | tf_op jit(solution)/shard_map/ppermute | solution.py:200
  61.7 7.6 %project.1 = (bf16[512,128]{1,0:T(8,128)(2,1)S(1)}, bf16[512,128]{1,0:T(8,128)(2,1)S(1)}, bf16[512,1024]{1,0:T(8,128)(2,1)S(1)}, bf16[8,160,128]{2,1,0:T(8,128)(2,1)}) custom-call(s32[2]{0:T(128)S(1)} %pad_add_fusion.refs_0_, s32[4]{0:T(128)S(1)} %copy-done.32, bf16[512,2048]{1,0:T(8,128)(2,1)S(1)} %turn.1.refs_3_.refs_2_, ...), custom_call_target="tpu_custom_call" | custom-call | flops 2684354560 | bytes 5242880 | tf_op jit(solution)/shard_map/project/pallas_call | solution.py:487
  69.3 1.0 copy-done.42
  70.3 0.7 copy-done.44
  70.9 0.6 copy-done.46
  71.6 4.0 %all-to-all-start = ((bf16[16,80,128]{2,1,0:T(8,128)(2,1)}), bf16[16,80,128]{2,1,0:T(8,128)(2,1)S(1)}, u32[]{:S(2)}, u32[]{:S(2)}) async-start(bf16[16,80,128]{2,1,0:T(8,128)(2,1)} %bitcast.2), calls=%async_computation | async-start | bytes 655360 | tf_op jit(solution)/shard_map/all_to_all | solution.py:561
  75.6 2.0 %collective-permute-start.20 = (bf16[1536,128]{1,0:T(8,128)(2,1)S(1)}, bf16[1536,128]{1,0:T(8,128)(2,1)S(1)}, u32[]{:S(2)}, u32[]{:S(2)}) collective-permute-start(bf16[1536,128]{1,0:T(8,128)(2,1)S(1)} %collective-permute-done.19.refs_0_.refs_8_), channel_id=1, source_target_pairs={{0,8},{2,10},{8,16},{10,18},{16,24},{18,26},{24,28},{26,30},{28,20... | collective-permute-start | bytes 1179656 | tf_op jit(solution)/shard_map/ppermute | solution.py:200
  77.7 1.9 %collective-permute-start.23 = (bf16[1536,128]{1,0:T(8,128)(2,1)S(1)}, bf16[1536,128]{1,0:T(8,128)(2,1)S(1)}, u32[]{:S(2)}, u32[]{:S(2)}) collective-permute-start(bf16[1536,128]{1,0:T(8,128)(2,1)S(1)} %get-tuple-element.54), channel_id=1, source_target_pairs={{0,2},{2,0},{8,10},{10,8},{16,18},{18,16},{24,26},{26,24},{28,30},... | collective-permute-start | bytes 1179656 | tf_op jit(solution)/shard_map/ppermute | solution.py:200
  79.6 5.6 %collective-permute-done.20.refs_2_.refs_0_.refs_11_ = bf16[1536,128]{1,0:T(8,128)(2,1)S(1)} collective-permute-done((bf16[1536,128]{1,0:T(8,128)(2,1)S(1)}, bf16[1536,128]{1,0:T(8,128)(2,1)S(1)}, u32[]{:S(2)}, u32[]{:S(2)}) %collective-permute-start.20) | collective-permute-done | bytes 393248 | tf_op jit(solution)/shard_map/ppermute | solution.py:200
  85.2 1.4 %collective-permute-done.22.refs_3_.refs_1_.refs_12_ = bf16[1536,128]{1,0:T(8,128)(2,1)S(1)} collective-permute-done((bf16[1536,128]{1,0:T(8,128)(2,1)S(1)}, bf16[1536,128]{1,0:T(8,128)(2,1)S(1)}, u32[]{:S(2)}, u32[]{:S(2)}) %collective-permute-start.22) | collective-permute-done | bytes 393248 | tf_op jit(solution)/shard_map/ppermute | solution.py:200
  86.6 1.4 %mix.1 = bf16[16,80,128]{2,1,0:T(8,128)(2,1)} custom-call(s32[4]{0:T(128)S(1)} %copy-done.32, bf16[16,80,128]{2,1,0:T(8,128)(2,1)S(1)} %all-to-all-done.refs_1_, bf16[1536,128]{1,0:T(8,128)(2,1)S(1)} %collective-permute-done.20.refs_2_.refs_0_.refs_11_, bf16[1536,128]{1,0:T(8,128)(2,1)S(1)} %collective-permute-done.22.refs_3_.refs_1_.refs_12_), custom_call_target="tpu_custom_call" | custom-call | bytes 655360 | tf_op jit(solution)/shard_map/mix/pallas_call | solution.py:487
  88.1 5.4 %all-to-all-start.1 = ((bf16[16,80,128]{2,1,0:T(8,128)(2,1)}), bf16[16,80,128]{2,1,0:T(8,128)(2,1)}, u32[]{:S(2)}, u32[]{:S(2)}) async-start(bf16[16,80,128]{2,1,0:T(8,128)(2,1)} %mix.1), calls=%async_computation.1 | async-start | bytes 655360 | tf_op jit(solution)/shard_map/all_to_all | solution.py:569
  93.6 0.8 pack.15
  94.4 1.9 %collective-permute-start.24 = (bf16[1280,128]{1,0:T(8,128)(2,1)S(1)}, bf16[1280,128]{1,0:T(8,128)(2,1)S(1)}, u32[]{:S(2)}, u32[]{:S(2)}) collective-permute-start(bf16[1280,128]{1,0:T(8,128)(2,1)S(1)} %get-tuple-element.55), channel_id=1, source_target_pairs={{0,8},{2,10},{8,16},{10,18},{16,24},{18,26},{24,28},{26,30},{28,20... | collective-permute-start | bytes 983048 | tf_op jit(solution)/shard_map/ppermute | solution.py:200
  96.4 1.9 %collective-permute-start.26 = (bf16[1024,128]{1,0:T(8,128)(2,1)S(1)}, bf16[1024,128]{1,0:T(8,128)(2,1)S(1)}, u32[]{:S(2)}, u32[]{:S(2)}) collective-permute-start(bf16[1024,128]{1,0:T(8,128)(2,1)S(1)} %pack.16), channel_id=1, source_target_pairs={{0,2},{2,0},{8,10},{10,8},{16,18},{18,16},{24,26},{26,24},{28,30},... | collective-permute-start | bytes 786440 | tf_op jit(solution)/shard_map/ppermute | solution.py:200
  98.5 5.8 %collective-permute-done.26.refs_2_.refs_10_ = bf16[1024,128]{1,0:T(8,128)(2,1)S(1)} collective-permute-done((bf16[1024,128]{1,0:T(8,128)(2,1)S(1)}, bf16[1024,128]{1,0:T(8,128)(2,1)S(1)}, u32[]{:S(2)}, u32[]{:S(2)}) %collective-permute-start.26) | collective-permute-done | bytes 262176 | tf_op jit(solution)/shard_map/ppermute | solution.py:200
  104.4 1.1 collective-permute-done.25.refs_7_.refs_1_.refs_15_
  105.5 0.8 pack.17
  106.3 1.5 %collective-permute-start.28 = (bf16[512,128]{1,0:T(8,128)(2,1)}, bf16[512,128]{1,0:T(8,128)(2,1)}, u32[]{:S(2)}, u32[]{:S(2)}) collective-permute-start(bf16[512,128]{1,0:T(8,128)(2,1)} %get-tuple-element.58), channel_id=1, source_target_pairs={{0,2},{2,0},{8,10},{10,8},{16,18},{18,16},{24,26},{26,24},{28,30},... | collective-permute-start | bytes 393224 | tf_op jit(solution)/shard_map/ppermute | solution.py:200
  107.8 1.5 %collective-permute-start.29 = (bf16[512,128]{1,0:T(8,128)(2,1)}, bf16[512,128]{1,0:T(8,128)(2,1)}, u32[]{:S(2)}, u32[]{:S(2)}) collective-permute-start(bf16[512,128]{1,0:T(8,128)(2,1)} %get-tuple-element.59), channel_id=1, source_target_pairs={{0,8},{2,10},{8,16},{10,18},{16,24},{18,26},{24,28},{26,30},{28,20... | collective-permute-start | bytes 393224 | tf_op jit(solution)/shard_map/ppermute | solution.py:200
  109.3 0.5 collective-permute-start.30
  109.8 4.2 %within.1 = (f32[512,1024]{1,0:T(8,128)S(1)}, bf16[8,512,160]{2,1,0:T(8,128)(2,1)S(1)}) custom-call(s32[2]{0:T(128)S(1)} %pad_add_fusion.refs_0_, s32[4]{0:T(128)S(1)} %copy-done.32, bf16[512,128]{1,0:T(8,128)(2,1)S(1)} %copy-done.45, bf16[512,128]{1,0:T(8,128)(2,1)S(1)} %copy-done.47, bf16[512,1024]{1,0:T(8,128)(2,1)S(1)} %copy-done.43, ...), custom_call_target="tpu_custom_call" | custom-call | flops 1073741824 | bytes 4194304 | tf_op jit(solution)/shard_map/within/pallas_call | solution.py:487
  114.0 1.3 %copy-done.1 = bf16[8,512,160]{2,1,0:T(8,128)(2,1)} copy-done((bf16[8,512,160]{2,1,0:T(8,128)(2,1)}, bf16[8,512,160]{2,1,0:T(8,128)(2,1)S(1)}, u32[]{:S(2)}) %copy-start.1) | copy-done | bytes 1310744
  115.3 1.6 %copy-done.2 = bf16[8,512,160]{2,1,0:T(8,128)(2,1)S(1)} copy-done((bf16[8,512,160]{2,1,0:T(8,128)(2,1)S(1)}, bf16[8,512,160]{2,1,0:T(8,128)(2,1)}, u32[]{:S(2)}) %copy-start.2) | copy-done | bytes 1310744
  117.0 2.1 %finish.1.refs_1_ = bf16[512,1024]{1,0:T(8,128)(2,1)S(1)} custom-call(s32[2]{0:T(128)S(1)} %pad_add_fusion.refs_0_, s32[4]{0:T(128)S(1)} %copy-done.32, f32[512,1024]{1,0:T(8,128)S(1)} %get-tuple-element.49.refs_2_, bf16[8,512,160]{2,1,0:T(8,128)(2,1)S(1)} %copy-done.2, bf16[8,160,128]{2,1,0:T(8,128)(2,1)} %bitcast.3.refs_4_, f32[1,1024]{1,0:T(1,128)S(1)} %bitcast.5, ...), custom_call_target="tpu_custom_call" | custom-call | flops 167772160 | bytes 4194304 | tf_op jit(solution)/shard_map/finish/pallas_call | solution.py:487
  119.2 3.7 %out.1.refs_0_ = bf16[16,512,128]{2,1,0:T(8,128)(2,1)S(1)} custom-call(s32[2]{0:T(128)S(1)} %pad_add_fusion.refs_0_, bf16[512,1024]{1,0:T(8,128)(2,1)S(1)} %finish.1.refs_1_, bf16[512,128]{1,0:T(8,128)(2,1)S(1)} %copy-done.27, bf16[512,128]{1,0:T(8,128)(2,1)S(1)} %copy-done.29, bf16[512,128]{1,0:T(8,128)(2,1)S(1)} %copy-done.8, ...), custom_call_target="tpu_custom_call" | custom-call | flops 2147483648 | bytes 4194304 | tf_op jit(solution)/shard_map/out/pallas_call | solution.py:487
  123.0 2.6 %collective-permute-done.31.refs_1_ = bf16[8,512,128]{2,1,0:T(8,128)(2,1)S(1)} collective-permute-done((bf16[8,512,128]{2,1,0:T(8,128)(2,1)S(1)}, bf16[8,512,128]{2,1,0:T(8,128)(2,1)S(1)}, u32[]{:S(2)}, u32[]{:S(2)}) %collective-permute-start.31) | collective-permute-done | bytes 1048608 | tf_op jit(solution)/shard_map/ppermute | solution.py:588
  125.7 1.3 %add.3 = bf16[512,1024]{1,0:T(8,128)(2,1)} custom-call(bf16[16,512,128]{2,1,0:T(8,128)(2,1)S(1)} %out.1.refs_0_, bf16[8,512,128]{2,1,0:T(8,128)(2,1)S(1)} %collective-permute-done.31.refs_1_), custom_call_target="tpu_custom_call" | custom-call | bytes 4194304 | tf_op jit(solution)/shard_map/add/pallas_call | solution.py:487
  (120 shorter events, 1.4 us)
Async XLA Ops:
  0.0 30.8 %copy-start = (bf16[512,2048]{1,0:T(8,128)(2,1)S(1)}, bf16[512,2048]{1,0:T(8,128)(2,1)}, u32[]{:S(2)}) copy-start(bf16[512,2048]{1,0:T(8,128)(2,1)} %refs_3_.1) | copy-start | bytes 6291460
  2.7 7.2 %collective-permute-start.1 = (bf16[64,1280]{1,0:T(8,128)(2,1)S(1)}, bf16[64,1280]{1,0:T(8,128)(2,1)S(1)}, u32[]{:S(2)}, u32[]{:S(2)}) collective-permute-start(bf16[64,1280]{1,0:T(8,128)(2,1)S(1)} %get-tuple-element.34.refs_1_.refs_9_), channel_id=1, source_target_pairs={{0,2},{2,0},{8,10},{10,8},{16,18},{18,16},{24,26},{26,24},{28,30},... | collective-permute-start | bytes 491528 | tf_op jit(solution)/shard_map/ppermute | solution.py:200
  5.7 5.7 %collective-permute-start.2 = (bf16[64,1280]{1,0:T(8,128)(2,1)S(1)}, bf16[64,1280]{1,0:T(8,128)(2,1)S(1)}, u32[]{:S(2)}, u32[]{:S(2)}) collective-permute-start(bf16[64,1280]{1,0:T(8,128)(2,1)S(1)} %get-tuple-element.33.refs_0_.refs_8_), channel_id=1, source_target_pairs={{0,8},{2,10},{8,16},{10,18},{16,24},{18,26},{24,28},{26,30},{28,20... | collective-permute-start | bytes 491528 | tf_op jit(solution)/shard_map/ppermute | solution.py:200
  7.3 5.4 %collective-permute-start.3 = (bf16[64,1280]{1,0:T(8,128)(2,1)S(1)}, bf16[64,1280]{1,0:T(8,128)(2,1)S(1)}, u32[]{:S(2)}, u32[]{:S(2)}) collective-permute-start(bf16[64,1280]{1,0:T(8,128)(2,1)S(1)} %get-tuple-element.33.refs_0_.refs_8_), channel_id=1, source_target_pairs={{0,4},{2,6},{8,0},{10,2},{16,8},{18,10},{24,16},{26,18},{28,24},{3... | collective-permute-start | bytes 491528 | tf_op jit(solution)/shard_map/ppermute | solution.py:200
  9.9 16.7 %copy-start.20 = (bf16[64,1280]{1,0:T(8,128)(2,1)}, bf16[64,1280]{1,0:T(8,128)(2,1)S(1)}, u32[]{:S(2)}) copy-start(bf16[64,1280]{1,0:T(8,128)(2,1)S(1)} %collective-permute-done.1.refs_2_.refs_10_) | copy-start | bytes 491524
  11.4 15.7 %copy-start.22 = (bf16[64,1280]{1,0:T(8,128)(2,1)}, bf16[64,1280]{1,0:T(8,128)(2,1)S(1)}, u32[]{:S(2)}) copy-start(bf16[64,1280]{1,0:T(8,128)(2,1)S(1)} %collective-permute-done.2.refs_3_.refs_11_) | copy-start | bytes 491524
  12.7 14.4 %copy-start.24 = (bf16[64,1280]{1,0:T(8,128)(2,1)}, bf16[64,1280]{1,0:T(8,128)(2,1)S(1)}, u32[]{:S(2)}) copy-start(bf16[64,1280]{1,0:T(8,128)(2,1)S(1)} %collective-permute-done.3.refs_4_.refs_12_) | copy-start | bytes 491524
  13.6 11.5 %collective-permute-start.5 = (bf16[192,1280]{1,0:T(8,128)(2,1)S(1)}, bf16[192,1280]{1,0:T(8,128)(2,1)S(1)}, u32[]{:S(2)}, u32[]{:S(2)}) collective-permute-start(bf16[192,1280]{1,0:T(8,128)(2,1)S(1)} %get-tuple-element.36), channel_id=1, source_target_pairs={{0,8},{2,10},{8,16},{10,18},{16,24},{18,26},{24,28},{26,30},{28,20... | collective-permute-start | bytes 1474568 | tf_op jit(solution)/shard_map/ppermute | solution.py:200
  15.2 11.5 %collective-permute-start.6 = (bf16[192,1280]{1,0:T(8,128)(2,1)S(1)}, bf16[192,1280]{1,0:T(8,128)(2,1)S(1)}, u32[]{:S(2)}, u32[]{:S(2)}) collective-permute-start(bf16[192,1280]{1,0:T(8,128)(2,1)S(1)} %get-tuple-element.37), channel_id=1, source_target_pairs={{0,4},{2,6},{8,0},{10,2},{16,8},{18,10},{24,16},{26,18},{28,24},{3... | collective-permute-start | bytes 1474568 | tf_op jit(solution)/shard_map/ppermute | solution.py:200
  15.6 14.1 %collective-permute-start = (bf16[2048,128]{1,0:T(8,128)(2,1)}, bf16[2048,128]{1,0:T(8,128)(2,1)}, u32[]{:S(2)}, u32[]{:S(2)}) collective-permute-start(bf16[2048,128]{1,0:T(8,128)(2,1)} %refs_4_.2), channel_id=1, source_target_pairs={{0,1},{1,0},{2,3},{3,2},{4,5},{5,4},{6,7},{7,6},{8,9},{9,8},{10,11... | collective-permute-start | bytes 1572872 | tf_op jit(solution)/shard_map/ppermute | solution.py:522
  15.6 14.6 %collective-permute-start.4 = (bf16[192,1280]{1,0:T(8,128)(2,1)}, bf16[192,1280]{1,0:T(8,128)(2,1)}, u32[]{:S(2)}, u32[]{:S(2)}) collective-permute-start(bf16[192,1280]{1,0:T(8,128)(2,1)} %get-tuple-element.35), channel_id=1, source_target_pairs={{0,2},{2,0},{8,10},{10,8},{16,18},{18,16},{24,26},{26,24},{28,30},... | collective-permute-start | bytes 1474568 | tf_op jit(solution)/shard_map/ppermute | solution.py:200
  25.1 14.8 %collective-permute-start.8 = (bf16[192,1280]{1,0:T(8,128)(2,1)S(1)}, bf16[192,1280]{1,0:T(8,128)(2,1)}, u32[]{:S(2)}, u32[]{:S(2)}) collective-permute-start(bf16[192,1280]{1,0:T(8,128)(2,1)S(1)} %collective-permute-done.5.refs_0_.refs_1_.refs_14_), channel_id=1, source_target_pairs={{0,8},{2,10},{8,16},{10,18},{16,24},{18,26},{24,28},{26,30},{28,20... | collective-permute-start | bytes 1474568 | tf_op jit(solution)/shard_map/ppermute | solution.py:200
  26.6 13.2 %collective-permute-start.9 = (bf16[192,1280]{1,0:T(8,128)(2,1)S(1)}, bf16[192,1280]{1,0:T(8,128)(2,1)}, u32[]{:S(2)}, u32[]{:S(2)}) collective-permute-start(bf16[192,1280]{1,0:T(8,128)(2,1)S(1)} %collective-permute-done.6.refs_1_.refs_2_.refs_15_), channel_id=1, source_target_pairs={{0,4},{2,6},{8,0},{10,2},{16,8},{18,10},{24,16},{26,18},{28,24},{3... | collective-permute-start | bytes 1474568 | tf_op jit(solution)/shard_map/ppermute | solution.py:200
  28.1 28.7 %copy-start.26 = (bf16[512,128]{1,0:T(8,128)(2,1)}, bf16[512,128]{1,0:T(8,128)(2,1)S(1)}, u32[]{:S(2)}) copy-start(bf16[512,128]{1,0:T(8,128)(2,1)S(1)} %get-tuple-element.38.refs_0_.refs_2_) | copy-start | bytes 393220
  28.1 28.7 %copy-start.28 = (bf16[512,128]{1,0:T(8,128)(2,1)}, bf16[512,128]{1,0:T(8,128)(2,1)S(1)}, u32[]{:S(2)}) copy-start(bf16[512,128]{1,0:T(8,128)(2,1)S(1)} %get-tuple-element.39.refs_1_.refs_3_) | copy-start | bytes 393220
  28.1 10.4 %collective-permute-start.10 = (bf16[512,128]{1,0:T(8,128)(2,1)S(1)}, bf16[512,128]{1,0:T(8,128)(2,1)S(1)}, u32[]{:S(2)}, u32[]{:S(2)}) collective-permute-start(bf16[512,128]{1,0:T(8,128)(2,1)S(1)} %get-tuple-element.38.refs_0_.refs_2_), channel_id=1, source_target_pairs={{0,8},{2,10},{8,16},{10,18},{16,24},{18,26},{24,28},{26,30},{28,20... | collective-permute-start | bytes 393224 | tf_op jit(solution)/shard_map/ppermute | solution.py:200
  29.7 10.1 %collective-permute-start.11 = (bf16[512,128]{1,0:T(8,128)(2,1)S(1)}, bf16[512,128]{1,0:T(8,128)(2,1)S(1)}, u32[]{:S(2)}, u32[]{:S(2)}) collective-permute-start(bf16[512,128]{1,0:T(8,128)(2,1)S(1)} %get-tuple-element.38.refs_0_.refs_2_), channel_id=1, source_target_pairs={{0,4},{2,6},{8,0},{10,2},{16,8},{18,10},{24,16},{26,18},{28,24},{3... | collective-permute-start | bytes 393224 | tf_op jit(solution)/shard_map/ppermute | solution.py:200
  30.2 9.7 %collective-permute-start.12 = (bf16[512,128]{1,0:T(8,128)(2,1)S(1)}, bf16[512,128]{1,0:T(8,128)(2,1)S(1)}, u32[]{:S(2)}, u32[]{:S(2)}) collective-permute-start(bf16[512,128]{1,0:T(8,128)(2,1)S(1)} %get-tuple-element.39.refs_1_.refs_3_), channel_id=1, source_target_pairs={{0,2},{2,0},{8,10},{10,8},{16,18},{18,16},{24,26},{26,24},{28,30},... | collective-permute-start | bytes 393224 | tf_op jit(solution)/shard_map/ppermute | solution.py:200
  38.5 18.3 %copy-start.3 = (bf16[512,128]{1,0:T(8,128)(2,1)}, bf16[512,128]{1,0:T(8,128)(2,1)S(1)}, u32[]{:S(2)}) copy-start(bf16[512,128]{1,0:T(8,128)(2,1)S(1)} %collective-permute-done.10.refs_5_.refs_3_) | copy-start | bytes 393220
  39.8 16.9 %copy-start.5 = (bf16[512,128]{1,0:T(8,128)(2,1)}, bf16[512,128]{1,0:T(8,128)(2,1)S(1)}, u32[]{:S(2)}) copy-start(bf16[512,128]{1,0:T(8,128)(2,1)S(1)} %collective-permute-done.11.refs_6_.refs_4_) | copy-start | bytes 393220
  39.9 16.9 %copy-start.7 = (bf16[512,128]{1,0:T(8,128)(2,1)}, bf16[512,128]{1,0:T(8,128)(2,1)S(1)}, u32[]{:S(2)}) copy-start(bf16[512,128]{1,0:T(8,128)(2,1)S(1)} %collective-permute-done.12.refs_7_.refs_2_.refs_4_) | copy-start | bytes 393220
  41.2 20.4 %copy-start.21 = (bf16[64,1280]{1,0:T(8,128)(2,1)S(1)}, bf16[64,1280]{1,0:T(8,128)(2,1)}, u32[]{:S(2)}) copy-start(bf16[64,1280]{1,0:T(8,128)(2,1)} %copy-done.20) | copy-start | bytes 491524
  41.2 20.4 %copy-start.23 = (bf16[64,1280]{1,0:T(8,128)(2,1)S(1)}, bf16[64,1280]{1,0:T(8,128)(2,1)}, u32[]{:S(2)}) copy-start(bf16[64,1280]{1,0:T(8,128)(2,1)} %copy-done.22) | copy-start | bytes 491524
  41.2 20.4 %copy-start.25 = (bf16[64,1280]{1,0:T(8,128)(2,1)S(1)}, bf16[64,1280]{1,0:T(8,128)(2,1)}, u32[]{:S(2)}) copy-start(bf16[64,1280]{1,0:T(8,128)(2,1)} %copy-done.24) | copy-start | bytes 491524
  41.2 20.4 %copy-start.35 = (bf16[256,1024]{1,0:T(8,128)(2,1)S(1)}, bf16[256,1024]{1,0:T(8,128)(2,1)}, u32[]{:S(2)}) copy-start(bf16[256,1024]{1,0:T(8,128)(2,1)} %refs_4_.3) | copy-start | bytes 1572868
  41.3 20.4 %copy-start.36 = (f32[160,128]{1,0:T(8,128)S(1)}, f32[160,128]{1,0:T(8,128)}, u32[]{:S(2)}) copy-start(f32[160,128]{1,0:T(8,128)} %constant.14.clone.refs_5_) | copy-start | bytes 245764
  41.3 20.4 %copy-start.38 = (f32[160,128]{1,0:T(8,128)S(1)}, f32[160,128]{1,0:T(8,128)}, u32[]{:S(2)}) copy-start(f32[160,128]{1,0:T(8,128)} %constant.15.clone.refs_6_) | copy-start | bytes 245764
  41.3 20.4 %copy-start.40 = (f32[160,8]{1,0:T(8,128)S(1)}, f32[160,8]{1,0:T(8,128)}, u32[]{:S(2)}) copy-start(f32[160,8]{1,0:T(8,128)} %constant.17.refs_7_) | copy-start | bytes 15364
  41.3 12.8 %collective-permute-start.14 = (bf16[160,1280]{1,0:T(8,128)(2,1)S(1)}, bf16[160,1280]{1,0:T(8,128)(2,1)S(1)}, u32[]{:S(2)}, u32[]{:S(2)}) collective-permute-start(bf16[160,1280]{1,0:T(8,128)(2,1)S(1)} %get-tuple-element.41), channel_id=1, source_target_pairs={{0,8},{2,10},{8,16},{10,18},{16,24},{18,26},{24,28},{26,30},{28,20... | collective-permute-start | bytes 1228808 | tf_op jit(solution)/shard_map/ppermute | solution.py:200
  42.9 11.2 %collective-permute-start.15 = (bf16[160,1280]{1,0:T(8,128)(2,1)S(1)}, bf16[160,1280]{1,0:T(8,128)(2,1)S(1)}, u32[]{:S(2)}, u32[]{:S(2)}) collective-permute-start(bf16[160,1280]{1,0:T(8,128)(2,1)S(1)} %get-tuple-element.42), channel_id=1, source_target_pairs={{0,4},{2,6},{8,0},{10,2},{16,8},{18,10},{24,16},{26,18},{28,24},{3... | collective-permute-start | bytes 1228808 | tf_op jit(solution)/shard_map/ppermute | solution.py:200
  43.4 10.7 %collective-permute-start.7 = (bf16[128,1280]{1,0:T(8,128)(2,1)S(1)}, bf16[128,1280]{1,0:T(8,128)(2,1)S(1)}, u32[]{:S(2)}, u32[]{:S(2)}) collective-permute-start(bf16[128,1280]{1,0:T(8,128)(2,1)S(1)} %pack.10), channel_id=1, source_target_pairs={{0,2},{2,0},{8,10},{10,8},{16,18},{18,16},{24,26},{26,24},{28,30},... | collective-permute-start | bytes 983048 | tf_op jit(solution)/shard_map/ppermute | solution.py:200
  44.0 15.4 %collective-permute-start.13 = (bf16[128,1280]{1,0:T(8,128)(2,1)S(1)}, bf16[128,1280]{1,0:T(8,128)(2,1)S(1)}, u32[]{:S(2)}, u32[]{:S(2)}) collective-permute-start(bf16[128,1280]{1,0:T(8,128)(2,1)S(1)} %get-tuple-element.40), channel_id=1, source_target_pairs={{0,2},{2,0},{8,10},{10,8},{16,18},{18,16},{24,26},{26,24},{28,30},... | collective-permute-start | bytes 983048 | tf_op jit(solution)/shard_map/ppermute | solution.py:200
  54.2 5.7 %collective-permute-start.16 = (bf16[64,1280]{1,0:T(8,128)(2,1)S(1)}, bf16[64,1280]{1,0:T(8,128)(2,1)S(1)}, u32[]{:S(2)}, u32[]{:S(2)}) collective-permute-start(bf16[64,1280]{1,0:T(8,128)(2,1)S(1)} %get-tuple-element.43), channel_id=1, source_target_pairs={{0,2},{2,0},{8,10},{10,8},{16,18},{18,16},{24,26},{26,24},{28,30},... | collective-permute-start | bytes 491528 | tf_op jit(solution)/shard_map/ppermute | solution.py:200
  54.8 5.3 %collective-permute-start.17 = (bf16[64,1280]{1,0:T(8,128)(2,1)S(1)}, bf16[64,1280]{1,0:T(8,128)(2,1)S(1)}, u32[]{:S(2)}, u32[]{:S(2)}) collective-permute-start(bf16[64,1280]{1,0:T(8,128)(2,1)S(1)} %get-tuple-element.44), channel_id=1, source_target_pairs={{0,8},{2,10},{8,16},{10,18},{16,24},{18,26},{24,28},{26,30},{28,20... | collective-permute-start | bytes 491528 | tf_op jit(solution)/shard_map/ppermute | solution.py:200
  56.3 5.3 %collective-permute-start.18 = (bf16[64,1280]{1,0:T(8,128)(2,1)S(1)}, bf16[64,1280]{1,0:T(8,128)(2,1)S(1)}, u32[]{:S(2)}, u32[]{:S(2)}) collective-permute-start(bf16[64,1280]{1,0:T(8,128)(2,1)S(1)} %get-tuple-element.45), channel_id=1, source_target_pairs={{0,4},{2,6},{8,0},{10,2},{16,8},{18,10},{24,16},{26,18},{28,24},{3... | collective-permute-start | bytes 491528 | tf_op jit(solution)/shard_map/ppermute | solution.py:200
  57.8 17.7 %collective-permute-start.19 = (bf16[1536,128]{1,0:T(8,128)(2,1)}, bf16[1536,128]{1,0:T(8,128)(2,1)S(1)}, u32[]{:S(2)}, u32[]{:S(2)}) collective-permute-start(bf16[1536,128]{1,0:T(8,128)(2,1)} %get-tuple-element.52), channel_id=1, source_target_pairs={{0,8},{2,10},{8,16},{10,18},{16,24},{18,26},{24,28},{26,30},{28,20... | collective-permute-start | bytes 1179656 | tf_op jit(solution)/shard_map/ppermute | solution.py:200
  59.4 18.2 %collective-permute-start.21 = (bf16[1536,128]{1,0:T(8,128)(2,1)}, bf16[1536,128]{1,0:T(8,128)(2,1)S(1)}, u32[]{:S(2)}, u32[]{:S(2)}) collective-permute-start(bf16[1536,128]{1,0:T(8,128)(2,1)} %get-tuple-element.53), channel_id=1, source_target_pairs={{0,4},{2,6},{8,0},{10,2},{16,8},{18,10},{24,16},{26,18},{28,24},{3... | collective-permute-start | bytes 1179656 | tf_op jit(solution)/shard_map/ppermute | solution.py:200
  71.6 15.1 %all-to-all-start = ((bf16[16,80,128]{2,1,0:T(8,128)(2,1)}), bf16[16,80,128]{2,1,0:T(8,128)(2,1)S(1)}, u32[]{:S(2)}, u32[]{:S(2)}) async-start(bf16[16,80,128]{2,1,0:T(8,128)(2,1)} %bitcast.2), calls=%async_computation | async-start | bytes 655360 | tf_op jit(solution)/shard_map/all_to_all | solution.py:561
  75.6 20.9 %copy-start.10 = (bf16[1536,128]{1,0:T(8,128)(2,1)}, bf16[1536,128]{1,0:T(8,128)(2,1)S(1)}, u32[]{:S(2)}) copy-start(bf16[1536,128]{1,0:T(8,128)(2,1)S(1)} %collective-permute-done.19.refs_0_.refs_8_) | copy-start | bytes 1179652
  75.6 9.6 %collective-permute-start.20 = (bf16[1536,128]{1,0:T(8,128)(2,1)S(1)}, bf16[1536,128]{1,0:T(8,128)(2,1)S(1)}, u32[]{:S(2)}, u32[]{:S(2)}) collective-permute-start(bf16[1536,128]{1,0:T(8,128)(2,1)S(1)} %collective-permute-done.19.refs_0_.refs_8_), channel_id=1, source_target_pairs={{0,8},{2,10},{8,16},{10,18},{16,24},{18,26},{24,28},{26,30},{28,20... | collective-permute-start | bytes 1179656 | tf_op jit(solution)/shard_map/ppermute | solution.py:200
  77.6 18.9 %copy-start.12 = (bf16[1536,128]{1,0:T(8,128)(2,1)}, bf16[1536,128]{1,0:T(8,128)(2,1)S(1)}, u32[]{:S(2)}) copy-start(bf16[1536,128]{1,0:T(8,128)(2,1)S(1)} %collective-permute-done.21.refs_1_.refs_9_) | copy-start | bytes 1179652
  77.6 9.1 %collective-permute-start.22 = (bf16[1536,128]{1,0:T(8,128)(2,1)S(1)}, bf16[1536,128]{1,0:T(8,128)(2,1)S(1)}, u32[]{:S(2)}, u32[]{:S(2)}) collective-permute-start(bf16[1536,128]{1,0:T(8,128)(2,1)S(1)} %collective-permute-done.21.refs_1_.refs_9_), channel_id=1, source_target_pairs={{0,4},{2,6},{8,0},{10,2},{16,8},{18,10},{24,16},{26,18},{28,24},{3... | collective-permute-start | bytes 1179656 | tf_op jit(solution)/shard_map/ppermute | solution.py:200
  77.7 15.9 %collective-permute-start.23 = (bf16[1536,128]{1,0:T(8,128)(2,1)S(1)}, bf16[1536,128]{1,0:T(8,128)(2,1)S(1)}, u32[]{:S(2)}, u32[]{:S(2)}) collective-permute-start(bf16[1536,128]{1,0:T(8,128)(2,1)S(1)} %get-tuple-element.54), channel_id=1, source_target_pairs={{0,2},{2,0},{8,10},{10,8},{16,18},{18,16},{24,26},{26,24},{28,30},... | collective-permute-start | bytes 1179656 | tf_op jit(solution)/shard_map/ppermute | solution.py:200
  88.1 27.2 %all-to-all-start.1 = ((bf16[16,80,128]{2,1,0:T(8,128)(2,1)}), bf16[16,80,128]{2,1,0:T(8,128)(2,1)}, u32[]{:S(2)}, u32[]{:S(2)}) async-start(bf16[16,80,128]{2,1,0:T(8,128)(2,1)} %mix.1), calls=%async_computation.1 | async-start | bytes 655360 | tf_op jit(solution)/shard_map/all_to_all | solution.py:569
  93.5 16.3 %copy-start.37 = (f32[160,128]{1,0:T(8,128)S(1)}, f32[160,128]{1,0:T(8,128)}, u32[]{:S(2)}) copy-start(f32[160,128]{1,0:T(8,128)} %constant.14.clone.refs_5_) | copy-start | bytes 245764
  93.5 16.3 %copy-start.39 = (f32[160,128]{1,0:T(8,128)S(1)}, f32[160,128]{1,0:T(8,128)}, u32[]{:S(2)}) copy-start(f32[160,128]{1,0:T(8,128)} %constant.15.clone.refs_6_) | copy-start | bytes 245764
  93.5 16.3 %copy-start.41 = (f32[8,160]{1,0:T(8,128)S(1)}, f32[8,160]{1,0:T(8,128)}, u32[]{:S(2)}) copy-start(f32[8,160]{1,0:T(8,128)} %constant.16.clone.refs_7_) | copy-start | bytes 15364
  93.5 16.3 %copy-start.43 = (bf16[512,1024]{1,0:T(8,128)(2,1)S(1)}, bf16[512,1024]{1,0:T(8,128)(2,1)}, u32[]{:S(2)}) copy-start(bf16[512,1024]{1,0:T(8,128)(2,1)} %copy-done.42) | copy-start | bytes 3145732
  93.6 16.3 %copy-start.45 = (bf16[512,128]{1,0:T(8,128)(2,1)S(1)}, bf16[512,128]{1,0:T(8,128)(2,1)}, u32[]{:S(2)}) copy-start(bf16[512,128]{1,0:T(8,128)(2,1)} %copy-done.44) | copy-start | bytes 393220
  93.6 16.3 %copy-start.47 = (bf16[512,128]{1,0:T(8,128)(2,1)S(1)}, bf16[512,128]{1,0:T(8,128)(2,1)}, u32[]{:S(2)}) copy-start(bf16[512,128]{1,0:T(8,128)(2,1)} %copy-done.46) | copy-start | bytes 393220
  93.6 16.2 %copy-start.14 = (bf16[1536,128]{1,0:T(8,128)(2,1)}, bf16[1536,128]{1,0:T(8,128)(2,1)S(1)}, u32[]{:S(2)}) copy-start(bf16[1536,128]{1,0:T(8,128)(2,1)S(1)} %collective-permute-done.23.refs_2_.refs_7_) | copy-start | bytes 1179652
  94.4 10.0 %collective-permute-start.24 = (bf16[1280,128]{1,0:T(8,128)(2,1)S(1)}, bf16[1280,128]{1,0:T(8,128)(2,1)S(1)}, u32[]{:S(2)}, u32[]{:S(2)}) collective-permute-start(bf16[1280,128]{1,0:T(8,128)(2,1)S(1)} %get-tuple-element.55), channel_id=1, source_target_pairs={{0,8},{2,10},{8,16},{10,18},{16,24},{18,26},{24,28},{26,30},{28,20... | collective-permute-start | bytes 983048 | tf_op jit(solution)/shard_map/ppermute | solution.py:200
  96.3 9.2 %collective-permute-start.25 = (bf16[1280,128]{1,0:T(8,128)(2,1)S(1)}, bf16[1280,128]{1,0:T(8,128)(2,1)S(1)}, u32[]{:S(2)}, u32[]{:S(2)}) collective-permute-start(bf16[1280,128]{1,0:T(8,128)(2,1)S(1)} %get-tuple-element.56), channel_id=1, source_target_pairs={{0,4},{2,6},{8,0},{10,2},{16,8},{18,10},{24,16},{26,18},{28,24},{3... | collective-permute-start | bytes 983048 | tf_op jit(solution)/shard_map/ppermute | solution.py:200
  96.4 7.8 %collective-permute-start.26 = (bf16[1024,128]{1,0:T(8,128)(2,1)S(1)}, bf16[1024,128]{1,0:T(8,128)(2,1)S(1)}, u32[]{:S(2)}, u32[]{:S(2)}) collective-permute-start(bf16[1024,128]{1,0:T(8,128)(2,1)S(1)} %pack.16), channel_id=1, source_target_pairs={{0,2},{2,0},{8,10},{10,8},{16,18},{18,16},{24,26},{26,24},{28,30},... | collective-permute-start | bytes 786440 | tf_op jit(solution)/shard_map/ppermute | solution.py:200
  98.4 20.6 %collective-permute-start.27 = (bf16[1024,128]{1,0:T(8,128)(2,1)}, bf16[1024,128]{1,0:T(8,128)(2,1)}, u32[]{:S(2)}, u32[]{:S(2)}) collective-permute-start(bf16[1024,128]{1,0:T(8,128)(2,1)} %get-tuple-element.57), channel_id=1, source_target_pairs={{0,2},{2,0},{8,10},{10,8},{16,18},{18,16},{24,26},{26,24},{28,30},... | collective-permute-start | bytes 786440 | tf_op jit(solution)/shard_map/ppermute | solution.py:200
  104.3 5.5 %copy-start.17 = (bf16[1024,128]{1,0:T(8,128)(2,1)}, bf16[1024,128]{1,0:T(8,128)(2,1)S(1)}, u32[]{:S(2)}) copy-start(bf16[1024,128]{1,0:T(8,128)(2,1)S(1)} %collective-permute-done.26.refs_2_.refs_10_) | copy-start | bytes 786436
  106.3 9.0 %copy-start.33 = (f32[1024]{0:T(1024)S(1)}, f32[1024]{0:T(1024)}, u32[]{:S(2)}) copy-start(f32[1024]{0:T(1024)} %param.21) | copy-start | bytes 12292
  106.3 12.8 %collective-permute-start.28 = (bf16[512,128]{1,0:T(8,128)(2,1)}, bf16[512,128]{1,0:T(8,128)(2,1)}, u32[]{:S(2)}, u32[]{:S(2)}) collective-permute-start(bf16[512,128]{1,0:T(8,128)(2,1)} %get-tuple-element.58), channel_id=1, source_target_pairs={{0,2},{2,0},{8,10},{10,8},{16,18},{18,16},{24,26},{26,24},{28,30},... | collective-permute-start | bytes 393224 | tf_op jit(solution)/shard_map/ppermute | solution.py:200
  107.8 11.3 %collective-permute-start.29 = (bf16[512,128]{1,0:T(8,128)(2,1)}, bf16[512,128]{1,0:T(8,128)(2,1)}, u32[]{:S(2)}, u32[]{:S(2)}) collective-permute-start(bf16[512,128]{1,0:T(8,128)(2,1)} %get-tuple-element.59), channel_id=1, source_target_pairs={{0,8},{2,10},{8,16},{10,18},{16,24},{18,26},{24,28},{26,30},{28,20... | collective-permute-start | bytes 393224 | tf_op jit(solution)/shard_map/ppermute | solution.py:200
  109.3 9.8 %collective-permute-start.30 = (bf16[512,128]{1,0:T(8,128)(2,1)}, bf16[512,128]{1,0:T(8,128)(2,1)}, u32[]{:S(2)}, u32[]{:S(2)}) collective-permute-start(bf16[512,128]{1,0:T(8,128)(2,1)} %get-tuple-element.60), channel_id=1, source_target_pairs={{0,4},{2,6},{8,0},{10,2},{16,8},{18,10},{24,16},{26,18},{28,24},{3... | collective-permute-start | bytes 393224 | tf_op jit(solution)/shard_map/ppermute | solution.py:200
  116.9 2.2 %copy-start.13 = (bf16[1536,128]{1,0:T(8,128)(2,1)S(1)}, bf16[1536,128]{1,0:T(8,128)(2,1)}, u32[]{:S(2)}) copy-start(bf16[1536,128]{1,0:T(8,128)(2,1)} %copy-done.12) | copy-start | bytes 1179652
  116.9 2.2 %copy-start.15 = (bf16[1536,128]{1,0:T(8,128)(2,1)S(1)}, bf16[1536,128]{1,0:T(8,128)(2,1)}, u32[]{:S(2)}) copy-start(bf16[1536,128]{1,0:T(8,128)(2,1)} %copy-done.14) | copy-start | bytes 1179652
  116.9 2.2 %copy-start.18 = (bf16[1024,128]{1,0:T(8,128)(2,1)S(1)}, bf16[1024,128]{1,0:T(8,128)(2,1)}, u32[]{:S(2)}) copy-start(bf16[1024,128]{1,0:T(8,128)(2,1)} %copy-done.17) | copy-start | bytes 786436
  122.9 2.7 %collective-permute-start.31 = (bf16[8,512,128]{2,1,0:T(8,128)(2,1)S(1)}, bf16[8,512,128]{2,1,0:T(8,128)(2,1)S(1)}, u32[]{:S(2)}, u32[]{:S(2)}) collective-permute-start(bf16[8,512,128]{2,1,0:T(8,128)(2,1)S(1)} %slice.4), channel_id=1, source_target_pairs={{0,1},{1,0},{2,3},{3,2},{4,5},{5,4},{6,7},{7,6},{8,9},{9,8},{10,11... | collective-permute-start | bytes 3145736 | tf_op jit(solution)/shard_map/ppermute | solution.py:588
  (18 other events, 25.5 us)

commit v4 on v3

--- a/solution.py
+++ b/solution.py
@@ -17,6 +17,7 @@
 VMEM = pl.BlockSpec(memory_space=pltpu.VMEM)
 SMEM = pl.BlockSpec(memory_space=pltpu.SMEM)
 ANY = pl.BlockSpec(memory_space=pl.ANY)
+HBM = pl.BlockSpec(memory_space=pltpu.HBM)
 
 
 def carried_in(value, axis, combine, identity):
@@ -316,12 +317,12 @@
     return pl.pallas_call(
         join_kernel,
         out_shape=[jax.ShapeDtypeStruct((rows // 2, wide), values.dtype)] * 2,
-        in_specs=[ANY] * 3,
+        in_specs=[HBM] * 3,
         out_specs=[VMEM] * 2,
         scratch_shapes=[pltpu.SemaphoreType.DMA((6,))],
         compiler_params=params(4),
         name="join",
-    )(values, query, keys)
+    )(stay(values), stay(query), stay(keys))
 
 
 def turn_kernel(rows, info, tokens, turned):
@@ -389,8 +390,7 @@
         ).astype(jnp.bfloat16)
 
 
-def within_kernel(heads, width, info, lengths, query, keys, values, first, second, scale, within,
-                  maps):
+def within_kernel(heads, width, info, lengths, query, keys, values, within):
     count = query.shape[0]
     cut = count // 2
     lanes = lax.broadcasted_iota(jnp.int32, (1, heads * F), 1)
@@ -411,12 +411,7 @@
             cols = slice(h * width, (h + 1) * width)
             within[low:high, cols] = jnp.dot(
                 weights, values[:high, cols], preferred_element_type=jnp.float32
-            )
-    for h in range(heads):
-        a = lax.dot_general(query[...], table_of(first, h), NT, preferred_element_type=jnp.float32)
-        b = lax.dot_general(query[...], table_of(second, h), NT, preferred_element_type=jnp.float32)
-        mapped = ((a + scale[0:1, :]) * (b + scale[1:2, :])) * scale[3:4, :]
-        maps[h] = mapped.astype(jnp.bfloat16)
+            ).astype(within.dtype)
 
 
 def mix_kernel(blocks, count, lengths, states, mixed):
@@ -438,15 +433,23 @@
         mixed[b] = total.astype(jnp.bfloat16)
 
 
-def finish_kernel(heads, width, info, lengths, within, maps, carried, gains, normed):
+def finish_kernel(heads, width, info, lengths, within, query, carried, gains, first, second, scale,
+                  normed):
     count = within.shape[0]
+    rows = query[...]
+    maps = []
+    for h in range(heads):
+        a = lax.dot_general(rows, table_of(first, h), NT, preferred_element_type=jnp.float32)
+        b = lax.dot_general(rows, table_of(second, h), NT, preferred_element_type=jnp.float32)
+        mapped = ((a + scale[0:1, :]) * (b + scale[1:2, :])) * scale[3:4, :]
+        maps.append(mapped.astype(jnp.bfloat16))
     positions = lax.broadcasted_iota(jnp.int32, (count, 1), 0) + info[0] * count
     begin = request_of(jnp.zeros((1, 1), jnp.int32) + info[0] * count, lengths)
     follows = jnp.where(request_of(positions, lengths) == begin, 1.0, 0.0)
     for h in range(heads):
         cross = jnp.dot(maps[h], carried[h], preferred_element_type=jnp.float32)
         cols = slice(h * width, (h + 1) * width)
-        combined = within[:, cols] + follows * cross
+        combined = within[:, cols].astype(jnp.float32) + follows * cross
         factor = lax.rsqrt(jnp.mean(combined * combined, axis=-1, keepdims=True) + EPSILON)
         normed[:, cols] = (combined * factor * gains[:, cols]).astype(jnp.bfloat16)
 
@@ -477,18 +480,52 @@
         out[:, k * tile : (k + 1) * tile] = total.astype(jnp.bfloat16)
 
 
-def call(kernel, name, mebibytes, cost, shapes, scalars, arrays, late=()):
+def stay(array):
+    return pltpu.with_memory_space_constraint(array, pltpu.HBM)
+
+
+def call(kernel, name, mebibytes, cost, shapes, scalars, arrays, late=(), far=(), out_far=()):
     shapes = [jax.ShapeDtypeStruct(shape, kind) for shape, kind in shapes]
-    given = len(scalars) + len(arrays)
+    n, m, k = len(scalars), len(arrays), len(shapes)
+    held = [arrays[i] for i in far] + [shapes[i] for i in out_far]
+    arrays = [stay(array) if i in far else array for i, array in enumerate(arrays)]
+    shapes = [
+        pltpu.HBM(shape.shape, shape.dtype) if i in out_far else shape
+        for i, shape in enumerate(shapes)
+    ]
+    scratch = [pltpu.VMEM(array.shape, array.dtype) for array in held]
+    if held:
+        scratch.append(pltpu.SemaphoreType.DMA((len(held),)))
 
     def body(*refs):
-        kernel(*refs[:given], *refs[given + len(late) :])
+        given, made = list(refs[: n + m]), list(refs[n + m + len(late) :])
+        outs, buffers = made[:k], made[k:]
+        copies = []
+        for at, i in enumerate(far):
+            copies.append(pltpu.make_async_copy(given[n + i], buffers[at], buffers[-1].at[at]))
+            given[n + i] = buffers[at]
+        for copy in copies:
+            copy.start()
+        for copy in copies:
+            copy.wait()
+        copies = []
+        for at, i in enumerate(out_far, len(far)):
+            copies.append(pltpu.make_async_copy(buffers[at], outs[i], buffers[-1].at[at]))
+            outs[i] = buffers[at]
+        kernel(*given, *outs)
+        for copy in copies:
+            copy.start()
+        for copy in copies:
+            copy.wait()
 
     return pl.pallas_call(
         body,
         out_shape=shapes,
-        in_specs=[SMEM] * len(scalars) + [VMEM] * len(arrays) + [ANY] * len(late),
-        out_specs=[VMEM] * len(shapes),
+        in_specs=[SMEM] * n
+        + [HBM if i in far else VMEM for i in range(m)]
+        + [ANY] * len(late),
+        out_specs=[HBM if i in out_far else VMEM for i in range(k)],
+        scratch_shapes=scratch,
         compiler_params=params(mebibytes),
         cost_estimate=pl.CostEstimate(flops=cost[0], bytes_accessed=cost[1], transcendentals=0),
         name=name,
@@ -555,29 +592,28 @@
             ((count, wide), half),
             ((heads, FEATS, width), half),
         ],
-        [info, lengths], [turned, low, adapter_up, first, second, scale.T, *pieces],
+        [info, lengths], [turned, low, adapter_up, first, second, scale.T, *pieces], out_far=(0, 1, 2),
     )
     parts = state.reshape(blocks, heads * FEATS // blocks, width)
     parts = lax.all_to_all(parts, "dp", 0, 0, tiled=True)
+    (within,) = call(
+        functools.partial(within_kernel, heads, width), "within", 12,
+        (4 * count * count * wide, 8 * count * wide), [((count, wide), half)],
+        [info, lengths], [query, keys, values], far=(0, 1, 2),
+    )
     out_fourth = out_chain.send(())
     out_chain.send(())
     out_gathered = next(out_chain)
     (mixed,) = call(
         functools.partial(mix_kernel, blocks, count), "mix", 4, (0, 4 * parts.size),
-        [(parts.shape, half)], [lengths], [parts], out_third[:2],
+        [(parts.shape, half)], [lengths], [parts], (within,),
     )
     carried = lax.all_to_all(mixed, "dp", 0, 0, tiled=True).reshape(heads, FEATS, width)
-    within, maps = call(
-        functools.partial(within_kernel, heads, width), "within", 12,
-        (4 * count * count * wide, 8 * count * wide),
-        [((count, wide), jnp.float32), ((heads, count, FEATS), half)],
-        [info, lengths], [query, keys, values, first, second, scale],
-    )
     (normed,) = call(
         functools.partial(finish_kernel, heads, width), "finish", 10,
         (2 * count * FEATS * wide, 8 * count * wide), [((count, wide), half)],
         [info, lengths],
-        [within, maps, carried, head_gain.reshape(1, -1)], out_fourth[:2],
+        [within, query, carried, head_gain.reshape(1, -1), first, second, scale], far=(1, 4, 5, 6),
     )
     pieces, layout = [piece for piece, _ in out_gathered], [places for _, places in out_gathered]
     (partial,) = call(

time: 128 us -> 119 us (0.930)
  waiting for transfers between devices: 46.5 us -> 39.6 us
  local copies, waits for them, and re-layouts: 8.96 us -> 2.46 us
  Pallas kernels: 28.8 us -> 33.5 us
    ppermute x30, waiting for transfers between devices: 43.8 us -> 36.9 us  [send(): return lax.ppermute(value, 'dp', pairs)]
    unnamed x96 -> x70, local copies, waits for them, and re-layouts: 8.89 us -> 2.39 us
    pallas_call x8, Pallas kernels: 23.8 us -> 26.6 us  [call(): pl.pallas_call(body, out_shape=shapes, in_specs=[SMEM] * n + [HBM if i in...]
  transfers between devices with their start and end apart: 34 -> 34, of which waited for: 15 -> 13; matrix products, arithmetic and copies ran while one was open for 0% -> 0% of each run, Pallas kernels for 17% -> 21%
where the time goes in v4:
time: 119 us; the launch traced here: 118 us
  starting transfers between devices  42.4 us (36%)
  waiting for transfers between devices  39.6 us (33%)
  Pallas kernels  33.5 us (28%)
  local copies, waits for them, and re-layouts  2.46 us (2%)
    ppermute x30, waiting for transfers between devices, send(): return lax.ppermute(value, 'dp', pairs)  36.9 us
    ppermute x30, starting transfers between devices, send(): return lax.ppermute(value, 'dp', pairs)  32.7 us
    pallas_call x8, Pallas kernels, call(): pl.pallas_call(body, out_shape=shapes, in_specs=[SMEM] * n + [HBM if i in...  26.6 us
    pallas_call x9, Pallas kernels, pack(): pl.pallas_call(functools.partial(pack_kernel, recipes, len(sources)), out...  5.69 us
    all_to_all x1, starting transfers between devices, per_device_fast(): lax.all_to_all(mixed, 'dp', 0, 0, tiled=True).reshape(heads, FEATS, width)  5.68 us
    all_to_all x1, starting transfers between devices, per_device_fast(): parts = lax.all_to_all(parts, 'dp', 0, 0, tiled=True)  3.97 us
    ppermute x1, waiting for transfers between devices, per_device_fast(): received = lax.ppermute(partial[blocks // 2:], 'mp', [(0, 1), (1, 0)])  2.65 us
    unnamed x70, local copies, waits for them, and re-layouts  2.39 us
  transfers between devices with their start and end apart: 34, of which 13 were waited for; matrix products, arithmetic and copies ran while one was open for 0% of the time, Pallas kernels for 21%

profile of v4, /device:TPU:0, one launch (start us, length us, event | category | flops | bytes accessed | tf_op | source)
XLA Modules:
  0.0 118.4 jit_solution(12267727210913309958)
XLA Ops:
  0.0 1.2 %join.1 = (bf16[64,1280]{1,0:T(8,128)(2,1)S(1)}, bf16[64,1280]{1,0:T(8,128)(2,1)S(1)}) custom-call(bf16[128,1024]{1,0:T(8,128)(2,1)} %values.1, bf16[128,128]{1,0:T(8,128)(2,1)} %query.1, bf16[128,128]{1,0:T(8,128)(2,1)} %keys.1), custom_call_target="tpu_custom_call" | custom-call | tf_op jit(solution)/shard_map/join/pallas_call | solution.py:317
  1.2 3.0 %collective-permute-start.1 = (bf16[64,1280]{1,0:T(8,128)(2,1)S(1)}, bf16[64,1280]{1,0:T(8,128)(2,1)S(1)}, u32[]{:S(2)}, u32[]{:S(2)}) collective-permute-start(bf16[64,1280]{1,0:T(8,128)(2,1)S(1)} %get-tuple-element.32.refs_1_.refs_9_), channel_id=1, source_target_pairs={{0,2},{2,0},{8,10},{10,8},{16,18},{18,16},{24,26},{26,24},{28,30},... | collective-permute-start | bytes 491528 | tf_op jit(solution)/shard_map/ppermute | solution.py:201
  4.2 1.6 %collective-permute-start.2 = (bf16[64,1280]{1,0:T(8,128)(2,1)S(1)}, bf16[64,1280]{1,0:T(8,128)(2,1)S(1)}, u32[]{:S(2)}, u32[]{:S(2)}) collective-permute-start(bf16[64,1280]{1,0:T(8,128)(2,1)S(1)} %get-tuple-element.31.refs_0_.refs_8_), channel_id=1, source_target_pairs={{0,8},{2,10},{8,16},{10,18},{16,24},{18,26},{24,28},{26,30},{28,20... | collective-permute-start | bytes 491528 | tf_op jit(solution)/shard_map/ppermute | solution.py:201
  5.8 0.4 collective-permute-start.3
  6.3 2.2 %collective-permute-done.1.refs_2_.refs_10_ = bf16[64,1280]{1,0:T(8,128)(2,1)S(1)} collective-permute-done((bf16[64,1280]{1,0:T(8,128)(2,1)S(1)}, bf16[64,1280]{1,0:T(8,128)(2,1)S(1)}, u32[]{:S(2)}, u32[]{:S(2)}) %collective-permute-start.1) | collective-permute-done | bytes 163872 | tf_op jit(solution)/shard_map/ppermute | solution.py:201
  8.4 1.5 %collective-permute-done.2.refs_3_.refs_11_ = bf16[64,1280]{1,0:T(8,128)(2,1)S(1)} collective-permute-done((bf16[64,1280]{1,0:T(8,128)(2,1)S(1)}, bf16[64,1280]{1,0:T(8,128)(2,1)S(1)}, u32[]{:S(2)}, u32[]{:S(2)}) %collective-permute-start.2) | collective-permute-done | bytes 163872 | tf_op jit(solution)/shard_map/ppermute | solution.py:201
  9.9 1.3 %collective-permute-done.3.refs_4_.refs_12_ = bf16[64,1280]{1,0:T(8,128)(2,1)S(1)} collective-permute-done((bf16[64,1280]{1,0:T(8,128)(2,1)S(1)}, bf16[64,1280]{1,0:T(8,128)(2,1)S(1)}, u32[]{:S(2)}, u32[]{:S(2)}) %collective-permute-start.3) | collective-permute-done | bytes 163872 | tf_op jit(solution)/shard_map/ppermute | solution.py:201
  11.2 0.9 pack.9
  12.1 1.6 %collective-permute-start.5 = (bf16[192,1280]{1,0:T(8,128)(2,1)S(1)}, bf16[192,1280]{1,0:T(8,128)(2,1)S(1)}, u32[]{:S(2)}, u32[]{:S(2)}) collective-permute-start(bf16[192,1280]{1,0:T(8,128)(2,1)S(1)} %get-tuple-element.34), channel_id=1, source_target_pairs={{0,8},{2,10},{8,16},{10,18},{16,24},{18,26},{24,28},{26,30},{28,20... | collective-permute-start | bytes 1474568 | tf_op jit(solution)/shard_map/ppermute | solution.py:201
  13.6 0.4 collective-permute-start.6
  14.1 0.5 collective-permute-start.4
  14.6 8.9 %collective-permute-done.5.refs_0_.refs_1_.refs_14_ = bf16[192,1280]{1,0:T(8,128)(2,1)S(1)} collective-permute-done((bf16[192,1280]{1,0:T(8,128)(2,1)S(1)}, bf16[192,1280]{1,0:T(8,128)(2,1)S(1)}, u32[]{:S(2)}, u32[]{:S(2)}) %collective-permute-start.5) | collective-permute-done | bytes 491552 | tf_op jit(solution)/shard_map/ppermute | solution.py:201
  23.6 1.6 %collective-permute-start.8 = (bf16[192,1280]{1,0:T(8,128)(2,1)S(1)}, bf16[192,1280]{1,0:T(8,128)(2,1)}, u32[]{:S(2)}, u32[]{:S(2)}) collective-permute-start(bf16[192,1280]{1,0:T(8,128)(2,1)S(1)} %collective-permute-done.5.refs_0_.refs_1_.refs_14_), channel_id=1, source_target_pairs={{0,8},{2,10},{8,16},{10,18},{16,24},{18,26},{24,28},{26,30},{28,20... | collective-permute-start | bytes 1474568 | tf_op jit(solution)/shard_map/ppermute | solution.py:201
  25.1 0.5 collective-permute-start.9
  25.6 0.9 copy-done.6
  26.6 1.6 %collective-permute-start.10 = (bf16[512,128]{1,0:T(8,128)(2,1)S(1)}, bf16[512,128]{1,0:T(8,128)(2,1)S(1)}, u32[]{:S(2)}, u32[]{:S(2)}) collective-permute-start(bf16[512,128]{1,0:T(8,128)(2,1)S(1)} %get-tuple-element.36.refs_0_.refs_2_), channel_id=1, source_target_pairs={{0,8},{2,10},{8,16},{10,18},{16,24},{18,26},{24,28},{26,30},{28,20... | collective-permute-start | bytes 393224 | tf_op jit(solution)/shard_map/ppermute | solution.py:201
  28.2 0.5 collective-permute-start.11
  28.7 0.5 collective-permute-start.12
  29.2 0.1 pad_add_fusion.refs_0_
  29.3 1.2 turn.1.refs_3_.refs_2_
  30.5 2.3 %low.1.refs_4_.refs_3_ = bf16[512,256]{1,0:T(8,128)(2,1)S(1)} custom-call(s32[2]{0:T(128)S(1)} %pad_add_fusion.refs_0_, s32[4]{0:T(128)S(1)} %copy-done.25, s32[4]{0:T(128)S(1)} %copy-done.32, bf16[512,2048]{1,0:T(8,128)(2,1)S(1)} %copy-done, bf16[2048,128]{1,0:T(8,128)(2,1)S(1)} %copy-done.1, bf16[2048,128]{1,0:T(8,128)(2,1)} %collective-permute-done.refs_5_), custom_call_target="tpu_custom_call" | custom-call | flops 536870912 | bytes 2097152 | tf_op jit(solution)/shard_map/low/pallas_call | solution.py:521
  32.9 4.1 %collective-permute-done.10.refs_5_.refs_3_ = bf16[512,128]{1,0:T(8,128)(2,1)S(1)} collective-permute-done((bf16[512,128]{1,0:T(8,128)(2,1)S(1)}, bf16[512,128]{1,0:T(8,128)(2,1)S(1)}, u32[]{:S(2)}, u32[]{:S(2)}) %collective-permute-start.10) | collective-permute-done | bytes 131104 | tf_op jit(solution)/shard_map/ppermute | solution.py:201
  37.0 1.3 %collective-permute-done.11.refs_6_.refs_4_ = bf16[512,128]{1,0:T(8,128)(2,1)S(1)} collective-permute-done((bf16[512,128]{1,0:T(8,128)(2,1)S(1)}, bf16[512,128]{1,0:T(8,128)(2,1)S(1)}, u32[]{:S(2)}, u32[]{:S(2)}) %collective-permute-start.11) | collective-permute-done | bytes 131104 | tf_op jit(solution)/shard_map/ppermute | solution.py:201
  38.4 1.3 %pack.12 = (bf16[160,1280]{1,0:T(8,128)(2,1)S(1)}, bf16[160,1280]{1,0:T(8,128)(2,1)S(1)}, bf16[128,1280]{1,0:T(8,128)(2,1)S(1)}) custom-call(bf16[192,1280]{1,0:T(8,128)(2,1)} %collective-permute-done.8.refs_0_.refs_17_.refs_5_, bf16[192,1280]{1,0:T(8,128)(2,1)} %collective-permute-done.9.refs_1_.refs_18_.refs_6_, ...), custom_call_target="tpu_custom_call" | custom-call | tf_op jit(solution)/shard_map/pack/pallas_call | solution.py:214
  39.7 1.6 %collective-permute-start.14 = (bf16[160,1280]{1,0:T(8,128)(2,1)S(1)}, bf16[160,1280]{1,0:T(8,128)(2,1)S(1)}, u32[]{:S(2)}, u32[]{:S(2)}) collective-permute-start(bf16[160,1280]{1,0:T(8,128)(2,1)S(1)} %get-tuple-element.39), channel_id=1, source_target_pairs={{0,8},{2,10},{8,16},{10,18},{16,24},{18,26},{24,28},{26,30},{28,20... | collective-permute-start | bytes 1228808 | tf_op jit(solution)/shard_map/ppermute | solution.py:201
  41.3 0.4 collective-permute-start.15
  41.8 0.6 collective-permute-start.7
  42.4 1.5 %collective-permute-start.13 = (bf16[128,1280]{1,0:T(8,128)(2,1)S(1)}, bf16[128,1280]{1,0:T(8,128)(2,1)S(1)}, u32[]{:S(2)}, u32[]{:S(2)}) collective-permute-start(bf16[128,1280]{1,0:T(8,128)(2,1)S(1)} %get-tuple-element.38), channel_id=1, source_target_pairs={{0,2},{2,0},{8,10},{10,8},{16,18},{18,16},{24,26},{26,24},{28,30},... | collective-permute-start | bytes 983048 | tf_op jit(solution)/shard_map/ppermute | solution.py:201
  43.9 8.6 %collective-permute-done.7.refs_2_.refs_16_ = bf16[128,1280]{1,0:T(8,128)(2,1)S(1)} collective-permute-done((bf16[128,1280]{1,0:T(8,128)(2,1)S(1)}, bf16[128,1280]{1,0:T(8,128)(2,1)S(1)}, u32[]{:S(2)}, u32[]{:S(2)}) %collective-permute-start.7) | collective-permute-done | bytes 327712 | tf_op jit(solution)/shard_map/ppermute | solution.py:201
  52.6 0.6 collective-permute-start.16
  53.2 1.6 %collective-permute-start.17 = (bf16[64,1280]{1,0:T(8,128)(2,1)S(1)}, bf16[64,1280]{1,0:T(8,128)(2,1)S(1)}, u32[]{:S(2)}, u32[]{:S(2)}) collective-permute-start(bf16[64,1280]{1,0:T(8,128)(2,1)S(1)} %get-tuple-element.42), channel_id=1, source_target_pairs={{0,8},{2,10},{8,16},{10,18},{16,24},{18,26},{24,28},{26,30},{28,20... | collective-permute-start | bytes 491528 | tf_op jit(solution)/shard_map/ppermute | solution.py:201
  54.8 0.4 collective-permute-start.18
  55.2 0.9 pack.14
  56.1 1.6 %collective-permute-start.20 = (bf16[1536,128]{1,0:T(8,128)(2,1)S(1)}, bf16[1536,128]{1,0:T(8,128)(2,1)S(1)}, u32[]{:S(2)}, u32[]{:S(2)}) collective-permute-start(bf16[1536,128]{1,0:T(8,128)(2,1)S(1)} %get-tuple-element.49), channel_id=1, source_target_pairs={{0,8},{2,10},{8,16},{10,18},{16,24},{18,26},{24,28},{26,30},{28,20... | collective-permute-start | bytes 1179656 | tf_op jit(solution)/shard_map/ppermute | solution.py:201
  57.7 0.5 collective-permute-start.21
  58.1 0.4 collective-permute-done.17.refs_23_
  58.5 1.6 %collective-permute-done.18.refs_24_ = bf16[64,1280]{1,0:T(8,128)(2,1)S(1)} collective-permute-done((bf16[64,1280]{1,0:T(8,128)(2,1)S(1)}, bf16[64,1280]{1,0:T(8,128)(2,1)S(1)}, u32[]{:S(2)}, u32[]{:S(2)}) %collective-permute-start.18) | collective-permute-done | bytes 163872 | tf_op jit(solution)/shard_map/ppermute | solution.py:201
  60.2 8.2 %project.1 = (bf16[512,128]{1,0:T(8,128)(2,1)}, bf16[512,128]{1,0:T(8,128)(2,1)}, bf16[512,1024]{1,0:T(8,128)(2,1)}, bf16[8,160,128]{2,1,0:T(8,128)(2,1)}) custom-call(s32[2]{0:T(128)S(1)} %pad_add_fusion.refs_0_, s32[4]{0:T(128)S(1)} %copy-done.25, bf16[512,2048]{1,0:T(8,128)(2,1)S(1)} %turn.1.refs_3_.refs_2_, bf16[512,256]{1,0:T(8,128)(2,1)S(1)} %low.1.refs_4_.refs_3_, ...), custom_call_target="tpu_custom_call" | custom-call | flops 2684354560 | bytes 5242880 | tf_op jit(solution)/shard_map/project/pallas_call | solution.py:521
  68.4 4.0 %all-to-all-start = ((bf16[16,80,128]{2,1,0:T(8,128)(2,1)}), bf16[16,80,128]{2,1,0:T(8,128)(2,1)S(1)}, u32[]{:S(2)}, u32[]{:S(2)}) async-start(bf16[16,80,128]{2,1,0:T(8,128)(2,1)} %bitcast.2), calls=%async_computation | async-start | bytes 655360 | tf_op jit(solution)/shard_map/all_to_all | solution.py:598
  72.3 1.9 %collective-permute-start.19 = (bf16[1536,128]{1,0:T(8,128)(2,1)}, bf16[1536,128]{1,0:T(8,128)(2,1)S(1)}, u32[]{:S(2)}, u32[]{:S(2)}) collective-permute-start(bf16[1536,128]{1,0:T(8,128)(2,1)} %get-tuple-element.48), channel_id=1, source_target_pairs={{0,2},{2,0},{8,10},{10,8},{16,18},{18,16},{24,26},{26,24},{28,30},... | collective-permute-start | bytes 1179656 | tf_op jit(solution)/shard_map/ppermute | solution.py:201
  74.3 1.5 %collective-permute-start.23 = (bf16[1536,128]{1,0:T(8,128)(2,1)S(1)}, bf16[1536,128]{1,0:T(8,128)(2,1)S(1)}, u32[]{:S(2)}, u32[]{:S(2)}) collective-permute-start(bf16[1536,128]{1,0:T(8,128)(2,1)S(1)} %collective-permute-done.20.refs_0_.refs_8_), channel_id=1, source_target_pairs={{0,8},{2,10},{8,16},{10,18},{16,24},{18,26},{24,28},{26,30},{28,20... | collective-permute-start | bytes 1179656 | tf_op jit(solution)/shard_map/ppermute | solution.py:201
  75.7 0.6 collective-permute-start.24
  76.3 0.7 copy-done.26
  77.0 0.7 copy-done.29
  77.6 4.6 %within.1.refs_2_ = bf16[512,1024]{1,0:T(8,128)(2,1)S(1)} custom-call(s32[2]{0:T(128)S(1)} %copy-done.29, s32[4]{0:T(128)S(1)} %copy-done.26, bf16[512,128]{1,0:T(8,128)(2,1)} %get-tuple-element.44.refs_2_.refs_3_, bf16[512,128]{1,0:T(8,128)(2,1)} %get-tuple-element.45.refs_3_, bf16[512,1024]{1,0:T(8,128)(2,1)} %get-tuple-element.46.refs_4_), custom_call_target="tpu_custom_call" | custom-call | flops 1073741824 | bytes 4194304 | tf_op jit(solution)/shard_map/within/pallas_call | solution.py:521
  82.2 1.4 %mix.1 = bf16[16,80,128]{2,1,0:T(8,128)(2,1)} custom-call(s32[4]{0:T(128)S(1)} %copy-done.26, bf16[16,80,128]{2,1,0:T(8,128)(2,1)S(1)} %all-to-all-done.refs_1_, bf16[512,1024]{1,0:T(8,128)(2,1)S(1)} %within.1.refs_2_), custom_call_target="tpu_custom_call" | custom-call | bytes 655360 | tf_op jit(solution)/shard_map/mix/pallas_call | solution.py:521
  83.6 5.7 %all-to-all-start.1 = ((bf16[16,80,128]{2,1,0:T(8,128)(2,1)}), bf16[16,80,128]{2,1,0:T(8,128)(2,1)S(1)}, u32[]{:S(2)}, u32[]{:S(2)}) async-start(bf16[16,80,128]{2,1,0:T(8,128)(2,1)} %mix.1), calls=%async_computation.1 | async-start | bytes 655360 | tf_op jit(solution)/shard_map/all_to_all | solution.py:611
  89.4 0.8 pack.16
  90.2 1.9 %collective-permute-start.26 = (bf16[1280,128]{1,0:T(8,128)(2,1)S(1)}, bf16[1280,128]{1,0:T(8,128)(2,1)S(1)}, u32[]{:S(2)}, u32[]{:S(2)}) collective-permute-start(bf16[1280,128]{1,0:T(8,128)(2,1)S(1)} %get-tuple-element.52), channel_id=1, source_target_pairs={{0,8},{2,10},{8,16},{10,18},{16,24},{18,26},{24,28},{26,30},{28,20... | collective-permute-start | bytes 983048 | tf_op jit(solution)/shard_map/ppermute | solution.py:201
  92.1 0.1 collective-permute-start.27
  92.2 1.0 pack.15
  93.2 2.0 %collective-permute-start.22 = (bf16[1024,128]{1,0:T(8,128)(2,1)S(1)}, bf16[1024,128]{1,0:T(8,128)(2,1)S(1)}, u32[]{:S(2)}, u32[]{:S(2)}) collective-permute-start(bf16[1024,128]{1,0:T(8,128)(2,1)S(1)} %pack.15), channel_id=1, source_target_pairs={{0,2},{2,0},{8,10},{10,8},{16,18},{18,16},{24,26},{26,24},{28,30},... | collective-permute-start | bytes 786440 | tf_op jit(solution)/shard_map/ppermute | solution.py:201
  95.2 0.1 collective-permute-start.25
  95.3 5.1 %collective-permute-done.22.refs_2_.refs_10_ = bf16[1024,128]{1,0:T(8,128)(2,1)S(1)} collective-permute-done((bf16[1024,128]{1,0:T(8,128)(2,1)S(1)}, bf16[1024,128]{1,0:T(8,128)(2,1)S(1)}, u32[]{:S(2)}, u32[]{:S(2)}) %collective-permute-start.22) | collective-permute-done | bytes 262176 | tf_op jit(solution)/shard_map/ppermute | solution.py:201
  100.4 1.0 collective-permute-done.27.refs_1_.refs_15_
  101.3 0.8 pack.17
  102.1 1.5 %collective-permute-start.28 = (bf16[512,128]{1,0:T(8,128)(2,1)}, bf16[512,128]{1,0:T(8,128)(2,1)}, u32[]{:S(2)}, u32[]{:S(2)}) collective-permute-start(bf16[512,128]{1,0:T(8,128)(2,1)} %get-tuple-element.54), channel_id=1, source_target_pairs={{0,2},{2,0},{8,10},{10,8},{16,18},{18,16},{24,26},{26,24},{28,30},... | collective-permute-start | bytes 393224 | tf_op jit(solution)/shard_map/ppermute | solution.py:201
  103.6 1.6 %collective-permute-start.29 = (bf16[512,128]{1,0:T(8,128)(2,1)}, bf16[512,128]{1,0:T(8,128)(2,1)}, u32[]{:S(2)}, u32[]{:S(2)}) collective-permute-start(bf16[512,128]{1,0:T(8,128)(2,1)} %get-tuple-element.55), channel_id=1, source_target_pairs={{0,8},{2,10},{8,16},{10,18},{16,24},{18,26},{24,28},{26,30},{28,20... | collective-permute-start | bytes 393224 | tf_op jit(solution)/shard_map/ppermute | solution.py:201
  105.2 0.5 collective-permute-start.30
  105.7 3.8 %finish.1.refs_1_ = bf16[512,1024]{1,0:T(8,128)(2,1)S(1)} custom-call(s32[2]{0:T(128)S(1)} %copy-done.30, s32[4]{0:T(128)S(1)} %copy-done.27, bf16[512,1024]{1,0:T(8,128)(2,1)S(1)} %within.1.refs_2_, bf16[512,128]{1,0:T(8,128)(2,1)} %get-tuple-element.44.refs_2_.refs_3_, bf16[8,160,128]{2,1,0:T(8,128)(2,1)S(1)} %bitcast.5, f32[1,1024]{1,0:T(1,128)S(1)} %bitcast.6, ...), custom_call_target="tpu_custom_call" | custom-call | flops 167772160 | bytes 4194304 | tf_op jit(solution)/shard_map/finish/pallas_call | solution.py:521
  109.5 1.0 collective-permute-done.30.refs_18_
  110.6 3.8 %out.1.refs_0_ = bf16[16,512,128]{2,1,0:T(8,128)(2,1)S(1)} custom-call(s32[2]{0:T(128)S(1)} %copy-done.30, bf16[512,1024]{1,0:T(8,128)(2,1)S(1)} %finish.1.refs_1_, bf16[512,128]{1,0:T(8,128)(2,1)S(1)} %copy-done.20, bf16[512,128]{1,0:T(8,128)(2,1)S(1)} %copy-done.22, bf16[512,128]{1,0:T(8,128)(2,1)S(1)} %collective-permute-done.12.refs_7_.refs_2_.refs_4_, ...), custom_call_target="tpu_custom_call" | custom-call | flops 2147483648 | bytes 4194304 | tf_op jit(solution)/shard_map/out/pallas_call | solution.py:521
  114.5 2.6 %collective-permute-done.31.refs_1_ = bf16[8,512,128]{2,1,0:T(8,128)(2,1)S(1)} collective-permute-done((bf16[8,512,128]{2,1,0:T(8,128)(2,1)S(1)}, bf16[8,512,128]{2,1,0:T(8,128)(2,1)S(1)}, u32[]{:S(2)}, u32[]{:S(2)}) %collective-permute-start.31) | collective-permute-done | bytes 1048608 | tf_op jit(solution)/shard_map/ppermute | solution.py:624
  117.1 1.3 %add.3 = bf16[512,1024]{1,0:T(8,128)(2,1)} custom-call(bf16[16,512,128]{2,1,0:T(8,128)(2,1)S(1)} %out.1.refs_0_, bf16[8,512,128]{2,1,0:T(8,128)(2,1)S(1)} %collective-permute-done.31.refs_1_), custom_call_target="tpu_custom_call" | custom-call | bytes 4194304 | tf_op jit(solution)/shard_map/add/pallas_call | solution.py:521
  (94 shorter events, 0.4 us)
Async XLA Ops:
  0.0 29.3 %copy-start = (bf16[512,2048]{1,0:T(8,128)(2,1)S(1)}, bf16[512,2048]{1,0:T(8,128)(2,1)}, u32[]{:S(2)}) copy-start(bf16[512,2048]{1,0:T(8,128)(2,1)} %refs_3_.1) | copy-start | bytes 6291460
  1.2 23.9 %copy-start.9 = (bf16[64,1280]{1,0:T(8,128)(2,1)}, bf16[64,1280]{1,0:T(8,128)(2,1)S(1)}, u32[]{:S(2)}) copy-start(bf16[64,1280]{1,0:T(8,128)(2,1)S(1)} %get-tuple-element.31.refs_0_.refs_8_) | copy-start | bytes 491524
  1.2 24.4 %copy-start.11 = (bf16[64,1280]{1,0:T(8,128)(2,1)}, bf16[64,1280]{1,0:T(8,128)(2,1)S(1)}, u32[]{:S(2)}) copy-start(bf16[64,1280]{1,0:T(8,128)(2,1)S(1)} %get-tuple-element.32.refs_1_.refs_9_) | copy-start | bytes 491524
  1.2 7.2 %collective-permute-start.1 = (bf16[64,1280]{1,0:T(8,128)(2,1)S(1)}, bf16[64,1280]{1,0:T(8,128)(2,1)S(1)}, u32[]{:S(2)}, u32[]{:S(2)}) collective-permute-start(bf16[64,1280]{1,0:T(8,128)(2,1)S(1)} %get-tuple-element.32.refs_1_.refs_9_), channel_id=1, source_target_pairs={{0,2},{2,0},{8,10},{10,8},{16,18},{18,16},{24,26},{26,24},{28,30},... | collective-permute-start | bytes 491528 | tf_op jit(solution)/shard_map/ppermute | solution.py:201
  4.2 5.7 %collective-permute-start.2 = (bf16[64,1280]{1,0:T(8,128)(2,1)S(1)}, bf16[64,1280]{1,0:T(8,128)(2,1)S(1)}, u32[]{:S(2)}, u32[]{:S(2)}) collective-permute-start(bf16[64,1280]{1,0:T(8,128)(2,1)S(1)} %get-tuple-element.31.refs_0_.refs_8_), channel_id=1, source_target_pairs={{0,8},{2,10},{8,16},{10,18},{16,24},{18,26},{24,28},{26,30},{28,20... | collective-permute-start | bytes 491528 | tf_op jit(solution)/shard_map/ppermute | solution.py:201
  5.8 5.4 %collective-permute-start.3 = (bf16[64,1280]{1,0:T(8,128)(2,1)S(1)}, bf16[64,1280]{1,0:T(8,128)(2,1)S(1)}, u32[]{:S(2)}, u32[]{:S(2)}) collective-permute-start(bf16[64,1280]{1,0:T(8,128)(2,1)S(1)} %get-tuple-element.31.refs_0_.refs_8_), channel_id=1, source_target_pairs={{0,4},{2,6},{8,0},{10,2},{16,8},{18,10},{24,16},{26,18},{28,24},{3... | collective-permute-start | bytes 491528 | tf_op jit(solution)/shard_map/ppermute | solution.py:201
  8.4 17.2 %copy-start.13 = (bf16[64,1280]{1,0:T(8,128)(2,1)}, bf16[64,1280]{1,0:T(8,128)(2,1)S(1)}, u32[]{:S(2)}) copy-start(bf16[64,1280]{1,0:T(8,128)(2,1)S(1)} %collective-permute-done.1.refs_2_.refs_10_) | copy-start | bytes 491524
  9.9 15.7 %copy-start.15 = (bf16[64,1280]{1,0:T(8,128)(2,1)}, bf16[64,1280]{1,0:T(8,128)(2,1)S(1)}, u32[]{:S(2)}) copy-start(bf16[64,1280]{1,0:T(8,128)(2,1)S(1)} %collective-permute-done.2.refs_3_.refs_11_) | copy-start | bytes 491524
  11.2 14.4 %copy-start.17 = (bf16[64,1280]{1,0:T(8,128)(2,1)}, bf16[64,1280]{1,0:T(8,128)(2,1)S(1)}, u32[]{:S(2)}) copy-start(bf16[64,1280]{1,0:T(8,128)(2,1)S(1)} %collective-permute-done.3.refs_4_.refs_12_) | copy-start | bytes 491524
  12.1 11.5 %collective-permute-start.5 = (bf16[192,1280]{1,0:T(8,128)(2,1)S(1)}, bf16[192,1280]{1,0:T(8,128)(2,1)S(1)}, u32[]{:S(2)}, u32[]{:S(2)}) collective-permute-start(bf16[192,1280]{1,0:T(8,128)(2,1)S(1)} %get-tuple-element.34), channel_id=1, source_target_pairs={{0,8},{2,10},{8,16},{10,18},{16,24},{18,26},{24,28},{26,30},{28,20... | collective-permute-start | bytes 1474568 | tf_op jit(solution)/shard_map/ppermute | solution.py:201
  13.6 11.5 %collective-permute-start.6 = (bf16[192,1280]{1,0:T(8,128)(2,1)S(1)}, bf16[192,1280]{1,0:T(8,128)(2,1)S(1)}, u32[]{:S(2)}, u32[]{:S(2)}) collective-permute-start(bf16[192,1280]{1,0:T(8,128)(2,1)S(1)} %get-tuple-element.35), channel_id=1, source_target_pairs={{0,4},{2,6},{8,0},{10,2},{16,8},{18,10},{24,16},{26,18},{28,24},{3... | collective-permute-start | bytes 1474568 | tf_op jit(solution)/shard_map/ppermute | solution.py:201
  14.1 14.1 %collective-permute-start = (bf16[2048,128]{1,0:T(8,128)(2,1)}, bf16[2048,128]{1,0:T(8,128)(2,1)}, u32[]{:S(2)}, u32[]{:S(2)}) collective-permute-start(bf16[2048,128]{1,0:T(8,128)(2,1)} %refs_4_.2), channel_id=1, source_target_pairs={{0,1},{1,0},{2,3},{3,2},{4,5},{5,4},{6,7},{7,6},{8,9},{9,8},{10,11... | collective-permute-start | bytes 1572872 | tf_op jit(solution)/shard_map/ppermute | solution.py:559
  14.1 14.6 %collective-permute-start.4 = (bf16[192,1280]{1,0:T(8,128)(2,1)}, bf16[192,1280]{1,0:T(8,128)(2,1)}, u32[]{:S(2)}, u32[]{:S(2)}) collective-permute-start(bf16[192,1280]{1,0:T(8,128)(2,1)} %get-tuple-element.33), channel_id=1, source_target_pairs={{0,2},{2,0},{8,10},{10,8},{16,18},{18,16},{24,26},{26,24},{28,30},... | collective-permute-start | bytes 1474568 | tf_op jit(solution)/shard_map/ppermute | solution.py:201
  23.6 14.8 %collective-permute-start.8 = (bf16[192,1280]{1,0:T(8,128)(2,1)S(1)}, bf16[192,1280]{1,0:T(8,128)(2,1)}, u32[]{:S(2)}, u32[]{:S(2)}) collective-permute-start(bf16[192,1280]{1,0:T(8,128)(2,1)S(1)} %collective-permute-done.5.refs_0_.refs_1_.refs_14_), channel_id=1, source_target_pairs={{0,8},{2,10},{8,16},{10,18},{16,24},{18,26},{24,28},{26,30},{28,20... | collective-permute-start | bytes 1474568 | tf_op jit(solution)/shard_map/ppermute | solution.py:201
  25.1 13.2 %collective-permute-start.9 = (bf16[192,1280]{1,0:T(8,128)(2,1)S(1)}, bf16[192,1280]{1,0:T(8,128)(2,1)}, u32[]{:S(2)}, u32[]{:S(2)}) collective-permute-start(bf16[192,1280]{1,0:T(8,128)(2,1)S(1)} %collective-permute-done.6.refs_1_.refs_2_.refs_15_), channel_id=1, source_target_pairs={{0,4},{2,6},{8,0},{10,2},{16,8},{18,10},{24,16},{26,18},{28,24},{3... | collective-permute-start | bytes 1474568 | tf_op jit(solution)/shard_map/ppermute | solution.py:201
  26.6 28.6 %copy-start.19 = (bf16[512,128]{1,0:T(8,128)(2,1)}, bf16[512,128]{1,0:T(8,128)(2,1)S(1)}, u32[]{:S(2)}) copy-start(bf16[512,128]{1,0:T(8,128)(2,1)S(1)} %get-tuple-element.36.refs_0_.refs_2_) | copy-start | bytes 393220
  26.6 28.6 %copy-start.21 = (bf16[512,128]{1,0:T(8,128)(2,1)}, bf16[512,128]{1,0:T(8,128)(2,1)S(1)}, u32[]{:S(2)}) copy-start(bf16[512,128]{1,0:T(8,128)(2,1)S(1)} %get-tuple-element.37.refs_1_.refs_3_) | copy-start | bytes 393220
  26.6 10.4 %collective-permute-start.10 = (bf16[512,128]{1,0:T(8,128)(2,1)S(1)}, bf16[512,128]{1,0:T(8,128)(2,1)S(1)}, u32[]{:S(2)}, u32[]{:S(2)}) collective-permute-start(bf16[512,128]{1,0:T(8,128)(2,1)S(1)} %get-tuple-element.36.refs_0_.refs_2_), channel_id=1, source_target_pairs={{0,8},{2,10},{8,16},{10,18},{16,24},{18,26},{24,28},{26,30},{28,20... | collective-permute-start | bytes 393224 | tf_op jit(solution)/shard_map/ppermute | solution.py:201
  28.2 10.1 %collective-permute-start.11 = (bf16[512,128]{1,0:T(8,128)(2,1)S(1)}, bf16[512,128]{1,0:T(8,128)(2,1)S(1)}, u32[]{:S(2)}, u32[]{:S(2)}) collective-permute-start(bf16[512,128]{1,0:T(8,128)(2,1)S(1)} %get-tuple-element.36.refs_0_.refs_2_), channel_id=1, source_target_pairs={{0,4},{2,6},{8,0},{10,2},{16,8},{18,10},{24,16},{26,18},{28,24},{3... | collective-permute-start | bytes 393224 | tf_op jit(solution)/shard_map/ppermute | solution.py:201
  28.7 9.7 %collective-permute-start.12 = (bf16[512,128]{1,0:T(8,128)(2,1)S(1)}, bf16[512,128]{1,0:T(8,128)(2,1)S(1)}, u32[]{:S(2)}, u32[]{:S(2)}) collective-permute-start(bf16[512,128]{1,0:T(8,128)(2,1)S(1)} %get-tuple-element.37.refs_1_.refs_3_), channel_id=1, source_target_pairs={{0,2},{2,0},{8,10},{10,8},{16,18},{18,16},{24,26},{26,24},{28,30},... | collective-permute-start | bytes 393224 | tf_op jit(solution)/shard_map/ppermute | solution.py:201
  29.3 30.8 %copy-start.28 = (s32[2]{0:T(128)}, s32[2]{0:T(128)S(1)}, u32[]{:S(2)}) copy-start(s32[2]{0:T(128)S(1)} %pad_add_fusion.refs_0_) | copy-start | bytes 28
  29.3 1.2 %copy-start.32 = (s32[4]{0:T(128)S(1)}, s32[4]{0:T(128)}, u32[]{:S(2)}) copy-start(s32[4]{0:T(128)} %refs_2_.1) | copy-start | bytes 52
  39.6 20.5 %copy-start.10 = (bf16[64,1280]{1,0:T(8,128)(2,1)S(1)}, bf16[64,1280]{1,0:T(8,128)(2,1)}, u32[]{:S(2)}) copy-start(bf16[64,1280]{1,0:T(8,128)(2,1)} %copy-done.9) | copy-start | bytes 491524
  39.6 20.5 %copy-start.12 = (bf16[64,1280]{1,0:T(8,128)(2,1)S(1)}, bf16[64,1280]{1,0:T(8,128)(2,1)}, u32[]{:S(2)}) copy-start(bf16[64,1280]{1,0:T(8,128)(2,1)} %copy-done.11) | copy-start | bytes 491524
  39.6 20.5 %copy-start.14 = (bf16[64,1280]{1,0:T(8,128)(2,1)S(1)}, bf16[64,1280]{1,0:T(8,128)(2,1)}, u32[]{:S(2)}) copy-start(bf16[64,1280]{1,0:T(8,128)(2,1)} %copy-done.13) | copy-start | bytes 491524
  39.6 20.5 %copy-start.16 = (bf16[64,1280]{1,0:T(8,128)(2,1)S(1)}, bf16[64,1280]{1,0:T(8,128)(2,1)}, u32[]{:S(2)}) copy-start(bf16[64,1280]{1,0:T(8,128)(2,1)} %copy-done.15) | copy-start | bytes 491524
  39.7 20.5 %copy-start.18 = (bf16[64,1280]{1,0:T(8,128)(2,1)S(1)}, bf16[64,1280]{1,0:T(8,128)(2,1)}, u32[]{:S(2)}) copy-start(bf16[64,1280]{1,0:T(8,128)(2,1)} %copy-done.17) | copy-start | bytes 491524
  39.7 20.5 %copy-start.23 = (f32[160,128]{1,0:T(8,128)S(1)}, f32[160,128]{1,0:T(8,128)}, u32[]{:S(2)}) copy-start(f32[160,128]{1,0:T(8,128)} %constant.14.clone.refs_5_.refs_6_) | copy-start | bytes 245764
  39.7 20.4 %copy-start.24 = (f32[160,128]{1,0:T(8,128)S(1)}, f32[160,128]{1,0:T(8,128)}, u32[]{:S(2)}) copy-start(f32[160,128]{1,0:T(8,128)} %constant.15.clone.refs_6_.refs_7_) | copy-start | bytes 245764
  39.7 20.4 %copy-start.33 = (bf16[256,1024]{1,0:T(8,128)(2,1)S(1)}, bf16[256,1024]{1,0:T(8,128)(2,1)}, u32[]{:S(2)}) copy-start(bf16[256,1024]{1,0:T(8,128)(2,1)} %refs_4_.3) | copy-start | bytes 1572868
  39.7 20.4 %copy-start.34 = (f32[160,8]{1,0:T(8,128)S(1)}, f32[160,8]{1,0:T(8,128)}, u32[]{:S(2)}) copy-start(f32[160,8]{1,0:T(8,128)} %constant.17.refs_7_) | copy-start | bytes 15364
  39.7 12.8 %collective-permute-start.14 = (bf16[160,1280]{1,0:T(8,128)(2,1)S(1)}, bf16[160,1280]{1,0:T(8,128)(2,1)S(1)}, u32[]{:S(2)}, u32[]{:S(2)}) collective-permute-start(bf16[160,1280]{1,0:T(8,128)(2,1)S(1)} %get-tuple-element.39), channel_id=1, source_target_pairs={{0,8},{2,10},{8,16},{10,18},{16,24},{18,26},{24,28},{26,30},{28,20... | collective-permute-start | bytes 1228808 | tf_op jit(solution)/shard_map/ppermute | solution.py:201
  41.3 11.2 %collective-permute-start.15 = (bf16[160,1280]{1,0:T(8,128)(2,1)S(1)}, bf16[160,1280]{1,0:T(8,128)(2,1)S(1)}, u32[]{:S(2)}, u32[]{:S(2)}) collective-permute-start(bf16[160,1280]{1,0:T(8,128)(2,1)S(1)} %get-tuple-element.40), channel_id=1, source_target_pairs={{0,4},{2,6},{8,0},{10,2},{16,8},{18,10},{24,16},{26,18},{28,24},{3... | collective-permute-start | bytes 1228808 | tf_op jit(solution)/shard_map/ppermute | solution.py:201
  41.8 10.7 %collective-permute-start.7 = (bf16[128,1280]{1,0:T(8,128)(2,1)S(1)}, bf16[128,1280]{1,0:T(8,128)(2,1)S(1)}, u32[]{:S(2)}, u32[]{:S(2)}) collective-permute-start(bf16[128,1280]{1,0:T(8,128)(2,1)S(1)} %pack.10), channel_id=1, source_target_pairs={{0,2},{2,0},{8,10},{10,8},{16,18},{18,16},{24,26},{26,24},{28,30},... | collective-permute-start | bytes 983048 | tf_op jit(solution)/shard_map/ppermute | solution.py:201
  42.4 15.2 %collective-permute-start.13 = (bf16[128,1280]{1,0:T(8,128)(2,1)S(1)}, bf16[128,1280]{1,0:T(8,128)(2,1)S(1)}, u32[]{:S(2)}, u32[]{:S(2)}) collective-permute-start(bf16[128,1280]{1,0:T(8,128)(2,1)S(1)} %get-tuple-element.38), channel_id=1, source_target_pairs={{0,2},{2,0},{8,10},{10,8},{16,18},{18,16},{24,26},{26,24},{28,30},... | collective-permute-start | bytes 983048 | tf_op jit(solution)/shard_map/ppermute | solution.py:201
  52.6 5.5 %collective-permute-start.16 = (bf16[64,1280]{1,0:T(8,128)(2,1)S(1)}, bf16[64,1280]{1,0:T(8,128)(2,1)S(1)}, u32[]{:S(2)}, u32[]{:S(2)}) collective-permute-start(bf16[64,1280]{1,0:T(8,128)(2,1)S(1)} %get-tuple-element.41), channel_id=1, source_target_pairs={{0,2},{2,0},{8,10},{10,8},{16,18},{18,16},{24,26},{26,24},{28,30},... | collective-permute-start | bytes 491528 | tf_op jit(solution)/shard_map/ppermute | solution.py:201
  53.2 5.3 %collective-permute-start.17 = (bf16[64,1280]{1,0:T(8,128)(2,1)S(1)}, bf16[64,1280]{1,0:T(8,128)(2,1)S(1)}, u32[]{:S(2)}, u32[]{:S(2)}) collective-permute-start(bf16[64,1280]{1,0:T(8,128)(2,1)S(1)} %get-tuple-element.42), channel_id=1, source_target_pairs={{0,8},{2,10},{8,16},{10,18},{16,24},{18,26},{24,28},{26,30},{28,20... | collective-permute-start | bytes 491528 | tf_op jit(solution)/shard_map/ppermute | solution.py:201
  54.8 5.3 %collective-permute-start.18 = (bf16[64,1280]{1,0:T(8,128)(2,1)S(1)}, bf16[64,1280]{1,0:T(8,128)(2,1)S(1)}, u32[]{:S(2)}, u32[]{:S(2)}) collective-permute-start(bf16[64,1280]{1,0:T(8,128)(2,1)S(1)} %get-tuple-element.43), channel_id=1, source_target_pairs={{0,4},{2,6},{8,0},{10,2},{16,8},{18,10},{24,16},{26,18},{28,24},{3... | collective-permute-start | bytes 491528 | tf_op jit(solution)/shard_map/ppermute | solution.py:201
  56.1 18.2 %collective-permute-start.20 = (bf16[1536,128]{1,0:T(8,128)(2,1)S(1)}, bf16[1536,128]{1,0:T(8,128)(2,1)S(1)}, u32[]{:S(2)}, u32[]{:S(2)}) collective-permute-start(bf16[1536,128]{1,0:T(8,128)(2,1)S(1)} %get-tuple-element.49), channel_id=1, source_target_pairs={{0,8},{2,10},{8,16},{10,18},{16,24},{18,26},{24,28},{26,30},{28,20... | collective-permute-start | bytes 1179656 | tf_op jit(solution)/shard_map/ppermute | solution.py:201
  57.7 18.1 %collective-permute-start.21 = (bf16[1536,128]{1,0:T(8,128)(2,1)S(1)}, bf16[1536,128]{1,0:T(8,128)(2,1)}, u32[]{:S(2)}, u32[]{:S(2)}) collective-permute-start(bf16[1536,128]{1,0:T(8,128)(2,1)S(1)} %get-tuple-element.50), channel_id=1, source_target_pairs={{0,4},{2,6},{8,0},{10,2},{16,8},{18,10},{24,16},{26,18},{28,24},{3... | collective-permute-start | bytes 1179656 | tf_op jit(solution)/shard_map/ppermute | solution.py:201
  68.4 13.9 %all-to-all-start = ((bf16[16,80,128]{2,1,0:T(8,128)(2,1)}), bf16[16,80,128]{2,1,0:T(8,128)(2,1)S(1)}, u32[]{:S(2)}, u32[]{:S(2)}) async-start(bf16[16,80,128]{2,1,0:T(8,128)(2,1)} %bitcast.2), calls=%async_computation | async-start | bytes 655360 | tf_op jit(solution)/shard_map/all_to_all | solution.py:598
  72.3 17.0 %collective-permute-start.19 = (bf16[1536,128]{1,0:T(8,128)(2,1)}, bf16[1536,128]{1,0:T(8,128)(2,1)S(1)}, u32[]{:S(2)}, u32[]{:S(2)}) collective-permute-start(bf16[1536,128]{1,0:T(8,128)(2,1)} %get-tuple-element.48), channel_id=1, source_target_pairs={{0,2},{2,0},{8,10},{10,8},{16,18},{18,16},{24,26},{26,24},{28,30},... | collective-permute-start | bytes 1179656 | tf_op jit(solution)/shard_map/ppermute | solution.py:201
  74.3 15.1 %collective-permute-start.23 = (bf16[1536,128]{1,0:T(8,128)(2,1)S(1)}, bf16[1536,128]{1,0:T(8,128)(2,1)S(1)}, u32[]{:S(2)}, u32[]{:S(2)}) collective-permute-start(bf16[1536,128]{1,0:T(8,128)(2,1)S(1)} %collective-permute-done.20.refs_0_.refs_8_), channel_id=1, source_target_pairs={{0,8},{2,10},{8,16},{10,18},{16,24},{18,26},{24,28},{26,30},{28,20... | collective-permute-start | bytes 1179656 | tf_op jit(solution)/shard_map/ppermute | solution.py:201
  75.7 13.6 %collective-permute-start.24 = (bf16[1536,128]{1,0:T(8,128)(2,1)}, bf16[1536,128]{1,0:T(8,128)(2,1)S(1)}, u32[]{:S(2)}, u32[]{:S(2)}) collective-permute-start(bf16[1536,128]{1,0:T(8,128)(2,1)} %collective-permute-done.21.refs_1_.refs_9_), channel_id=1, source_target_pairs={{0,4},{2,6},{8,0},{10,2},{16,8},{18,10},{24,16},{26,18},{28,24},{3... | collective-permute-start | bytes 1179656 | tf_op jit(solution)/shard_map/ppermute | solution.py:201
  83.6 22.1 %copy-start.27 = (s32[4]{0:T(128)S(1)}, s32[4]{0:T(128)}, u32[]{:S(2)}) copy-start(s32[4]{0:T(128)} %refs_1_.9) | copy-start | bytes 52
  83.6 22.1 %copy-start.30 = (s32[2]{0:T(128)S(1)}, s32[2]{0:T(128)}, u32[]{:S(2)}) copy-start(s32[2]{0:T(128)} %copy-done.28) | copy-start | bytes 28
  83.6 22.1 %copy-start.31 = (f32[1024]{0:T(1024)S(1)}, f32[1024]{0:T(1024)}, u32[]{:S(2)}) copy-start(f32[1024]{0:T(1024)} %param.21) | copy-start | bytes 12292
  83.6 22.0 %all-to-all-start.1 = ((bf16[16,80,128]{2,1,0:T(8,128)(2,1)}), bf16[16,80,128]{2,1,0:T(8,128)(2,1)S(1)}, u32[]{:S(2)}, u32[]{:S(2)}) async-start(bf16[16,80,128]{2,1,0:T(8,128)(2,1)} %mix.1), calls=%async_computation.1 | async-start | bytes 655360 | tf_op jit(solution)/shard_map/all_to_all | solution.py:611
  90.2 10.2 %collective-permute-start.26 = (bf16[1280,128]{1,0:T(8,128)(2,1)S(1)}, bf16[1280,128]{1,0:T(8,128)(2,1)S(1)}, u32[]{:S(2)}, u32[]{:S(2)}) collective-permute-start(bf16[1280,128]{1,0:T(8,128)(2,1)S(1)} %get-tuple-element.52), channel_id=1, source_target_pairs={{0,8},{2,10},{8,16},{10,18},{16,24},{18,26},{24,28},{26,30},{28,20... | collective-permute-start | bytes 983048 | tf_op jit(solution)/shard_map/ppermute | solution.py:201
  92.1 18.4 %copy-start.20 = (bf16[512,128]{1,0:T(8,128)(2,1)S(1)}, bf16[512,128]{1,0:T(8,128)(2,1)}, u32[]{:S(2)}) copy-start(bf16[512,128]{1,0:T(8,128)(2,1)} %copy-done.19) | copy-start | bytes 393220
  92.1 9.2 %collective-permute-start.27 = (bf16[1280,128]{1,0:T(8,128)(2,1)S(1)}, bf16[1280,128]{1,0:T(8,128)(2,1)S(1)}, u32[]{:S(2)}, u32[]{:S(2)}) collective-permute-start(bf16[1280,128]{1,0:T(8,128)(2,1)S(1)} %get-tuple-element.53), channel_id=1, source_target_pairs={{0,4},{2,6},{8,0},{10,2},{16,8},{18,10},{24,16},{26,18},{28,24},{3... | collective-permute-start | bytes 983048 | tf_op jit(solution)/shard_map/ppermute | solution.py:201
  93.2 7.1 %collective-permute-start.22 = (bf16[1024,128]{1,0:T(8,128)(2,1)S(1)}, bf16[1024,128]{1,0:T(8,128)(2,1)S(1)}, u32[]{:S(2)}, u32[]{:S(2)}) collective-permute-start(bf16[1024,128]{1,0:T(8,128)(2,1)S(1)} %pack.15), channel_id=1, source_target_pairs={{0,2},{2,0},{8,10},{10,8},{16,18},{18,16},{24,26},{26,24},{28,30},... | collective-permute-start | bytes 786440 | tf_op jit(solution)/shard_map/ppermute | solution.py:201
  95.2 14.3 %collective-permute-start.25 = (bf16[1024,128]{1,0:T(8,128)(2,1)}, bf16[1024,128]{1,0:T(8,128)(2,1)}, u32[]{:S(2)}, u32[]{:S(2)}) collective-permute-start(bf16[1024,128]{1,0:T(8,128)(2,1)} %get-tuple-element.51), channel_id=1, source_target_pairs={{0,2},{2,0},{8,10},{10,8},{16,18},{18,16},{24,26},{26,24},{28,30},... | collective-permute-start | bytes 786440 | tf_op jit(solution)/shard_map/ppermute | solution.py:201
  100.3 4.8 %copy-start.7 = (bf16[1024,128]{1,0:T(8,128)(2,1)}, bf16[1024,128]{1,0:T(8,128)(2,1)S(1)}, u32[]{:S(2)}) copy-start(bf16[1024,128]{1,0:T(8,128)(2,1)S(1)} %collective-permute-done.22.refs_2_.refs_10_) | copy-start | bytes 786436
  100.4 4.8 %copy-start.2 = (bf16[1280,128]{1,0:T(8,128)(2,1)}, bf16[1280,128]{1,0:T(8,128)(2,1)S(1)}, u32[]{:S(2)}) copy-start(bf16[1280,128]{1,0:T(8,128)(2,1)S(1)} %collective-permute-done.26.refs_0_.refs_14_) | copy-start | bytes 983044
  101.3 3.9 %copy-start.4 = (bf16[1280,128]{1,0:T(8,128)(2,1)}, bf16[1280,128]{1,0:T(8,128)(2,1)S(1)}, u32[]{:S(2)}) copy-start(bf16[1280,128]{1,0:T(8,128)(2,1)S(1)} %collective-permute-done.27.refs_1_.refs_15_) | copy-start | bytes 983044
  102.1 7.4 %collective-permute-start.28 = (bf16[512,128]{1,0:T(8,128)(2,1)}, bf16[512,128]{1,0:T(8,128)(2,1)}, u32[]{:S(2)}, u32[]{:S(2)}) collective-permute-start(bf16[512,128]{1,0:T(8,128)(2,1)} %get-tuple-element.54), channel_id=1, source_target_pairs={{0,2},{2,0},{8,10},{10,8},{16,18},{18,16},{24,26},{26,24},{28,30},... | collective-permute-start | bytes 393224 | tf_op jit(solution)/shard_map/ppermute | solution.py:201
  103.6 5.9 %collective-permute-start.29 = (bf16[512,128]{1,0:T(8,128)(2,1)}, bf16[512,128]{1,0:T(8,128)(2,1)}, u32[]{:S(2)}, u32[]{:S(2)}) collective-permute-start(bf16[512,128]{1,0:T(8,128)(2,1)} %get-tuple-element.55), channel_id=1, source_target_pairs={{0,8},{2,10},{8,16},{10,18},{16,24},{18,26},{24,28},{26,30},{28,20... | collective-permute-start | bytes 393224 | tf_op jit(solution)/shard_map/ppermute | solution.py:201
  105.2 5.3 %collective-permute-start.30 = (bf16[512,128]{1,0:T(8,128)(2,1)}, bf16[512,128]{1,0:T(8,128)(2,1)}, u32[]{:S(2)}, u32[]{:S(2)}) collective-permute-start(bf16[512,128]{1,0:T(8,128)(2,1)} %get-tuple-element.56), channel_id=1, source_target_pairs={{0,4},{2,6},{8,0},{10,2},{16,8},{18,10},{24,16},{26,18},{28,24},{3... | collective-permute-start | bytes 393224 | tf_op jit(solution)/shard_map/ppermute | solution.py:201
  105.7 4.8 %copy-start.3 = (bf16[1280,128]{1,0:T(8,128)(2,1)S(1)}, bf16[1280,128]{1,0:T(8,128)(2,1)}, u32[]{:S(2)}) copy-start(bf16[1280,128]{1,0:T(8,128)(2,1)} %copy-done.2) | copy-start | bytes 983044
  105.7 4.8 %copy-start.5 = (bf16[1280,128]{1,0:T(8,128)(2,1)S(1)}, bf16[1280,128]{1,0:T(8,128)(2,1)}, u32[]{:S(2)}) copy-start(bf16[1280,128]{1,0:T(8,128)(2,1)} %copy-done.4) | copy-start | bytes 983044
  105.7 4.8 %copy-start.8 = (bf16[1024,128]{1,0:T(8,128)(2,1)S(1)}, bf16[1024,128]{1,0:T(8,128)(2,1)}, u32[]{:S(2)}) copy-start(bf16[1024,128]{1,0:T(8,128)(2,1)} %copy-done.7) | copy-start | bytes 786436
  105.7 4.9 %copy-start.22 = (bf16[512,128]{1,0:T(8,128)(2,1)S(1)}, bf16[512,128]{1,0:T(8,128)(2,1)}, u32[]{:S(2)}) copy-start(bf16[512,128]{1,0:T(8,128)(2,1)} %copy-done.21) | copy-start | bytes 393220
  114.4 2.7 %collective-permute-start.31 = (bf16[8,512,128]{2,1,0:T(8,128)(2,1)S(1)}, bf16[8,512,128]{2,1,0:T(8,128)(2,1)S(1)}, u32[]{:S(2)}, u32[]{:S(2)}) collective-permute-start(bf16[8,512,128]{2,1,0:T(8,128)(2,1)S(1)} %slice.4), channel_id=1, source_target_pairs={{0,1},{1,0},{2,3},{3,2},{4,5},{5,4},{6,7},{7,6},{8,9},{9,8},{10,11... | collective-permute-start | bytes 3145736 | tf_op jit(solution)/shard_map/ppermute | solution.py:624
  (5 other events, 4.7 us)

commit v5 on v4

--- a/solution.py
+++ b/solution.py
@@ -572,11 +572,11 @@
     second_round = chain.send(())
     third = next(chain)
     out_alone, out_pair = pack(
-        [[(0, 0, wide // 2)], [(0, wide // 2, wide // 2)]], [out_weight], second_round[:2]
+        [[(0, 0, wide // 2)], [(0, wide // 2, wide // 2)]], [out_weight], second_round[:2] + (turned, low)
     )
     out_chain = gather_rows(out_alone, out_pair)
     out_first = next(out_chain)
-    chain.send((turned, low) + out_first)
+    chain.send(out_first)
     out_second = out_chain.send(third[:2])
     fifth = chain.send(())
     gathered = next(chain)
@@ -585,7 +585,7 @@
     pieces, layout = [piece for piece, _ in gathered], [places for _, places in gathered]
     query, keys, values, state = call(
         functools.partial(project_kernel, layout, rows, heads, width), "project", 14,
-        (2 * count * depth * total, 2 * depth * total),
+        (count * depth * total // 2, depth * total // 2),
         [
             ((count, small), half),
             ((count, small), half),
@@ -598,7 +598,7 @@
     parts = lax.all_to_all(parts, "dp", 0, 0, tiled=True)
     (within,) = call(
         functools.partial(within_kernel, heads, width), "within", 12,
-        (4 * count * count * wide, 8 * count * wide), [((count, wide), half)],
+        (12 * count * count * wide, 24 * count * wide), [((count, wide), half)],
         [info, lengths], [query, keys, values], far=(0, 1, 2),
     )
     out_fourth = out_chain.send(())

time: 119 us -> 116 us (0.975)
  Pallas kernels: 33.5 us -> 31 us
  waiting for transfers between devices: 39.6 us -> 38 us
  starting transfers between devices: 42.4 us -> 43.8 us
    ppermute x30, waiting for transfers between devices: 36.9 us -> 34.9 us  [send(): return lax.ppermute(value, 'dp', pairs)]
    pallas_call x8, Pallas kernels: 26.6 us -> 25.1 us  [call(): pl.pallas_call(body, out_shape=shapes, in_specs=[SMEM] * n + [HBM if i in...]
    unnamed x70 -> x40, local copies, waits for them, and re-layouts: 2.39 us -> 2.42 us
  transfers between devices with their start and end apart: 34 -> 34, of which waited for: 13 -> 15; matrix products, arithmetic and copies ran while one was open for 0% -> 0% of each run, Pallas kernels for 21% -> 21%
where the time goes in v5:
time: 116 us
  starting transfers between devices  43.8 us (38%)
  waiting for transfers between devices  38 us (33%)
  Pallas kernels  31 us (27%)
  local copies, waits for them, and re-layouts  2.49 us (2%)
    ppermute x30, waiting for transfers between devices, send(): return lax.ppermute(value, 'dp', pairs)  34.9 us
    ppermute x30, starting transfers between devices, send(): return lax.ppermute(value, 'dp', pairs)  33.5 us
    pallas_call x8, Pallas kernels, call(): pl.pallas_call(body, out_shape=shapes, in_specs=[SMEM] * n + [HBM if i in...  25.1 us
    all_to_all x1, starting transfers between devices, per_device_fast(): lax.all_to_all(mixed, 'dp', 0, 0, tiled=True).reshape(heads, FEATS, width)  5.25 us
    all_to_all x1, starting transfers between devices, per_device_fast(): parts = lax.all_to_all(parts, 'dp', 0, 0, tiled=True)  4.96 us
    pallas_call x9, Pallas kernels, pack(): pl.pallas_call(functools.partial(pack_kernel, recipes, len(sources)), out...  4.77 us
    ppermute x1, waiting for transfers between devices, per_device_fast(): received = lax.ppermute(partial[blocks // 2:], 'mp', [(0, 1), (1, 0)])  2.65 us
    unnamed x40, local copies, waits for them, and re-layouts  2.42 us
  transfers between devices with their start and end apart: 34, of which 15 were waited for; matrix products, arithmetic and copies ran while one was open for 0% of the time, Pallas kernels for 21%

profile of v5, /device:TPU:0, one launch (start us, length us, event | category | flops | bytes accessed | tf_op | source)
XLA Modules:
  0.0 115.7 jit_solution(12218285630618336218)
XLA Ops:
  0.0 1.1 join.1
  1.1 3.0 %collective-permute-start.1 = (bf16[64,1280]{1,0:T(8,128)(2,1)S(1)}, bf16[64,1280]{1,0:T(8,128)(2,1)S(1)}, u32[]{:S(2)}, u32[]{:S(2)}) collective-permute-start(bf16[64,1280]{1,0:T(8,128)(2,1)S(1)} %get-tuple-element.32.refs_1_.refs_9_), channel_id=1, source_target_pairs={{0,2},{2,0},{8,10},{10,8},{16,18},{18,16},{24,26},{26,24},{28,30},... | collective-permute-start | bytes 491528 | tf_op jit(solution)/shard_map/ppermute | solution.py:201
  4.1 1.5 %collective-permute-start.3 = (bf16[64,1280]{1,0:T(8,128)(2,1)S(1)}, bf16[64,1280]{1,0:T(8,128)(2,1)S(1)}, u32[]{:S(2)}, u32[]{:S(2)}) collective-permute-start(bf16[64,1280]{1,0:T(8,128)(2,1)S(1)} %get-tuple-element.31.refs_0_.refs_8_), channel_id=1, source_target_pairs={{0,4},{2,6},{8,0},{10,2},{16,8},{18,10},{24,16},{26,18},{28,24},{3... | collective-permute-start | bytes 491528 | tf_op jit(solution)/shard_map/ppermute | solution.py:201
  5.6 0.5 collective-permute-start.2
  6.1 2.2 %collective-permute-done.1.refs_2_.refs_10_ = bf16[64,1280]{1,0:T(8,128)(2,1)S(1)} collective-permute-done((bf16[64,1280]{1,0:T(8,128)(2,1)S(1)}, bf16[64,1280]{1,0:T(8,128)(2,1)S(1)}, u32[]{:S(2)}, u32[]{:S(2)}) %collective-permute-start.1) | collective-permute-done | bytes 163872 | tf_op jit(solution)/shard_map/ppermute | solution.py:201
  8.3 1.5 %collective-permute-done.3.refs_4_.refs_12_ = bf16[64,1280]{1,0:T(8,128)(2,1)S(1)} collective-permute-done((bf16[64,1280]{1,0:T(8,128)(2,1)S(1)}, bf16[64,1280]{1,0:T(8,128)(2,1)S(1)}, u32[]{:S(2)}, u32[]{:S(2)}) %collective-permute-start.3) | collective-permute-done | bytes 163872 | tf_op jit(solution)/shard_map/ppermute | solution.py:201
  9.7 1.2 %collective-permute-done.2.refs_3_.refs_11_ = bf16[64,1280]{1,0:T(8,128)(2,1)S(1)} collective-permute-done((bf16[64,1280]{1,0:T(8,128)(2,1)S(1)}, bf16[64,1280]{1,0:T(8,128)(2,1)S(1)}, u32[]{:S(2)}, u32[]{:S(2)}) %collective-permute-start.2) | collective-permute-done | bytes 163872 | tf_op jit(solution)/shard_map/ppermute | solution.py:201
  11.0 0.9 pack.9
  11.8 0.5 collective-permute-start.5
  12.3 1.5 %collective-permute-start.6 = (bf16[192,1280]{1,0:T(8,128)(2,1)S(1)}, bf16[192,1280]{1,0:T(8,128)(2,1)S(1)}, u32[]{:S(2)}, u32[]{:S(2)}) collective-permute-start(bf16[192,1280]{1,0:T(8,128)(2,1)S(1)} %get-tuple-element.35), channel_id=1, source_target_pairs={{0,4},{2,6},{8,0},{10,2},{16,8},{18,10},{24,16},{26,18},{28,24},{3... | collective-permute-start | bytes 1474568 | tf_op jit(solution)/shard_map/ppermute | solution.py:201
  13.9 0.5 collective-permute-start.4
  14.4 8.9 %collective-permute-done.5.refs_0_.refs_1_.refs_14_ = bf16[192,1280]{1,0:T(8,128)(2,1)S(1)} collective-permute-done((bf16[192,1280]{1,0:T(8,128)(2,1)S(1)}, bf16[192,1280]{1,0:T(8,128)(2,1)S(1)}, u32[]{:S(2)}, u32[]{:S(2)}) %collective-permute-start.5) | collective-permute-done | bytes 491552 | tf_op jit(solution)/shard_map/ppermute | solution.py:201
  23.3 0.6 collective-permute-start.8
  24.0 1.4 %collective-permute-start.9 = (bf16[192,1280]{1,0:T(8,128)(2,1)S(1)}, bf16[192,1280]{1,0:T(8,128)(2,1)S(1)}, u32[]{:S(2)}, u32[]{:S(2)}) collective-permute-start(bf16[192,1280]{1,0:T(8,128)(2,1)S(1)} %collective-permute-done.6.refs_1_.refs_2_.refs_15_), channel_id=1, source_target_pairs={{0,4},{2,6},{8,0},{10,2},{16,8},{18,10},{24,16},{26,18},{28,24},{3... | collective-permute-start | bytes 1474568 | tf_op jit(solution)/shard_map/ppermute | solution.py:201
  25.4 1.6 %copy-done = bf16[512,2048]{1,0:T(8,128)(2,1)S(1)} copy-done((bf16[512,2048]{1,0:T(8,128)(2,1)S(1)}, bf16[512,2048]{1,0:T(8,128)(2,1)}, u32[]{:S(2)}) %copy-start) | copy-done | bytes 2097176
  27.0 1.2 %turn.1.refs_3_.refs_2_ = bf16[512,2048]{1,0:T(8,128)(2,1)S(1)} custom-call(s32[2]{0:T(128)S(1)} %pad_add_fusion.refs_0_, bf16[512,2048]{1,0:T(8,128)(2,1)S(1)} %copy-done), custom_call_target="tpu_custom_call" | custom-call | bytes 4194304 | tf_op jit(solution)/shard_map/turn/pallas_call | solution.py:521
  28.3 2.4 %low.1.refs_4_.refs_3_ = bf16[512,256]{1,0:T(8,128)(2,1)S(1)} custom-call(s32[2]{0:T(128)S(1)} %pad_add_fusion.refs_0_, s32[4]{0:T(128)S(1)} %copy-done.16, s32[4]{0:T(128)S(1)} %copy-done.18, bf16[512,2048]{1,0:T(8,128)(2,1)S(1)} %copy-done, bf16[2048,128]{1,0:T(8,128)(2,1)S(1)} %copy-done.4, bf16[2048,128]{1,0:T(8,128)(2,1)} %collective-permute-done.refs_5_), custom_call_target="tpu_custom_call" | custom-call | flops 536870912 | bytes 2097152 | tf_op jit(solution)/shard_map/low/pallas_call | solution.py:521
  30.7 0.6 collective-permute-start.12
  31.3 1.6 %collective-permute-start.11 = (bf16[512,128]{1,0:T(8,128)(2,1)S(1)}, bf16[512,128]{1,0:T(8,128)(2,1)S(1)}, u32[]{:S(2)}, u32[]{:S(2)}) collective-permute-start(bf16[512,128]{1,0:T(8,128)(2,1)S(1)} %get-tuple-element.36.refs_0_.refs_2_), channel_id=1, source_target_pairs={{0,4},{2,6},{8,0},{10,2},{16,8},{18,10},{24,16},{26,18},{28,24},{3... | collective-permute-start | bytes 393224 | tf_op jit(solution)/shard_map/ppermute | solution.py:201
  32.9 0.4 collective-permute-start.10
  33.3 2.5 %collective-permute-done.12.refs_5_.refs_2_.refs_4_ = bf16[512,128]{1,0:T(8,128)(2,1)S(1)} collective-permute-done((bf16[512,128]{1,0:T(8,128)(2,1)S(1)}, bf16[512,128]{1,0:T(8,128)(2,1)S(1)}, u32[]{:S(2)}, u32[]{:S(2)}) %collective-permute-start.12) | collective-permute-done | bytes 131104 | tf_op jit(solution)/shard_map/ppermute | solution.py:201
  35.8 1.4 %collective-permute-done.11.refs_4_.refs_6_ = bf16[512,128]{1,0:T(8,128)(2,1)S(1)} collective-permute-done((bf16[512,128]{1,0:T(8,128)(2,1)S(1)}, bf16[512,128]{1,0:T(8,128)(2,1)S(1)}, u32[]{:S(2)}, u32[]{:S(2)}) %collective-permute-start.11) | collective-permute-done | bytes 131104 | tf_op jit(solution)/shard_map/ppermute | solution.py:201
  37.2 1.0 collective-permute-done.10.refs_3_.refs_5_
  38.2 0.1 pack.12
  38.3 0.6 collective-permute-start.14
  39.0 1.4 %collective-permute-start.15 = (bf16[160,1280]{1,0:T(8,128)(2,1)S(1)}, bf16[160,1280]{1,0:T(8,128)(2,1)S(1)}, u32[]{:S(2)}, u32[]{:S(2)}) collective-permute-start(bf16[160,1280]{1,0:T(8,128)(2,1)S(1)} %get-tuple-element.40), channel_id=1, source_target_pairs={{0,4},{2,6},{8,0},{10,2},{16,8},{18,10},{24,16},{26,18},{28,24},{3... | collective-permute-start | bytes 1228808 | tf_op jit(solution)/shard_map/ppermute | solution.py:201
  40.4 1.9 %collective-permute-start.7 = (bf16[128,1280]{1,0:T(8,128)(2,1)S(1)}, bf16[128,1280]{1,0:T(8,128)(2,1)S(1)}, u32[]{:S(2)}, u32[]{:S(2)}) collective-permute-start(bf16[128,1280]{1,0:T(8,128)(2,1)S(1)} %pack.10), channel_id=1, source_target_pairs={{0,2},{2,0},{8,10},{10,8},{16,18},{18,16},{24,26},{26,24},{28,30},... | collective-permute-start | bytes 983048 | tf_op jit(solution)/shard_map/ppermute | solution.py:201
  42.3 0.2 collective-permute-start.13
  42.5 8.6 %collective-permute-done.7.refs_2_.refs_16_ = bf16[128,1280]{1,0:T(8,128)(2,1)S(1)} collective-permute-done((bf16[128,1280]{1,0:T(8,128)(2,1)S(1)}, bf16[128,1280]{1,0:T(8,128)(2,1)S(1)}, u32[]{:S(2)}, u32[]{:S(2)}) %collective-permute-start.7) | collective-permute-done | bytes 327712 | tf_op jit(solution)/shard_map/ppermute | solution.py:201
  51.2 1.5 %collective-permute-start.16 = (bf16[64,1280]{1,0:T(8,128)(2,1)S(1)}, bf16[64,1280]{1,0:T(8,128)(2,1)S(1)}, u32[]{:S(2)}, u32[]{:S(2)}) collective-permute-start(bf16[64,1280]{1,0:T(8,128)(2,1)S(1)} %get-tuple-element.41), channel_id=1, source_target_pairs={{0,2},{2,0},{8,10},{10,8},{16,18},{18,16},{24,26},{26,24},{28,30},... | collective-permute-start | bytes 491528 | tf_op jit(solution)/shard_map/ppermute | solution.py:201
  52.7 0.5 collective-permute-start.17
  53.2 1.6 %collective-permute-start.18 = (bf16[64,1280]{1,0:T(8,128)(2,1)S(1)}, bf16[64,1280]{1,0:T(8,128)(2,1)S(1)}, u32[]{:S(2)}, u32[]{:S(2)}) collective-permute-start(bf16[64,1280]{1,0:T(8,128)(2,1)S(1)} %get-tuple-element.43), channel_id=1, source_target_pairs={{0,4},{2,6},{8,0},{10,2},{16,8},{18,10},{24,16},{26,18},{28,24},{3... | collective-permute-start | bytes 491528 | tf_op jit(solution)/shard_map/ppermute | solution.py:201
  54.7 1.0 pack.14
  55.7 0.5 collective-permute-start.20
  56.2 1.6 %collective-permute-start.21 = (bf16[1536,128]{1,0:T(8,128)(2,1)}, bf16[1536,128]{1,0:T(8,128)(2,1)}, u32[]{:S(2)}, u32[]{:S(2)}) collective-permute-start(bf16[1536,128]{1,0:T(8,128)(2,1)} %get-tuple-element.50), channel_id=1, source_target_pairs={{0,4},{2,6},{8,0},{10,2},{16,8},{18,10},{24,16},{26,18},{28,24},{3... | collective-permute-start | bytes 1179656 | tf_op jit(solution)/shard_map/ppermute | solution.py:201
  57.8 0.2 collective-permute-done.17.refs_23_
  58.0 0.5 collective-permute-done.18.refs_24_
  58.5 6.6 %project.1 = (bf16[512,128]{1,0:T(8,128)(2,1)}, bf16[512,128]{1,0:T(8,128)(2,1)}, bf16[512,1024]{1,0:T(8,128)(2,1)}, bf16[8,160,128]{2,1,0:T(8,128)(2,1)S(1)}) custom-call(s32[2]{0:T(128)S(1)} %pad_add_fusion.refs_0_, s32[4]{0:T(128)S(1)} %copy-done.16, bf16[512,2048]{1,0:T(8,128)(2,1)S(1)} %turn.1.refs_3_.refs_2_, bf16[512,256]{1,0:T(8,128)(2,1)S(1)} %low.1.refs_4_.refs_3_, ...), custom_call_target="tpu_custom_call" | custom-call | flops 671088640 | bytes 1310720 | tf_op jit(solution)/shard_map/project/pallas_call | solution.py:521
  65.1 0.7 copy-done.9
  65.9 5.0 %all-to-all-start = ((bf16[16,80,128]{2,1,0:T(8,128)(2,1)}), bf16[16,80,128]{2,1,0:T(8,128)(2,1)S(1)}, u32[]{:S(2)}, u32[]{:S(2)}) async-start(bf16[16,80,128]{2,1,0:T(8,128)(2,1)} %bitcast.6), calls=%async_computation | async-start | bytes 655360 | tf_op jit(solution)/shard_map/all_to_all | solution.py:598
  70.8 1.9 %collective-permute-start.19 = (bf16[1536,128]{1,0:T(8,128)(2,1)}, bf16[1536,128]{1,0:T(8,128)(2,1)S(1)}, u32[]{:S(2)}, u32[]{:S(2)}) collective-permute-start(bf16[1536,128]{1,0:T(8,128)(2,1)} %copy-done.19), channel_id=1, source_target_pairs={{0,2},{2,0},{8,10},{10,8},{16,18},{18,16},{24,26},{26,24},{28,30},... | collective-permute-start | bytes 1179656 | tf_op jit(solution)/shard_map/ppermute | solution.py:201
  72.8 1.5 %collective-permute-start.23 = (bf16[1536,128]{1,0:T(8,128)(2,1)}, bf16[1536,128]{1,0:T(8,128)(2,1)S(1)}, u32[]{:S(2)}, u32[]{:S(2)}) collective-permute-start(bf16[1536,128]{1,0:T(8,128)(2,1)} %collective-permute-done.20.refs_0_.refs_8_), channel_id=1, source_target_pairs={{0,8},{2,10},{8,16},{10,18},{16,24},{18,26},{24,28},{26,30},{28,20... | collective-permute-start | bytes 1179656 | tf_op jit(solution)/shard_map/ppermute | solution.py:201
  74.2 0.6 collective-permute-start.24
  74.8 4.6 %within.1.refs_2_ = bf16[512,1024]{1,0:T(8,128)(2,1)S(1)} custom-call(s32[2]{0:T(128)S(1)} %pad_add_fusion.refs_0_, s32[4]{0:T(128)S(1)} %copy-done.16, bf16[512,128]{1,0:T(8,128)(2,1)} %get-tuple-element.44.refs_2_.refs_3_, bf16[512,128]{1,0:T(8,128)(2,1)} %get-tuple-element.45.refs_3_, bf16[512,1024]{1,0:T(8,128)(2,1)} %get-tuple-element.46.refs_4_), custom_call_target="tpu_custom_call" | custom-call | flops 3221225472 | bytes 12582912 | tf_op jit(solution)/shard_map/within/pallas_call | solution.py:521
  79.4 0.5 all-to-all-done.refs_1_
  79.9 1.4 %mix.1 = bf16[16,80,128]{2,1,0:T(8,128)(2,1)} custom-call(s32[4]{0:T(128)S(1)} %copy-done.16, bf16[16,80,128]{2,1,0:T(8,128)(2,1)S(1)} %all-to-all-done.refs_1_, bf16[512,1024]{1,0:T(8,128)(2,1)S(1)} %within.1.refs_2_), custom_call_target="tpu_custom_call" | custom-call | bytes 655360 | tf_op jit(solution)/shard_map/mix/pallas_call | solution.py:521
  81.3 5.2 %all-to-all-start.1 = ((bf16[16,80,128]{2,1,0:T(8,128)(2,1)}), bf16[16,80,128]{2,1,0:T(8,128)(2,1)S(1)}, u32[]{:S(2)}, u32[]{:S(2)}) async-start(bf16[16,80,128]{2,1,0:T(8,128)(2,1)} %mix.1), calls=%async_computation.1 | async-start | bytes 655360 | tf_op jit(solution)/shard_map/all_to_all | solution.py:611
  86.6 0.8 pack.16
  87.3 1.9 %collective-permute-start.26 = (bf16[1280,128]{1,0:T(8,128)(2,1)S(1)}, bf16[1280,128]{1,0:T(8,128)(2,1)S(1)}, u32[]{:S(2)}, u32[]{:S(2)}) collective-permute-start(bf16[1280,128]{1,0:T(8,128)(2,1)S(1)} %get-tuple-element.52), channel_id=1, source_target_pairs={{0,8},{2,10},{8,16},{10,18},{16,24},{18,26},{24,28},{26,30},{28,20... | collective-permute-start | bytes 983048 | tf_op jit(solution)/shard_map/ppermute | solution.py:201
  89.3 0.1 collective-permute-start.27
  89.4 1.1 pack.15
  90.5 2.0 %collective-permute-start.22 = (bf16[1024,128]{1,0:T(8,128)(2,1)S(1)}, bf16[1024,128]{1,0:T(8,128)(2,1)S(1)}, u32[]{:S(2)}, u32[]{:S(2)}) collective-permute-start(bf16[1024,128]{1,0:T(8,128)(2,1)S(1)} %pack.15), channel_id=1, source_target_pairs={{0,2},{2,0},{8,10},{10,8},{16,18},{18,16},{24,26},{26,24},{28,30},... | collective-permute-start | bytes 786440 | tf_op jit(solution)/shard_map/ppermute | solution.py:201
  92.5 0.1 collective-permute-start.25
  92.6 5.0 %collective-permute-done.22.refs_2_.refs_10_ = bf16[1024,128]{1,0:T(8,128)(2,1)S(1)} collective-permute-done((bf16[1024,128]{1,0:T(8,128)(2,1)S(1)}, bf16[1024,128]{1,0:T(8,128)(2,1)S(1)}, u32[]{:S(2)}, u32[]{:S(2)}) %collective-permute-start.22) | collective-permute-done | bytes 262176 | tf_op jit(solution)/shard_map/ppermute | solution.py:201
  97.6 0.9 collective-permute-done.27.refs_1_.refs_15_
  98.5 0.8 pack.17
  99.3 1.5 %collective-permute-start.28 = (bf16[512,128]{1,0:T(8,128)(2,1)}, bf16[512,128]{1,0:T(8,128)(2,1)}, u32[]{:S(2)}, u32[]{:S(2)}) collective-permute-start(bf16[512,128]{1,0:T(8,128)(2,1)} %get-tuple-element.54), channel_id=1, source_target_pairs={{0,2},{2,0},{8,10},{10,8},{16,18},{18,16},{24,26},{26,24},{28,30},... | collective-permute-start | bytes 393224 | tf_op jit(solution)/shard_map/ppermute | solution.py:201
  100.8 1.6 %collective-permute-start.29 = (bf16[512,128]{1,0:T(8,128)(2,1)}, bf16[512,128]{1,0:T(8,128)(2,1)}, u32[]{:S(2)}, u32[]{:S(2)}) collective-permute-start(bf16[512,128]{1,0:T(8,128)(2,1)} %get-tuple-element.55), channel_id=1, source_target_pairs={{0,8},{2,10},{8,16},{10,18},{16,24},{18,26},{24,28},{26,30},{28,20... | collective-permute-start | bytes 393224 | tf_op jit(solution)/shard_map/ppermute | solution.py:201
  102.4 0.4 collective-permute-start.30
  102.9 3.8 %finish.1.refs_1_ = bf16[512,1024]{1,0:T(8,128)(2,1)S(1)} custom-call(s32[2]{0:T(128)S(1)} %pad_add_fusion.refs_0_, s32[4]{0:T(128)S(1)} %copy-done.16, bf16[512,1024]{1,0:T(8,128)(2,1)S(1)} %within.1.refs_2_, bf16[512,128]{1,0:T(8,128)(2,1)} %get-tuple-element.44.refs_2_.refs_3_, bf16[8,160,128]{2,1,0:T(8,128)(2,1)S(1)} %bitcast.5, f32[1,1024]{1,0:T(1,128)S(1)} %bitcast.7, ...), custom_call_target="tpu_custom_call" | custom-call | flops 167772160 | bytes 4194304 | tf_op jit(solution)/shard_map/finish/pallas_call | solution.py:521
  106.7 1.0 collective-permute-done.30.refs_18_
  107.7 3.9 %out.1.refs_0_ = bf16[16,512,128]{2,1,0:T(8,128)(2,1)S(1)} custom-call(s32[2]{0:T(128)S(1)} %pad_add_fusion.refs_0_, bf16[512,1024]{1,0:T(8,128)(2,1)S(1)} %finish.1.refs_1_, bf16[512,128]{1,0:T(8,128)(2,1)S(1)} %copy-done.12, bf16[512,128]{1,0:T(8,128)(2,1)S(1)} %copy-done.14, bf16[512,128]{1,0:T(8,128)(2,1)S(1)} %collective-permute-done.12.refs_5_.refs_2_.refs_4_, ...), custom_call_target="tpu_custom_call" | custom-call | flops 2147483648 | bytes 4194304 | tf_op jit(solution)/shard_map/out/pallas_call | solution.py:521
  111.7 2.6 %collective-permute-done.31.refs_1_ = bf16[8,512,128]{2,1,0:T(8,128)(2,1)S(1)} collective-permute-done((bf16[8,512,128]{2,1,0:T(8,128)(2,1)S(1)}, bf16[8,512,128]{2,1,0:T(8,128)(2,1)S(1)}, u32[]{:S(2)}, u32[]{:S(2)}) %collective-permute-start.31) | collective-permute-done | bytes 1048608 | tf_op jit(solution)/shard_map/ppermute | solution.py:624
  114.4 1.3 %add.3 = bf16[512,1024]{1,0:T(8,128)(2,1)} custom-call(bf16[16,512,128]{2,1,0:T(8,128)(2,1)S(1)} %out.1.refs_0_, bf16[8,512,128]{2,1,0:T(8,128)(2,1)S(1)} %collective-permute-done.31.refs_1_), custom_call_target="tpu_custom_call" | custom-call | bytes 4194304 | tf_op jit(solution)/shard_map/add/pallas_call | solution.py:521
  (64 shorter events, 0.4 us)
Async XLA Ops:
  1.1 7.2 %collective-permute-start.1 = (bf16[64,1280]{1,0:T(8,128)(2,1)S(1)}, bf16[64,1280]{1,0:T(8,128)(2,1)S(1)}, u32[]{:S(2)}, u32[]{:S(2)}) collective-permute-start(bf16[64,1280]{1,0:T(8,128)(2,1)S(1)} %get-tuple-element.32.refs_1_.refs_9_), channel_id=1, source_target_pairs={{0,2},{2,0},{8,10},{10,8},{16,18},{18,16},{24,26},{26,24},{28,30},... | collective-permute-start | bytes 491528 | tf_op jit(solution)/shard_map/ppermute | solution.py:201
  4.1 5.7 %collective-permute-start.3 = (bf16[64,1280]{1,0:T(8,128)(2,1)S(1)}, bf16[64,1280]{1,0:T(8,128)(2,1)S(1)}, u32[]{:S(2)}, u32[]{:S(2)}) collective-permute-start(bf16[64,1280]{1,0:T(8,128)(2,1)S(1)} %get-tuple-element.31.refs_0_.refs_8_), channel_id=1, source_target_pairs={{0,4},{2,6},{8,0},{10,2},{16,8},{18,10},{24,16},{26,18},{28,24},{3... | collective-permute-start | bytes 491528 | tf_op jit(solution)/shard_map/ppermute | solution.py:201
  5.6 5.4 %collective-permute-start.2 = (bf16[64,1280]{1,0:T(8,128)(2,1)S(1)}, bf16[64,1280]{1,0:T(8,128)(2,1)S(1)}, u32[]{:S(2)}, u32[]{:S(2)}) collective-permute-start(bf16[64,1280]{1,0:T(8,128)(2,1)S(1)} %get-tuple-element.31.refs_0_.refs_8_), channel_id=1, source_target_pairs={{0,8},{2,10},{8,16},{10,18},{16,24},{18,26},{24,28},{26,30},{28,20... | collective-permute-start | bytes 491528 | tf_op jit(solution)/shard_map/ppermute | solution.py:201
  11.8 11.5 %collective-permute-start.5 = (bf16[192,1280]{1,0:T(8,128)(2,1)S(1)}, bf16[192,1280]{1,0:T(8,128)(2,1)S(1)}, u32[]{:S(2)}, u32[]{:S(2)}) collective-permute-start(bf16[192,1280]{1,0:T(8,128)(2,1)S(1)} %get-tuple-element.34), channel_id=1, source_target_pairs={{0,8},{2,10},{8,16},{10,18},{16,24},{18,26},{24,28},{26,30},{28,20... | collective-permute-start | bytes 1474568 | tf_op jit(solution)/shard_map/ppermute | solution.py:201
  12.3 11.6 %collective-permute-start.6 = (bf16[192,1280]{1,0:T(8,128)(2,1)S(1)}, bf16[192,1280]{1,0:T(8,128)(2,1)S(1)}, u32[]{:S(2)}, u32[]{:S(2)}) collective-permute-start(bf16[192,1280]{1,0:T(8,128)(2,1)S(1)} %get-tuple-element.35), channel_id=1, source_target_pairs={{0,4},{2,6},{8,0},{10,2},{16,8},{18,10},{24,16},{26,18},{28,24},{3... | collective-permute-start | bytes 1474568 | tf_op jit(solution)/shard_map/ppermute | solution.py:201
  13.9 14.4 %collective-permute-start = (bf16[2048,128]{1,0:T(8,128)(2,1)}, bf16[2048,128]{1,0:T(8,128)(2,1)}, u32[]{:S(2)}, u32[]{:S(2)}) collective-permute-start(bf16[2048,128]{1,0:T(8,128)(2,1)} %refs_4_.2), channel_id=1, source_target_pairs={{0,1},{1,0},{2,3},{3,2},{4,5},{5,4},{6,7},{7,6},{8,9},{9,8},{10,11... | collective-permute-start | bytes 1572872 | tf_op jit(solution)/shard_map/ppermute | solution.py:559
  13.9 19.1 %collective-permute-start.4 = (bf16[192,1280]{1,0:T(8,128)(2,1)}, bf16[192,1280]{1,0:T(8,128)(2,1)S(1)}, u32[]{:S(2)}, u32[]{:S(2)}) collective-permute-start(bf16[192,1280]{1,0:T(8,128)(2,1)} %get-tuple-element.33), channel_id=1, source_target_pairs={{0,2},{2,0},{8,10},{10,8},{16,18},{18,16},{24,26},{26,24},{28,30},... | collective-permute-start | bytes 1474568 | tf_op jit(solution)/shard_map/ppermute | solution.py:201
  23.3 14.8 %collective-permute-start.8 = (bf16[192,1280]{1,0:T(8,128)(2,1)S(1)}, bf16[192,1280]{1,0:T(8,128)(2,1)S(1)}, u32[]{:S(2)}, u32[]{:S(2)}) collective-permute-start(bf16[192,1280]{1,0:T(8,128)(2,1)S(1)} %collective-permute-done.5.refs_0_.refs_1_.refs_14_), channel_id=1, source_target_pairs={{0,8},{2,10},{8,16},{10,18},{16,24},{18,26},{24,28},{26,30},{28,20... | collective-permute-start | bytes 1474568 | tf_op jit(solution)/shard_map/ppermute | solution.py:201
  24.0 14.2 %collective-permute-start.9 = (bf16[192,1280]{1,0:T(8,128)(2,1)S(1)}, bf16[192,1280]{1,0:T(8,128)(2,1)S(1)}, u32[]{:S(2)}, u32[]{:S(2)}) collective-permute-start(bf16[192,1280]{1,0:T(8,128)(2,1)S(1)} %collective-permute-done.6.refs_1_.refs_2_.refs_15_), channel_id=1, source_target_pairs={{0,4},{2,6},{8,0},{10,2},{16,8},{18,10},{24,16},{26,18},{28,24},{3... | collective-permute-start | bytes 1474568 | tf_op jit(solution)/shard_map/ppermute | solution.py:201
  25.4 1.6 %copy-start = (bf16[512,2048]{1,0:T(8,128)(2,1)S(1)}, bf16[512,2048]{1,0:T(8,128)(2,1)}, u32[]{:S(2)}) copy-start(bf16[512,2048]{1,0:T(8,128)(2,1)} %refs_3_.1) | copy-start | bytes 6291460
  27.0 1.2 %copy-start.4 = (bf16[2048,128]{1,0:T(8,128)(2,1)S(1)}, bf16[2048,128]{1,0:T(8,128)(2,1)}, u32[]{:S(2)}) copy-start(bf16[2048,128]{1,0:T(8,128)(2,1)} %refs_4_.2) | copy-start | bytes 1572868
  27.0 1.3 %copy-start.16 = (s32[4]{0:T(128)S(1)}, s32[4]{0:T(128)}, u32[]{:S(2)}) copy-start(s32[4]{0:T(128)} %refs_1_.9) | copy-start | bytes 52
  27.0 1.3 %copy-start.18 = (s32[4]{0:T(128)S(1)}, s32[4]{0:T(128)}, u32[]{:S(2)}) copy-start(s32[4]{0:T(128)} %refs_2_.1) | copy-start | bytes 52
  28.2 2.4 %copy-start.10 = (bf16[1024,128]{1,0:T(8,128)(2,1)S(1)}, bf16[1024,128]{1,0:T(8,128)(2,1)}, u32[]{:S(2)}) copy-start(bf16[1024,128]{1,0:T(8,128)(2,1)} %refs_0_.2) | copy-start | bytes 786436
  30.7 24.0 %copy-start.11 = (bf16[512,128]{1,0:T(8,128)(2,1)}, bf16[512,128]{1,0:T(8,128)(2,1)S(1)}, u32[]{:S(2)}) copy-start(bf16[512,128]{1,0:T(8,128)(2,1)S(1)} %get-tuple-element.36.refs_0_.refs_2_) | copy-start | bytes 393220
  30.7 24.0 %copy-start.13 = (bf16[512,128]{1,0:T(8,128)(2,1)}, bf16[512,128]{1,0:T(8,128)(2,1)S(1)}, u32[]{:S(2)}) copy-start(bf16[512,128]{1,0:T(8,128)(2,1)S(1)} %get-tuple-element.37.refs_1_.refs_3_) | copy-start | bytes 393220
  30.7 5.0 %collective-permute-start.12 = (bf16[512,128]{1,0:T(8,128)(2,1)S(1)}, bf16[512,128]{1,0:T(8,128)(2,1)S(1)}, u32[]{:S(2)}, u32[]{:S(2)}) collective-permute-start(bf16[512,128]{1,0:T(8,128)(2,1)S(1)} %get-tuple-element.37.refs_1_.refs_3_), channel_id=1, source_target_pairs={{0,2},{2,0},{8,10},{10,8},{16,18},{18,16},{24,26},{26,24},{28,30},... | collective-permute-start | bytes 393224 | tf_op jit(solution)/shard_map/ppermute | solution.py:201
  31.3 5.9 %collective-permute-start.11 = (bf16[512,128]{1,0:T(8,128)(2,1)S(1)}, bf16[512,128]{1,0:T(8,128)(2,1)S(1)}, u32[]{:S(2)}, u32[]{:S(2)}) collective-permute-start(bf16[512,128]{1,0:T(8,128)(2,1)S(1)} %get-tuple-element.36.refs_0_.refs_2_), channel_id=1, source_target_pairs={{0,4},{2,6},{8,0},{10,2},{16,8},{18,10},{24,16},{26,18},{28,24},{3... | collective-permute-start | bytes 393224 | tf_op jit(solution)/shard_map/ppermute | solution.py:201
  32.9 5.2 %collective-permute-start.10 = (bf16[512,128]{1,0:T(8,128)(2,1)S(1)}, bf16[512,128]{1,0:T(8,128)(2,1)S(1)}, u32[]{:S(2)}, u32[]{:S(2)}) collective-permute-start(bf16[512,128]{1,0:T(8,128)(2,1)S(1)} %get-tuple-element.36.refs_0_.refs_2_), channel_id=1, source_target_pairs={{0,8},{2,10},{8,16},{10,18},{16,24},{18,26},{24,28},{26,30},{28,20... | collective-permute-start | bytes 393224 | tf_op jit(solution)/shard_map/ppermute | solution.py:201
  38.2 16.6 %copy-start.1 = (bf16[512,128]{1,0:T(8,128)(2,1)}, bf16[512,128]{1,0:T(8,128)(2,1)S(1)}, u32[]{:S(2)}) copy-start(bf16[512,128]{1,0:T(8,128)(2,1)S(1)} %collective-permute-done.10.refs_3_.refs_5_) | copy-start | bytes 393220
  38.3 20.2 %copy-start.3 = (bf16[256,1024]{1,0:T(8,128)(2,1)S(1)}, bf16[256,1024]{1,0:T(8,128)(2,1)}, u32[]{:S(2)}) copy-start(bf16[256,1024]{1,0:T(8,128)(2,1)} %refs_4_.3) | copy-start | bytes 1572868
  38.3 20.2 %copy-start.5 = (f32[160,128]{1,0:T(8,128)S(1)}, f32[160,128]{1,0:T(8,128)}, u32[]{:S(2)}) copy-start(f32[160,128]{1,0:T(8,128)} %constant.15.clone.refs_6_.refs_7_) | copy-start | bytes 245764
  38.3 20.2 %copy-start.6 = (f32[160,128]{1,0:T(8,128)S(1)}, f32[160,128]{1,0:T(8,128)}, u32[]{:S(2)}) copy-start(f32[160,128]{1,0:T(8,128)} %constant.14.clone.refs_5_.refs_6_) | copy-start | bytes 245764
  38.3 20.2 %copy-start.15 = (f32[160,8]{1,0:T(8,128)S(1)}, f32[160,8]{1,0:T(8,128)}, u32[]{:S(2)}) copy-start(f32[160,8]{1,0:T(8,128)} %constant.17.refs_7_) | copy-start | bytes 15364
  38.3 12.8 %collective-permute-start.14 = (bf16[160,1280]{1,0:T(8,128)(2,1)S(1)}, bf16[160,1280]{1,0:T(8,128)(2,1)S(1)}, u32[]{:S(2)}, u32[]{:S(2)}) collective-permute-start(bf16[160,1280]{1,0:T(8,128)(2,1)S(1)} %get-tuple-element.39), channel_id=1, source_target_pairs={{0,8},{2,10},{8,16},{10,18},{16,24},{18,26},{24,28},{26,30},{28,20... | collective-permute-start | bytes 1228808 | tf_op jit(solution)/shard_map/ppermute | solution.py:201
  39.0 12.2 %collective-permute-start.15 = (bf16[160,1280]{1,0:T(8,128)(2,1)S(1)}, bf16[160,1280]{1,0:T(8,128)(2,1)S(1)}, u32[]{:S(2)}, u32[]{:S(2)}) collective-permute-start(bf16[160,1280]{1,0:T(8,128)(2,1)S(1)} %get-tuple-element.40), channel_id=1, source_target_pairs={{0,4},{2,6},{8,0},{10,2},{16,8},{18,10},{24,16},{26,18},{28,24},{3... | collective-permute-start | bytes 1228808 | tf_op jit(solution)/shard_map/ppermute | solution.py:201
  40.4 10.7 %collective-permute-start.7 = (bf16[128,1280]{1,0:T(8,128)(2,1)S(1)}, bf16[128,1280]{1,0:T(8,128)(2,1)S(1)}, u32[]{:S(2)}, u32[]{:S(2)}) collective-permute-start(bf16[128,1280]{1,0:T(8,128)(2,1)S(1)} %pack.10), channel_id=1, source_target_pairs={{0,2},{2,0},{8,10},{10,8},{16,18},{18,16},{24,26},{26,24},{28,30},... | collective-permute-start | bytes 983048 | tf_op jit(solution)/shard_map/ppermute | solution.py:201
  42.3 13.9 %collective-permute-start.13 = (bf16[128,1280]{1,0:T(8,128)(2,1)S(1)}, bf16[128,1280]{1,0:T(8,128)(2,1)S(1)}, u32[]{:S(2)}, u32[]{:S(2)}) collective-permute-start(bf16[128,1280]{1,0:T(8,128)(2,1)S(1)} %get-tuple-element.38), channel_id=1, source_target_pairs={{0,2},{2,0},{8,10},{10,8},{16,18},{18,16},{24,26},{26,24},{28,30},... | collective-permute-start | bytes 983048 | tf_op jit(solution)/shard_map/ppermute | solution.py:201
  51.2 6.6 %collective-permute-start.16 = (bf16[64,1280]{1,0:T(8,128)(2,1)S(1)}, bf16[64,1280]{1,0:T(8,128)(2,1)S(1)}, u32[]{:S(2)}, u32[]{:S(2)}) collective-permute-start(bf16[64,1280]{1,0:T(8,128)(2,1)S(1)} %get-tuple-element.41), channel_id=1, source_target_pairs={{0,2},{2,0},{8,10},{10,8},{16,18},{18,16},{24,26},{26,24},{28,30},... | collective-permute-start | bytes 491528 | tf_op jit(solution)/shard_map/ppermute | solution.py:201
  52.7 5.3 %collective-permute-start.17 = (bf16[64,1280]{1,0:T(8,128)(2,1)S(1)}, bf16[64,1280]{1,0:T(8,128)(2,1)S(1)}, u32[]{:S(2)}, u32[]{:S(2)}) collective-permute-start(bf16[64,1280]{1,0:T(8,128)(2,1)S(1)} %get-tuple-element.42), channel_id=1, source_target_pairs={{0,8},{2,10},{8,16},{10,18},{16,24},{18,26},{24,28},{26,30},{28,20... | collective-permute-start | bytes 491528 | tf_op jit(solution)/shard_map/ppermute | solution.py:201
  53.2 5.3 %collective-permute-start.18 = (bf16[64,1280]{1,0:T(8,128)(2,1)S(1)}, bf16[64,1280]{1,0:T(8,128)(2,1)S(1)}, u32[]{:S(2)}, u32[]{:S(2)}) collective-permute-start(bf16[64,1280]{1,0:T(8,128)(2,1)S(1)} %get-tuple-element.43), channel_id=1, source_target_pairs={{0,4},{2,6},{8,0},{10,2},{16,8},{18,10},{24,16},{26,18},{28,24},{3... | collective-permute-start | bytes 491528 | tf_op jit(solution)/shard_map/ppermute | solution.py:201
  55.7 2.3 %copy-start.19 = (bf16[1536,128]{1,0:T(8,128)(2,1)}, bf16[1536,128]{1,0:T(8,128)(2,1)S(1)}, u32[]{:S(2)}) copy-start(bf16[1536,128]{1,0:T(8,128)(2,1)S(1)} %get-tuple-element.48) | copy-start | bytes 1179652
  55.7 17.0 %collective-permute-start.20 = (bf16[1536,128]{1,0:T(8,128)(2,1)}, bf16[1536,128]{1,0:T(8,128)(2,1)}, u32[]{:S(2)}, u32[]{:S(2)}) collective-permute-start(bf16[1536,128]{1,0:T(8,128)(2,1)} %get-tuple-element.49), channel_id=1, source_target_pairs={{0,8},{2,10},{8,16},{10,18},{16,24},{18,26},{24,28},{26,30},{28,20... | collective-permute-start | bytes 1179656 | tf_op jit(solution)/shard_map/ppermute | solution.py:201
  56.2 18.0 %collective-permute-start.21 = (bf16[1536,128]{1,0:T(8,128)(2,1)}, bf16[1536,128]{1,0:T(8,128)(2,1)}, u32[]{:S(2)}, u32[]{:S(2)}) collective-permute-start(bf16[1536,128]{1,0:T(8,128)(2,1)} %get-tuple-element.50), channel_id=1, source_target_pairs={{0,4},{2,6},{8,0},{10,2},{16,8},{18,10},{24,16},{26,18},{28,24},{3... | collective-permute-start | bytes 1179656 | tf_op jit(solution)/shard_map/ppermute | solution.py:201
  65.1 0.8 copy-start.9
  65.9 14.0 %all-to-all-start = ((bf16[16,80,128]{2,1,0:T(8,128)(2,1)}), bf16[16,80,128]{2,1,0:T(8,128)(2,1)S(1)}, u32[]{:S(2)}, u32[]{:S(2)}) async-start(bf16[16,80,128]{2,1,0:T(8,128)(2,1)} %bitcast.6), calls=%async_computation | async-start | bytes 655360 | tf_op jit(solution)/shard_map/all_to_all | solution.py:598
  70.8 15.7 %collective-permute-start.19 = (bf16[1536,128]{1,0:T(8,128)(2,1)}, bf16[1536,128]{1,0:T(8,128)(2,1)S(1)}, u32[]{:S(2)}, u32[]{:S(2)}) collective-permute-start(bf16[1536,128]{1,0:T(8,128)(2,1)} %copy-done.19), channel_id=1, source_target_pairs={{0,2},{2,0},{8,10},{10,8},{16,18},{18,16},{24,26},{26,24},{28,30},... | collective-permute-start | bytes 1179656 | tf_op jit(solution)/shard_map/ppermute | solution.py:201
  72.8 13.8 %collective-permute-start.23 = (bf16[1536,128]{1,0:T(8,128)(2,1)}, bf16[1536,128]{1,0:T(8,128)(2,1)S(1)}, u32[]{:S(2)}, u32[]{:S(2)}) collective-permute-start(bf16[1536,128]{1,0:T(8,128)(2,1)} %collective-permute-done.20.refs_0_.refs_8_), channel_id=1, source_target_pairs={{0,8},{2,10},{8,16},{10,18},{16,24},{18,26},{24,28},{26,30},{28,20... | collective-permute-start | bytes 1179656 | tf_op jit(solution)/shard_map/ppermute | solution.py:201
  74.2 12.3 %collective-permute-start.24 = (bf16[1536,128]{1,0:T(8,128)(2,1)}, bf16[1536,128]{1,0:T(8,128)(2,1)S(1)}, u32[]{:S(2)}, u32[]{:S(2)}) collective-permute-start(bf16[1536,128]{1,0:T(8,128)(2,1)} %collective-permute-done.21.refs_1_.refs_9_), channel_id=1, source_target_pairs={{0,4},{2,6},{8,0},{10,2},{16,8},{18,10},{24,16},{26,18},{28,24},{3... | collective-permute-start | bytes 1179656 | tf_op jit(solution)/shard_map/ppermute | solution.py:201
  81.3 21.6 %copy-start.17 = (f32[1024]{0:T(1024)S(1)}, f32[1024]{0:T(1024)}, u32[]{:S(2)}) copy-start(f32[1024]{0:T(1024)} %param.21) | copy-start | bytes 12292
  81.3 21.5 %all-to-all-start.1 = ((bf16[16,80,128]{2,1,0:T(8,128)(2,1)}), bf16[16,80,128]{2,1,0:T(8,128)(2,1)S(1)}, u32[]{:S(2)}, u32[]{:S(2)}) async-start(bf16[16,80,128]{2,1,0:T(8,128)(2,1)} %mix.1), calls=%async_computation.1 | async-start | bytes 655360 | tf_op jit(solution)/shard_map/all_to_all | solution.py:611
  87.3 10.2 %collective-permute-start.26 = (bf16[1280,128]{1,0:T(8,128)(2,1)S(1)}, bf16[1280,128]{1,0:T(8,128)(2,1)S(1)}, u32[]{:S(2)}, u32[]{:S(2)}) collective-permute-start(bf16[1280,128]{1,0:T(8,128)(2,1)S(1)} %get-tuple-element.52), channel_id=1, source_target_pairs={{0,8},{2,10},{8,16},{10,18},{16,24},{18,26},{24,28},{26,30},{28,20... | collective-permute-start | bytes 983048 | tf_op jit(solution)/shard_map/ppermute | solution.py:201
  89.3 18.4 %copy-start.2 = (bf16[512,128]{1,0:T(8,128)(2,1)S(1)}, bf16[512,128]{1,0:T(8,128)(2,1)}, u32[]{:S(2)}) copy-start(bf16[512,128]{1,0:T(8,128)(2,1)} %copy-done.1) | copy-start | bytes 393220
  89.3 9.2 %collective-permute-start.27 = (bf16[1280,128]{1,0:T(8,128)(2,1)S(1)}, bf16[1280,128]{1,0:T(8,128)(2,1)S(1)}, u32[]{:S(2)}, u32[]{:S(2)}) collective-permute-start(bf16[1280,128]{1,0:T(8,128)(2,1)S(1)} %get-tuple-element.53), channel_id=1, source_target_pairs={{0,4},{2,6},{8,0},{10,2},{16,8},{18,10},{24,16},{26,18},{28,24},{3... | collective-permute-start | bytes 983048 | tf_op jit(solution)/shard_map/ppermute | solution.py:201
  90.5 7.1 %collective-permute-start.22 = (bf16[1024,128]{1,0:T(8,128)(2,1)S(1)}, bf16[1024,128]{1,0:T(8,128)(2,1)S(1)}, u32[]{:S(2)}, u32[]{:S(2)}) collective-permute-start(bf16[1024,128]{1,0:T(8,128)(2,1)S(1)} %pack.15), channel_id=1, source_target_pairs={{0,2},{2,0},{8,10},{10,8},{16,18},{18,16},{24,26},{26,24},{28,30},... | collective-permute-start | bytes 786440 | tf_op jit(solution)/shard_map/ppermute | solution.py:201
  92.5 14.1 %collective-permute-start.25 = (bf16[1024,128]{1,0:T(8,128)(2,1)}, bf16[1024,128]{1,0:T(8,128)(2,1)}, u32[]{:S(2)}, u32[]{:S(2)}) collective-permute-start(bf16[1024,128]{1,0:T(8,128)(2,1)} %get-tuple-element.51), channel_id=1, source_target_pairs={{0,2},{2,0},{8,10},{10,8},{16,18},{18,16},{24,26},{26,24},{28,30},... | collective-permute-start | bytes 786440 | tf_op jit(solution)/shard_map/ppermute | solution.py:201
  98.5 3.9 %copy-start.7 = (bf16[1280,128]{1,0:T(8,128)(2,1)}, bf16[1280,128]{1,0:T(8,128)(2,1)S(1)}, u32[]{:S(2)}) copy-start(bf16[1280,128]{1,0:T(8,128)(2,1)S(1)} %collective-permute-done.27.refs_1_.refs_15_) | copy-start | bytes 983044
  99.3 7.3 %collective-permute-start.28 = (bf16[512,128]{1,0:T(8,128)(2,1)}, bf16[512,128]{1,0:T(8,128)(2,1)}, u32[]{:S(2)}, u32[]{:S(2)}) collective-permute-start(bf16[512,128]{1,0:T(8,128)(2,1)} %get-tuple-element.54), channel_id=1, source_target_pairs={{0,2},{2,0},{8,10},{10,8},{16,18},{18,16},{24,26},{26,24},{28,30},... | collective-permute-start | bytes 393224 | tf_op jit(solution)/shard_map/ppermute | solution.py:201
  100.8 5.9 %collective-permute-start.29 = (bf16[512,128]{1,0:T(8,128)(2,1)}, bf16[512,128]{1,0:T(8,128)(2,1)}, u32[]{:S(2)}, u32[]{:S(2)}) collective-permute-start(bf16[512,128]{1,0:T(8,128)(2,1)} %get-tuple-element.55), channel_id=1, source_target_pairs={{0,8},{2,10},{8,16},{10,18},{16,24},{18,26},{24,28},{26,30},{28,20... | collective-permute-start | bytes 393224 | tf_op jit(solution)/shard_map/ppermute | solution.py:201
  102.4 5.3 %collective-permute-start.30 = (bf16[512,128]{1,0:T(8,128)(2,1)}, bf16[512,128]{1,0:T(8,128)(2,1)}, u32[]{:S(2)}, u32[]{:S(2)}) collective-permute-start(bf16[512,128]{1,0:T(8,128)(2,1)} %get-tuple-element.56), channel_id=1, source_target_pairs={{0,4},{2,6},{8,0},{10,2},{16,8},{18,10},{24,16},{26,18},{28,24},{3... | collective-permute-start | bytes 393224 | tf_op jit(solution)/shard_map/ppermute | solution.py:201
  102.8 4.9 %copy-start.8 = (bf16[1280,128]{1,0:T(8,128)(2,1)S(1)}, bf16[1280,128]{1,0:T(8,128)(2,1)}, u32[]{:S(2)}) copy-start(bf16[1280,128]{1,0:T(8,128)(2,1)} %copy-done.7) | copy-start | bytes 983044
  102.8 4.9 %copy-start.12 = (bf16[512,128]{1,0:T(8,128)(2,1)S(1)}, bf16[512,128]{1,0:T(8,128)(2,1)}, u32[]{:S(2)}) copy-start(bf16[512,128]{1,0:T(8,128)(2,1)} %copy-done.11) | copy-start | bytes 393220
  102.8 4.9 %copy-start.14 = (bf16[512,128]{1,0:T(8,128)(2,1)S(1)}, bf16[512,128]{1,0:T(8,128)(2,1)}, u32[]{:S(2)}) copy-start(bf16[512,128]{1,0:T(8,128)(2,1)} %copy-done.13) | copy-start | bytes 393220
  111.7 2.7 %collective-permute-start.31 = (bf16[8,512,128]{2,1,0:T(8,128)(2,1)S(1)}, bf16[8,512,128]{2,1,0:T(8,128)(2,1)S(1)}, u32[]{:S(2)}, u32[]{:S(2)}) collective-permute-start(bf16[8,512,128]{2,1,0:T(8,128)(2,1)S(1)} %slice.4), channel_id=1, source_target_pairs={{0,1},{1,0},{2,3},{3,2},{4,5},{5,4},{6,7},{7,6},{8,9},{9,8},{10,11... | collective-permute-start | bytes 3145736 | tf_op jit(solution)/shard_map/ppermute | solution.py:624

commit v6 on v5

--- a/solution.py
+++ b/solution.py
@@ -454,23 +454,43 @@
         normed[:, cols] = (combined * factor * gains[:, cols]).astype(jnp.bfloat16)
 
 
+def out_block(layout, tile, blocks, info, normed, pieces, near):
+    depth = normed.shape[1]
+    step = depth // 4
+    pair = (near, near + blocks // 2)
+    total = None
+    for row in range(0, depth, step):
+        both = jnp.concatenate(
+            [piece_rows(pieces, layout, slot, row, step) for slot in pair], axis=1
+        )
+        term = jnp.dot(normed[:, row : row + step], both, preferred_element_type=jnp.float32)
+        total = term if total is None else total + term
+    found = []
+    for k, slot in enumerate(pair):
+        place = place_of(info[0], slot)
+        at = jnp.where(place // (blocks // 2) == info[1], 0, blocks // 2) + place % (blocks // 2)
+        found.append((at, total[:, k * tile : (k + 1) * tile].astype(jnp.bfloat16)))
+    return found
+
+
 def out_kernel(layout, tile, blocks, info, normed, *refs):
     pieces, (out,) = refs[: len(layout)], refs[len(layout) :]
-    depth = normed.shape[1]
-    step = depth // 4
     for near in range(blocks // 2):
-        pair = (near, near + blocks // 2)
-        total = None
-        for row in range(0, depth, step):
-            both = jnp.concatenate(
-                [piece_rows(pieces, layout, slot, row, step) for slot in pair], axis=1
-            )
-            term = jnp.dot(normed[:, row : row + step], both, preferred_element_type=jnp.float32)
-            total = term if total is None else total + term
-        for k, slot in enumerate(pair):
-            place = place_of(info[0], slot)
-            at = jnp.where(place // (blocks // 2) == info[1], 0, blocks // 2) + place % (blocks // 2)
-            out[at] = total[:, k * tile : (k + 1) * tile].astype(jnp.bfloat16)
+        if near != blocks // 4:
+            for at, part in out_block(layout, tile, blocks, info, normed, pieces, near):
+                out[at] = part
+
+
+def last_kernel(layout, tile, blocks, info, normed, *refs):
+    pieces, (_, out, held, done) = refs[: len(layout)], refs[len(layout) :]
+    copies = []
+    for at, part in out_block(layout, tile, blocks, info, normed, pieces, blocks // 4):
+        k = len(copies)
+        held[k] = part
+        copies.append(pltpu.make_async_copy(held.at[k], out.at[at], done.at[k]))
+        copies[-1].start()
+    for copy in copies:
+        copy.wait()
 
 
 def add_kernel(partial, received, out):
@@ -602,8 +622,6 @@
         [info, lengths], [query, keys, values], far=(0, 1, 2),
     )
     out_fourth = out_chain.send(())
-    out_chain.send(())
-    out_gathered = next(out_chain)
     (mixed,) = call(
         functools.partial(mix_kernel, blocks, count), "mix", 4, (0, 4 * parts.size),
         [(parts.shape, half)], [lengths], [parts], (within,),
@@ -615,12 +633,29 @@
         [info, lengths],
         [within, query, carried, head_gain.reshape(1, -1), first, second, scale], far=(1, 4, 5, 6),
     )
-    pieces, layout = [piece for piece, _ in out_gathered], [places for _, places in out_gathered]
+    out_chain.send((normed,))
+    out_gathered = next(out_chain)
+    far_slots = (blocks // 4, 3 * blocks // 4)
+    early = [(p, l) for p, l in out_gathered if not all(place[0] in far_slots for place in l)]
+    last = [(p, l) for p, l in out_gathered if any(place[0] in far_slots for place in l)]
     (partial,) = call(
-        functools.partial(out_kernel, layout, tile, blocks), "out", 12,
+        functools.partial(out_kernel, [l for _, l in early], tile, blocks), "out", 12,
         (2 * count * wide * blocks * tile, 4 * count * blocks * tile),
-        [((blocks, count, tile), half)], [info], [normed, *pieces],
-    )
+        [((blocks, count, tile), half)], [info], [normed] + [p for p, _ in early],
+    )
+    partial = pl.pallas_call(
+        functools.partial(last_kernel, [l for _, l in last], tile, blocks),
+        out_shape=jax.ShapeDtypeStruct(partial.shape, partial.dtype),
+        in_specs=[SMEM] + [VMEM] * (1 + len(last)) + [ANY],
+        out_specs=ANY,
+        scratch_shapes=[
+            pltpu.VMEM((2, count, tile), half),
+            pltpu.SemaphoreType.DMA((2,)),
+        ],
+        input_output_aliases={2 + len(last): 0},
+        compiler_params=params(8),
+        name="last",
+    )(info, normed, *[p for p, _ in last], partial)
     received = lax.ppermute(partial[blocks // 2 :], "mp", [(0, 1), (1, 0)])
     (result,) = call(
         add_kernel, "add", 8, (0, 8 * count * wide), [((count, blocks // 2 * tile), half)], [],

time: 116 us -> 113 us (0.974)
  waiting for transfers between devices: 38 us -> 32.6 us
  Pallas kernels: 31 us -> 32.2 us
    ppermute x30, waiting for transfers between devices: 34.9 us -> 27.3 us  [send(): return lax.ppermute(value, 'dp', pairs)]
    all_to_all x1, waiting for transfers between devices: 0.01 us -> 2.22 us  [per_device_fast(): lax.all_to_all(mixed, 'dp', 0, 0, tiled=True).reshape(heads, FEATS, width)]
    pallas_call x0 -> x1, Pallas kernels: none -> 1.35 us  [per_device_fast(): pl.pallas_call(functools.partial(last_kernel, [l for _, l in last], tile,...]
    unnamed x40 -> x36, local copies, waits for them, and re-layouts: 2.42 us -> 3.14 us
  transfers between devices with their start and end apart: 34 -> 34, of which waited for: 15 -> 11; matrix products, arithmetic and copies ran while one was open for 0% -> 0% of each run, Pallas kernels for 21% -> 25%
where the time goes in v6:
time: 113 us; the launch traced here: 112 us
  starting transfers between devices  43.6 us (39%)
  waiting for transfers between devices  32.6 us (29%)
  Pallas kernels  32.2 us (28%)
  local copies, waits for them, and re-layouts  3.21 us (3%)
    ppermute x30, starting transfers between devices, send(): return lax.ppermute(value, 'dp', pairs)  33.6 us
    ppermute x30, waiting for transfers between devices, send(): return lax.ppermute(value, 'dp', pairs)  27.3 us
    pallas_call x8, Pallas kernels, call(): pl.pallas_call(body, out_shape=shapes, in_specs=[SMEM] * n + [HBM if i in...  24.9 us
    all_to_all x1, starting transfers between devices, per_device_fast(): lax.all_to_all(mixed, 'dp', 0, 0, tiled=True).reshape(heads, FEATS, width)  5.11 us
    pallas_call x9, Pallas kernels, pack(): pl.pallas_call(functools.partial(pack_kernel, recipes, len(sources)), out...  4.92 us
    all_to_all x1, starting transfers between devices, per_device_fast(): parts = lax.all_to_all(parts, 'dp', 0, 0, tiled=True)  4.89 us
    unnamed x36, local copies, waits for them, and re-layouts  3.14 us
    ppermute x1, waiting for transfers between devices, per_device_fast(): received = lax.ppermute(partial[blocks // 2:], 'mp', [(0, 1), (1, 0)])  2.65 us
  transfers between devices with their start and end apart: 34, of which 11 were waited for; matrix products, arithmetic and copies ran while one was open for 0% of the time, Pallas kernels for 25%

profile of v6, /device:TPU:0, one launch (start us, length us, event | category | flops | bytes accessed | tf_op | source)
XLA Modules:
  0.0 112.2 jit_solution(17335279804313827609)
XLA Ops:
  0.0 1.1 join.1
  1.1 3.0 %collective-permute-start.1 = (bf16[64,1280]{1,0:T(8,128)(2,1)S(1)}, bf16[64,1280]{1,0:T(8,128)(2,1)S(1)}, u32[]{:S(2)}, u32[]{:S(2)}) collective-permute-start(bf16[64,1280]{1,0:T(8,128)(2,1)S(1)} %get-tuple-element.32.refs_1_.refs_9_), channel_id=1, source_target_pairs={{0,2},{2,0},{8,10},{10,8},{16,18},{18,16},{24,26},{26,24},{28,30},... | collective-permute-start | bytes 491528 | tf_op jit(solution)/shard_map/ppermute | solution.py:201
  4.1 1.5 %collective-permute-start.3 = (bf16[64,1280]{1,0:T(8,128)(2,1)S(1)}, bf16[64,1280]{1,0:T(8,128)(2,1)S(1)}, u32[]{:S(2)}, u32[]{:S(2)}) collective-permute-start(bf16[64,1280]{1,0:T(8,128)(2,1)S(1)} %get-tuple-element.31.refs_0_.refs_8_), channel_id=1, source_target_pairs={{0,4},{2,6},{8,0},{10,2},{16,8},{18,10},{24,16},{26,18},{28,24},{3... | collective-permute-start | bytes 491528 | tf_op jit(solution)/shard_map/ppermute | solution.py:201
  5.6 0.5 collective-permute-start.2
  6.1 2.2 %collective-permute-done.1.refs_2_.refs_10_ = bf16[64,1280]{1,0:T(8,128)(2,1)S(1)} collective-permute-done((bf16[64,1280]{1,0:T(8,128)(2,1)S(1)}, bf16[64,1280]{1,0:T(8,128)(2,1)S(1)}, u32[]{:S(2)}, u32[]{:S(2)}) %collective-permute-start.1) | collective-permute-done | bytes 163872 | tf_op jit(solution)/shard_map/ppermute | solution.py:201
  8.3 1.5 %collective-permute-done.3.refs_4_.refs_12_ = bf16[64,1280]{1,0:T(8,128)(2,1)S(1)} collective-permute-done((bf16[64,1280]{1,0:T(8,128)(2,1)S(1)}, bf16[64,1280]{1,0:T(8,128)(2,1)S(1)}, u32[]{:S(2)}, u32[]{:S(2)}) %collective-permute-start.3) | collective-permute-done | bytes 163872 | tf_op jit(solution)/shard_map/ppermute | solution.py:201
  9.7 1.2 %collective-permute-done.2.refs_3_.refs_11_ = bf16[64,1280]{1,0:T(8,128)(2,1)S(1)} collective-permute-done((bf16[64,1280]{1,0:T(8,128)(2,1)S(1)}, bf16[64,1280]{1,0:T(8,128)(2,1)S(1)}, u32[]{:S(2)}, u32[]{:S(2)}) %collective-permute-start.2) | collective-permute-done | bytes 163872 | tf_op jit(solution)/shard_map/ppermute | solution.py:201
  11.0 0.9 pack.9
  11.8 0.5 collective-permute-start.5
  12.3 1.5 %collective-permute-start.6 = (bf16[192,1280]{1,0:T(8,128)(2,1)S(1)}, bf16[192,1280]{1,0:T(8,128)(2,1)S(1)}, u32[]{:S(2)}, u32[]{:S(2)}) collective-permute-start(bf16[192,1280]{1,0:T(8,128)(2,1)S(1)} %get-tuple-element.35), channel_id=1, source_target_pairs={{0,4},{2,6},{8,0},{10,2},{16,8},{18,10},{24,16},{26,18},{28,24},{3... | collective-permute-start | bytes 1474568 | tf_op jit(solution)/shard_map/ppermute | solution.py:201
  13.9 0.5 collective-permute-start.4
  14.4 8.9 %collective-permute-done.5.refs_0_.refs_1_.refs_14_ = bf16[192,1280]{1,0:T(8,128)(2,1)S(1)} collective-permute-done((bf16[192,1280]{1,0:T(8,128)(2,1)S(1)}, bf16[192,1280]{1,0:T(8,128)(2,1)S(1)}, u32[]{:S(2)}, u32[]{:S(2)}) %collective-permute-start.5) | collective-permute-done | bytes 491552 | tf_op jit(solution)/shard_map/ppermute | solution.py:201
  23.3 0.6 collective-permute-start.8
  24.0 1.4 %collective-permute-start.9 = (bf16[192,1280]{1,0:T(8,128)(2,1)S(1)}, bf16[192,1280]{1,0:T(8,128)(2,1)S(1)}, u32[]{:S(2)}, u32[]{:S(2)}) collective-permute-start(bf16[192,1280]{1,0:T(8,128)(2,1)S(1)} %collective-permute-done.6.refs_1_.refs_2_.refs_15_), channel_id=1, source_target_pairs={{0,4},{2,6},{8,0},{10,2},{16,8},{18,10},{24,16},{26,18},{28,24},{3... | collective-permute-start | bytes 1474568 | tf_op jit(solution)/shard_map/ppermute | solution.py:201
  25.4 0.1 pad_add_fusion.refs_0_.info
  25.4 1.6 %copy-done = bf16[512,2048]{1,0:T(8,128)(2,1)S(1)} copy-done((bf16[512,2048]{1,0:T(8,128)(2,1)S(1)}, bf16[512,2048]{1,0:T(8,128)(2,1)}, u32[]{:S(2)}) %copy-start) | copy-done | bytes 2097176
  27.0 1.2 %turn.1.refs_3_.refs_2_ = bf16[512,2048]{1,0:T(8,128)(2,1)S(1)} custom-call(s32[2]{0:T(128)S(1)} %pad_add_fusion.refs_0_.info, bf16[512,2048]{1,0:T(8,128)(2,1)S(1)} %copy-done), custom_call_target="tpu_custom_call" | custom-call | bytes 4194304 | tf_op jit(solution)/shard_map/turn/pallas_call | solution.py:541
  28.3 2.4 %low.1.refs_4_.refs_3_ = bf16[512,256]{1,0:T(8,128)(2,1)S(1)} custom-call(s32[2]{0:T(128)S(1)} %pad_add_fusion.refs_0_.info, s32[4]{0:T(128)S(1)} %copy-done.14, s32[4]{0:T(128)S(1)} %copy-done.16, bf16[512,2048]{1,0:T(8,128)(2,1)S(1)} %copy-done, bf16[2048,128]{1,0:T(8,128)(2,1)S(1)} %copy-done.4, bf16[2048,128]{1,0:T(8,128)(2,1)} %collective-permute-done.refs_5_), custom_call_target="tpu_custom_call" | custom-call | flops 536870912 | bytes 2097152 | tf_op jit(solution)/shard_map/low/pallas_call | solution.py:541
  30.8 0.6 collective-permute-start.12
  31.3 1.6 %collective-permute-start.11 = (bf16[512,128]{1,0:T(8,128)(2,1)S(1)}, bf16[512,128]{1,0:T(8,128)(2,1)S(1)}, u32[]{:S(2)}, u32[]{:S(2)}) collective-permute-start(bf16[512,128]{1,0:T(8,128)(2,1)S(1)} %get-tuple-element.36.refs_0_.refs_2_), channel_id=1, source_target_pairs={{0,4},{2,6},{8,0},{10,2},{16,8},{18,10},{24,16},{26,18},{28,24},{3... | collective-permute-start | bytes 393224 | tf_op jit(solution)/shard_map/ppermute | solution.py:201
  33.0 0.4 collective-permute-start.10
  33.3 2.5 %collective-permute-done.12.refs_5_.refs_2_.refs_4_ = bf16[512,128]{1,0:T(8,128)(2,1)S(1)} collective-permute-done((bf16[512,128]{1,0:T(8,128)(2,1)S(1)}, bf16[512,128]{1,0:T(8,128)(2,1)S(1)}, u32[]{:S(2)}, u32[]{:S(2)}) %collective-permute-start.12) | collective-permute-done | bytes 131104 | tf_op jit(solution)/shard_map/ppermute | solution.py:201
  35.8 1.4 %collective-permute-done.11.refs_4_.refs_6_ = bf16[512,128]{1,0:T(8,128)(2,1)S(1)} collective-permute-done((bf16[512,128]{1,0:T(8,128)(2,1)S(1)}, bf16[512,128]{1,0:T(8,128)(2,1)S(1)}, u32[]{:S(2)}, u32[]{:S(2)}) %collective-permute-start.11) | collective-permute-done | bytes 131104 | tf_op jit(solution)/shard_map/ppermute | solution.py:201
  37.2 1.0 collective-permute-done.10.refs_3_.refs_5_
  38.2 0.1 pack.12
  38.3 0.6 collective-permute-start.14
  39.0 1.5 %collective-permute-start.15 = (bf16[160,1280]{1,0:T(8,128)(2,1)S(1)}, bf16[160,1280]{1,0:T(8,128)(2,1)S(1)}, u32[]{:S(2)}, u32[]{:S(2)}) collective-permute-start(bf16[160,1280]{1,0:T(8,128)(2,1)S(1)} %get-tuple-element.40), channel_id=1, source_target_pairs={{0,4},{2,6},{8,0},{10,2},{16,8},{18,10},{24,16},{26,18},{28,24},{3... | collective-permute-start | bytes 1228808 | tf_op jit(solution)/shard_map/ppermute | solution.py:201
  40.4 1.9 %collective-permute-start.7 = (bf16[128,1280]{1,0:T(8,128)(2,1)S(1)}, bf16[128,1280]{1,0:T(8,128)(2,1)S(1)}, u32[]{:S(2)}, u32[]{:S(2)}) collective-permute-start(bf16[128,1280]{1,0:T(8,128)(2,1)S(1)} %pack.10), channel_id=1, source_target_pairs={{0,2},{2,0},{8,10},{10,8},{16,18},{18,16},{24,26},{26,24},{28,30},... | collective-permute-start | bytes 983048 | tf_op jit(solution)/shard_map/ppermute | solution.py:201
  42.3 0.2 collective-permute-start.13
  42.5 8.6 %collective-permute-done.7.refs_2_.refs_16_ = bf16[128,1280]{1,0:T(8,128)(2,1)S(1)} collective-permute-done((bf16[128,1280]{1,0:T(8,128)(2,1)S(1)}, bf16[128,1280]{1,0:T(8,128)(2,1)S(1)}, u32[]{:S(2)}, u32[]{:S(2)}) %collective-permute-start.7) | collective-permute-done | bytes 327712 | tf_op jit(solution)/shard_map/ppermute | solution.py:201
  51.2 1.5 %collective-permute-start.16 = (bf16[64,1280]{1,0:T(8,128)(2,1)S(1)}, bf16[64,1280]{1,0:T(8,128)(2,1)S(1)}, u32[]{:S(2)}, u32[]{:S(2)}) collective-permute-start(bf16[64,1280]{1,0:T(8,128)(2,1)S(1)} %get-tuple-element.41), channel_id=1, source_target_pairs={{0,2},{2,0},{8,10},{10,8},{16,18},{18,16},{24,26},{26,24},{28,30},... | collective-permute-start | bytes 491528 | tf_op jit(solution)/shard_map/ppermute | solution.py:201
  52.7 0.5 collective-permute-start.17
  53.2 1.5 %collective-permute-start.18 = (bf16[64,1280]{1,0:T(8,128)(2,1)S(1)}, bf16[64,1280]{1,0:T(8,128)(2,1)S(1)}, u32[]{:S(2)}, u32[]{:S(2)}) collective-permute-start(bf16[64,1280]{1,0:T(8,128)(2,1)S(1)} %get-tuple-element.43), channel_id=1, source_target_pairs={{0,4},{2,6},{8,0},{10,2},{16,8},{18,10},{24,16},{26,18},{28,24},{3... | collective-permute-start | bytes 491528 | tf_op jit(solution)/shard_map/ppermute | solution.py:201
  54.7 1.0 pack.14
  55.8 0.7 copy-done.17
  56.5 0.5 collective-permute-start.19
  57.0 1.5 %collective-permute-start.21 = (bf16[1536,128]{1,0:T(8,128)(2,1)}, bf16[1536,128]{1,0:T(8,128)(2,1)}, u32[]{:S(2)}, u32[]{:S(2)}) collective-permute-start(bf16[1536,128]{1,0:T(8,128)(2,1)} %get-tuple-element.49), channel_id=1, source_target_pairs={{0,4},{2,6},{8,0},{10,2},{16,8},{18,10},{24,16},{26,18},{28,24},{3... | collective-permute-start | bytes 1179656 | tf_op jit(solution)/shard_map/ppermute | solution.py:201
  58.6 6.7 %project.1 = (bf16[512,128]{1,0:T(8,128)(2,1)}, bf16[512,128]{1,0:T(8,128)(2,1)}, bf16[512,1024]{1,0:T(8,128)(2,1)}, bf16[8,160,128]{2,1,0:T(8,128)(2,1)S(1)}) custom-call(s32[2]{0:T(128)S(1)} %pad_add_fusion.refs_0_.info, s32[4]{0:T(128)S(1)} %copy-done.14, bf16[512,2048]{1,0:T(8,128)(2,1)S(1)} %turn.1.refs_3_.refs_2_, ...), custom_call_target="tpu_custom_call" | custom-call | flops 671088640 | bytes 1310720 | tf_op jit(solution)/shard_map/project/pallas_call | solution.py:541
  65.3 0.7 copy-done.7
  66.0 4.9 %all-to-all-start = ((bf16[16,80,128]{2,1,0:T(8,128)(2,1)}), bf16[16,80,128]{2,1,0:T(8,128)(2,1)S(1)}, u32[]{:S(2)}, u32[]{:S(2)}) async-start(bf16[16,80,128]{2,1,0:T(8,128)(2,1)} %bitcast.6), calls=%async_computation | async-start | bytes 655360 | tf_op jit(solution)/shard_map/all_to_all | solution.py:618
  70.9 1.9 %collective-permute-start.23 = (bf16[1536,128]{1,0:T(8,128)(2,1)}, bf16[1536,128]{1,0:T(8,128)(2,1)S(1)}, u32[]{:S(2)}, u32[]{:S(2)}) collective-permute-start(bf16[1536,128]{1,0:T(8,128)(2,1)} %copy-done.17), channel_id=1, source_target_pairs={{0,2},{2,0},{8,10},{10,8},{16,18},{18,16},{24,26},{26,24},{28,30},... | collective-permute-start | bytes 1179656 | tf_op jit(solution)/shard_map/ppermute | solution.py:201
  72.9 1.5 %collective-permute-start.20 = (bf16[1536,128]{1,0:T(8,128)(2,1)}, bf16[1536,128]{1,0:T(8,128)(2,1)S(1)}, u32[]{:S(2)}, u32[]{:S(2)}) collective-permute-start(bf16[1536,128]{1,0:T(8,128)(2,1)} %collective-permute-done.19.refs_0_.refs_8_), channel_id=1, source_target_pairs={{0,8},{2,10},{8,16},{10,18},{16,24},{18,26},{24,28},{26,30},{28,20... | collective-permute-start | bytes 1179656 | tf_op jit(solution)/shard_map/ppermute | solution.py:201
  74.3 0.6 collective-permute-start.22
  74.9 4.6 %within.1.refs_2_ = bf16[512,1024]{1,0:T(8,128)(2,1)S(1)} custom-call(s32[2]{0:T(128)S(1)} %pad_add_fusion.refs_0_.info, s32[4]{0:T(128)S(1)} %copy-done.14, bf16[512,128]{1,0:T(8,128)(2,1)} %get-tuple-element.44.refs_2_.refs_3_, bf16[512,128]{1,0:T(8,128)(2,1)} %get-tuple-element.45.refs_3_, bf16[512,1024]{1,0:T(8,128)(2,1)} %get-tuple-element.46.refs_4_), custom_call_target="tpu_custom_call" | custom-call | flops 3221225472 | bytes 12582912 | tf_op jit(solution)/shard_map/within/pallas_call | solution.py:541
  79.5 0.5 all-to-all-done.refs_1_
  80.0 1.4 %mix.1 = bf16[16,80,128]{2,1,0:T(8,128)(2,1)} custom-call(s32[4]{0:T(128)S(1)} %copy-done.14, bf16[16,80,128]{2,1,0:T(8,128)(2,1)S(1)} %all-to-all-done.refs_1_, bf16[512,1024]{1,0:T(8,128)(2,1)S(1)} %within.1.refs_2_), custom_call_target="tpu_custom_call" | custom-call | bytes 655360 | tf_op jit(solution)/shard_map/mix/pallas_call | solution.py:541
  81.4 5.1 %all-to-all-start.1 = ((bf16[16,80,128]{2,1,0:T(8,128)(2,1)}), bf16[16,80,128]{2,1,0:T(8,128)(2,1)S(1)}, u32[]{:S(2)}, u32[]{:S(2)}) async-start(bf16[16,80,128]{2,1,0:T(8,128)(2,1)} %mix.1), calls=%async_computation.1 | async-start | bytes 655360 | tf_op jit(solution)/shard_map/all_to_all | solution.py:629
  86.5 1.0 pack.15
  87.5 1.9 %collective-permute-start.24 = (bf16[1280,128]{1,0:T(8,128)(2,1)}, bf16[1280,128]{1,0:T(8,128)(2,1)S(1)}, u32[]{:S(2)}, u32[]{:S(2)}) collective-permute-start(bf16[1280,128]{1,0:T(8,128)(2,1)} %get-tuple-element.51), channel_id=1, source_target_pairs={{0,8},{2,10},{8,16},{10,18},{16,24},{18,26},{24,28},{26,30},{28,20... | collective-permute-start | bytes 983048 | tf_op jit(solution)/shard_map/ppermute | solution.py:201
  89.5 0.1 collective-permute-start.25
  89.6 1.8 %pack.16 = bf16[1024,128]{1,0:T(8,128)(2,1)} custom-call(bf16[1536,128]{1,0:T(8,128)(2,1)} %collective-permute-done.19.refs_0_.refs_8_, bf16[1536,128]{1,0:T(8,128)(2,1)} %collective-permute-done.21.refs_1_.refs_9_), custom_call_target="tpu_custom_call" | custom-call | tf_op jit(solution)/shard_map/pack/pallas_call | solution.py:214
  91.4 1.9 %collective-permute-start.26 = (bf16[1024,128]{1,0:T(8,128)(2,1)}, bf16[1024,128]{1,0:T(8,128)(2,1)}, u32[]{:S(2)}, u32[]{:S(2)}) collective-permute-start(bf16[1024,128]{1,0:T(8,128)(2,1)} %pack.16), channel_id=1, source_target_pairs={{0,2},{2,0},{8,10},{10,8},{16,18},{18,16},{24,26},{26,24},{28,30},... | collective-permute-start | bytes 786440 | tf_op jit(solution)/shard_map/ppermute | solution.py:201
  93.3 0.1 collective-permute-start.30
  93.4 2.2 %all-to-all-done.1 = bf16[16,80,128]{2,1,0:T(8,128)(2,1)S(1)} async-done(((bf16[16,80,128]{2,1,0:T(8,128)(2,1)}), bf16[16,80,128]{2,1,0:T(8,128)(2,1)S(1)}, u32[]{:S(2)}, u32[]{:S(2)}) %all-to-all-start.1) | async-done | bytes 327712 | tf_op jit(solution)/shard_map/all_to_all | solution.py:629
  95.7 3.8 %finish.1.refs_3_.refs_1_.normed = bf16[512,1024]{1,0:T(8,128)(2,1)S(1)} custom-call(s32[2]{0:T(128)S(1)} %pad_add_fusion.refs_0_.info, s32[4]{0:T(128)S(1)} %copy-done.14, bf16[512,1024]{1,0:T(8,128)(2,1)S(1)} %within.1.refs_2_, bf16[512,128]{1,0:T(8,128)(2,1)} %get-tuple-element.44.refs_2_.refs_3_, bf16[8,160,128]{2,1,0:T(8,128)(2,1)S(1)} %bitcast.5, ...), custom_call_target="tpu_custom_call" | custom-call | flops 167772160 | bytes 4194304 | tf_op jit(solution)/shard_map/finish/pallas_call | solution.py:541
  99.5 1.6 %collective-permute-start.27 = (bf16[512,128]{1,0:T(8,128)(2,1)S(1)}, bf16[512,128]{1,0:T(8,128)(2,1)S(1)}, u32[]{:S(2)}, u32[]{:S(2)}) collective-permute-start(bf16[512,128]{1,0:T(8,128)(2,1)S(1)} %get-tuple-element.53), channel_id=1, source_target_pairs={{0,2},{2,0},{8,10},{10,8},{16,18},{18,16},{24,26},{26,24},{28,30},... | collective-permute-start | bytes 393224 | tf_op jit(solution)/shard_map/ppermute | solution.py:201
  101.1 0.5 collective-permute-start.28
  101.6 1.6 %collective-permute-start.29 = (bf16[512,128]{1,0:T(8,128)(2,1)S(1)}, bf16[512,128]{1,0:T(8,128)(2,1)S(1)}, u32[]{:S(2)}, u32[]{:S(2)}) collective-permute-start(bf16[512,128]{1,0:T(8,128)(2,1)S(1)} %get-tuple-element.55), channel_id=1, source_target_pairs={{0,4},{2,6},{8,0},{10,2},{16,8},{18,10},{24,16},{26,18},{28,24},{3... | collective-permute-start | bytes 393224 | tf_op jit(solution)/shard_map/ppermute | solution.py:201
  103.2 3.5 %out.1.refs_5_ = bf16[16,512,128]{2,1,0:T(8,128)(2,1)S(1)} custom-call(s32[2]{0:T(128)S(1)} %pad_add_fusion.refs_0_.info, bf16[512,1024]{1,0:T(8,128)(2,1)S(1)} %finish.1.refs_3_.refs_1_.normed, bf16[512,128]{1,0:T(8,128)(2,1)S(1)} %copy-done.10, bf16[512,128]{1,0:T(8,128)(2,1)S(1)} %copy-done.12, ...), custom_call_target="tpu_custom_call" | custom-call | flops 2147483648 | bytes 4194304 | tf_op jit(solution)/shard_map/out/pallas_call | solution.py:541
  106.7 1.3 %last.1.refs_0_ = bf16[16,512,128]{2,1,0:T(8,128)(2,1)S(1)} custom-call(s32[2]{0:T(128)S(1)} %pad_add_fusion.refs_0_.info, bf16[512,1024]{1,0:T(8,128)(2,1)S(1)} %finish.1.refs_3_.refs_1_.normed, bf16[1280,128]{1,0:T(8,128)(2,1)S(1)} %collective-permute-done.24.refs_0_.refs_14_, ...), custom_call_target="tpu_custom_call", output_to_operand_aliasing={{}: (7, {})} | custom-call | tf_op jit(solution)/shard_map/last/pallas_call | solution.py:646
  108.1 0.1 slice.4
  108.2 0.1 collective-permute-start.31
  108.2 2.6 %collective-permute-done.31.refs_1_ = bf16[8,512,128]{2,1,0:T(8,128)(2,1)S(1)} collective-permute-done((bf16[8,512,128]{2,1,0:T(8,128)(2,1)S(1)}, bf16[8,512,128]{2,1,0:T(8,128)(2,1)S(1)}, u32[]{:S(2)}, u32[]{:S(2)}) %collective-permute-start.31) | collective-permute-done | bytes 1048608 | tf_op jit(solution)/shard_map/ppermute | solution.py:659
  110.9 1.3 %add.3 = bf16[512,1024]{1,0:T(8,128)(2,1)} custom-call(bf16[16,512,128]{2,1,0:T(8,128)(2,1)S(1)} %last.1.refs_0_, bf16[8,512,128]{2,1,0:T(8,128)(2,1)S(1)} %collective-permute-done.31.refs_1_), custom_call_target="tpu_custom_call" | custom-call | bytes 4194304 | tf_op jit(solution)/shard_map/add/pallas_call | solution.py:541
  (61 shorter events, 0.2 us)
Async XLA Ops:
  1.1 7.2 %collective-permute-start.1 = (bf16[64,1280]{1,0:T(8,128)(2,1)S(1)}, bf16[64,1280]{1,0:T(8,128)(2,1)S(1)}, u32[]{:S(2)}, u32[]{:S(2)}) collective-permute-start(bf16[64,1280]{1,0:T(8,128)(2,1)S(1)} %get-tuple-element.32.refs_1_.refs_9_), channel_id=1, source_target_pairs={{0,2},{2,0},{8,10},{10,8},{16,18},{18,16},{24,26},{26,24},{28,30},... | collective-permute-start | bytes 491528 | tf_op jit(solution)/shard_map/ppermute | solution.py:201
  4.1 5.7 %collective-permute-start.3 = (bf16[64,1280]{1,0:T(8,128)(2,1)S(1)}, bf16[64,1280]{1,0:T(8,128)(2,1)S(1)}, u32[]{:S(2)}, u32[]{:S(2)}) collective-permute-start(bf16[64,1280]{1,0:T(8,128)(2,1)S(1)} %get-tuple-element.31.refs_0_.refs_8_), channel_id=1, source_target_pairs={{0,4},{2,6},{8,0},{10,2},{16,8},{18,10},{24,16},{26,18},{28,24},{3... | collective-permute-start | bytes 491528 | tf_op jit(solution)/shard_map/ppermute | solution.py:201
  5.6 5.4 %collective-permute-start.2 = (bf16[64,1280]{1,0:T(8,128)(2,1)S(1)}, bf16[64,1280]{1,0:T(8,128)(2,1)S(1)}, u32[]{:S(2)}, u32[]{:S(2)}) collective-permute-start(bf16[64,1280]{1,0:T(8,128)(2,1)S(1)} %get-tuple-element.31.refs_0_.refs_8_), channel_id=1, source_target_pairs={{0,8},{2,10},{8,16},{10,18},{16,24},{18,26},{24,28},{26,30},{28,20... | collective-permute-start | bytes 491528 | tf_op jit(solution)/shard_map/ppermute | solution.py:201
  11.8 11.5 %collective-permute-start.5 = (bf16[192,1280]{1,0:T(8,128)(2,1)S(1)}, bf16[192,1280]{1,0:T(8,128)(2,1)S(1)}, u32[]{:S(2)}, u32[]{:S(2)}) collective-permute-start(bf16[192,1280]{1,0:T(8,128)(2,1)S(1)} %get-tuple-element.34), channel_id=1, source_target_pairs={{0,8},{2,10},{8,16},{10,18},{16,24},{18,26},{24,28},{26,30},{28,20... | collective-permute-start | bytes 1474568 | tf_op jit(solution)/shard_map/ppermute | solution.py:201
  12.3 11.6 %collective-permute-start.6 = (bf16[192,1280]{1,0:T(8,128)(2,1)S(1)}, bf16[192,1280]{1,0:T(8,128)(2,1)S(1)}, u32[]{:S(2)}, u32[]{:S(2)}) collective-permute-start(bf16[192,1280]{1,0:T(8,128)(2,1)S(1)} %get-tuple-element.35), channel_id=1, source_target_pairs={{0,4},{2,6},{8,0},{10,2},{16,8},{18,10},{24,16},{26,18},{28,24},{3... | collective-permute-start | bytes 1474568 | tf_op jit(solution)/shard_map/ppermute | solution.py:201
  13.9 14.4 %collective-permute-start = (bf16[2048,128]{1,0:T(8,128)(2,1)}, bf16[2048,128]{1,0:T(8,128)(2,1)}, u32[]{:S(2)}, u32[]{:S(2)}) collective-permute-start(bf16[2048,128]{1,0:T(8,128)(2,1)} %refs_4_.2), channel_id=1, source_target_pairs={{0,1},{1,0},{2,3},{3,2},{4,5},{5,4},{6,7},{7,6},{8,9},{9,8},{10,11... | collective-permute-start | bytes 1572872 | tf_op jit(solution)/shard_map/ppermute | solution.py:579
  13.9 19.1 %collective-permute-start.4 = (bf16[192,1280]{1,0:T(8,128)(2,1)}, bf16[192,1280]{1,0:T(8,128)(2,1)S(1)}, u32[]{:S(2)}, u32[]{:S(2)}) collective-permute-start(bf16[192,1280]{1,0:T(8,128)(2,1)} %get-tuple-element.33), channel_id=1, source_target_pairs={{0,2},{2,0},{8,10},{10,8},{16,18},{18,16},{24,26},{26,24},{28,30},... | collective-permute-start | bytes 1474568 | tf_op jit(solution)/shard_map/ppermute | solution.py:201
  23.3 14.9 %collective-permute-start.8 = (bf16[192,1280]{1,0:T(8,128)(2,1)S(1)}, bf16[192,1280]{1,0:T(8,128)(2,1)S(1)}, u32[]{:S(2)}, u32[]{:S(2)}) collective-permute-start(bf16[192,1280]{1,0:T(8,128)(2,1)S(1)} %collective-permute-done.5.refs_0_.refs_1_.refs_14_), channel_id=1, source_target_pairs={{0,8},{2,10},{8,16},{10,18},{16,24},{18,26},{24,28},{26,30},{28,20... | collective-permute-start | bytes 1474568 | tf_op jit(solution)/shard_map/ppermute | solution.py:201
  24.0 14.2 %collective-permute-start.9 = (bf16[192,1280]{1,0:T(8,128)(2,1)S(1)}, bf16[192,1280]{1,0:T(8,128)(2,1)S(1)}, u32[]{:S(2)}, u32[]{:S(2)}) collective-permute-start(bf16[192,1280]{1,0:T(8,128)(2,1)S(1)} %collective-permute-done.6.refs_1_.refs_2_.refs_15_), channel_id=1, source_target_pairs={{0,4},{2,6},{8,0},{10,2},{16,8},{18,10},{24,16},{26,18},{28,24},{3... | collective-permute-start | bytes 1474568 | tf_op jit(solution)/shard_map/ppermute | solution.py:201
  25.4 1.6 %copy-start = (bf16[512,2048]{1,0:T(8,128)(2,1)S(1)}, bf16[512,2048]{1,0:T(8,128)(2,1)}, u32[]{:S(2)}) copy-start(bf16[512,2048]{1,0:T(8,128)(2,1)} %refs_3_.1) | copy-start | bytes 6291460
  27.0 1.2 %copy-start.4 = (bf16[2048,128]{1,0:T(8,128)(2,1)S(1)}, bf16[2048,128]{1,0:T(8,128)(2,1)}, u32[]{:S(2)}) copy-start(bf16[2048,128]{1,0:T(8,128)(2,1)} %refs_4_.2) | copy-start | bytes 1572868
  27.0 1.3 %copy-start.14 = (s32[4]{0:T(128)S(1)}, s32[4]{0:T(128)}, u32[]{:S(2)}) copy-start(s32[4]{0:T(128)} %refs_1_.9) | copy-start | bytes 52
  27.0 1.3 %copy-start.16 = (s32[4]{0:T(128)S(1)}, s32[4]{0:T(128)}, u32[]{:S(2)}) copy-start(s32[4]{0:T(128)} %refs_2_.1) | copy-start | bytes 52
  28.2 2.4 %copy-start.8 = (bf16[1024,128]{1,0:T(8,128)(2,1)S(1)}, bf16[1024,128]{1,0:T(8,128)(2,1)}, u32[]{:S(2)}) copy-start(bf16[1024,128]{1,0:T(8,128)(2,1)} %refs_0_.2) | copy-start | bytes 786436
  30.7 24.0 %copy-start.9 = (bf16[512,128]{1,0:T(8,128)(2,1)}, bf16[512,128]{1,0:T(8,128)(2,1)S(1)}, u32[]{:S(2)}) copy-start(bf16[512,128]{1,0:T(8,128)(2,1)S(1)} %get-tuple-element.36.refs_0_.refs_2_) | copy-start | bytes 393220
  30.7 24.0 %copy-start.11 = (bf16[512,128]{1,0:T(8,128)(2,1)}, bf16[512,128]{1,0:T(8,128)(2,1)S(1)}, u32[]{:S(2)}) copy-start(bf16[512,128]{1,0:T(8,128)(2,1)S(1)} %get-tuple-element.37.refs_1_.refs_3_) | copy-start | bytes 393220
  30.8 5.0 %collective-permute-start.12 = (bf16[512,128]{1,0:T(8,128)(2,1)S(1)}, bf16[512,128]{1,0:T(8,128)(2,1)S(1)}, u32[]{:S(2)}, u32[]{:S(2)}) collective-permute-start(bf16[512,128]{1,0:T(8,128)(2,1)S(1)} %get-tuple-element.37.refs_1_.refs_3_), channel_id=1, source_target_pairs={{0,2},{2,0},{8,10},{10,8},{16,18},{18,16},{24,26},{26,24},{28,30},... | collective-permute-start | bytes 393224 | tf_op jit(solution)/shard_map/ppermute | solution.py:201
  31.3 5.9 %collective-permute-start.11 = (bf16[512,128]{1,0:T(8,128)(2,1)S(1)}, bf16[512,128]{1,0:T(8,128)(2,1)S(1)}, u32[]{:S(2)}, u32[]{:S(2)}) collective-permute-start(bf16[512,128]{1,0:T(8,128)(2,1)S(1)} %get-tuple-element.36.refs_0_.refs_2_), channel_id=1, source_target_pairs={{0,4},{2,6},{8,0},{10,2},{16,8},{18,10},{24,16},{26,18},{28,24},{3... | collective-permute-start | bytes 393224 | tf_op jit(solution)/shard_map/ppermute | solution.py:201
  33.0 5.2 %collective-permute-start.10 = (bf16[512,128]{1,0:T(8,128)(2,1)S(1)}, bf16[512,128]{1,0:T(8,128)(2,1)S(1)}, u32[]{:S(2)}, u32[]{:S(2)}) collective-permute-start(bf16[512,128]{1,0:T(8,128)(2,1)S(1)} %get-tuple-element.36.refs_0_.refs_2_), channel_id=1, source_target_pairs={{0,8},{2,10},{8,16},{10,18},{16,24},{18,26},{24,28},{26,30},{28,20... | collective-permute-start | bytes 393224 | tf_op jit(solution)/shard_map/ppermute | solution.py:201
  38.2 16.6 %copy-start.1 = (bf16[512,128]{1,0:T(8,128)(2,1)}, bf16[512,128]{1,0:T(8,128)(2,1)S(1)}, u32[]{:S(2)}) copy-start(bf16[512,128]{1,0:T(8,128)(2,1)S(1)} %collective-permute-done.10.refs_3_.refs_5_) | copy-start | bytes 393220
  38.3 20.3 %copy-start.3 = (bf16[256,1024]{1,0:T(8,128)(2,1)S(1)}, bf16[256,1024]{1,0:T(8,128)(2,1)}, u32[]{:S(2)}) copy-start(bf16[256,1024]{1,0:T(8,128)(2,1)} %refs_4_.3) | copy-start | bytes 1572868
  38.3 20.3 %copy-start.5 = (f32[160,128]{1,0:T(8,128)S(1)}, f32[160,128]{1,0:T(8,128)}, u32[]{:S(2)}) copy-start(f32[160,128]{1,0:T(8,128)} %constant.15.clone.refs_6_.refs_7_) | copy-start | bytes 245764
  38.3 20.3 %copy-start.6 = (f32[160,128]{1,0:T(8,128)S(1)}, f32[160,128]{1,0:T(8,128)}, u32[]{:S(2)}) copy-start(f32[160,128]{1,0:T(8,128)} %constant.14.clone.refs_5_.refs_6_) | copy-start | bytes 245764
  38.3 20.3 %copy-start.13 = (f32[160,8]{1,0:T(8,128)S(1)}, f32[160,8]{1,0:T(8,128)}, u32[]{:S(2)}) copy-start(f32[160,8]{1,0:T(8,128)} %constant.17.refs_7_) | copy-start | bytes 15364
  38.3 12.8 %collective-permute-start.14 = (bf16[160,1280]{1,0:T(8,128)(2,1)S(1)}, bf16[160,1280]{1,0:T(8,128)(2,1)S(1)}, u32[]{:S(2)}, u32[]{:S(2)}) collective-permute-start(bf16[160,1280]{1,0:T(8,128)(2,1)S(1)} %get-tuple-element.39), channel_id=1, source_target_pairs={{0,8},{2,10},{8,16},{10,18},{16,24},{18,26},{24,28},{26,30},{28,20... | collective-permute-start | bytes 1228808 | tf_op jit(solution)/shard_map/ppermute | solution.py:201
  39.0 12.2 %collective-permute-start.15 = (bf16[160,1280]{1,0:T(8,128)(2,1)S(1)}, bf16[160,1280]{1,0:T(8,128)(2,1)S(1)}, u32[]{:S(2)}, u32[]{:S(2)}) collective-permute-start(bf16[160,1280]{1,0:T(8,128)(2,1)S(1)} %get-tuple-element.40), channel_id=1, source_target_pairs={{0,4},{2,6},{8,0},{10,2},{16,8},{18,10},{24,16},{26,18},{28,24},{3... | collective-permute-start | bytes 1228808 | tf_op jit(solution)/shard_map/ppermute | solution.py:201
  40.4 10.7 %collective-permute-start.7 = (bf16[128,1280]{1,0:T(8,128)(2,1)S(1)}, bf16[128,1280]{1,0:T(8,128)(2,1)S(1)}, u32[]{:S(2)}, u32[]{:S(2)}) collective-permute-start(bf16[128,1280]{1,0:T(8,128)(2,1)S(1)} %pack.10), channel_id=1, source_target_pairs={{0,2},{2,0},{8,10},{10,8},{16,18},{18,16},{24,26},{26,24},{28,30},... | collective-permute-start | bytes 983048 | tf_op jit(solution)/shard_map/ppermute | solution.py:201
  42.3 14.7 %collective-permute-start.13 = (bf16[128,1280]{1,0:T(8,128)(2,1)S(1)}, bf16[128,1280]{1,0:T(8,128)(2,1)S(1)}, u32[]{:S(2)}, u32[]{:S(2)}) collective-permute-start(bf16[128,1280]{1,0:T(8,128)(2,1)S(1)} %get-tuple-element.38), channel_id=1, source_target_pairs={{0,2},{2,0},{8,10},{10,8},{16,18},{18,16},{24,26},{26,24},{28,30},... | collective-permute-start | bytes 983048 | tf_op jit(solution)/shard_map/ppermute | solution.py:201
  51.2 7.3 %collective-permute-start.16 = (bf16[64,1280]{1,0:T(8,128)(2,1)S(1)}, bf16[64,1280]{1,0:T(8,128)(2,1)S(1)}, u32[]{:S(2)}, u32[]{:S(2)}) collective-permute-start(bf16[64,1280]{1,0:T(8,128)(2,1)S(1)} %get-tuple-element.41), channel_id=1, source_target_pairs={{0,2},{2,0},{8,10},{10,8},{16,18},{18,16},{24,26},{26,24},{28,30},... | collective-permute-start | bytes 491528 | tf_op jit(solution)/shard_map/ppermute | solution.py:201
  52.7 5.8 %collective-permute-start.17 = (bf16[64,1280]{1,0:T(8,128)(2,1)S(1)}, bf16[64,1280]{1,0:T(8,128)(2,1)S(1)}, u32[]{:S(2)}, u32[]{:S(2)}) collective-permute-start(bf16[64,1280]{1,0:T(8,128)(2,1)S(1)} %get-tuple-element.42), channel_id=1, source_target_pairs={{0,8},{2,10},{8,16},{10,18},{16,24},{18,26},{24,28},{26,30},{28,20... | collective-permute-start | bytes 491528 | tf_op jit(solution)/shard_map/ppermute | solution.py:201
  53.2 5.4 %collective-permute-start.18 = (bf16[64,1280]{1,0:T(8,128)(2,1)S(1)}, bf16[64,1280]{1,0:T(8,128)(2,1)S(1)}, u32[]{:S(2)}, u32[]{:S(2)}) collective-permute-start(bf16[64,1280]{1,0:T(8,128)(2,1)S(1)} %get-tuple-element.43), channel_id=1, source_target_pairs={{0,4},{2,6},{8,0},{10,2},{16,8},{18,10},{24,16},{26,18},{28,24},{3... | collective-permute-start | bytes 491528 | tf_op jit(solution)/shard_map/ppermute | solution.py:201
  55.7 0.7 copy-start.17
  56.5 16.4 %collective-permute-start.19 = (bf16[1536,128]{1,0:T(8,128)(2,1)}, bf16[1536,128]{1,0:T(8,128)(2,1)}, u32[]{:S(2)}, u32[]{:S(2)}) collective-permute-start(bf16[1536,128]{1,0:T(8,128)(2,1)} %get-tuple-element.48), channel_id=1, source_target_pairs={{0,8},{2,10},{8,16},{10,18},{16,24},{18,26},{24,28},{26,30},{28,20... | collective-permute-start | bytes 1179656 | tf_op jit(solution)/shard_map/ppermute | solution.py:201
  57.0 17.3 %collective-permute-start.21 = (bf16[1536,128]{1,0:T(8,128)(2,1)}, bf16[1536,128]{1,0:T(8,128)(2,1)}, u32[]{:S(2)}, u32[]{:S(2)}) collective-permute-start(bf16[1536,128]{1,0:T(8,128)(2,1)} %get-tuple-element.49), channel_id=1, source_target_pairs={{0,4},{2,6},{8,0},{10,2},{16,8},{18,10},{24,16},{26,18},{28,24},{3... | collective-permute-start | bytes 1179656 | tf_op jit(solution)/shard_map/ppermute | solution.py:201
  65.3 0.7 copy-start.7
  66.0 13.9 %all-to-all-start = ((bf16[16,80,128]{2,1,0:T(8,128)(2,1)}), bf16[16,80,128]{2,1,0:T(8,128)(2,1)S(1)}, u32[]{:S(2)}, u32[]{:S(2)}) async-start(bf16[16,80,128]{2,1,0:T(8,128)(2,1)} %bitcast.6), calls=%async_computation | async-start | bytes 655360 | tf_op jit(solution)/shard_map/all_to_all | solution.py:618
  70.9 15.6 %collective-permute-start.23 = (bf16[1536,128]{1,0:T(8,128)(2,1)}, bf16[1536,128]{1,0:T(8,128)(2,1)S(1)}, u32[]{:S(2)}, u32[]{:S(2)}) collective-permute-start(bf16[1536,128]{1,0:T(8,128)(2,1)} %copy-done.17), channel_id=1, source_target_pairs={{0,2},{2,0},{8,10},{10,8},{16,18},{18,16},{24,26},{26,24},{28,30},... | collective-permute-start | bytes 1179656 | tf_op jit(solution)/shard_map/ppermute | solution.py:201
  72.9 13.6 %collective-permute-start.20 = (bf16[1536,128]{1,0:T(8,128)(2,1)}, bf16[1536,128]{1,0:T(8,128)(2,1)S(1)}, u32[]{:S(2)}, u32[]{:S(2)}) collective-permute-start(bf16[1536,128]{1,0:T(8,128)(2,1)} %collective-permute-done.19.refs_0_.refs_8_), channel_id=1, source_target_pairs={{0,8},{2,10},{8,16},{10,18},{16,24},{18,26},{24,28},{26,30},{28,20... | collective-permute-start | bytes 1179656 | tf_op jit(solution)/shard_map/ppermute | solution.py:201
  74.3 12.2 %collective-permute-start.22 = (bf16[1536,128]{1,0:T(8,128)(2,1)}, bf16[1536,128]{1,0:T(8,128)(2,1)S(1)}, u32[]{:S(2)}, u32[]{:S(2)}) collective-permute-start(bf16[1536,128]{1,0:T(8,128)(2,1)} %collective-permute-done.21.refs_1_.refs_9_), channel_id=1, source_target_pairs={{0,4},{2,6},{8,0},{10,2},{16,8},{18,10},{24,16},{26,18},{28,24},{3... | collective-permute-start | bytes 1179656 | tf_op jit(solution)/shard_map/ppermute | solution.py:201
  79.5 16.2 %copy-start.15 = (f32[1024]{0:T(1024)S(1)}, f32[1024]{0:T(1024)}, u32[]{:S(2)}) copy-start(f32[1024]{0:T(1024)} %param.21) | copy-start | bytes 12292
  81.4 14.3 %all-to-all-start.1 = ((bf16[16,80,128]{2,1,0:T(8,128)(2,1)}), bf16[16,80,128]{2,1,0:T(8,128)(2,1)S(1)}, u32[]{:S(2)}, u32[]{:S(2)}) async-start(bf16[16,80,128]{2,1,0:T(8,128)(2,1)} %mix.1), calls=%async_computation.1 | async-start | bytes 655360 | tf_op jit(solution)/shard_map/all_to_all | solution.py:629
  87.5 11.9 %collective-permute-start.24 = (bf16[1280,128]{1,0:T(8,128)(2,1)}, bf16[1280,128]{1,0:T(8,128)(2,1)S(1)}, u32[]{:S(2)}, u32[]{:S(2)}) collective-permute-start(bf16[1280,128]{1,0:T(8,128)(2,1)} %get-tuple-element.51), channel_id=1, source_target_pairs={{0,8},{2,10},{8,16},{10,18},{16,24},{18,26},{24,28},{26,30},{28,20... | collective-permute-start | bytes 983048 | tf_op jit(solution)/shard_map/ppermute | solution.py:201
  89.5 10.0 %collective-permute-start.25 = (bf16[1280,128]{1,0:T(8,128)(2,1)}, bf16[1280,128]{1,0:T(8,128)(2,1)S(1)}, u32[]{:S(2)}, u32[]{:S(2)}) collective-permute-start(bf16[1280,128]{1,0:T(8,128)(2,1)} %get-tuple-element.52), channel_id=1, source_target_pairs={{0,4},{2,6},{8,0},{10,2},{16,8},{18,10},{24,16},{26,18},{28,24},{3... | collective-permute-start | bytes 983048 | tf_op jit(solution)/shard_map/ppermute | solution.py:201
  91.4 8.1 %collective-permute-start.26 = (bf16[1024,128]{1,0:T(8,128)(2,1)}, bf16[1024,128]{1,0:T(8,128)(2,1)}, u32[]{:S(2)}, u32[]{:S(2)}) collective-permute-start(bf16[1024,128]{1,0:T(8,128)(2,1)} %pack.16), channel_id=1, source_target_pairs={{0,2},{2,0},{8,10},{10,8},{16,18},{18,16},{24,26},{26,24},{28,30},... | collective-permute-start | bytes 786440 | tf_op jit(solution)/shard_map/ppermute | solution.py:201
  93.3 9.9 %collective-permute-start.30 = (bf16[1024,128]{1,0:T(8,128)(2,1)}, bf16[1024,128]{1,0:T(8,128)(2,1)}, u32[]{:S(2)}, u32[]{:S(2)}) collective-permute-start(bf16[1024,128]{1,0:T(8,128)(2,1)} %get-tuple-element.56), channel_id=1, source_target_pairs={{0,2},{2,0},{8,10},{10,8},{16,18},{18,16},{24,26},{26,24},{28,30},... | collective-permute-start | bytes 786440 | tf_op jit(solution)/shard_map/ppermute | solution.py:201
  95.7 7.5 %copy-start.2 = (bf16[512,128]{1,0:T(8,128)(2,1)S(1)}, bf16[512,128]{1,0:T(8,128)(2,1)}, u32[]{:S(2)}) copy-start(bf16[512,128]{1,0:T(8,128)(2,1)} %copy-done.1) | copy-start | bytes 393220
  95.7 7.5 %copy-start.10 = (bf16[512,128]{1,0:T(8,128)(2,1)S(1)}, bf16[512,128]{1,0:T(8,128)(2,1)}, u32[]{:S(2)}) copy-start(bf16[512,128]{1,0:T(8,128)(2,1)} %copy-done.9) | copy-start | bytes 393220
  95.7 7.5 %copy-start.12 = (bf16[512,128]{1,0:T(8,128)(2,1)S(1)}, bf16[512,128]{1,0:T(8,128)(2,1)}, u32[]{:S(2)}) copy-start(bf16[512,128]{1,0:T(8,128)(2,1)} %copy-done.11) | copy-start | bytes 393220
  99.5 7.2 %collective-permute-start.27 = (bf16[512,128]{1,0:T(8,128)(2,1)S(1)}, bf16[512,128]{1,0:T(8,128)(2,1)S(1)}, u32[]{:S(2)}, u32[]{:S(2)}) collective-permute-start(bf16[512,128]{1,0:T(8,128)(2,1)S(1)} %get-tuple-element.53), channel_id=1, source_target_pairs={{0,2},{2,0},{8,10},{10,8},{16,18},{18,16},{24,26},{26,24},{28,30},... | collective-permute-start | bytes 393224 | tf_op jit(solution)/shard_map/ppermute | solution.py:201
  101.1 5.6 %collective-permute-start.28 = (bf16[512,128]{1,0:T(8,128)(2,1)S(1)}, bf16[512,128]{1,0:T(8,128)(2,1)S(1)}, u32[]{:S(2)}, u32[]{:S(2)}) collective-permute-start(bf16[512,128]{1,0:T(8,128)(2,1)S(1)} %get-tuple-element.54), channel_id=1, source_target_pairs={{0,8},{2,10},{8,16},{10,18},{16,24},{18,26},{24,28},{26,30},{28,20... | collective-permute-start | bytes 393224 | tf_op jit(solution)/shard_map/ppermute | solution.py:201
  101.6 5.1 %collective-permute-start.29 = (bf16[512,128]{1,0:T(8,128)(2,1)S(1)}, bf16[512,128]{1,0:T(8,128)(2,1)S(1)}, u32[]{:S(2)}, u32[]{:S(2)}) collective-permute-start(bf16[512,128]{1,0:T(8,128)(2,1)S(1)} %get-tuple-element.55), channel_id=1, source_target_pairs={{0,4},{2,6},{8,0},{10,2},{16,8},{18,10},{24,16},{26,18},{28,24},{3... | collective-permute-start | bytes 393224 | tf_op jit(solution)/shard_map/ppermute | solution.py:201
  108.2 2.7 %collective-permute-start.31 = (bf16[8,512,128]{2,1,0:T(8,128)(2,1)S(1)}, bf16[8,512,128]{2,1,0:T(8,128)(2,1)S(1)}, u32[]{:S(2)}, u32[]{:S(2)}) collective-permute-start(bf16[8,512,128]{2,1,0:T(8,128)(2,1)S(1)} %slice.4), channel_id=1, source_target_pairs={{0,1},{1,0},{2,3},{3,2},{4,5},{5,4},{6,7},{7,6},{8,9},{9,8},{10,11... | collective-permute-start | bytes 3145736 | tf_op jit(solution)/shard_map/ppermute | solution.py:659

commit v7 on v6

--- a/solution.py
+++ b/solution.py
@@ -347,7 +347,7 @@
 
 
 def project_kernel(layout, rows, heads, width, info, lengths, tokens, low, up, first, second,
-                   scale, *refs):
+                   scale, *refs, flush):
     pieces, (query, keys, values, state) = refs[: len(layout)], refs[len(layout) :]
     count, depth = tokens.shape
     wide = heads * width
@@ -370,6 +370,8 @@
     query[...] = both[:, :small].astype(jnp.bfloat16)
     key_rows = both[:, small:].astype(jnp.bfloat16)
     keys[...] = key_rows
+    flush[0]()
+    flush[1]()
     positions = lax.broadcasted_iota(jnp.int32, (1, count), 1) + info[0] * count
     end = request_of(jnp.full((1, 1), count - 1, jnp.int32) + info[0] * count, lengths)
     tail = jnp.where(request_of(positions, lengths) == end, 1.0, 0.0)
@@ -384,6 +386,7 @@
         total = product(cols)
         total += jnp.dot(low[...], up[:, cols], preferred_element_type=jnp.float32)
         values[:, cols] = total.astype(jnp.bfloat16)
+    flush[2]()
     for h in range(heads):
         state[h] = jnp.dot(
             maps[h], values[:, h * width : (h + 1) * width], preferred_element_type=jnp.float32
@@ -504,7 +507,7 @@
     return pltpu.with_memory_space_constraint(array, pltpu.HBM)
 
 
-def call(kernel, name, mebibytes, cost, shapes, scalars, arrays, late=(), far=(), out_far=()):
+def call(kernel, name, mebibytes, cost, shapes, scalars, arrays, late=(), far=(), out_far=(), flush=False):
     shapes = [jax.ShapeDtypeStruct(shape, kind) for shape, kind in shapes]
     n, m, k = len(scalars), len(arrays), len(shapes)
     held = [arrays[i] for i in far] + [shapes[i] for i in out_far]
@@ -532,9 +535,12 @@
         for at, i in enumerate(out_far, len(far)):
             copies.append(pltpu.make_async_copy(buffers[at], outs[i], buffers[-1].at[at]))
             outs[i] = buffers[at]
-        kernel(*given, *outs)
-        for copy in copies:
-            copy.start()
+        if flush:
+            kernel(*given, *outs, flush=[copy.start for copy in copies])
+        else:
+            kernel(*given, *outs)
+            for copy in copies:
+                copy.start()
         for copy in copies:
             copy.wait()
 
@@ -612,7 +618,7 @@
             ((count, wide), half),
             ((heads, FEATS, width), half),
         ],
-        [info, lengths], [turned, low, adapter_up, first, second, scale.T, *pieces], out_far=(0, 1, 2),
+        [info, lengths], [turned, low, adapter_up, first, second, scale.T, *pieces], out_far=(0, 1, 2), flush=True,
     )
     parts = state.reshape(blocks, heads * FEATS // blocks, width)
     parts = lax.all_to_all(parts, "dp", 0, 0, tiled=True)

time: 113 us -> 113 us (level)
  no operation moved by 1% of the time
where the time goes in v7:
time: 113 us; the launch traced here: 112 us
  starting transfers between devices  43.6 us (39%)
  waiting for transfers between devices  32.6 us (29%)
  Pallas kernels  32.2 us (28%)
  local copies, waits for them, and re-layouts  3.21 us (3%)
    ppermute x30, starting transfers between devices, send(): return lax.ppermute(value, 'dp', pairs)  33.6 us
    ppermute x30, waiting for transfers between devices, send(): return lax.ppermute(value, 'dp', pairs)  27.3 us
    pallas_call x8, Pallas kernels, call(): pl.pallas_call(body, out_shape=shapes, in_specs=[SMEM] * n + [HBM if i in...  24.9 us
    all_to_all x1, starting transfers between devices, per_device_fast(): lax.all_to_all(mixed, 'dp', 0, 0, tiled=True).reshape(heads, FEATS, width)  5.11 us
    pallas_call x9, Pallas kernels, pack(): pl.pallas_call(functools.partial(pack_kernel, recipes, len(sources)), out...  4.92 us
    all_to_all x1, starting transfers between devices, per_device_fast(): parts = lax.all_to_all(parts, 'dp', 0, 0, tiled=True)  4.89 us
    unnamed x36, local copies, waits for them, and re-layouts  3.14 us
    ppermute x1, waiting for transfers between devices, per_device_fast(): received = lax.ppermute(partial[blocks // 2:], 'mp', [(0, 1), (1, 0)])  2.65 us
  transfers between devices with their start and end apart: 34, of which 11 were waited for; matrix products, arithmetic and copies ran while one was open for 0% of the time, Pallas kernels for 25%

profile of v7, /device:TPU:0, one launch (start us, length us, event | category | flops | bytes accessed | tf_op | source)
XLA Modules:
  0.0 112.2 jit_solution(17335279804313827609)
XLA Ops:
  0.0 1.1 join.1
  1.1 3.0 %collective-permute-start.1 = (bf16[64,1280]{1,0:T(8,128)(2,1)S(1)}, bf16[64,1280]{1,0:T(8,128)(2,1)S(1)}, u32[]{:S(2)}, u32[]{:S(2)}) collective-permute-start(bf16[64,1280]{1,0:T(8,128)(2,1)S(1)} %get-tuple-element.32.refs_1_.refs_9_), channel_id=1, source_target_pairs={{0,2},{2,0},{8,10},{10,8},{16,18},{18,16},{24,26},{26,24},{28,30},... | collective-permute-start | bytes 491528 | tf_op jit(solution)/shard_map/ppermute | solution.py:201
  4.1 1.5 %collective-permute-start.3 = (bf16[64,1280]{1,0:T(8,128)(2,1)S(1)}, bf16[64,1280]{1,0:T(8,128)(2,1)S(1)}, u32[]{:S(2)}, u32[]{:S(2)}) collective-permute-start(bf16[64,1280]{1,0:T(8,128)(2,1)S(1)} %get-tuple-element.31.refs_0_.refs_8_), channel_id=1, source_target_pairs={{0,4},{2,6},{8,0},{10,2},{16,8},{18,10},{24,16},{26,18},{28,24},{3... | collective-permute-start | bytes 491528 | tf_op jit(solution)/shard_map/ppermute | solution.py:201
  5.6 0.5 collective-permute-start.2
  6.1 2.2 %collective-permute-done.1.refs_2_.refs_10_ = bf16[64,1280]{1,0:T(8,128)(2,1)S(1)} collective-permute-done((bf16[64,1280]{1,0:T(8,128)(2,1)S(1)}, bf16[64,1280]{1,0:T(8,128)(2,1)S(1)}, u32[]{:S(2)}, u32[]{:S(2)}) %collective-permute-start.1) | collective-permute-done | bytes 163872 | tf_op jit(solution)/shard_map/ppermute | solution.py:201
  8.3 1.5 %collective-permute-done.3.refs_4_.refs_12_ = bf16[64,1280]{1,0:T(8,128)(2,1)S(1)} collective-permute-done((bf16[64,1280]{1,0:T(8,128)(2,1)S(1)}, bf16[64,1280]{1,0:T(8,128)(2,1)S(1)}, u32[]{:S(2)}, u32[]{:S(2)}) %collective-permute-start.3) | collective-permute-done | bytes 163872 | tf_op jit(solution)/shard_map/ppermute | solution.py:201
  9.7 1.2 %collective-permute-done.2.refs_3_.refs_11_ = bf16[64,1280]{1,0:T(8,128)(2,1)S(1)} collective-permute-done((bf16[64,1280]{1,0:T(8,128)(2,1)S(1)}, bf16[64,1280]{1,0:T(8,128)(2,1)S(1)}, u32[]{:S(2)}, u32[]{:S(2)}) %collective-permute-start.2) | collective-permute-done | bytes 163872 | tf_op jit(solution)/shard_map/ppermute | solution.py:201
  11.0 0.9 pack.9
  11.8 0.5 collective-permute-start.5
  12.3 1.5 %collective-permute-start.6 = (bf16[192,1280]{1,0:T(8,128)(2,1)S(1)}, bf16[192,1280]{1,0:T(8,128)(2,1)S(1)}, u32[]{:S(2)}, u32[]{:S(2)}) collective-permute-start(bf16[192,1280]{1,0:T(8,128)(2,1)S(1)} %get-tuple-element.35), channel_id=1, source_target_pairs={{0,4},{2,6},{8,0},{10,2},{16,8},{18,10},{24,16},{26,18},{28,24},{3... | collective-permute-start | bytes 1474568 | tf_op jit(solution)/shard_map/ppermute | solution.py:201
  13.9 0.5 collective-permute-start.4
  14.4 8.9 %collective-permute-done.5.refs_0_.refs_1_.refs_14_ = bf16[192,1280]{1,0:T(8,128)(2,1)S(1)} collective-permute-done((bf16[192,1280]{1,0:T(8,128)(2,1)S(1)}, bf16[192,1280]{1,0:T(8,128)(2,1)S(1)}, u32[]{:S(2)}, u32[]{:S(2)}) %collective-permute-start.5) | collective-permute-done | bytes 491552 | tf_op jit(solution)/shard_map/ppermute | solution.py:201
  23.3 0.6 collective-permute-start.8
  24.0 1.4 %collective-permute-start.9 = (bf16[192,1280]{1,0:T(8,128)(2,1)S(1)}, bf16[192,1280]{1,0:T(8,128)(2,1)S(1)}, u32[]{:S(2)}, u32[]{:S(2)}) collective-permute-start(bf16[192,1280]{1,0:T(8,128)(2,1)S(1)} %collective-permute-done.6.refs_1_.refs_2_.refs_15_), channel_id=1, source_target_pairs={{0,4},{2,6},{8,0},{10,2},{16,8},{18,10},{24,16},{26,18},{28,24},{3... | collective-permute-start | bytes 1474568 | tf_op jit(solution)/shard_map/ppermute | solution.py:201
  25.4 0.1 pad_add_fusion.refs_0_.info
  25.4 1.6 %copy-done = bf16[512,2048]{1,0:T(8,128)(2,1)S(1)} copy-done((bf16[512,2048]{1,0:T(8,128)(2,1)S(1)}, bf16[512,2048]{1,0:T(8,128)(2,1)}, u32[]{:S(2)}) %copy-start) | copy-done | bytes 2097176
  27.0 1.2 %turn.1.refs_3_.refs_2_ = bf16[512,2048]{1,0:T(8,128)(2,1)S(1)} custom-call(s32[2]{0:T(128)S(1)} %pad_add_fusion.refs_0_.info, bf16[512,2048]{1,0:T(8,128)(2,1)S(1)} %copy-done), custom_call_target="tpu_custom_call" | custom-call | bytes 4194304 | tf_op jit(solution)/shard_map/turn/pallas_call | solution.py:547
  28.3 2.4 %low.1.refs_4_.refs_3_ = bf16[512,256]{1,0:T(8,128)(2,1)S(1)} custom-call(s32[2]{0:T(128)S(1)} %pad_add_fusion.refs_0_.info, s32[4]{0:T(128)S(1)} %copy-done.14, s32[4]{0:T(128)S(1)} %copy-done.16, bf16[512,2048]{1,0:T(8,128)(2,1)S(1)} %copy-done, bf16[2048,128]{1,0:T(8,128)(2,1)S(1)} %copy-done.4, bf16[2048,128]{1,0:T(8,128)(2,1)} %collective-permute-done.refs_5_), custom_call_target="tpu_custom_call" | custom-call | flops 536870912 | bytes 2097152 | tf_op jit(solution)/shard_map/low/pallas_call | solution.py:547
  30.8 0.6 collective-permute-start.12
  31.3 1.6 %collective-permute-start.11 = (bf16[512,128]{1,0:T(8,128)(2,1)S(1)}, bf16[512,128]{1,0:T(8,128)(2,1)S(1)}, u32[]{:S(2)}, u32[]{:S(2)}) collective-permute-start(bf16[512,128]{1,0:T(8,128)(2,1)S(1)} %get-tuple-element.36.refs_0_.refs_2_), channel_id=1, source_target_pairs={{0,4},{2,6},{8,0},{10,2},{16,8},{18,10},{24,16},{26,18},{28,24},{3... | collective-permute-start | bytes 393224 | tf_op jit(solution)/shard_map/ppermute | solution.py:201
  33.0 0.4 collective-permute-start.10
  33.3 2.5 %collective-permute-done.12.refs_5_.refs_2_.refs_4_ = bf16[512,128]{1,0:T(8,128)(2,1)S(1)} collective-permute-done((bf16[512,128]{1,0:T(8,128)(2,1)S(1)}, bf16[512,128]{1,0:T(8,128)(2,1)S(1)}, u32[]{:S(2)}, u32[]{:S(2)}) %collective-permute-start.12) | collective-permute-done | bytes 131104 | tf_op jit(solution)/shard_map/ppermute | solution.py:201
  35.8 1.4 %collective-permute-done.11.refs_4_.refs_6_ = bf16[512,128]{1,0:T(8,128)(2,1)S(1)} collective-permute-done((bf16[512,128]{1,0:T(8,128)(2,1)S(1)}, bf16[512,128]{1,0:T(8,128)(2,1)S(1)}, u32[]{:S(2)}, u32[]{:S(2)}) %collective-permute-start.11) | collective-permute-done | bytes 131104 | tf_op jit(solution)/shard_map/ppermute | solution.py:201
  37.2 1.0 collective-permute-done.10.refs_3_.refs_5_
  38.2 0.1 pack.12
  38.3 0.6 collective-permute-start.14
  39.0 1.5 %collective-permute-start.15 = (bf16[160,1280]{1,0:T(8,128)(2,1)S(1)}, bf16[160,1280]{1,0:T(8,128)(2,1)S(1)}, u32[]{:S(2)}, u32[]{:S(2)}) collective-permute-start(bf16[160,1280]{1,0:T(8,128)(2,1)S(1)} %get-tuple-element.40), channel_id=1, source_target_pairs={{0,4},{2,6},{8,0},{10,2},{16,8},{18,10},{24,16},{26,18},{28,24},{3... | collective-permute-start | bytes 1228808 | tf_op jit(solution)/shard_map/ppermute | solution.py:201
  40.4 1.9 %collective-permute-start.7 = (bf16[128,1280]{1,0:T(8,128)(2,1)S(1)}, bf16[128,1280]{1,0:T(8,128)(2,1)S(1)}, u32[]{:S(2)}, u32[]{:S(2)}) collective-permute-start(bf16[128,1280]{1,0:T(8,128)(2,1)S(1)} %pack.10), channel_id=1, source_target_pairs={{0,2},{2,0},{8,10},{10,8},{16,18},{18,16},{24,26},{26,24},{28,30},... | collective-permute-start | bytes 983048 | tf_op jit(solution)/shard_map/ppermute | solution.py:201
  42.3 0.2 collective-permute-start.13
  42.5 8.6 %collective-permute-done.7.refs_2_.refs_16_ = bf16[128,1280]{1,0:T(8,128)(2,1)S(1)} collective-permute-done((bf16[128,1280]{1,0:T(8,128)(2,1)S(1)}, bf16[128,1280]{1,0:T(8,128)(2,1)S(1)}, u32[]{:S(2)}, u32[]{:S(2)}) %collective-permute-start.7) | collective-permute-done | bytes 327712 | tf_op jit(solution)/shard_map/ppermute | solution.py:201
  51.2 1.5 %collective-permute-start.16 = (bf16[64,1280]{1,0:T(8,128)(2,1)S(1)}, bf16[64,1280]{1,0:T(8,128)(2,1)S(1)}, u32[]{:S(2)}, u32[]{:S(2)}) collective-permute-start(bf16[64,1280]{1,0:T(8,128)(2,1)S(1)} %get-tuple-element.41), channel_id=1, source_target_pairs={{0,2},{2,0},{8,10},{10,8},{16,18},{18,16},{24,26},{26,24},{28,30},... | collective-permute-start | bytes 491528 | tf_op jit(solution)/shard_map/ppermute | solution.py:201
  52.7 0.5 collective-permute-start.17
  53.2 1.5 %collective-permute-start.18 = (bf16[64,1280]{1,0:T(8,128)(2,1)S(1)}, bf16[64,1280]{1,0:T(8,128)(2,1)S(1)}, u32[]{:S(2)}, u32[]{:S(2)}) collective-permute-start(bf16[64,1280]{1,0:T(8,128)(2,1)S(1)} %get-tuple-element.43), channel_id=1, source_target_pairs={{0,4},{2,6},{8,0},{10,2},{16,8},{18,10},{24,16},{26,18},{28,24},{3... | collective-permute-start | bytes 491528 | tf_op jit(solution)/shard_map/ppermute | solution.py:201
  54.7 1.0 pack.14
  55.8 0.7 copy-done.17
  56.5 0.5 collective-permute-start.19
  57.0 1.5 %collective-permute-start.21 = (bf16[1536,128]{1,0:T(8,128)(2,1)}, bf16[1536,128]{1,0:T(8,128)(2,1)}, u32[]{:S(2)}, u32[]{:S(2)}) collective-permute-start(bf16[1536,128]{1,0:T(8,128)(2,1)} %get-tuple-element.49), channel_id=1, source_target_pairs={{0,4},{2,6},{8,0},{10,2},{16,8},{18,10},{24,16},{26,18},{28,24},{3... | collective-permute-start | bytes 1179656 | tf_op jit(solution)/shard_map/ppermute | solution.py:201
  58.6 6.7 %project.1 = (bf16[512,128]{1,0:T(8,128)(2,1)}, bf16[512,128]{1,0:T(8,128)(2,1)}, bf16[512,1024]{1,0:T(8,128)(2,1)}, bf16[8,160,128]{2,1,0:T(8,128)(2,1)S(1)}) custom-call(s32[2]{0:T(128)S(1)} %pad_add_fusion.refs_0_.info, s32[4]{0:T(128)S(1)} %copy-done.14, bf16[512,2048]{1,0:T(8,128)(2,1)S(1)} %turn.1.refs_3_.refs_2_, ...), custom_call_target="tpu_custom_call" | custom-call | flops 671088640 | bytes 1310720 | tf_op jit(solution)/shard_map/project/pallas_call | solution.py:547
  65.3 0.7 copy-done.7
  66.0 4.9 %all-to-all-start = ((bf16[16,80,128]{2,1,0:T(8,128)(2,1)}), bf16[16,80,128]{2,1,0:T(8,128)(2,1)S(1)}, u32[]{:S(2)}, u32[]{:S(2)}) async-start(bf16[16,80,128]{2,1,0:T(8,128)(2,1)} %bitcast.6), calls=%async_computation | async-start | bytes 655360 | tf_op jit(solution)/shard_map/all_to_all | solution.py:624
  70.9 1.9 %collective-permute-start.23 = (bf16[1536,128]{1,0:T(8,128)(2,1)}, bf16[1536,128]{1,0:T(8,128)(2,1)S(1)}, u32[]{:S(2)}, u32[]{:S(2)}) collective-permute-start(bf16[1536,128]{1,0:T(8,128)(2,1)} %copy-done.17), channel_id=1, source_target_pairs={{0,2},{2,0},{8,10},{10,8},{16,18},{18,16},{24,26},{26,24},{28,30},... | collective-permute-start | bytes 1179656 | tf_op jit(solution)/shard_map/ppermute | solution.py:201
  72.9 1.5 %collective-permute-start.20 = (bf16[1536,128]{1,0:T(8,128)(2,1)}, bf16[1536,128]{1,0:T(8,128)(2,1)S(1)}, u32[]{:S(2)}, u32[]{:S(2)}) collective-permute-start(bf16[1536,128]{1,0:T(8,128)(2,1)} %collective-permute-done.19.refs_0_.refs_8_), channel_id=1, source_target_pairs={{0,8},{2,10},{8,16},{10,18},{16,24},{18,26},{24,28},{26,30},{28,20... | collective-permute-start | bytes 1179656 | tf_op jit(solution)/shard_map/ppermute | solution.py:201
  74.3 0.6 collective-permute-start.22
  74.9 4.6 %within.1.refs_2_ = bf16[512,1024]{1,0:T(8,128)(2,1)S(1)} custom-call(s32[2]{0:T(128)S(1)} %pad_add_fusion.refs_0_.info, s32[4]{0:T(128)S(1)} %copy-done.14, bf16[512,128]{1,0:T(8,128)(2,1)} %get-tuple-element.44.refs_2_.refs_3_, bf16[512,128]{1,0:T(8,128)(2,1)} %get-tuple-element.45.refs_3_, bf16[512,1024]{1,0:T(8,128)(2,1)} %get-tuple-element.46.refs_4_), custom_call_target="tpu_custom_call" | custom-call | flops 3221225472 | bytes 12582912 | tf_op jit(solution)/shard_map/within/pallas_call | solution.py:547
  79.5 0.5 all-to-all-done.refs_1_
  80.0 1.4 %mix.1 = bf16[16,80,128]{2,1,0:T(8,128)(2,1)} custom-call(s32[4]{0:T(128)S(1)} %copy-done.14, bf16[16,80,128]{2,1,0:T(8,128)(2,1)S(1)} %all-to-all-done.refs_1_, bf16[512,1024]{1,0:T(8,128)(2,1)S(1)} %within.1.refs_2_), custom_call_target="tpu_custom_call" | custom-call | bytes 655360 | tf_op jit(solution)/shard_map/mix/pallas_call | solution.py:547
  81.4 5.1 %all-to-all-start.1 = ((bf16[16,80,128]{2,1,0:T(8,128)(2,1)}), bf16[16,80,128]{2,1,0:T(8,128)(2,1)S(1)}, u32[]{:S(2)}, u32[]{:S(2)}) async-start(bf16[16,80,128]{2,1,0:T(8,128)(2,1)} %mix.1), calls=%async_computation.1 | async-start | bytes 655360 | tf_op jit(solution)/shard_map/all_to_all | solution.py:635
  86.5 1.0 pack.15
  87.5 1.9 %collective-permute-start.24 = (bf16[1280,128]{1,0:T(8,128)(2,1)}, bf16[1280,128]{1,0:T(8,128)(2,1)S(1)}, u32[]{:S(2)}, u32[]{:S(2)}) collective-permute-start(bf16[1280,128]{1,0:T(8,128)(2,1)} %get-tuple-element.51), channel_id=1, source_target_pairs={{0,8},{2,10},{8,16},{10,18},{16,24},{18,26},{24,28},{26,30},{28,20... | collective-permute-start | bytes 983048 | tf_op jit(solution)/shard_map/ppermute | solution.py:201
  89.5 0.1 collective-permute-start.25
  89.6 1.8 %pack.16 = bf16[1024,128]{1,0:T(8,128)(2,1)} custom-call(bf16[1536,128]{1,0:T(8,128)(2,1)} %collective-permute-done.19.refs_0_.refs_8_, bf16[1536,128]{1,0:T(8,128)(2,1)} %collective-permute-done.21.refs_1_.refs_9_), custom_call_target="tpu_custom_call" | custom-call | tf_op jit(solution)/shard_map/pack/pallas_call | solution.py:214
  91.4 1.9 %collective-permute-start.26 = (bf16[1024,128]{1,0:T(8,128)(2,1)}, bf16[1024,128]{1,0:T(8,128)(2,1)}, u32[]{:S(2)}, u32[]{:S(2)}) collective-permute-start(bf16[1024,128]{1,0:T(8,128)(2,1)} %pack.16), channel_id=1, source_target_pairs={{0,2},{2,0},{8,10},{10,8},{16,18},{18,16},{24,26},{26,24},{28,30},... | collective-permute-start | bytes 786440 | tf_op jit(solution)/shard_map/ppermute | solution.py:201
  93.3 0.1 collective-permute-start.30
  93.4 2.2 %all-to-all-done.1 = bf16[16,80,128]{2,1,0:T(8,128)(2,1)S(1)} async-done(((bf16[16,80,128]{2,1,0:T(8,128)(2,1)}), bf16[16,80,128]{2,1,0:T(8,128)(2,1)S(1)}, u32[]{:S(2)}, u32[]{:S(2)}) %all-to-all-start.1) | async-done | bytes 327712 | tf_op jit(solution)/shard_map/all_to_all | solution.py:635
  95.7 3.8 %finish.1.refs_3_.refs_1_.normed = bf16[512,1024]{1,0:T(8,128)(2,1)S(1)} custom-call(s32[2]{0:T(128)S(1)} %pad_add_fusion.refs_0_.info, s32[4]{0:T(128)S(1)} %copy-done.14, bf16[512,1024]{1,0:T(8,128)(2,1)S(1)} %within.1.refs_2_, bf16[512,128]{1,0:T(8,128)(2,1)} %get-tuple-element.44.refs_2_.refs_3_, bf16[8,160,128]{2,1,0:T(8,128)(2,1)S(1)} %bitcast.5, ...), custom_call_target="tpu_custom_call" | custom-call | flops 167772160 | bytes 4194304 | tf_op jit(solution)/shard_map/finish/pallas_call | solution.py:547
  99.5 1.6 %collective-permute-start.27 = (bf16[512,128]{1,0:T(8,128)(2,1)S(1)}, bf16[512,128]{1,0:T(8,128)(2,1)S(1)}, u32[]{:S(2)}, u32[]{:S(2)}) collective-permute-start(bf16[512,128]{1,0:T(8,128)(2,1)S(1)} %get-tuple-element.53), channel_id=1, source_target_pairs={{0,2},{2,0},{8,10},{10,8},{16,18},{18,16},{24,26},{26,24},{28,30},... | collective-permute-start | bytes 393224 | tf_op jit(solution)/shard_map/ppermute | solution.py:201
  101.1 0.5 collective-permute-start.28
  101.6 1.6 %collective-permute-start.29 = (bf16[512,128]{1,0:T(8,128)(2,1)S(1)}, bf16[512,128]{1,0:T(8,128)(2,1)S(1)}, u32[]{:S(2)}, u32[]{:S(2)}) collective-permute-start(bf16[512,128]{1,0:T(8,128)(2,1)S(1)} %get-tuple-element.55), channel_id=1, source_target_pairs={{0,4},{2,6},{8,0},{10,2},{16,8},{18,10},{24,16},{26,18},{28,24},{3... | collective-permute-start | bytes 393224 | tf_op jit(solution)/shard_map/ppermute | solution.py:201
  103.2 3.5 %out.1.refs_5_ = bf16[16,512,128]{2,1,0:T(8,128)(2,1)S(1)} custom-call(s32[2]{0:T(128)S(1)} %pad_add_fusion.refs_0_.info, bf16[512,1024]{1,0:T(8,128)(2,1)S(1)} %finish.1.refs_3_.refs_1_.normed, bf16[512,128]{1,0:T(8,128)(2,1)S(1)} %copy-done.10, bf16[512,128]{1,0:T(8,128)(2,1)S(1)} %copy-done.12, ...), custom_call_target="tpu_custom_call" | custom-call | flops 2147483648 | bytes 4194304 | tf_op jit(solution)/shard_map/out/pallas_call | solution.py:547
  106.7 1.3 %last.1.refs_0_ = bf16[16,512,128]{2,1,0:T(8,128)(2,1)S(1)} custom-call(s32[2]{0:T(128)S(1)} %pad_add_fusion.refs_0_.info, bf16[512,1024]{1,0:T(8,128)(2,1)S(1)} %finish.1.refs_3_.refs_1_.normed, bf16[1280,128]{1,0:T(8,128)(2,1)S(1)} %collective-permute-done.24.refs_0_.refs_14_, ...), custom_call_target="tpu_custom_call", output_to_operand_aliasing={{}: (7, {})} | custom-call | tf_op jit(solution)/shard_map/last/pallas_call | solution.py:652
  108.1 0.1 slice.4
  108.2 0.1 collective-permute-start.31
  108.2 2.6 %collective-permute-done.31.refs_1_ = bf16[8,512,128]{2,1,0:T(8,128)(2,1)S(1)} collective-permute-done((bf16[8,512,128]{2,1,0:T(8,128)(2,1)S(1)}, bf16[8,512,128]{2,1,0:T(8,128)(2,1)S(1)}, u32[]{:S(2)}, u32[]{:S(2)}) %collective-permute-start.31) | collective-permute-done | bytes 1048608 | tf_op jit(solution)/shard_map/ppermute | solution.py:665
  110.9 1.3 %add.3 = bf16[512,1024]{1,0:T(8,128)(2,1)} custom-call(bf16[16,512,128]{2,1,0:T(8,128)(2,1)S(1)} %last.1.refs_0_, bf16[8,512,128]{2,1,0:T(8,128)(2,1)S(1)} %collective-permute-done.31.refs_1_), custom_call_target="tpu_custom_call" | custom-call | bytes 4194304 | tf_op jit(solution)/shard_map/add/pallas_call | solution.py:547
  (61 shorter events, 0.2 us)
Async XLA Ops:
  1.1 7.2 %collective-permute-start.1 = (bf16[64,1280]{1,0:T(8,128)(2,1)S(1)}, bf16[64,1280]{1,0:T(8,128)(2,1)S(1)}, u32[]{:S(2)}, u32[]{:S(2)}) collective-permute-start(bf16[64,1280]{1,0:T(8,128)(2,1)S(1)} %get-tuple-element.32.refs_1_.refs_9_), channel_id=1, source_target_pairs={{0,2},{2,0},{8,10},{10,8},{16,18},{18,16},{24,26},{26,24},{28,30},... | collective-permute-start | bytes 491528 | tf_op jit(solution)/shard_map/ppermute | solution.py:201
  4.1 5.7 %collective-permute-start.3 = (bf16[64,1280]{1,0:T(8,128)(2,1)S(1)}, bf16[64,1280]{1,0:T(8,128)(2,1)S(1)}, u32[]{:S(2)}, u32[]{:S(2)}) collective-permute-start(bf16[64,1280]{1,0:T(8,128)(2,1)S(1)} %get-tuple-element.31.refs_0_.refs_8_), channel_id=1, source_target_pairs={{0,4},{2,6},{8,0},{10,2},{16,8},{18,10},{24,16},{26,18},{28,24},{3... | collective-permute-start | bytes 491528 | tf_op jit(solution)/shard_map/ppermute | solution.py:201
  5.6 5.4 %collective-permute-start.2 = (bf16[64,1280]{1,0:T(8,128)(2,1)S(1)}, bf16[64,1280]{1,0:T(8,128)(2,1)S(1)}, u32[]{:S(2)}, u32[]{:S(2)}) collective-permute-start(bf16[64,1280]{1,0:T(8,128)(2,1)S(1)} %get-tuple-element.31.refs_0_.refs_8_), channel_id=1, source_target_pairs={{0,8},{2,10},{8,16},{10,18},{16,24},{18,26},{24,28},{26,30},{28,20... | collective-permute-start | bytes 491528 | tf_op jit(solution)/shard_map/ppermute | solution.py:201
  11.8 11.5 %collective-permute-start.5 = (bf16[192,1280]{1,0:T(8,128)(2,1)S(1)}, bf16[192,1280]{1,0:T(8,128)(2,1)S(1)}, u32[]{:S(2)}, u32[]{:S(2)}) collective-permute-start(bf16[192,1280]{1,0:T(8,128)(2,1)S(1)} %get-tuple-element.34), channel_id=1, source_target_pairs={{0,8},{2,10},{8,16},{10,18},{16,24},{18,26},{24,28},{26,30},{28,20... | collective-permute-start | bytes 1474568 | tf_op jit(solution)/shard_map/ppermute | solution.py:201
  12.3 11.6 %collective-permute-start.6 = (bf16[192,1280]{1,0:T(8,128)(2,1)S(1)}, bf16[192,1280]{1,0:T(8,128)(2,1)S(1)}, u32[]{:S(2)}, u32[]{:S(2)}) collective-permute-start(bf16[192,1280]{1,0:T(8,128)(2,1)S(1)} %get-tuple-element.35), channel_id=1, source_target_pairs={{0,4},{2,6},{8,0},{10,2},{16,8},{18,10},{24,16},{26,18},{28,24},{3... | collective-permute-start | bytes 1474568 | tf_op jit(solution)/shard_map/ppermute | solution.py:201
  13.9 14.4 %collective-permute-start = (bf16[2048,128]{1,0:T(8,128)(2,1)}, bf16[2048,128]{1,0:T(8,128)(2,1)}, u32[]{:S(2)}, u32[]{:S(2)}) collective-permute-start(bf16[2048,128]{1,0:T(8,128)(2,1)} %refs_4_.2), channel_id=1, source_target_pairs={{0,1},{1,0},{2,3},{3,2},{4,5},{5,4},{6,7},{7,6},{8,9},{9,8},{10,11... | collective-permute-start | bytes 1572872 | tf_op jit(solution)/shard_map/ppermute | solution.py:585
  13.9 19.1 %collective-permute-start.4 = (bf16[192,1280]{1,0:T(8,128)(2,1)}, bf16[192,1280]{1,0:T(8,128)(2,1)S(1)}, u32[]{:S(2)}, u32[]{:S(2)}) collective-permute-start(bf16[192,1280]{1,0:T(8,128)(2,1)} %get-tuple-element.33), channel_id=1, source_target_pairs={{0,2},{2,0},{8,10},{10,8},{16,18},{18,16},{24,26},{26,24},{28,30},... | collective-permute-start | bytes 1474568 | tf_op jit(solution)/shard_map/ppermute | solution.py:201
  23.3 14.9 %collective-permute-start.8 = (bf16[192,1280]{1,0:T(8,128)(2,1)S(1)}, bf16[192,1280]{1,0:T(8,128)(2,1)S(1)}, u32[]{:S(2)}, u32[]{:S(2)}) collective-permute-start(bf16[192,1280]{1,0:T(8,128)(2,1)S(1)} %collective-permute-done.5.refs_0_.refs_1_.refs_14_), channel_id=1, source_target_pairs={{0,8},{2,10},{8,16},{10,18},{16,24},{18,26},{24,28},{26,30},{28,20... | collective-permute-start | bytes 1474568 | tf_op jit(solution)/shard_map/ppermute | solution.py:201
  24.0 14.2 %collective-permute-start.9 = (bf16[192,1280]{1,0:T(8,128)(2,1)S(1)}, bf16[192,1280]{1,0:T(8,128)(2,1)S(1)}, u32[]{:S(2)}, u32[]{:S(2)}) collective-permute-start(bf16[192,1280]{1,0:T(8,128)(2,1)S(1)} %collective-permute-done.6.refs_1_.refs_2_.refs_15_), channel_id=1, source_target_pairs={{0,4},{2,6},{8,0},{10,2},{16,8},{18,10},{24,16},{26,18},{28,24},{3... | collective-permute-start | bytes 1474568 | tf_op jit(solution)/shard_map/ppermute | solution.py:201
  25.4 1.6 %copy-start = (bf16[512,2048]{1,0:T(8,128)(2,1)S(1)}, bf16[512,2048]{1,0:T(8,128)(2,1)}, u32[]{:S(2)}) copy-start(bf16[512,2048]{1,0:T(8,128)(2,1)} %refs_3_.1) | copy-start | bytes 6291460
  27.0 1.2 %copy-start.4 = (bf16[2048,128]{1,0:T(8,128)(2,1)S(1)}, bf16[2048,128]{1,0:T(8,128)(2,1)}, u32[]{:S(2)}) copy-start(bf16[2048,128]{1,0:T(8,128)(2,1)} %refs_4_.2) | copy-start | bytes 1572868
  27.0 1.3 %copy-start.14 = (s32[4]{0:T(128)S(1)}, s32[4]{0:T(128)}, u32[]{:S(2)}) copy-start(s32[4]{0:T(128)} %refs_1_.9) | copy-start | bytes 52
  27.0 1.3 %copy-start.16 = (s32[4]{0:T(128)S(1)}, s32[4]{0:T(128)}, u32[]{:S(2)}) copy-start(s32[4]{0:T(128)} %refs_2_.1) | copy-start | bytes 52
  28.2 2.4 %copy-start.8 = (bf16[1024,128]{1,0:T(8,128)(2,1)S(1)}, bf16[1024,128]{1,0:T(8,128)(2,1)}, u32[]{:S(2)}) copy-start(bf16[1024,128]{1,0:T(8,128)(2,1)} %refs_0_.2) | copy-start | bytes 786436
  30.7 24.0 %copy-start.9 = (bf16[512,128]{1,0:T(8,128)(2,1)}, bf16[512,128]{1,0:T(8,128)(2,1)S(1)}, u32[]{:S(2)}) copy-start(bf16[512,128]{1,0:T(8,128)(2,1)S(1)} %get-tuple-element.36.refs_0_.refs_2_) | copy-start | bytes 393220
  30.7 24.0 %copy-start.11 = (bf16[512,128]{1,0:T(8,128)(2,1)}, bf16[512,128]{1,0:T(8,128)(2,1)S(1)}, u32[]{:S(2)}) copy-start(bf16[512,128]{1,0:T(8,128)(2,1)S(1)} %get-tuple-element.37.refs_1_.refs_3_) | copy-start | bytes 393220
  30.8 5.0 %collective-permute-start.12 = (bf16[512,128]{1,0:T(8,128)(2,1)S(1)}, bf16[512,128]{1,0:T(8,128)(2,1)S(1)}, u32[]{:S(2)}, u32[]{:S(2)}) collective-permute-start(bf16[512,128]{1,0:T(8,128)(2,1)S(1)} %get-tuple-element.37.refs_1_.refs_3_), channel_id=1, source_target_pairs={{0,2},{2,0},{8,10},{10,8},{16,18},{18,16},{24,26},{26,24},{28,30},... | collective-permute-start | bytes 393224 | tf_op jit(solution)/shard_map/ppermute | solution.py:201
  31.3 5.9 %collective-permute-start.11 = (bf16[512,128]{1,0:T(8,128)(2,1)S(1)}, bf16[512,128]{1,0:T(8,128)(2,1)S(1)}, u32[]{:S(2)}, u32[]{:S(2)}) collective-permute-start(bf16[512,128]{1,0:T(8,128)(2,1)S(1)} %get-tuple-element.36.refs_0_.refs_2_), channel_id=1, source_target_pairs={{0,4},{2,6},{8,0},{10,2},{16,8},{18,10},{24,16},{26,18},{28,24},{3... | collective-permute-start | bytes 393224 | tf_op jit(solution)/shard_map/ppermute | solution.py:201
  33.0 5.2 %collective-permute-start.10 = (bf16[512,128]{1,0:T(8,128)(2,1)S(1)}, bf16[512,128]{1,0:T(8,128)(2,1)S(1)}, u32[]{:S(2)}, u32[]{:S(2)}) collective-permute-start(bf16[512,128]{1,0:T(8,128)(2,1)S(1)} %get-tuple-element.36.refs_0_.refs_2_), channel_id=1, source_target_pairs={{0,8},{2,10},{8,16},{10,18},{16,24},{18,26},{24,28},{26,30},{28,20... | collective-permute-start | bytes 393224 | tf_op jit(solution)/shard_map/ppermute | solution.py:201
  38.2 16.6 %copy-start.1 = (bf16[512,128]{1,0:T(8,128)(2,1)}, bf16[512,128]{1,0:T(8,128)(2,1)S(1)}, u32[]{:S(2)}) copy-start(bf16[512,128]{1,0:T(8,128)(2,1)S(1)} %collective-permute-done.10.refs_3_.refs_5_) | copy-start | bytes 393220
  38.3 20.3 %copy-start.3 = (bf16[256,1024]{1,0:T(8,128)(2,1)S(1)}, bf16[256,1024]{1,0:T(8,128)(2,1)}, u32[]{:S(2)}) copy-start(bf16[256,1024]{1,0:T(8,128)(2,1)} %refs_4_.3) | copy-start | bytes 1572868
  38.3 20.3 %copy-start.5 = (f32[160,128]{1,0:T(8,128)S(1)}, f32[160,128]{1,0:T(8,128)}, u32[]{:S(2)}) copy-start(f32[160,128]{1,0:T(8,128)} %constant.15.clone.refs_6_.refs_7_) | copy-start | bytes 245764
  38.3 20.3 %copy-start.6 = (f32[160,128]{1,0:T(8,128)S(1)}, f32[160,128]{1,0:T(8,128)}, u32[]{:S(2)}) copy-start(f32[160,128]{1,0:T(8,128)} %constant.14.clone.refs_5_.refs_6_) | copy-start | bytes 245764
  38.3 20.3 %copy-start.13 = (f32[160,8]{1,0:T(8,128)S(1)}, f32[160,8]{1,0:T(8,128)}, u32[]{:S(2)}) copy-start(f32[160,8]{1,0:T(8,128)} %constant.17.refs_7_) | copy-start | bytes 15364
  38.3 12.8 %collective-permute-start.14 = (bf16[160,1280]{1,0:T(8,128)(2,1)S(1)}, bf16[160,1280]{1,0:T(8,128)(2,1)S(1)}, u32[]{:S(2)}, u32[]{:S(2)}) collective-permute-start(bf16[160,1280]{1,0:T(8,128)(2,1)S(1)} %get-tuple-element.39), channel_id=1, source_target_pairs={{0,8},{2,10},{8,16},{10,18},{16,24},{18,26},{24,28},{26,30},{28,20... | collective-permute-start | bytes 1228808 | tf_op jit(solution)/shard_map/ppermute | solution.py:201
  39.0 12.2 %collective-permute-start.15 = (bf16[160,1280]{1,0:T(8,128)(2,1)S(1)}, bf16[160,1280]{1,0:T(8,128)(2,1)S(1)}, u32[]{:S(2)}, u32[]{:S(2)}) collective-permute-start(bf16[160,1280]{1,0:T(8,128)(2,1)S(1)} %get-tuple-element.40), channel_id=1, source_target_pairs={{0,4},{2,6},{8,0},{10,2},{16,8},{18,10},{24,16},{26,18},{28,24},{3... | collective-permute-start | bytes 1228808 | tf_op jit(solution)/shard_map/ppermute | solution.py:201
  40.4 10.7 %collective-permute-start.7 = (bf16[128,1280]{1,0:T(8,128)(2,1)S(1)}, bf16[128,1280]{1,0:T(8,128)(2,1)S(1)}, u32[]{:S(2)}, u32[]{:S(2)}) collective-permute-start(bf16[128,1280]{1,0:T(8,128)(2,1)S(1)} %pack.10), channel_id=1, source_target_pairs={{0,2},{2,0},{8,10},{10,8},{16,18},{18,16},{24,26},{26,24},{28,30},... | collective-permute-start | bytes 983048 | tf_op jit(solution)/shard_map/ppermute | solution.py:201
  42.3 14.7 %collective-permute-start.13 = (bf16[128,1280]{1,0:T(8,128)(2,1)S(1)}, bf16[128,1280]{1,0:T(8,128)(2,1)S(1)}, u32[]{:S(2)}, u32[]{:S(2)}) collective-permute-start(bf16[128,1280]{1,0:T(8,128)(2,1)S(1)} %get-tuple-element.38), channel_id=1, source_target_pairs={{0,2},{2,0},{8,10},{10,8},{16,18},{18,16},{24,26},{26,24},{28,30},... | collective-permute-start | bytes 983048 | tf_op jit(solution)/shard_map/ppermute | solution.py:201
  51.2 7.3 %collective-permute-start.16 = (bf16[64,1280]{1,0:T(8,128)(2,1)S(1)}, bf16[64,1280]{1,0:T(8,128)(2,1)S(1)}, u32[]{:S(2)}, u32[]{:S(2)}) collective-permute-start(bf16[64,1280]{1,0:T(8,128)(2,1)S(1)} %get-tuple-element.41), channel_id=1, source_target_pairs={{0,2},{2,0},{8,10},{10,8},{16,18},{18,16},{24,26},{26,24},{28,30},... | collective-permute-start | bytes 491528 | tf_op jit(solution)/shard_map/ppermute | solution.py:201
  52.7 5.8 %collective-permute-start.17 = (bf16[64,1280]{1,0:T(8,128)(2,1)S(1)}, bf16[64,1280]{1,0:T(8,128)(2,1)S(1)}, u32[]{:S(2)}, u32[]{:S(2)}) collective-permute-start(bf16[64,1280]{1,0:T(8,128)(2,1)S(1)} %get-tuple-element.42), channel_id=1, source_target_pairs={{0,8},{2,10},{8,16},{10,18},{16,24},{18,26},{24,28},{26,30},{28,20... | collective-permute-start | bytes 491528 | tf_op jit(solution)/shard_map/ppermute | solution.py:201
  53.2 5.4 %collective-permute-start.18 = (bf16[64,1280]{1,0:T(8,128)(2,1)S(1)}, bf16[64,1280]{1,0:T(8,128)(2,1)S(1)}, u32[]{:S(2)}, u32[]{:S(2)}) collective-permute-start(bf16[64,1280]{1,0:T(8,128)(2,1)S(1)} %get-tuple-element.43), channel_id=1, source_target_pairs={{0,4},{2,6},{8,0},{10,2},{16,8},{18,10},{24,16},{26,18},{28,24},{3... | collective-permute-start | bytes 491528 | tf_op jit(solution)/shard_map/ppermute | solution.py:201
  55.7 0.7 copy-start.17
  56.5 16.4 %collective-permute-start.19 = (bf16[1536,128]{1,0:T(8,128)(2,1)}, bf16[1536,128]{1,0:T(8,128)(2,1)}, u32[]{:S(2)}, u32[]{:S(2)}) collective-permute-start(bf16[1536,128]{1,0:T(8,128)(2,1)} %get-tuple-element.48), channel_id=1, source_target_pairs={{0,8},{2,10},{8,16},{10,18},{16,24},{18,26},{24,28},{26,30},{28,20... | collective-permute-start | bytes 1179656 | tf_op jit(solution)/shard_map/ppermute | solution.py:201
  57.0 17.3 %collective-permute-start.21 = (bf16[1536,128]{1,0:T(8,128)(2,1)}, bf16[1536,128]{1,0:T(8,128)(2,1)}, u32[]{:S(2)}, u32[]{:S(2)}) collective-permute-start(bf16[1536,128]{1,0:T(8,128)(2,1)} %get-tuple-element.49), channel_id=1, source_target_pairs={{0,4},{2,6},{8,0},{10,2},{16,8},{18,10},{24,16},{26,18},{28,24},{3... | collective-permute-start | bytes 1179656 | tf_op jit(solution)/shard_map/ppermute | solution.py:201
  65.3 0.7 copy-start.7
  66.0 13.9 %all-to-all-start = ((bf16[16,80,128]{2,1,0:T(8,128)(2,1)}), bf16[16,80,128]{2,1,0:T(8,128)(2,1)S(1)}, u32[]{:S(2)}, u32[]{:S(2)}) async-start(bf16[16,80,128]{2,1,0:T(8,128)(2,1)} %bitcast.6), calls=%async_computation | async-start | bytes 655360 | tf_op jit(solution)/shard_map/all_to_all | solution.py:624
  70.9 15.6 %collective-permute-start.23 = (bf16[1536,128]{1,0:T(8,128)(2,1)}, bf16[1536,128]{1,0:T(8,128)(2,1)S(1)}, u32[]{:S(2)}, u32[]{:S(2)}) collective-permute-start(bf16[1536,128]{1,0:T(8,128)(2,1)} %copy-done.17), channel_id=1, source_target_pairs={{0,2},{2,0},{8,10},{10,8},{16,18},{18,16},{24,26},{26,24},{28,30},... | collective-permute-start | bytes 1179656 | tf_op jit(solution)/shard_map/ppermute | solution.py:201
  72.9 13.6 %collective-permute-start.20 = (bf16[1536,128]{1,0:T(8,128)(2,1)}, bf16[1536,128]{1,0:T(8,128)(2,1)S(1)}, u32[]{:S(2)}, u32[]{:S(2)}) collective-permute-start(bf16[1536,128]{1,0:T(8,128)(2,1)} %collective-permute-done.19.refs_0_.refs_8_), channel_id=1, source_target_pairs={{0,8},{2,10},{8,16},{10,18},{16,24},{18,26},{24,28},{26,30},{28,20... | collective-permute-start | bytes 1179656 | tf_op jit(solution)/shard_map/ppermute | solution.py:201
  74.3 12.2 %collective-permute-start.22 = (bf16[1536,128]{1,0:T(8,128)(2,1)}, bf16[1536,128]{1,0:T(8,128)(2,1)S(1)}, u32[]{:S(2)}, u32[]{:S(2)}) collective-permute-start(bf16[1536,128]{1,0:T(8,128)(2,1)} %collective-permute-done.21.refs_1_.refs_9_), channel_id=1, source_target_pairs={{0,4},{2,6},{8,0},{10,2},{16,8},{18,10},{24,16},{26,18},{28,24},{3... | collective-permute-start | bytes 1179656 | tf_op jit(solution)/shard_map/ppermute | solution.py:201
  79.5 16.2 %copy-start.15 = (f32[1024]{0:T(1024)S(1)}, f32[1024]{0:T(1024)}, u32[]{:S(2)}) copy-start(f32[1024]{0:T(1024)} %param.21) | copy-start | bytes 12292
  81.4 14.3 %all-to-all-start.1 = ((bf16[16,80,128]{2,1,0:T(8,128)(2,1)}), bf16[16,80,128]{2,1,0:T(8,128)(2,1)S(1)}, u32[]{:S(2)}, u32[]{:S(2)}) async-start(bf16[16,80,128]{2,1,0:T(8,128)(2,1)} %mix.1), calls=%async_computation.1 | async-start | bytes 655360 | tf_op jit(solution)/shard_map/all_to_all | solution.py:635
  87.5 11.9 %collective-permute-start.24 = (bf16[1280,128]{1,0:T(8,128)(2,1)}, bf16[1280,128]{1,0:T(8,128)(2,1)S(1)}, u32[]{:S(2)}, u32[]{:S(2)}) collective-permute-start(bf16[1280,128]{1,0:T(8,128)(2,1)} %get-tuple-element.51), channel_id=1, source_target_pairs={{0,8},{2,10},{8,16},{10,18},{16,24},{18,26},{24,28},{26,30},{28,20... | collective-permute-start | bytes 983048 | tf_op jit(solution)/shard_map/ppermute | solution.py:201
  89.5 10.0 %collective-permute-start.25 = (bf16[1280,128]{1,0:T(8,128)(2,1)}, bf16[1280,128]{1,0:T(8,128)(2,1)S(1)}, u32[]{:S(2)}, u32[]{:S(2)}) collective-permute-start(bf16[1280,128]{1,0:T(8,128)(2,1)} %get-tuple-element.52), channel_id=1, source_target_pairs={{0,4},{2,6},{8,0},{10,2},{16,8},{18,10},{24,16},{26,18},{28,24},{3... | collective-permute-start | bytes 983048 | tf_op jit(solution)/shard_map/ppermute | solution.py:201
  91.4 8.1 %collective-permute-start.26 = (bf16[1024,128]{1,0:T(8,128)(2,1)}, bf16[1024,128]{1,0:T(8,128)(2,1)}, u32[]{:S(2)}, u32[]{:S(2)}) collective-permute-start(bf16[1024,128]{1,0:T(8,128)(2,1)} %pack.16), channel_id=1, source_target_pairs={{0,2},{2,0},{8,10},{10,8},{16,18},{18,16},{24,26},{26,24},{28,30},... | collective-permute-start | bytes 786440 | tf_op jit(solution)/shard_map/ppermute | solution.py:201
  93.3 9.9 %collective-permute-start.30 = (bf16[1024,128]{1,0:T(8,128)(2,1)}, bf16[1024,128]{1,0:T(8,128)(2,1)}, u32[]{:S(2)}, u32[]{:S(2)}) collective-permute-start(bf16[1024,128]{1,0:T(8,128)(2,1)} %get-tuple-element.56), channel_id=1, source_target_pairs={{0,2},{2,0},{8,10},{10,8},{16,18},{18,16},{24,26},{26,24},{28,30},... | collective-permute-start | bytes 786440 | tf_op jit(solution)/shard_map/ppermute | solution.py:201
  95.7 7.5 %copy-start.2 = (bf16[512,128]{1,0:T(8,128)(2,1)S(1)}, bf16[512,128]{1,0:T(8,128)(2,1)}, u32[]{:S(2)}) copy-start(bf16[512,128]{1,0:T(8,128)(2,1)} %copy-done.1) | copy-start | bytes 393220
  95.7 7.5 %copy-start.10 = (bf16[512,128]{1,0:T(8,128)(2,1)S(1)}, bf16[512,128]{1,0:T(8,128)(2,1)}, u32[]{:S(2)}) copy-start(bf16[512,128]{1,0:T(8,128)(2,1)} %copy-done.9) | copy-start | bytes 393220
  95.7 7.5 %copy-start.12 = (bf16[512,128]{1,0:T(8,128)(2,1)S(1)}, bf16[512,128]{1,0:T(8,128)(2,1)}, u32[]{:S(2)}) copy-start(bf16[512,128]{1,0:T(8,128)(2,1)} %copy-done.11) | copy-start | bytes 393220
  99.5 7.2 %collective-permute-start.27 = (bf16[512,128]{1,0:T(8,128)(2,1)S(1)}, bf16[512,128]{1,0:T(8,128)(2,1)S(1)}, u32[]{:S(2)}, u32[]{:S(2)}) collective-permute-start(bf16[512,128]{1,0:T(8,128)(2,1)S(1)} %get-tuple-element.53), channel_id=1, source_target_pairs={{0,2},{2,0},{8,10},{10,8},{16,18},{18,16},{24,26},{26,24},{28,30},... | collective-permute-start | bytes 393224 | tf_op jit(solution)/shard_map/ppermute | solution.py:201
  101.1 5.6 %collective-permute-start.28 = (bf16[512,128]{1,0:T(8,128)(2,1)S(1)}, bf16[512,128]{1,0:T(8,128)(2,1)S(1)}, u32[]{:S(2)}, u32[]{:S(2)}) collective-permute-start(bf16[512,128]{1,0:T(8,128)(2,1)S(1)} %get-tuple-element.54), channel_id=1, source_target_pairs={{0,8},{2,10},{8,16},{10,18},{16,24},{18,26},{24,28},{26,30},{28,20... | collective-permute-start | bytes 393224 | tf_op jit(solution)/shard_map/ppermute | solution.py:201
  101.6 5.1 %collective-permute-start.29 = (bf16[512,128]{1,0:T(8,128)(2,1)S(1)}, bf16[512,128]{1,0:T(8,128)(2,1)S(1)}, u32[]{:S(2)}, u32[]{:S(2)}) collective-permute-start(bf16[512,128]{1,0:T(8,128)(2,1)S(1)} %get-tuple-element.55), channel_id=1, source_target_pairs={{0,4},{2,6},{8,0},{10,2},{16,8},{18,10},{24,16},{26,18},{28,24},{3... | collective-permute-start | bytes 393224 | tf_op jit(solution)/shard_map/ppermute | solution.py:201
  108.2 2.7 %collective-permute-start.31 = (bf16[8,512,128]{2,1,0:T(8,128)(2,1)S(1)}, bf16[8,512,128]{2,1,0:T(8,128)(2,1)S(1)}, u32[]{:S(2)}, u32[]{:S(2)}) collective-permute-start(bf16[8,512,128]{2,1,0:T(8,128)(2,1)S(1)} %slice.4), channel_id=1, source_target_pairs={{0,1},{1,0},{2,3},{3,2},{4,5},{5,4},{6,7},{7,6},{8,9},{9,8},{10,11... | collective-permute-start | bytes 3145736 | tf_op jit(solution)/shard_map/ppermute | solution.py:665
